TPU v7x, 32 devices: a whole 2x2x4 slice. The times are simulated.
32 devices in a mesh: seq: 8 (over y, x, core), fsdp: 4 (over z).
Axes of the slice: x: 2, y: 2, z: 4, core: 2. Of those that a mesh axis runs over, the one named last changes fastest.
Arguments:
- tokens: bfloat16 [4, 2048, 2048], P('fsdp', 'seq'), may hold values from -6 to 6
- cotangent: bfloat16 [4, 2048, 2048], P('fsdp', 'seq'), may hold values from -6 to 6
- starts: int32 [4, 4], P('fsdp'), may hold values from 0 to 2047, as said below
- adapter_ids: int32 [4, 4], P('fsdp'), may hold values from 0 to 7
- w_qkv: bfloat16 [2048, 6144], P('fsdp'), may hold values from -0.125 to 0.125
- w_out: bfloat16 [2048, 2048], P('fsdp'), may hold values from -0.5 to 0.5
- w_gu: bfloat16 [2048, 16384], P('fsdp'), may hold values from -0.125 to 0.125
- w_down: bfloat16 [8192, 2048], P('fsdp'), may hold values from -0.0625 to 0.0625
- a_qkv: bfloat16 [2048, 384], P('fsdp'), may hold values from -0.125 to 0.125
- b_qkv: bfloat16 [384, 2048], P(None, 'fsdp'), may hold values from -1.5 to 1.5
- a_out: bfloat16 [2048, 128], P('fsdp'), may hold values from -0.125 to 0.125
- b_out: bfloat16 [128, 2048], P(None, 'fsdp'), may hold values from -6 to 6
- a_gu: bfloat16 [2048, 256], P('fsdp'), may hold values from -0.125 to 0.125
- b_gu: bfloat16 [256, 8192], P(None, 'fsdp'), may hold values from -1.5 to 1.5
- a_down: bfloat16 [8192, 128], P('fsdp'), may hold values from -0.0625 to 0.0625
- b_down: bfloat16 [128, 2048], P(None, 'fsdp'), may hold values from -1.5 to 1.5
Outputs:
- activations: float32 [4, 2048, 2048], P('fsdp', 'seq')
- input_grad: float32 [4, 2048, 2048], P('fsdp', 'seq')
- g_a_qkv: float32 [2048, 384], P('fsdp')
- g_b_qkv: float32 [384, 2048], P(None, 'fsdp')
- g_a_out: float32 [2048, 128], P('fsdp')
- g_b_out: float32 [128, 2048], P(None, 'fsdp')
- g_a_gu: float32 [2048, 256], P('fsdp')
- g_b_gu: float32 [256, 8192], P(None, 'fsdp')
- g_a_down: float32 [8192, 128], P('fsdp')
- g_b_down: float32 [128, 2048], P(None, 'fsdp')
Inputs may be any that keep to these rules, and one draw needn't show every extreme that they name: starts[f, 0] is 0 and each row rises strictly, every start a token of the stream; in every stream one document begins within the first 256 tokens and ends within the last 256.
All inputs are finite; a program needn't handle non-finite values.
Results may differ from a plain program's by a relative error of at most 0.02.
The roundings to bfloat16 on the way count: a program that leaves them out, or rounds other values in their place, can miss the bound.
Values may be sent and summed in bfloat16 or wider, within the bound.
No kernel may reach another device: no remote copies, remote signals or barrier semaphores. Data moves between devices by JAX's collectives and lax.ppermute only.
A program may use at most 384 MiB of HBM per device.

v0:
```python
import jax
import jax.numpy as jnp
from jax import lax
from jax.sharding import PartitionSpec as P

HEAD_DIM = 128
RANK = 16


def layer_norm(values):
    centre = values - jnp.mean(values, axis=-1, keepdims=True)
    spread = jnp.mean(centre * centre, axis=-1, keepdims=True)
    factor = lax.rsqrt(spread + 1e-05)
    return (centre * factor, factor)


def norm_back(normed, factor, upstream):
    upstream_mean = jnp.mean(upstream, axis=-1, keepdims=True)
    cross_mean = jnp.mean(upstream * normed, axis=-1, keepdims=True)
    return factor * (upstream - upstream_mean - normed * cross_mean)


def doc_tables(places, first, chosen):
    within = first[None, :] <= places[:, None]
    begin = jnp.max(jnp.where(within, first[None, :], 0), axis=1)
    latest = jnp.sum(within.astype(jnp.int32), axis=1) - 1
    doc_order = jnp.arange(first.shape[0], dtype=jnp.int32)
    which = jnp.sum(jnp.where(doc_order[None, :] == latest[:, None], chosen[None, :], 0), axis=1)
    return (begin, which)


def rope_tables(position, head_dim):
    freqs = 10000.0 ** (-(jnp.arange(0, head_dim, 2, dtype=jnp.float32) / head_dim))
    angles = position.astype(jnp.float32)[:, None] * freqs[None, :]
    cosine = jnp.concatenate([jnp.cos(angles), jnp.cos(angles)], axis=-1)
    sine = jnp.concatenate([jnp.sin(angles), jnp.sin(angles)], axis=-1)
    return (cosine, sine)


def rotate(values, cosine, sine):
    half_dim = values.shape[-1] // 2
    turned = jnp.concatenate([-values[..., half_dim:], values[..., :half_dim]], axis=-1)
    return values * cosine[:, None, :] + turned * sine[:, None, :]


def rotate_back(upstream, cosine, sine):
    half_dim = upstream.shape[-1] // 2
    scaled = upstream * sine[:, None, :]
    return upstream * cosine[:, None, :] + jnp.concatenate(
        [scaled[..., half_dim:], -scaled[..., :half_dim]], axis=-1
    )


def inner_rows(left, right):
    return lax.dot_general(
        left, right, (((0,), (0,)), ((), ())), preferred_element_type=jnp.float32
    )


def inner_cols(left, right):
    return lax.dot_general(
        left, right, (((1,), (1,)), ((), ())), preferred_element_type=jnp.float32
    )


def adapter_fwd(inputs, down, up, select, segments):
    latent = jnp.dot(inputs, down, preferred_element_type=jnp.float32).astype(
        jnp.bfloat16
    ) * jnp.tile(select, (1, segments))
    span = up.shape[0] // segments
    pieces = [
        jnp.dot(
            latent[:, seg * span : (seg + 1) * span],
            up[seg * span : (seg + 1) * span],
            preferred_element_type=jnp.float32,
        )
        for seg in range(segments)
    ]
    return (latent, jnp.concatenate(pieces, axis=1))


def adapter_back(inputs, latent, upstream, down, up, select, segments):
    span = up.shape[0] // segments
    out_span = up.shape[1]
    grad_up = jnp.concatenate(
        [
            inner_rows(
                latent[:, seg * span : (seg + 1) * span],
                upstream[:, seg * out_span : (seg + 1) * out_span],
            )
            for seg in range(segments)
        ],
        axis=0,
    )
    latent_grad = jnp.concatenate(
        [
            inner_cols(
                upstream[:, seg * out_span : (seg + 1) * out_span],
                up[seg * span : (seg + 1) * span],
            )
            for seg in range(segments)
        ],
        axis=1,
    )
    latent_grad = (latent_grad * jnp.tile(select, (1, segments)).astype(jnp.float32)).astype(
        jnp.bfloat16
    )
    grad_down = inner_rows(inputs, latent_grad)
    back = inner_cols(latent_grad, down)
    return (grad_down, grad_up, back)


def frozen_fwd(inputs, weight):
    return (
        jnp.dot(
            inputs,
            lax.all_gather(weight, "fsdp", axis=0, tiled=True),
            preferred_element_type=jnp.float32,
        ),
        weight,
    )


def frozen_bwd(upstream, weight):
    return inner_cols(upstream, lax.all_gather(weight, "fsdp", axis=0, tiled=True))


def attend(query_h, key_h, value_h, begin, head_dim):
    length, local_width = query_h.shape
    local_heads = local_width // head_dim
    block_rows = min(512, length)
    block_count = length // block_rows
    score_scale = head_dim ** (-0.5)
    query_all = query_h.reshape(length, local_heads, head_dim)
    key_all = key_h.reshape(length, local_heads, head_dim)
    value_all = value_h.reshape(length, local_heads, head_dim)
    key_places = jnp.arange(length, dtype=jnp.int32)

    def one_block(block_index):
        start = block_index * block_rows
        query_block = lax.dynamic_slice_in_dim(query_all, start, block_rows, 0)
        rows = start + jnp.arange(block_rows, dtype=jnp.int32)
        row_begin = lax.dynamic_slice_in_dim(begin, start, block_rows, 0)
        allowed = (key_places[None, :] <= rows[:, None]) & (
            key_places[None, :] >= row_begin[:, None]
        )
        scores = (
            jnp.einsum("qhd,khd->hqk", query_block, key_all, preferred_element_type=jnp.float32)
            * score_scale
        )
        scores = jnp.where(allowed[None], scores, -1e30)
        row_top = jnp.max(scores, axis=-1, keepdims=True)
        expd = jnp.exp(scores - row_top)
        row_total = jnp.sum(expd, axis=-1, keepdims=True)
        probs = (expd / row_total).astype(jnp.bfloat16)
        mixed = jnp.einsum("hqk,khd->qhd", probs, value_all, preferred_element_type=jnp.float32)
        return (
            mixed.astype(jnp.bfloat16).reshape(block_rows, local_width),
            (row_top + jnp.log(row_total))[..., 0],
        )

    outputs, log_sums = lax.map(one_block, jnp.arange(block_count, dtype=jnp.int32))
    return (outputs.reshape(length, local_width), log_sums)


def attend_back(query_h, key_h, value_h, grad_h, log_sums, begin, head_dim):
    length, local_width = query_h.shape
    local_heads = local_width // head_dim
    block_rows = min(512, length)
    block_count = length // block_rows
    score_scale = head_dim ** (-0.5)
    query_all = query_h.reshape(length, local_heads, head_dim)
    key_all = key_h.reshape(length, local_heads, head_dim)
    value_all = value_h.reshape(length, local_heads, head_dim)
    grad_all = grad_h.reshape(length, local_heads, head_dim)
    key_places = jnp.arange(length, dtype=jnp.int32)

    def step(carry, inputs):
        key_grad, value_grad = carry
        block_index, block_lse = inputs
        start = block_index * block_rows
        query_block = lax.dynamic_slice_in_dim(query_all, start, block_rows, 0)
        grad_block = lax.dynamic_slice_in_dim(grad_all, start, block_rows, 0)
        rows = start + jnp.arange(block_rows, dtype=jnp.int32)
        row_begin = lax.dynamic_slice_in_dim(begin, start, block_rows, 0)
        allowed = (key_places[None, :] <= rows[:, None]) & (
            key_places[None, :] >= row_begin[:, None]
        )
        scores = (
            jnp.einsum("qhd,khd->hqk", query_block, key_all, preferred_element_type=jnp.float32)
            * score_scale
        )
        probs = jnp.where(allowed[None], jnp.exp(scores - block_lse[..., None]), 0.0)
        probs_low = probs.astype(jnp.bfloat16)
        prob_grad = jnp.einsum(
            "qhd,khd->hqk", grad_block, value_all, preferred_element_type=jnp.float32
        )
        row_delta = jnp.sum(prob_grad * probs, axis=-1, keepdims=True)
        score_grad = (probs * (prob_grad - row_delta)).astype(jnp.bfloat16)
        query_grad = (
            jnp.einsum("hqk,khd->qhd", score_grad, key_all, preferred_element_type=jnp.float32)
            * score_scale
        )
        key_grad = (
            key_grad
            + jnp.einsum(
                "hqk,qhd->khd", score_grad, query_block, preferred_element_type=jnp.float32
            )
            * score_scale
        )
        value_grad = value_grad + jnp.einsum(
            "hqk,qhd->khd", probs_low, grad_block, preferred_element_type=jnp.float32
        )
        return (
            (key_grad, value_grad),
            query_grad.astype(jnp.bfloat16).reshape(block_rows, local_width),
        )

    empty = jnp.zeros((length, local_heads, head_dim), jnp.float32)
    (key_grad, value_grad), query_grad = lax.scan(
        step, (empty, empty), (jnp.arange(block_count, dtype=jnp.int32), log_sums)
    )
    return (
        query_grad.reshape(length, local_width),
        key_grad.astype(jnp.bfloat16).reshape(length, local_width),
        value_grad.astype(jnp.bfloat16).reshape(length, local_width),
    )


def shards(
    tokens,
    cotangent,
    starts,
    adapter_ids,
    w_qkv,
    w_out,
    w_gu,
    w_down,
    a_qkv,
    b_qkv,
    a_out,
    b_out,
    a_gu,
    b_gu,
    a_down,
    b_down,
):
    gathered = (
        lax.all_gather(a_qkv, "fsdp", axis=0, tiled=True),
        lax.all_gather(b_qkv, "fsdp", axis=1, tiled=True),
        lax.all_gather(a_out, "fsdp", axis=0, tiled=True),
        lax.all_gather(b_out, "fsdp", axis=1, tiled=True),
        lax.all_gather(a_gu, "fsdp", axis=0, tiled=True),
        lax.all_gather(b_gu, "fsdp", axis=1, tiled=True),
        lax.all_gather(a_down, "fsdp", axis=0, tiled=True),
        lax.all_gather(b_down, "fsdp", axis=1, tiled=True),
    )
    (
        full_a_qkv,
        full_b_qkv,
        full_a_out,
        full_b_out,
        full_a_gu,
        full_b_gu,
        full_a_down,
        full_b_down,
    ) = gathered
    stream = tokens[0].astype(jnp.float32)
    cot_low = cotangent[0]
    tok_count, width = stream.shape
    seq_count = lax.axis_size("seq")
    seq_place = lax.axis_index("seq")
    stream_len = tok_count * seq_count
    first = starts[0]
    chosen = adapter_ids[0]
    local_places = seq_place * tok_count + jnp.arange(tok_count, dtype=jnp.int32)
    local_begin, which = doc_tables(local_places, first, chosen)
    columns = jnp.arange(full_a_out.shape[1], dtype=jnp.int32) // RANK
    select = (columns[None, :] == which[:, None]).astype(jnp.bfloat16)
    cosine, sine = rope_tables(local_places - local_begin, HEAD_DIM)
    head_count = width // HEAD_DIM
    first_norm, first_factor = layer_norm(stream)
    first_low = first_norm.astype(jnp.bfloat16)
    latent_qkv, extra_qkv = adapter_fwd(first_low, full_a_qkv, full_b_qkv, select, 3)
    qkv_main, held_qkv = frozen_fwd(first_low, w_qkv)
    qkv = qkv_main + extra_qkv
    query_rot = (
        rotate(qkv[:, :width].reshape(tok_count, head_count, HEAD_DIM), cosine, sine)
        .reshape(tok_count, width)
        .astype(jnp.bfloat16)
    )
    key_rot = (
        rotate(qkv[:, width : 2 * width].reshape(tok_count, head_count, HEAD_DIM), cosine, sine)
        .reshape(tok_count, width)
        .astype(jnp.bfloat16)
    )
    value_low = qkv[:, 2 * width :].astype(jnp.bfloat16)
    query_h, key_h, value_h = (
        lax.all_to_all(query_rot, "seq", split_axis=1, concat_axis=0, tiled=True),
        lax.all_to_all(key_rot, "seq", split_axis=1, concat_axis=0, tiled=True),
        lax.all_to_all(value_low, "seq", split_axis=1, concat_axis=0, tiled=True),
    )
    all_begin, all_which = doc_tables(jnp.arange(stream_len, dtype=jnp.int32), first, chosen)
    mixed_h, log_sums = attend(query_h, key_h, value_h, all_begin, HEAD_DIM)
    mixed = lax.all_to_all(mixed_h, "seq", split_axis=0, concat_axis=1, tiled=True)
    latent_out, extra_out = adapter_fwd(mixed, full_a_out, full_b_out, select, 1)
    out_main, held_out = frozen_fwd(mixed, w_out)
    second = stream + (out_main + extra_out)
    second_norm, second_factor = layer_norm(second)
    second_low = second_norm.astype(jnp.bfloat16)
    latent_gu, extra_gu = adapter_fwd(second_low, full_a_gu, full_b_gu, select, 2)
    gu_main, held_gu = frozen_fwd(second_low, w_gu)
    gate_up = gu_main + extra_gu
    ff_width = gate_up.shape[1] // 2
    gate = gate_up[:, :ff_width]
    upper = gate_up[:, ff_width:]
    sigma = jax.nn.sigmoid(gate)
    active = gate * sigma
    hidden = (active * upper).astype(jnp.bfloat16)
    latent_down, extra_down = adapter_fwd(hidden, full_a_down, full_b_down, select, 1)
    down_main, held_down = frozen_fwd(hidden, w_down)
    activations = second + (down_main + extra_down)
    grad_a_down, grad_b_down, hidden_extra = adapter_back(
        hidden, latent_down, cot_low, full_a_down, full_b_down, select, 1
    )
    hidden_grad = frozen_bwd(cot_low, held_down) + hidden_extra
    gate_grad = (hidden_grad * upper * sigma * (1.0 + gate * (1.0 - sigma))).astype(jnp.bfloat16)
    upper_grad = (hidden_grad * active).astype(jnp.bfloat16)
    gate_up_grad = jnp.concatenate([gate_grad, upper_grad], axis=1)
    grad_a_gu, grad_b_gu, second_extra = adapter_back(
        second_low, latent_gu, gate_up_grad, full_a_gu, full_b_gu, select, 2
    )
    second_norm_grad = frozen_bwd(gate_up_grad, held_gu) + second_extra
    second_grad = cot_low.astype(jnp.float32) + norm_back(
        second_norm, second_factor, second_norm_grad
    )
    branch_grad = second_grad.astype(jnp.bfloat16)
    grad_a_out, grad_b_out, mixed_extra = adapter_back(
        mixed, latent_out, branch_grad, full_a_out, full_b_out, select, 1
    )
    mixed_grad = (frozen_bwd(branch_grad, held_out) + mixed_extra).astype(jnp.bfloat16)
    mixed_grad_h = lax.all_to_all(mixed_grad, "seq", split_axis=1, concat_axis=0, tiled=True)
    query_grad_h, key_grad_h, value_grad_h = attend_back(
        query_h, key_h, value_h, mixed_grad_h, log_sums, all_begin, HEAD_DIM
    )
    query_grad, key_grad, value_grad = (
        lax.all_to_all(query_grad_h, "seq", split_axis=0, concat_axis=1, tiled=True),
        lax.all_to_all(key_grad_h, "seq", split_axis=0, concat_axis=1, tiled=True),
        lax.all_to_all(value_grad_h, "seq", split_axis=0, concat_axis=1, tiled=True),
    )
    query_pre = (
        rotate_back(
            query_grad.astype(jnp.float32).reshape(tok_count, head_count, HEAD_DIM), cosine, sine
        )
        .reshape(tok_count, width)
        .astype(jnp.bfloat16)
    )
    key_pre = (
        rotate_back(
            key_grad.astype(jnp.float32).reshape(tok_count, head_count, HEAD_DIM), cosine, sine
        )
        .reshape(tok_count, width)
        .astype(jnp.bfloat16)
    )
    qkv_grad = jnp.concatenate([query_pre, key_pre, value_grad], axis=1)
    grad_a_qkv, grad_b_qkv, first_extra = adapter_back(
        first_low, latent_qkv, qkv_grad, full_a_qkv, full_b_qkv, select, 3
    )
    first_norm_grad = frozen_bwd(qkv_grad, held_qkv) + first_extra
    input_grad = second_grad + norm_back(first_norm, first_factor, first_norm_grad)
    grads = (
        grad_a_qkv,
        grad_b_qkv,
        grad_a_out,
        grad_b_out,
        grad_a_gu,
        grad_b_gu,
        grad_a_down,
        grad_b_down,
    )
    shard_dims = (0, 1, 0, 1, 0, 1, 0, 1)
    summed = lax.psum(
        (grads[0], grads[1], grads[2], grads[3], grads[4], grads[5], grads[6], grads[7]),
        ("seq", "fsdp"),
    )
    fsdp_place = lax.axis_index("fsdp")
    fsdp_count = lax.axis_size("fsdp")
    totals = tuple(
        (
            lax.dynamic_slice_in_dim(
                whole,
                fsdp_place * (whole.shape[along] // fsdp_count),
                whole.shape[along] // fsdp_count,
                along,
            )
            for whole, along in zip(summed, shard_dims)
        )
    )
    return (
        activations[None],
        input_grad[None],
        totals[0],
        totals[1],
        totals[2],
        totals[3],
        totals[4],
        totals[5],
        totals[6],
        totals[7],
    )


def solution(mesh):
    placed = (
        P("fsdp", "seq", None),
        P("fsdp", "seq", None),
        P("fsdp", None),
        P("fsdp", None),
        P("fsdp", None),
        P("fsdp", None),
        P("fsdp", None),
        P("fsdp", None),
        P("fsdp", None),
        P(None, "fsdp"),
        P("fsdp", None),
        P(None, "fsdp"),
        P("fsdp", None),
        P(None, "fsdp"),
        P("fsdp", None),
        P(None, "fsdp"),
    )
    return jax.shard_map(
        shards,
        mesh=mesh,
        in_specs=placed,
        out_specs=(
            P("fsdp", "seq", None),
            P("fsdp", "seq", None),
            P("fsdp", None),
            P(None, "fsdp"),
            P("fsdp", None),
            P(None, "fsdp"),
            P("fsdp", None),
            P(None, "fsdp"),
            P("fsdp", None),
            P(None, "fsdp"),
        ),
        check_vma=False,
    )
```

profile of v0, /device:TPU:1, one launch (start us, length us, event | category | flops | bytes accessed | tf_op | source)
XLA Modules:
  0.0 3622.9 jit_solution(8189075003797754291)
XLA Ops:
  16.4 32.2 all-gather.12.cloned.1.call-done
  50.8 35.4 all-gather.14.cloned.1.call-done
  91.3 421.0 %all-gather.10.cloned.1.call-done = bf16[2048,6144]{1,0:T(8,128)(2,1)} async-done(((bf16[512,6144]{1,0:T(8,128)(2,1)}), bf16[2048,6144]{1,0:T(8,128)(2,1)}) %all-gather.10.cloned.1.call-update) | async-done | bytes 25165840 | tf_op jit(solution)/shard_map/all_gather | solution.py:117
  512.2 18.9 convolution_add_fusion.2
  531.1 4.8 fusion.151
  552.1 5.2 fusion.72
  559.7 4.0 all-to-all-start
  564.8 10.9 all-to-all-done
  575.7 7.4 all-to-all-start.1
  588.1 6.9 all-to-all-done.1
  595.0 7.7 all-to-all-start.2
  620.7 53.4 %while.30 = (s32[]{:T(128)}, bf16[4,512,256]{2,1,0:T(8,128)(2,1)}, f32[4,2,512]{2,1,0:T(2,128)}, s32[4]{0:T(128)S(1)}, s32[2048]{0:T(1024)}, /*index=5*/bf16[204...) while((s32[]{:T(128)}, bf16[4,512,256]{2,1,0:T(8,128)(2,1)}, ...), condition=%wide.region_9.10_spmd.clone.clone, body=%wide.region_6.9_spmd.clone.clone.sunk | while | flops 1102183936 | bytes 37268696 | solution.py:162
  624.1 3.3 fusion.237
  637.4 3.3 fusion.237
  650.8 3.3 fusion.237
  664.1 3.3 fusion.237
  674.2 7.9 all-to-all-start.3
  683.6 15.3 all_gather.44
  698.9 19.1 all_gather.45
  718.1 20.6 all_gather.51
  741.1 3.9 copy.163
  751.5 6.2 fusion.155
  761.9 26.5 all-gather.22.cloned.1.call-done
  788.4 6.3 fusion.83
  794.7 6.8 fusion.79
  801.5 549.6 %all-gather.24.cloned.1.call-done = bf16[8192,2048]{1,0:T(8,128)(2,1)} async-done(((bf16[2048,2048]{1,0:T(8,128)(2,1)}), bf16[8192,2048]{1,0:T(8,128)(2,1)}) %all-gather.24.cloned.1.call-update) | async-done | bytes 33554448 | tf_op jit(solution)/shard_map/all_gather | solution.py:117
  1351.1 24.9 fusion.98
  1376.0 1085.6 %all-gather.18.cloned.1.call-done = bf16[2048,16384]{1,0:T(8,128)(2,1)} async-done(((bf16[512,16384]{1,0:T(8,128)(2,1)}), bf16[2048,16384]{1,0:T(8,128)(2,1)}) %all-gather.18.cloned.1.call-update) | async-done | bytes 67108880 | tf_op jit(solution)/shard_map/all_gather | solution.py:117
  2461.6 35.2 convolution_add_fusion
  2496.8 10.3 all-gather.26.cloned.1.call-done
  2507.1 14.5 multiply_convert_fusion.2
  2521.5 3.7 fusion.77
  2529.0 28.9 fusion.40
  2557.8 3.5 fusion.150
  2568.8 4.3 all-to-all-start.4
  2573.1 4.2 fusion.91
  2590.0 123.9 %while.31 = (s32[]{:T(128)}, f32[2048,2,128]{0,2,1:T(8,128)S(1)}, f32[2048,2,128]{0,2,1:T(8,128)}, bf16[4,512,256]{2,1,0:T(8,128)(2,1)}, s32[4]{0:T(128)S(1)}, /...) while((s32[]{:T(128)}, f32[2048,2,128]{0,2,1:T(8,128)S(1)}, ...), condition=%wide.region_16.17_spmd.clone.clone, body=%wide.region_14.16_spmd.clone.clone.sunk | while | flops 2721840640 | bytes 139762544 | solution.py:220
  2596.9 4.7 multiply_reduce_fusion.4
  2601.6 3.9 multiply_convert_fusion.5
  2605.4 3.6 fusion.251
  2613.3 7.4 fusion.252
  2627.4 4.7 multiply_reduce_fusion.4
  2632.0 3.9 multiply_convert_fusion.5
  2635.9 3.6 fusion.251
  2643.8 8.0 fusion.252
  2658.4 4.7 multiply_reduce_fusion.4
  2663.1 3.9 multiply_convert_fusion.5
  2667.0 3.6 fusion.251
  2674.9 8.0 fusion.252
  2689.5 4.7 multiply_reduce_fusion.4
  2694.2 3.9 multiply_convert_fusion.5
  2698.1 3.6 fusion.251
  2706.0 8.0 fusion.252
  2716.0 6.9 all-to-all-start.6
  2722.9 7.7 pad_maximum_fusion
  2730.6 4.2 all-to-all-done.6
  2734.8 7.4 all-to-all-start.5
  2743.5 5.7 fusion.158
  2757.1 4.6 all-to-all-start.7
  2767.1 4.0 broadcast_multiply_fusion.1
  2799.2 17.9 fusion.156
  2818.9 13.6 fusion.45
  2832.5 3.5 fusion.149
  2838.1 761.1 %all-reduce.3.cloned.1.call-done = (f32[2048,384]{1,0:T(8,128)}, f32[384,2048]{1,0:T(8,128)}, f32[2048,128]{1,0:T(8,128)}, f32[128,2048]{1,0:T(8,128)}, f32[2048...) async-done(((f32[2048,384]{1,0:T(8,128)}, f32[384,2048]{1,0:T(8,128)}, f32[2048,128]{1,0:T(8,128)}, f32[128,2048]{1,0:T(8,128)}, ...) | async-done | bytes 24117264 | tf_op jit(solution)/shard_map/psum | solution.py:382
  (393 shorter events, 240.3 us)
Async XLA Ops:
  7.2 41.4 %all-gather.12.cloned.1.call-start = ((), (), s32[]{:S(2)}) async-start(), calls=%async_computation.9 | async-start | bytes 1966080 | tf_op jit(solution)/shard_map/all_gather | solution.py:249
  7.9 78.3 %all-gather.14.cloned.1.call-start = ((), (), s32[]{:S(2)}) async-start(), calls=%async_computation.10 | async-start | bytes 1966080 | tf_op jit(solution)/shard_map/all_gather | solution.py:250
  8.7 503.6 %all-gather.10.cloned.1.call-start = ((), (), s32[]{:S(2)}) async-start(), calls=%async_computation.8 | async-start | bytes 31457280 | tf_op jit(solution)/shard_map/all_gather | solution.py:117
  9.4 742.1 %all-gather.16.cloned.1.call-start = ((), (), s32[]{:S(2)}) async-start(), calls=%async_computation.11 | async-start | bytes 10485760 | tf_op jit(solution)/shard_map/all_gather | solution.py:117
  10.0 749.9 %all-gather.20.cloned.1.call-start = ((), (), s32[]{:S(2)}) async-start(), calls=%async_computation.13 | async-start | bytes 1310720 | tf_op jit(solution)/shard_map/all_gather | solution.py:253
  10.6 777.8 %all-gather.22.cloned.1.call-start = ((), (), s32[]{:S(2)}) async-start(), calls=%async_computation.14 | async-start | bytes 5242880 | tf_op jit(solution)/shard_map/all_gather | solution.py:254
  11.1 1340.0 %all-gather.24.cloned.1.call-start = ((), (), s32[]{:S(2)}) async-start(), calls=%async_computation.15 | async-start | bytes 41943040 | tf_op jit(solution)/shard_map/all_gather | solution.py:117
  11.9 2449.6 %all-gather.18.cloned.1.call-start = ((), (), s32[]{:S(2)}) async-start(), calls=%async_computation.12 | async-start | bytes 83886080 | tf_op jit(solution)/shard_map/all_gather | solution.py:117
  14.4 36.4 %copy-start.41 = (bf16[256,3,128]{0,2,1:T(8,128)(2,1)}, bf16[256,3,128]{0,2,1:T(8,128)(2,1)S(1)}, u32[]{:S(2)}) copy-start(bf16[256,3,128]{0,2,1:T(8,128)(2,1)S(1)} %tile.10) | copy-start | bytes 589828
  15.0 527.6 %copy-start.45 = (f32[256,128]{0,1:T(8,128)}, f32[256,128]{0,1:T(8,128)S(1)}, u32[]{:S(2)}) copy-start(f32[256,128]{0,1:T(8,128)S(1)} %get-tuple-element.413) | copy-start | bytes 393220
  16.0 496.3 %copy-start.65 = (f32[256]{0:T(256)}, f32[256]{0:T(256)S(1)}, u32[]{:S(2)}) copy-start(f32[256]{0:T(256)S(1)} %broadcast_multiply_fusion.7) | copy-start | bytes 3076
  16.4 495.8 %copy-start.67 = (f32[256]{0:T(256)}, f32[256]{0:T(256)S(1)}, u32[]{:S(2)}) copy-start(f32[256]{0:T(256)S(1)} %add_rsqrt_fusion.1) | copy-start | bytes 3076
  50.8 38.7 %copy-start.47 = (bf16[256,384]{1,0:T(8,128)(2,1)}, bf16[256,384]{1,0:T(8,128)(2,1)S(1)}, u32[]{:S(2)}) copy-start(bf16[256,384]{1,0:T(8,128)(2,1)S(1)} %fusion.86) | copy-start | bytes 589828
  549.9 7.5 copy-start.12
  557.4 6.4 copy-start.29
  559.7 16.0 all-to-all-start
  575.7 19.3 all-to-all-start.1
  595.0 9.9 copy-start.37
  595.0 19.6 all-to-all-start.2
  674.2 8.0 copy-start.14
  674.2 8.7 copy-start.59
  674.2 9.5 copy-start.63
  674.2 24.8 copy-start.64
  674.2 73.1 %all-to-all-start.3 = ((bf16[8,256,256]{2,1,0:T(8,128)(2,1)}), bf16[8,256,256]{2,1,0:T(8,128)(2,1)}, u32[]{:S(2)}, u32[]{:S(2)}) async-start(bf16[8,256,256]{2,1,0:T(8,128)(2,1)} %bitcast.272), calls=%async_computation.3 | async-start | bytes 2097152 | tf_op jit(solution)/shard_map/all_to_all | solution.py:305
  682.1 1824.9 %all-gather.26.cloned.1.call-start = ((), (), s32[]{:S(2)}) async-start(), calls=%async_computation.16 | async-start | bytes 2621440 | tf_op jit(solution)/shard_map/all_gather | solution.py:255
  741.1 1765.9 %copy-start.61 = (bf16[256,128]{1,0:T(8,128)(2,1)}, bf16[256,128]{1,0:T(8,128)(2,1)S(1)}, u32[]{:S(2)}) copy-start(bf16[256,128]{1,0:T(8,128)(2,1)S(1)} %fusion.88) | copy-start | bytes 196612
  751.5 6.2 copy-start.22
  759.8 28.6 copy-start.35
  761.9 32.8 copy-start.51
  788.4 6.3 copy-start.26
  794.7 556.5 %copy-start.15 = (bf16[1,256,2048]{2,1,0:T(8,128)(2,1)S(1)}, bf16[1,256,2048]{2,1,0:T(8,128)(2,1)}, u32[]{:S(2)}) copy-start(bf16[1,256,2048]{2,1,0:T(8,128)(2,1)} %param.21) | copy-start | bytes 3145732
  2507.1 14.5 copy-start.27
  2521.5 3.7 copy-start.30
  2557.8 6.3 slice-start
  2568.8 16.3 all-to-all-start.4
  2573.1 4.3 copy-start.11
  2573.1 5.7 copy-start.32
  2596.2 5.4 copy-start
  2605.4 3.7 copy-start.1
  2605.4 3.8 copy-start.5
  2626.7 5.4 copy-start
  2635.9 3.7 copy-start.1
  2635.9 3.8 copy-start.5
  2657.7 5.4 copy-start
  2667.0 3.7 copy-start.1
  2667.0 3.8 copy-start.5
  2688.8 5.4 copy-start
  2698.1 3.7 copy-start.1
  2698.1 3.8 copy-start.5
  2716.0 18.8 all-to-all-start.6
  2730.6 11.6 copy-start.16
  2734.8 8.7 copy-start.28
  2734.8 8.7 copy-start.62
  2734.8 22.3 all-to-all-start.5
  2743.5 5.7 copy-start.40
  2757.1 33.3 all-to-all-start.7
  2761.7 837.5 %all-reduce.3.cloned.1.call-start = ((), (), s32[]{:S(2)}) async-start(), calls=%async_computation.17 | async-start | bytes 48234496 | tf_op jit(solution)/shard_map/psum | solution.py:382
  2792.8 4.3 copy-start.54
  2793.3 3.7 copy-start.56
  2799.2 17.9 copy-start.4
  2799.2 17.9 copy-start.25
  2818.9 13.6 copy-start.42
  2818.9 13.6 copy-start.55
  2832.5 3.5 copy-start.10
  (42 other events, 89.0 us)
Sparse Core Ops, SparseCore 0:
  9.6 38.9 all-gather.11
  50.2 35.9 all-gather.13
  87.8 424.3 all-gather.9
  513.6 147.8 all-gather.15
  662.9 28.7 all-gather.19
  693.2 95.1 all-gather.21
  789.9 561.1 all-gather.23
  1352.7 1108.8 all-gather.17
  2463.1 43.8 all-gather.25
  2799.3 799.8 all-reduce.2
where the time goes:
time: 3630 us; the launch traced here: 3620 us
  waiting for transfers between devices  2950 us (81%)
  matrix products  339 us (9%)
  local copies, waits for them, and re-layouts  125 us (3%)
  other arithmetic  80.7 us (2%)
  blocking collectives  55 us (2%)
  starting transfers between devices  50.5 us (1%)
    all_gather x4, waiting for transfers between devices, frozen_fwd(): lax.all_gather(weight, 'fsdp', axis=0, tiled=True)  2060 us
    psum x1, waiting for transfers between devices, shards(): lax.psum((grads[0], grads[1], grads[2], grads[3], grads[4], grads[5], gra...  761 us
    dot_general x15, matrix products, inner_cols(): lax.dot_general(left, right, (((1,), (1,)), ((), ())), preferred_element_...  100 us
    dot_general x4, matrix products, frozen_fwd(): jnp.dot(inputs, lax.all_gather(weight, 'fsdp', axis=0, tiled=True), prefe...  78.1 us
  transfers between devices with their start and end apart: 18, of which 13 were waited for; matrix products, arithmetic and copies ran while one was open for 9% of the time, Pallas kernels for 0%

commit v1 on v0

--- a/solution.py
+++ b/solution.py
@@ -1,6 +1,10 @@
+import functools
+
 import jax
 import jax.numpy as jnp
 from jax import lax
+from jax.experimental import pallas as pl
+from jax.experimental.pallas import tpu as pltpu
 from jax.sharding import PartitionSpec as P
 
 HEAD_DIM = 128
@@ -410,6 +414,550 @@
     )
 
 
+BF = jnp.bfloat16
+F32 = jnp.float32
+CHIPS = 4
+PLANE = 8
+CHUNKS = 2
+LANES = 128
+
+
+def swap(value, bit):
+    return lax.ppermute(value, "seq", [(i, i ^ bit) for i in range(PLANE)])
+
+
+def plane_gather(block):
+    half = block.shape[0] // 2
+    over_x = swap(block, 2)
+    over_y = swap(block, 4)
+    far_a = swap(over_y[:half], 2)
+    far_b = swap(over_x[half:], 4)
+    return jnp.concatenate([block, over_x, over_y, far_a, far_b], axis=0)
+
+
+def plane_scatter(partial):
+    rows = partial.shape[0] // 4
+    half = rows // 2
+    low = partial.astype(BF)
+    own = partial[:rows].astype(F32)
+    to_x = jnp.concatenate([low[rows : rows + half], low[3 * rows : 3 * rows + half]], axis=0)
+    to_y = jnp.concatenate([low[2 * rows + half : 3 * rows], low[3 * rows + half :]], axis=0)
+    from_x = swap(to_x, 2)
+    from_y = swap(to_y, 4)
+    pass_y = (partial[2 * rows : 2 * rows + half].astype(F32) + from_x[half:].astype(F32)).astype(BF)
+    pass_x = (partial[rows + half : 2 * rows].astype(F32) + from_y[half:].astype(F32)).astype(BF)
+    got_y = swap(pass_y, 4)
+    got_x = swap(pass_x, 2)
+    upper = own[:half] + from_x[:half].astype(F32) + got_y.astype(F32)
+    lower = own[half:] + from_y[:half].astype(F32) + got_x.astype(F32)
+    return jnp.concatenate([upper, lower], axis=0)
+
+
+def dot(left, right):
+    return jnp.dot(left, right, preferred_element_type=F32)
+
+
+def lane_blocks(value):
+    count = value.shape[1] // LANES
+    return jnp.concatenate([value[:, k * LANES : (k + 1) * LANES] for k in range(count)], axis=0)
+
+
+def in_order(scalars, own, other, whole, blocks, rows):
+    chip, core = scalars[0], scalars[1]
+    for place in range(blocks):
+        start = pl.multiple_of(((place // 2) ^ chip) * rows, rows)
+
+        @pl.when(core == place % 2)
+        def _():
+            whole[place * rows : (place + 1) * rows, :] = own[pl.ds(start, rows), :]
+
+        @pl.when(core != place % 2)
+        def _():
+            whole[place * rows : (place + 1) * rows, :] = other[pl.ds(start, rows), :]
+
+
+def out_of_order(scalars, whole, own, other, blocks, rows):
+    chip, core = scalars[0], scalars[1]
+    for place in range(blocks):
+        start = pl.multiple_of(((place // 2) ^ chip) * rows, rows)
+
+        @pl.when(core == place % 2)
+        def _():
+            own[pl.ds(start, rows), :] = whole[place * rows : (place + 1) * rows, :]
+
+        @pl.when(core != place % 2)
+        def _():
+            other[pl.ds(start, rows), :] = whole[place * rows : (place + 1) * rows, :]
+
+
+def allowed_pairs(scalars, first_row, rows, width):
+    row = first_row + lax.broadcasted_iota(jnp.int32, (rows, 1), 0)
+    column = lax.broadcasted_iota(jnp.int32, (1, width), 1)
+    begin = jnp.zeros((rows, 1), jnp.int32)
+    for doc in range(4):
+        begin = jnp.where(scalars[2 + doc] <= row, jnp.maximum(begin, scalars[2 + doc]), begin)
+    return (column <= row) & (column >= begin)
+
+
+def inner(left, right, on_left, on_right):
+    return lax.dot_general(
+        left, right, (((on_left,), (on_right,)), ((), ())), preferred_element_type=F32
+    )
+
+
+def attend_kernel(blocks, rows, scalars, qa, ka, va, qb, kb, vb, out, lse, q_all, k_all, v_all):
+    in_order(scalars, qa, qb, q_all, blocks, rows)
+    in_order(scalars, ka, kb, k_all, blocks, rows)
+    in_order(scalars, va, vb, v_all, blocks, rows)
+    scale = HEAD_DIM**-0.5
+    for place in range(blocks):
+        here = slice(place * rows, (place + 1) * rows)
+        width = (place + 1) * rows
+        scores = inner(q_all[here, :], k_all[:width, :], 1, 1) * scale
+        scores = jnp.where(allowed_pairs(scalars, place * rows, rows, width), scores, -1e30)
+        top = jnp.max(scores, axis=1, keepdims=True)
+        expd = jnp.exp(scores - top)
+        total = jnp.sum(expd, axis=1, keepdims=True)
+        probs = (expd * (1.0 / total)).astype(BF)
+        out[here, :] = dot(probs, v_all[:width, :]).astype(BF)
+        lse[here, :] = jnp.broadcast_to(top + jnp.log(total), (rows, LANES))
+
+
+def attend_back_kernel(
+    blocks, rows, scalars, qa, ka, va, qb, kb, vb, grad, lse,
+    own, other, q_all, k_all, v_all, dq_all, dk_sum, dv_sum,
+):
+    in_order(scalars, qa, qb, q_all, blocks, rows)
+    in_order(scalars, ka, kb, k_all, blocks, rows)
+    in_order(scalars, va, vb, v_all, blocks, rows)
+    dk_sum[...] = jnp.zeros_like(dk_sum)
+    dv_sum[...] = jnp.zeros_like(dv_sum)
+    scale = HEAD_DIM**-0.5
+    for place in range(blocks):
+        here = slice(place * rows, (place + 1) * rows)
+        width = (place + 1) * rows
+        query = q_all[here, :]
+        upstream = grad[here, :]
+        scores = inner(query, k_all[:width, :], 1, 1) * scale
+        probs = jnp.where(
+            allowed_pairs(scalars, place * rows, rows, width),
+            jnp.exp(scores - lse[here, :1]),
+            0.0,
+        )
+        prob_grad = inner(upstream, v_all[:width, :], 1, 1)
+        delta = jnp.sum(prob_grad * probs, axis=1, keepdims=True)
+        score_grad = (probs * (prob_grad - delta)).astype(BF)
+        dq_all[here, :] = (dot(score_grad, k_all[:width, :]) * scale).astype(BF)
+        dk_sum[:width, :] += inner(score_grad, query, 0, 0)
+        dv_sum[:width, :] += inner(probs.astype(BF), upstream, 0, 0)
+    out_of_order(scalars, dq_all, own.at[0], other.at[0], blocks, rows)
+    dq_all[...] = (dk_sum[...] * scale).astype(BF)
+    out_of_order(scalars, dq_all, own.at[1], other.at[1], blocks, rows)
+    dq_all[...] = dv_sum[...].astype(BF)
+    out_of_order(scalars, dq_all, own.at[2], other.at[2], blocks, rows)
+
+
+def attend_plane(scalars, own, other, rows):
+    length = 2 * own.shape[0]
+    group = own.shape[0]
+    heads = own.shape[1] // (3 * HEAD_DIM)
+    blocks = length // rows
+    part = lambda k: pl.BlockSpec((group, HEAD_DIM), lambda h, _: (0, k * heads + h))
+    return pl.pallas_call(
+        functools.partial(attend_kernel, blocks, rows),
+        grid_spec=pltpu.PrefetchScalarGridSpec(
+            num_scalar_prefetch=1,
+            grid=(heads,),
+            in_specs=[part(0), part(1), part(2)] * 2,
+            out_specs=[
+                pl.BlockSpec((length, HEAD_DIM), lambda h, _: (0, h)),
+                pl.BlockSpec((length, LANES), lambda h, _: (0, h)),
+            ],
+            scratch_shapes=[pltpu.VMEM((length, HEAD_DIM), BF)] * 3,
+        ),
+        out_shape=[
+            jax.ShapeDtypeStruct((length, heads * HEAD_DIM), BF),
+            jax.ShapeDtypeStruct((length, heads * LANES), F32),
+        ],
+        compiler_params=pltpu.CompilerParams(vmem_limit_bytes=48 * 2**20),
+        cost_estimate=pl.CostEstimate(
+            flops=2 * heads * length * length * HEAD_DIM,
+            bytes_accessed=8 * length * heads * HEAD_DIM,
+            transcendentals=heads * length * length // 2,
+        ),
+    )(scalars, own, own, own, other, other, other)
+
+
+def attend_plane_back(scalars, own, other, grad, lse, rows):
+    length = 2 * own.shape[0]
+    group = own.shape[0]
+    heads = own.shape[1] // (3 * HEAD_DIM)
+    blocks = length // rows
+    part = lambda k: pl.BlockSpec((group, HEAD_DIM), lambda h, _: (0, k * heads + h))
+    result = pl.BlockSpec((3, group, HEAD_DIM), lambda h, _: (0, 0, h))
+    shape = jax.ShapeDtypeStruct((3, group, heads * HEAD_DIM), BF)
+    return pl.pallas_call(
+        functools.partial(attend_back_kernel, blocks, rows),
+        grid_spec=pltpu.PrefetchScalarGridSpec(
+            num_scalar_prefetch=1,
+            grid=(heads,),
+            in_specs=[part(0), part(1), part(2)] * 2
+            + [
+                pl.BlockSpec((length, HEAD_DIM), lambda h, _: (0, h)),
+                pl.BlockSpec((length, LANES), lambda h, _: (0, h)),
+            ],
+            out_specs=[result, result],
+            scratch_shapes=[pltpu.VMEM((length, HEAD_DIM), BF)] * 4
+            + [pltpu.VMEM((length, HEAD_DIM), F32)] * 2,
+        ),
+        out_shape=[shape, shape],
+        compiler_params=pltpu.CompilerParams(vmem_limit_bytes=48 * 2**20),
+        cost_estimate=pl.CostEstimate(
+            flops=5 * heads * length * length * HEAD_DIM,
+            bytes_accessed=20 * length * heads * HEAD_DIM,
+            transcendentals=heads * length * length // 2,
+        ),
+    )(scalars, own, own, own, other, other, other, grad, lse)
+
+
+def plane_shards(
+    tokens, cotangent, starts, adapter_ids,
+    w_qkv, w_out, w_gu, w_down, a_qkv, b_qkv, a_out, b_out, a_gu, b_gu, a_down, b_down,
+):
+    seat = lax.axis_index("seq")
+    z_count = lax.axis_size("fsdp")
+    core = seat % 2
+    chip = seat // 2
+    rows, width = tokens.shape[1:]
+    length = rows * PLANE
+    ff = w_gu.shape[1] // 2
+    ff_z = ff // z_count
+    ff_dev = ff_z // PLANE
+    ff_chunk = ff_dev // CHUNKS
+    quarter = w_qkv.shape[0]
+    latent = a_out.shape[1]
+    heads = width // HEAD_DIM
+    heads_dev = heads // PLANE
+    span = heads_dev * HEAD_DIM
+    first = starts[0]
+    chosen = adapter_ids[0]
+
+    def take(value, start, count, axis):
+        return lax.dynamic_slice_in_dim(value, start, count, axis)
+
+    head_columns = [
+        part * width + (2 * core + i) * quarter + chip * HEAD_DIM
+        for part in range(3)
+        for i in range(heads_dev)
+    ]
+    qkv_part = jnp.concatenate([take(w_qkv, at, HEAD_DIM, 1) for at in head_columns], axis=1)
+    qkv_own = lax.all_gather(qkv_part, "fsdp", axis=0, tiled=True)
+    qkv_oth = swap(qkv_own, 1)
+
+    share = quarter // PLANE
+    share_b = latent // PLANE
+    packed = jnp.concatenate(
+        [
+            lane_blocks(take(a_qkv, seat * share, share, 0)),
+            lane_blocks(take(a_out, seat * share, share, 0)),
+            lane_blocks(take(a_gu, seat * share, share, 0)),
+            lane_blocks(take(b_out, seat * share_b, share_b, 0)),
+            lane_blocks(take(b_down, seat * share_b, share_b, 0)),
+        ],
+        axis=0,
+    )
+    packed = lax.all_gather(packed, ("fsdp", "seq"), axis=0, tiled=False).reshape(
+        z_count, PLANE, packed.shape[0], LANES
+    )
+
+    def unpack_rows(start, blocks):
+        piece = packed[:, :, start : start + blocks * share]
+        piece = piece.reshape(z_count, PLANE, blocks, share, LANES).transpose(0, 1, 3, 2, 4)
+        return piece.reshape(width, blocks * LANES)
+
+    def unpack_columns(start):
+        blocks = width // z_count // LANES
+        piece = packed[:, :, start : start + blocks * share_b]
+        piece = piece.reshape(z_count, PLANE, blocks, share_b, LANES).transpose(1, 3, 0, 2, 4)
+        return piece.reshape(latent, width)
+
+    at = 0
+    full_a_qkv = unpack_rows(at, a_qkv.shape[1] // LANES)
+    at += a_qkv.shape[1] // LANES * share
+    full_a_out = unpack_rows(at, a_out.shape[1] // LANES)
+    at += a_out.shape[1] // LANES * share
+    full_a_gu = unpack_rows(at, a_gu.shape[1] // LANES)
+    at += a_gu.shape[1] // LANES * share
+    full_b_out = unpack_columns(at)
+    at += width // z_count // LANES * share_b
+    full_b_down = unpack_columns(at)
+
+    b_qkv_chip = lax.all_gather(
+        take(b_qkv, chip * HEAD_DIM, HEAD_DIM, 1), "fsdp", axis=1, tiled=True
+    )
+    b_qkv_own = take(b_qkv_chip, core * span, span, 1)
+    b_qkv_oth = take(b_qkv_chip, (1 - core) * span, span, 1)
+
+    full_out = lax.all_gather(
+        take(w_out, seat * share, share, 0), ("fsdp", "seq"), axis=0, tiled=True
+    )
+
+    b_gu_own = lax.all_gather(take(b_gu, seat * ff_dev, ff_dev, 1), "fsdp", axis=0, tiled=True)
+    b_gu_oth = swap(b_gu_own, 1)
+    gu_pairs = []
+    down_pairs = []
+    b_gu_pairs = []
+    for chunk in range(CHUNKS):
+        columns = [
+            half * ff + z * ff_z + seat * ff_dev + chunk * ff_chunk
+            for half in range(2)
+            for z in range(z_count)
+        ]
+        part = jnp.concatenate([take(w_gu, at, ff_chunk, 1) for at in columns], axis=1)
+        own = lax.all_gather(part, "fsdp", axis=0, tiled=True)
+        gu_pairs.append((own, swap(own, 1)))
+        at = seat * ff_dev + chunk * ff_chunk
+        part = jnp.concatenate([take(w_down, at, ff_chunk, 0), take(a_down, at, ff_chunk, 0)], axis=1)
+        own = lax.all_gather(part, "fsdp", axis=0, tiled=True)
+        down_pairs.append((own, swap(own, 1)))
+        pair = []
+        for whole in (b_gu_own, b_gu_oth):
+            by_z = whole.reshape(z_count, 2 * latent, ff_dev)
+            by_z = by_z[:, :, chunk * ff_chunk : (chunk + 1) * ff_chunk]
+            pair.append(by_z.transpose(1, 0, 2).reshape(2 * latent, z_count * ff_chunk))
+        b_gu_pairs.append(tuple(pair))
+
+    order = jnp.arange(CHIPS, dtype=jnp.int32) ^ chip
+    group_places = ((order * 2 + core)[:, None] * rows + jnp.arange(rows, dtype=jnp.int32)).reshape(-1)
+    group_begin, group_which = doc_tables(group_places, first, chosen)
+    adapters_at = jnp.arange(latent, dtype=jnp.int32) // RANK
+    group_select = (adapters_at[None, :] == group_which[:, None]).astype(BF)
+    select = group_select[:rows]
+    cosine, sine = rope_tables(group_places - group_begin, HEAD_DIM)
+    scalars = jnp.concatenate([jnp.stack([chip, core]).astype(jnp.int32), first])
+
+    stream = tokens[0].astype(F32)
+    cot_low = cotangent[0]
+    first_norm, first_factor = layer_norm(stream)
+    norm1 = plane_gather(first_norm.astype(BF))
+    z_qkv = dot(norm1, full_a_qkv).astype(BF) * jnp.tile(group_select, (1, 3))
+    z_parts = [z_qkv[:, k * latent : (k + 1) * latent] for k in range(3)]
+    b_parts_own = [b_qkv_own[k * latent : (k + 1) * latent] for k in range(3)]
+    b_parts_oth = [b_qkv_oth[k * latent : (k + 1) * latent] for k in range(3)]
+
+    def project(weight, ups):
+        pre = dot(norm1, weight) + jnp.concatenate(
+            [dot(z, up) for z, up in zip(z_parts, ups)], axis=1
+        )
+        turned = rotate(pre[:, : 2 * span].reshape(-1, 2 * heads_dev, HEAD_DIM), cosine, sine)
+        return jnp.concatenate([turned.reshape(-1, 2 * span), pre[:, 2 * span :]], axis=1).astype(BF)
+
+    sent = project(qkv_oth, b_parts_oth)
+    qkv_a = project(qkv_own, b_parts_own)
+    qkv_b = swap(sent, 1)
+    mixed_h, log_sums = attend_plane(scalars, qkv_a, qkv_b, rows)
+    mixed = lax.all_to_all(mixed_h, "seq", split_axis=0, concat_axis=1, tiled=True)
+
+    def natural(value):
+        return jnp.concatenate(
+            [
+                value[:, (j * z_count + z) * HEAD_DIM : (j * z_count + z + 1) * HEAD_DIM]
+                for z in range(z_count)
+                for j in range(CHIPS)
+            ],
+            axis=1,
+        )
+
+    def by_device(value):
+        return jnp.concatenate(
+            [
+                value[:, (z * CHIPS + j) * HEAD_DIM : (z * CHIPS + j + 1) * HEAD_DIM]
+                for j in range(CHIPS)
+                for z in range(z_count)
+            ],
+            axis=1,
+        )
+
+    mixed = natural(mixed)
+    z_out = dot(mixed, full_a_out).astype(BF) * select
+    second = stream + (dot(mixed, full_out) + dot(z_out, full_b_out))
+
+    second_norm, second_factor = layer_norm(second)
+    norm2 = plane_gather(second_norm.astype(BF))
+    cot_all = plane_gather(cot_low)
+    z_gu = dot(norm2, full_a_gu).astype(BF) * jnp.tile(group_select, (1, 2))
+    z_gate, z_up = z_gu[:, :latent], z_gu[:, latent:]
+    dz_down = (inner_cols(cot_all, full_b_down) * group_select.astype(F32)).astype(BF)
+    cot_wide = jnp.concatenate([cot_all, dz_down], axis=1)
+    down_sum = 0.0
+    norm_grad_sum = 0.0
+    latent_grad_sum = 0.0
+    grads_b_gu = []
+    grads_a_down = []
+    for chunk in range(CHUNKS):
+        for side in range(2):
+            gu = gu_pairs[chunk][side]
+            down = down_pairs[chunk][side]
+            ups = b_gu_pairs[chunk][side]
+            size = gu.shape[1] // 2
+            gate = dot(norm2, gu[:, :size]) + dot(z_gate, ups[:latent])
+            upper = dot(norm2, gu[:, size:]) + dot(z_up, ups[latent:])
+            sigma = jax.nn.sigmoid(gate)
+            active = gate * sigma
+            hidden = (active * upper).astype(BF)
+            hidden_grad = inner_cols(cot_wide, down)
+            gate_grad = (hidden_grad * upper * sigma * (1.0 + gate * (1.0 - sigma))).astype(BF)
+            upper_grad = (hidden_grad * active).astype(BF)
+            both = jnp.concatenate([gate_grad, upper_grad], axis=1)
+            norm_grad_sum = norm_grad_sum + inner_cols(both, gu)
+            latent_grad_sum = latent_grad_sum + jnp.concatenate(
+                [inner_cols(gate_grad, ups[:latent]), inner_cols(upper_grad, ups[latent:])], axis=1
+            )
+            down_sum = down_sum + dot(hidden, down)
+            grads_b_gu.append(
+                jnp.concatenate([inner_rows(z_gate, gate_grad), inner_rows(z_up, upper_grad)], axis=0)
+            )
+            grads_a_down.append(inner_rows(hidden, dz_down))
+
+    wide = plane_scatter(jnp.concatenate([norm_grad_sum, latent_grad_sum], axis=1))
+    dz_gu = (wide[:, width:] * jnp.tile(select, (1, 2)).astype(F32)).astype(BF)
+    second_norm_grad = wide[:, :width] + inner_cols(dz_gu, full_a_gu)
+    second_grad = cot_low.astype(F32) + norm_back(second_norm, second_factor, second_norm_grad)
+    branch_grad = second_grad.astype(BF)
+    dz_out = (inner_cols(branch_grad, full_b_out) * select.astype(F32)).astype(BF)
+    mixed_grad = (inner_cols(branch_grad, full_out) + inner_cols(dz_out, full_a_out)).astype(BF)
+    mixed_grad_h = lax.all_to_all(
+        by_device(mixed_grad), "seq", split_axis=1, concat_axis=0, tiled=True
+    )
+
+    wide = plane_scatter(down_sum)
+    z_down = wide[:, width:].astype(BF) * select
+    activations = second + (wide[:, :width] + dot(z_down, full_b_down))
+
+    grads_a, grads_b = attend_plane_back(scalars, qkv_a, qkv_b, mixed_grad_h, log_sums, rows)
+    grads_b = swap(grads_b, 1)
+
+    def unturn(parts):
+        pre = [
+            rotate_back(
+                part.astype(F32).reshape(-1, heads_dev, HEAD_DIM), cosine, sine
+            ).reshape(-1, span).astype(BF)
+            for part in (parts[0], parts[1])
+        ]
+        return [pre[0], pre[1], parts[2]]
+
+    parts_own = unturn(grads_a)
+    parts_oth = unturn(grads_b)
+    latent_grad = jnp.concatenate(
+        [
+            inner_cols(own, up_own) + inner_cols(oth, up_oth)
+            for own, up_own, oth, up_oth in zip(parts_own, b_parts_own, parts_oth, b_parts_oth)
+        ],
+        axis=1,
+    )
+    norm_grad = inner_cols(jnp.concatenate(parts_own, axis=1), qkv_own) + inner_cols(
+        jnp.concatenate(parts_oth, axis=1), qkv_oth
+    )
+    wide = plane_scatter(jnp.concatenate([norm_grad, latent_grad], axis=1))
+    dz_qkv = (wide[:, width:] * jnp.tile(select, (1, 3)).astype(F32)).astype(BF)
+    first_norm_grad = wide[:, :width] + inner_cols(dz_qkv, full_a_qkv)
+    input_grad = second_grad + norm_back(first_norm, first_factor, first_norm_grad)
+
+    def core_rows(value):
+        half = value.shape[1] // 2
+        return take(value, core * half, half, 1) + swap(take(value, (1 - core) * half, half, 1), 1)
+
+    def z_lanes(value):
+        count = value.shape[2] // LANES
+        return jnp.concatenate([value[:, :, k * LANES : (k + 1) * LANES] for k in range(count)], axis=1)
+
+    def chip_columns(value):
+        return jnp.concatenate(
+            [take(value, z * quarter + chip * LANES, LANES, 1) for z in range(z_count)], axis=1
+        )
+
+    def column_split(value):
+        size = value.shape[1] // z_count
+        return jnp.stack([value[:, z * size : (z + 1) * size] for z in range(z_count)])
+
+    def finish(pieces):
+        stacked = jnp.concatenate(pieces, axis=1)
+        summed = lax.psum_scatter(stacked, "fsdp", scatter_dimension=0, tiled=True)[0]
+        whole = lax.all_gather(summed, "seq", axis=0, tiled=False)
+        result = []
+        at = 0
+        for piece in pieces:
+            result.append(whole[:, at : at + piece.shape[1]])
+            at += piece.shape[1]
+        return result
+
+    slice_b_gu = []
+    slice_a_down = []
+    for chunk in range(CHUNKS):
+        mine, theirs = grads_b_gu[2 * chunk], grads_b_gu[2 * chunk + 1]
+        slice_b_gu.append(column_split(mine + swap(theirs, 1)))
+        mine, theirs = grads_a_down[2 * chunk], grads_a_down[2 * chunk + 1]
+        slice_a_down.append((mine + swap(theirs, 1)).reshape(z_count, ff_chunk, latent))
+    dz_gu_all = plane_gather(dz_gu)
+    slice_a_gu = inner_rows(chip_columns(norm2), dz_gu_all).reshape(z_count, LANES, 2 * latent)
+    slice_a_gu = z_lanes(core_rows(slice_a_gu))
+    z_down_all = plane_gather(z_down)
+    slice_b_down = core_rows(column_split(inner_rows(z_down_all, chip_columns(cot_all))))
+    dz_out_all = lax.all_gather(dz_out, "seq", axis=0, tiled=True)
+    rows_out = inner_rows(mixed_h, dz_out_all).reshape(heads_dev, HEAD_DIM, latent)
+    half = HEAD_DIM // 2
+    kept = take(rows_out, core * half, half, 1)
+    brought = swap(take(rows_out, (1 - core) * half, half, 1), 1)
+    slice_a_out = jnp.where(
+        core == 0,
+        jnp.concatenate([kept, brought], axis=0),
+        jnp.concatenate([brought, kept], axis=0),
+    )
+    slice_b_out = lax.psum_scatter(
+        inner_rows(z_out, branch_grad), "seq", scatter_dimension=0, tiled=True
+    )
+    slice_b_out = z_lanes(column_split(slice_b_out))
+    got = finish(slice_b_gu + slice_a_down + [slice_a_gu, slice_b_down, slice_a_out, slice_b_out])
+    g_b_gu = jnp.stack(got[:CHUNKS], axis=1)
+    g_b_gu = g_b_gu.transpose(2, 0, 1, 3).reshape(2 * latent, ff_z)
+    g_a_down = jnp.concatenate(got[CHUNKS : 2 * CHUNKS], axis=1).reshape(ff_z, latent)
+    g_a_gu, g_b_down, g_a_out, g_b_out = got[2 * CHUNKS :]
+    share_rows = LANES // 2
+
+    def from_rows(value, count):
+        value = value.reshape(PLANE, count, share_rows, LANES).transpose(0, 2, 1, 3)
+        return value.reshape(PLANE * share_rows, count * LANES)
+
+    def from_columns(value):
+        value = value.reshape(CHIPS, 2, -1, LANES).transpose(1, 2, 0, 3)
+        return value.reshape(-1, CHIPS * LANES)
+
+    g_a_gu = from_rows(g_a_gu, 2)
+    g_b_down = from_columns(g_b_down)
+    g_a_out = g_a_out.reshape(quarter, latent)
+    g_b_out = g_b_out.reshape(PLANE, -1, share_b, LANES).transpose(0, 2, 1, 3).reshape(latent, quarter)
+
+    dz_qkv_all = plane_gather(dz_qkv)
+    slice_a_qkv = inner_rows(chip_columns(norm1), dz_qkv_all).reshape(z_count, LANES, 3 * latent)
+    slice_a_qkv = z_lanes(core_rows(slice_a_qkv))
+    up_own = jnp.concatenate([inner_rows(z, g) for z, g in zip(z_parts, parts_own)], axis=0)
+    up_oth = jnp.concatenate([inner_rows(z, g) for z, g in zip(z_parts, parts_oth)], axis=0)
+    slice_b_qkv = jnp.where(
+        core == 0,
+        jnp.concatenate([up_own, up_oth], axis=1),
+        jnp.concatenate([up_oth, up_own], axis=1),
+    )
+    slice_b_qkv = core_rows(column_split(slice_b_qkv))
+    g_a_qkv, g_b_qkv = finish([slice_a_qkv, slice_b_qkv])
+    g_a_qkv = from_rows(g_a_qkv, 3)
+    g_b_qkv = from_columns(g_b_qkv)
+
+    return (
+        activations[None], input_grad[None],
+        g_a_qkv, g_b_qkv, g_a_out, g_b_out, g_a_gu, g_b_gu, g_a_down, g_b_down,
+    )
+
+
 def solution(mesh):
     placed = (
         P("fsdp", "seq", None),
@@ -429,8 +977,9 @@
         P("fsdp", None),
         P(None, "fsdp"),
     )
+    on_plane = mesh.shape["seq"] == PLANE and mesh.shape["fsdp"] == 4
     return jax.shard_map(
-        shards,
+        plane_shards if on_plane else shards,
         mesh=mesh,
         in_specs=placed,
         out_specs=(

time: 3630 us -> 1170 us (0.32)
  waiting for transfers between devices: 2950 us -> 546 us
  matrix products: 339 us -> 203 us
  local copies, waits for them, and re-layouts: 125 us -> 175 us
  Pallas kernels: 0 us -> 38.8 us
    all_gather x9, waiting for transfers between devices: 2160 us -> 312 us  [the longest x4 209 us: plane_shards(): own = lax.all_gather(part, 'fsdp', axis=0, tiled=True)]
    psum x1 -> x0, waiting for transfers between devices: 761 us -> none  [shards(): lax.psum((grads[0], grads[1], grads[2], grads[3], grads[4], grads[5], gra...]
    ppermute x0 -> x53, waiting for transfers between devices: none -> 166 us  [swap(): return lax.ppermute(value, 'seq', [(i, i ^ bit) for i in range(PLANE)])]
    dot_general x43 -> x34, matrix products: 217 us -> 90.8 us  [dot(): return jnp.dot(left, right, preferred_element_type=F32)]
    reduce_scatter x0 -> x3, waiting for transfers between devices: none -> 62.4 us  [the longest x2 62.4 us: finish(): lax.psum_scatter(stacked, 'fsdp', scatter_dimension=0, tiled=True)[0]]
    unnamed x142 -> x345, local copies, waits for them, and re-layouts: 21.6 us -> 76.5 us
    ppermute x0 -> x53, starting transfers between devices: none -> 53.2 us  [swap(): return lax.ppermute(value, 'seq', [(i, i ^ bit) for i in range(PLANE)])]
    all_to_all x8 -> x2, starting transfers between devices: 50.2 us -> 7.62 us  [the longest x1 3.81 us: plane_shards(): lax.all_to_all(by_device(mixed_grad), 'seq', split_axis=1, concat_axis=0,...]
  transfers between devices with their start and end apart: 18 -> 67, of which waited for: 13 -> 26; matrix products, arithmetic and copies ran while one was open for 9% -> 33% of each run, Pallas kernels for 0% -> 3%
where the time goes in v1:
time: 1170 us; the launch traced here: 1160 us
  waiting for transfers between devices  546 us (47%)
  matrix products  203 us (17%)
  local copies, waits for them, and re-layouts  175 us (15%)
  other arithmetic  72.1 us (6%)
  starting transfers between devices  61.4 us (5%)
  blocking collectives  45.9 us (4%)
  Pallas kernels  38.8 us (3%)
  between operations  17 us (1%)
    all_gather x4, waiting for transfers between devices, plane_shards(): own = lax.all_gather(part, 'fsdp', axis=0, tiled=True)  209 us
    ppermute x53, waiting for transfers between devices, swap(): return lax.ppermute(value, 'seq', [(i, i ^ bit) for i in range(PLANE)])  166 us
    dot_general x30, matrix products, inner_cols(): lax.dot_general(left, right, (((1,), (1,)), ((), ())), preferred_element_...  91.3 us
    dot_general x34, matrix products, dot(): return jnp.dot(left, right, preferred_element_type=F32)  90.8 us
    unnamed x345, local copies, waits for them, and re-layouts  76.5 us
    reduce_scatter x2, waiting for transfers between devices, finish(): lax.psum_scatter(stacked, 'fsdp', scatter_dimension=0, tiled=True)[0]  62.4 us
    all_gather x2, waiting for transfers between devices, finish(): whole = lax.all_gather(summed, 'seq', axis=0, tiled=False)  57.9 us
    ppermute x53, starting transfers between devices, swap(): return lax.ppermute(value, 'seq', [(i, i ^ bit) for i in range(PLANE)])  53.2 us
  transfers between devices with their start and end apart: 67, of which 26 were waited for; matrix products, arithmetic and copies ran while one was open for 33% of the time, Pallas kernels for 3%

profile of v1, /device:TPU:1, one launch (start us, length us, event | category | flops | bytes accessed | tf_op | source)
XLA Modules:
  0.0 1158.6 jit_solution(17664401175541138478)
XLA Ops:
  52.9 21.9 %all_gather.45 = bf16[1024,256]{1,0:T(8,128)(2,1)} all-gather(bf16[256,256]{1,0:T(8,128)(2,1)S(1)} %constant_dynamic-slice_fusion.22), channel_id=1, replica_groups=mesh['seq'=8,'fsdp'=4] {'fsdp'}, dimensions={0}, use_global_device_ids=true | all-gather | bytes 655360 | tf_op jit(solution)/shard_map/all_gather | solution.py:705
  74.8 3.3 collective-permute-start.11
  90.0 12.2 %all_gather.42 = bf16[384,512]{1,0:T(8,128)(2,1)S(1)} all-gather(bf16[384,128]{1,0:T(8,128)(2,1)} %constant_dynamic-slice_fusion.26), channel_id=1, replica_groups=mesh['seq'=8,'fsdp'=4] {'fsdp'}, dimensions={1}, use_global_device_ids=true | all-gather | bytes 491520 | tf_op jit(solution)/shard_map/all_gather | solution.py:695
  126.1 19.5 %collective-permute-done.3 = bf16[128,2048]{1,0:T(8,128)(2,1)S(1)} collective-permute-done((bf16[128,2048]{1,0:T(8,128)(2,1)S(1)}, bf16[128,2048]{1,0:T(8,128)(2,1)S(1)}, u32[]{:S(2)}, u32[]{:S(2)}) %collective-permute-start.3) | collective-permute-done | bytes 524320 | tf_op jit(solution)/shard_map/ppermute | solution.py:426
  146.5 12.2 %all-gather.27.cloned.1.call-done = bf16[16384,128]{1,0:T(8,128)(2,1)} async-done(((bf16[512,128]{1,0:T(8,128)(2,1)}), bf16[16384,128]{1,0:T(8,128)(2,1)}) %all-gather.27.cloned.1.call-update) | async-done | bytes 4194320 | tf_op jit(solution)/shard_map/all_gather | solution.py:669
  165.1 5.5 maximum_add_fusion.1
  175.1 3.4 maximum_add_fusion
  184.1 2.9 reshape.329
  187.0 4.6 slice_negate_fusion
  207.8 47.9 %all-gather.17.cloned.1.call-done = bf16[512,2176]{1,0:T(8,128)(2,1)} async-done(((bf16[128,2176]{1,0:T(8,128)(2,1)}), bf16[512,2176]{1,0:T(8,128)(2,1)}) %all-gather.17.cloned.1.call-update) | async-done | bytes 2228240 | tf_op jit(solution)/shard_map/all_gather | solution.py:721
  256.4 80.4 %all-gather.19.cloned.1.call-done = bf16[2048,1024]{1,0:T(8,128)(2,1)} async-done(((bf16[512,1024]{1,0:T(8,128)(2,1)}), bf16[2048,1024]{1,0:T(8,128)(2,1)}) %all-gather.19.cloned.1.call-update) | async-done | bytes 4194320 | tf_op jit(solution)/shard_map/all_gather | solution.py:717
  337.5 80.7 %all-gather.15.cloned.1.call-done = bf16[2048,1024]{1,0:T(8,128)(2,1)} async-done(((bf16[512,1024]{1,0:T(8,128)(2,1)}), bf16[2048,1024]{1,0:T(8,128)(2,1)}) %all-gather.15.cloned.1.call-update) | async-done | bytes 4194320 | tf_op jit(solution)/shard_map/all_gather | solution.py:717
  431.9 15.5 %shard_map.231 = (bf16[2048,256]{1,0:T(8,128)(2,1)S(1)}, f32[2048,256]{1,0:T(8,128)}) custom-call(s32[6]{0:T(128)S(1)} %pad_add_fusion.scalars, bf16[1024,768]{1,0:T(8,128)(2,1)S(1)} %pad_maximum_fusion.4.qa.ka.va, bf16[1024,768]{1,0:T(8,128)(2,1)S(1)} %pad_maximum_fusion.4.qa.ka.va, bf16[1024,768]{1,0:T(8,128)(2,1)S(1)} %pad_maximum_fusion.4.qa.ka.va, ...), custom_call_target="tpu_custom_call" | custom-call | flops 2147483648 | bytes 4194304 | tf_op jit(solution)/shard_map/pallas_call | solution.py:566
  448.8 3.8 all-to-all-start
  452.8 3.6 fusion.113
  456.9 3.9 fusion.268
  460.9 4.7 all-to-all-done
  467.7 33.2 %all-gather.13.cloned.1.call-done = bf16[2048,2048]{1,0:T(8,128)(2,1)} async-done(((bf16[64,2048]{1,0:T(8,128)(2,1)}), bf16[2048,2048]{1,0:T(8,128)(2,1)}) %all-gather.13.cloned.1.call-update) | async-done | bytes 8388624 | tf_op jit(solution)/shard_map/all_gather | solution.py:701
  500.9 5.7 fusion.297
  510.4 4.1 fusion.270
  515.7 4.3 fusion.269
  520.0 13.1 %collective-permute-done.7 = bf16[256,2048]{1,0:T(8,128)(2,1)S(1)} collective-permute-done((bf16[256,2048]{1,0:T(8,128)(2,1)S(1)}, bf16[256,2048]{1,0:T(8,128)(2,1)S(1)}, u32[]{:S(2)}, u32[]{:S(2)}) %collective-permute-start.7) | collective-permute-done | bytes 1048608 | tf_op jit(solution)/shard_map/ppermute | solution.py:426
  534.3 5.9 fusion.267
  543.2 7.1 collective-permute-done.8
  550.3 4.4 collective-permute-done.9
  559.3 4.0 fusion.87
  563.3 4.9 multiply_convert_fusion.5
  573.6 4.2 multiply_convert_fusion.3
  583.0 4.1 fusion.99
  587.1 5.0 multiply_convert_fusion.1
  598.8 6.5 multiply_convert_fusion.7
  614.4 9.4 fusion.45
  623.8 6.8 fusion.49
  630.6 6.8 fusion.41
  637.4 14.2 %add_add_fusion.1 = f32[1024,2048]{1,0:T(8,128)} fusion(f32[1024,2048]{1,0:T(8,128)} %fusion.49, f32[1024,2048]{1,0:T(8,128)} %fusion.41, f32[1024,2048]{1,0:T(8,128)} %fusion.45, bf16[2048,1024]{1,0:T(8,128)(2,1)} %collective-permute-done.13, bf16[1024,512]{0,1:T(8,128)(2,1)S(1)} %get-tuple-element.127, bf16[1024,512]{0,1:T(8,128)(2,1)S(1)} %get-tuple-element.126), kind=kOutput, calls=%fused_computation.12 | convolution fusion | flops 4305453056 | bytes 39845888 | tf_op jit(solution)/shard_map/dot_general | solution.py:65
  651.6 6.1 fusion
  661.9 6.8 fusion.299
  668.8 5.4 fusion.298
  674.2 5.1 fusion.300
  679.3 12.3 %fusion.296 = (bf16[1024,2176]{1,0:T(8,128)(2,1)}, f32[1024,2176]{1,0:T(8,128)S(1)}) fusion(bf16[1024,512]{0,1:T(8,128)(2,1)S(1)} %copy-done.45, bf16[512,2176]{1,0:T(8,128)(2,1)} %collective-permute-done.14, f32[1024,2176]{1,0:T(8,128)} %fusion.300, f32[1024,2176]{1,0:T(8,128)} %fusion.298, f32[1024,2176]{1,0:T(8,128)} %fusion.299), kind=kOutput, calls=%fused_computation.590 | convolution fusion | flops 2290614272 | bytes 43384832 | tf_op jit(solution)/shard_map/dot_general | solution.py:457
  706.1 18.6 %collective-permute-done.15 = bf16[256,2176]{1,0:T(8,128)(2,1)S(1)} collective-permute-done((bf16[256,2176]{1,0:T(8,128)(2,1)S(1)}, bf16[256,2176]{1,0:T(8,128)(2,1)S(1)}, u32[]{:S(2)}, u32[]{:S(2)}) %collective-permute-start.15) | collective-permute-done | bytes 1114144 | tf_op jit(solution)/shard_map/ppermute | solution.py:426
  728.4 17.7 %collective-permute-done.17 = bf16[256,2176]{1,0:T(8,128)(2,1)S(1)} collective-permute-done((bf16[256,2176]{1,0:T(8,128)(2,1)S(1)}, bf16[256,2176]{1,0:T(8,128)(2,1)S(1)}, u32[]{:S(2)}, u32[]{:S(2)}) %collective-permute-start.17) | collective-permute-done | bytes 1114144 | tf_op jit(solution)/shard_map/ppermute | solution.py:426
  746.2 11.9 %collective-permute-done.16 = bf16[128,2176]{1,0:T(8,128)(2,1)S(1)} collective-permute-done((bf16[128,2176]{1,0:T(8,128)(2,1)S(1)}, bf16[128,2176]{1,0:T(8,128)(2,1)S(1)}, u32[]{:S(2)}, u32[]{:S(2)}) %collective-permute-start.16) | collective-permute-done | bytes 557088 | tf_op jit(solution)/shard_map/ppermute | solution.py:426
  758.8 11.9 %collective-permute-done.24 = bf16[128,2304]{1,0:T(8,128)(2,1)S(1)} collective-permute-done((bf16[128,2304]{1,0:T(8,128)(2,1)S(1)}, bf16[128,2304]{1,0:T(8,128)(2,1)S(1)}, u32[]{:S(2)}, u32[]{:S(2)}) %collective-permute-start.24) | collective-permute-done | bytes 589856 | tf_op jit(solution)/shard_map/ppermute | solution.py:426
  792.0 11.9 %all_gather.50 = bf16[2048,128]{1,0:T(8,128)(2,1)S(1)} all-gather(bf16[256,128]{1,0:T(8,128)(2,1)S(1)} %fusion.126), channel_id=1, replica_groups=mesh['seq'=8,'fsdp'=4] {'seq'}, dimensions={0}, use_global_device_ids=true | all-gather | bytes 589824 | tf_op jit(solution)/shard_map/all_gather | solution.py:906
  803.8 6.4 fusion.265
  814.4 3.8 all-to-all-start.1
  825.3 7.3 collective-permute-done.49
  843.7 23.3 %shard_map.232 = (bf16[3,1024,256]{2,1,0:T(8,128)(2,1)S(1)}, bf16[3,1024,256]{2,1,0:T(8,128)(2,1)}) custom-call(s32[6]{0:T(128)S(1)} %copy-done.10, bf16[1024,768]{1,0:T(8,128)(2,1)S(1)} %copy-done.3, bf16[1024,768]{1,0:T(8,128)(2,1)S(1)} %copy-done.3, bf16[1024,768]{1,0:T(8,128)(2,1)S(1)} %copy-done.3, bf16[1024,768]{1,0:T(8,128)(2,1)} %copy-done.4, ...), custom_call_target="tpu_custom_call" | custom-call | flops 5368709120 | bytes 10485760 | tf_op jit(solution)/shard_map/pallas_call | solution.py:599
  884.1 2.9 slice_bitcast_fusion
  892.5 3.8 broadcast_multiply_fusion.1
  911.7 5.7 fusion.67
  917.4 6.9 convolution_add_fusion
  929.1 25.1 %collective-permute-done.30 = bf16[256,2432]{1,0:T(8,128)(2,1)S(1)} collective-permute-done((bf16[256,2432]{1,0:T(8,128)(2,1)S(1)}, bf16[256,2432]{1,0:T(8,128)(2,1)S(1)}, u32[]{:S(2)}, u32[]{:S(2)}) %collective-permute-start.30) | collective-permute-done | bytes 1245216 | tf_op jit(solution)/shard_map/ppermute | solution.py:426
  956.2 12.8 %collective-permute-done.31 = bf16[128,2432]{1,0:T(8,128)(2,1)S(1)} collective-permute-done((bf16[128,2432]{1,0:T(8,128)(2,1)S(1)}, bf16[128,2432]{1,0:T(8,128)(2,1)S(1)}, u32[]{:S(2)}, u32[]{:S(2)}) %collective-permute-start.31) | collective-permute-done | bytes 622624 | tf_op jit(solution)/shard_map/ppermute | solution.py:426
  971.9 11.2 collective-permute-done.29
  985.7 3.4 collective-permute-start.37
  990.4 3.3 collective-permute-done.34
  994.6 5.1 collective-permute-start.36
  1008.9 13.9 %reduce-scatter.4.cloned.1.call-done = f32[1,384,128]{2,1,0:T(8,128)} async-done(((f32[4,384,128]{2,1,0:T(8,128)}), f32[1,384,128]{2,1,0:T(8,128)}) %reduce-scatter.4.cloned.1.call-update) | async-done | bytes 196624 | tf_op jit(solution)/shard_map/reduce_scatter | solution.py:885
  1022.8 48.5 %reduce-scatter.8.cloned.1.call-done = f32[1,1088,128]{2,1,0:T(8,128)} async-done(((f32[4,1088,128]{2,1,0:T(8,128)}), f32[1,1088,128]{2,1,0:T(8,128)}) %reduce-scatter.8.cloned.1.call-update) | async-done | bytes 557072 | tf_op jit(solution)/shard_map/reduce_scatter | solution.py:885
  1076.3 22.7 %all-gather.23.cloned.1.call-done = f32[8,384,128]{2,1,0:T(8,128)} async-done(((f32[1,384,128]{2,1,0:T(8,128)}), f32[8,384,128]{2,1,0:T(8,128)}) %all-gather.23.cloned.1.call-update) | async-done | bytes 1572880 | tf_op jit(solution)/shard_map/all_gather | solution.py:886
  1103.4 35.2 %all-gather.25.cloned.1.call-done = f32[8,1088,128]{2,1,0:T(8,128)} async-done(((f32[1,1088,128]{2,1,0:T(8,128)}), f32[8,1088,128]{2,1,0:T(8,128)}) %all-gather.25.cloned.1.call-update) | async-done | bytes 4456464 | tf_op jit(solution)/shard_map/all_gather | solution.py:886
  1148.5 3.0 copy.236
  (703 shorter events, 319.7 us)
Async XLA Ops:
  7.2 95.0 %all-gather.11.cloned.1.call-start = ((), (), s32[]{:S(2)}) async-start(), calls=%async_computation.5 | async-start | bytes 3932160 | tf_op jit(solution)/shard_map/all_gather | solution.py:654
  14.0 144.6 %all-gather.27.cloned.1.call-start = ((), (), s32[]{:S(2)}) async-start(), calls=%async_computation.16 | async-start | bytes 4325376 | tf_op jit(solution)/shard_map/all_gather | solution.py:669
  24.6 182.9 %all-gather.21.cloned.1.call-start = ((), (), s32[]{:S(2)}) async-start(), calls=%async_computation.10 | async-start | bytes 2785280 | tf_op jit(solution)/shard_map/all_gather | solution.py:721
  27.7 228.0 %all-gather.17.cloned.1.call-start = ((), (), s32[]{:S(2)}) async-start(), calls=%async_computation.8 | async-start | bytes 2785280 | tf_op jit(solution)/shard_map/all_gather | solution.py:721
  28.7 308.1 %all-gather.19.cloned.1.call-start = ((), (), s32[]{:S(2)}) async-start(), calls=%async_computation.9 | async-start | bytes 5242880 | tf_op jit(solution)/shard_map/all_gather | solution.py:717
  45.4 372.7 %all-gather.15.cloned.1.call-start = ((), (), s32[]{:S(2)}) async-start(), calls=%async_computation.7 | async-start | bytes 5242880 | tf_op jit(solution)/shard_map/all_gather | solution.py:717
  46.0 454.9 %all-gather.13.cloned.1.call-start = ((), (), s32[]{:S(2)}) async-start(), calls=%async_computation.6 | async-start | bytes 8650752 | tf_op jit(solution)/shard_map/all_gather | solution.py:701
  46.0 68.1 %collective-permute-start.19 = (bf16[256,2048]{1,0:T(8,128)(2,1)}, bf16[256,2048]{1,0:T(8,128)(2,1)}, u32[]{:S(2)}, u32[]{:S(2)}) collective-permute-start(bf16[256,2048]{1,0:T(8,128)(2,1)} %bitcast.399), channel_id=1, source_target_pairs={{0,8},{4,12},{8,0},{12,4},{16,24},{20,28},{24,16},{28,20},{1,9},{5... | collective-permute-start | bytes 3145736 | tf_op jit(solution)/shard_map/ppermute | solution.py:426
  48.1 69.2 %collective-permute-start.20 = (bf16[256,2048]{1,0:T(8,128)(2,1)}, bf16[256,2048]{1,0:T(8,128)(2,1)}, u32[]{:S(2)}, u32[]{:S(2)}) collective-permute-start(bf16[256,2048]{1,0:T(8,128)(2,1)} %bitcast.400), channel_id=1, source_target_pairs={{0,16},{4,20},{8,24},{12,28},{16,0},{20,4},{24,8},{28,12},{1,17},{... | collective-permute-start | bytes 3145736 | tf_op jit(solution)/shard_map/ppermute | solution.py:426
  51.7 55.3 %collective-permute-start.1 = (bf16[256,2048]{1,0:T(8,128)(2,1)}, bf16[256,2048]{1,0:T(8,128)(2,1)}, u32[]{:S(2)}, u32[]{:S(2)}) collective-permute-start(bf16[256,2048]{1,0:T(8,128)(2,1)} %get-tuple-element.73), channel_id=1, source_target_pairs={{0,16},{4,20},{8,24},{12,28},{16,0},{20,4},{24,8},{28,12},{1,17},{... | collective-permute-start | bytes 3145736 | tf_op jit(solution)/shard_map/ppermute | solution.py:426
  51.9 67.5 %collective-permute-start = (bf16[256,2048]{1,0:T(8,128)(2,1)}, bf16[256,2048]{1,0:T(8,128)(2,1)}, u32[]{:S(2)}, u32[]{:S(2)}) collective-permute-start(bf16[256,2048]{1,0:T(8,128)(2,1)} %get-tuple-element.73), channel_id=1, source_target_pairs={{0,8},{4,12},{8,0},{12,4},{16,24},{20,28},{24,16},{28,20},{1,9},{5... | collective-permute-start | bytes 3145736 | tf_op jit(solution)/shard_map/ppermute | solution.py:426
  74.8 27.4 %collective-permute-start.11 = (bf16[1024,256]{1,0:T(8,128)(2,1)}, bf16[1024,256]{1,0:T(8,128)(2,1)}, u32[]{:S(2)}, u32[]{:S(2)}) collective-permute-start(bf16[1024,256]{1,0:T(8,128)(2,1)} %all_gather.45), channel_id=1, source_target_pairs={{0,4},{4,0},{8,12},{12,8},{16,20},{20,16},{24,28},{28,24},{1,5},{5... | collective-permute-start | bytes 1572872 | tf_op jit(solution)/shard_map/ppermute | solution.py:426
  102.2 62.8 %collective-permute-start.4 = (bf16[2048,768]{1,0:T(8,128)(2,1)}, bf16[2048,768]{1,0:T(8,128)(2,1)}, u32[]{:S(2)}, u32[]{:S(2)}) collective-permute-start(bf16[2048,768]{1,0:T(8,128)(2,1)} %all-gather.11.cloned.1.call-done), channel_id=1, source_target_pairs={{0,4},{4,0},{8,12},{12,8},{16,20},{20,16},{24,28},{28,24},{1,5},{5... | collective-permute-start | bytes 9437192 | tf_op jit(solution)/shard_map/ppermute | solution.py:426
  108.1 17.2 %collective-permute-start.2 = (bf16[128,2048]{1,0:T(8,128)(2,1)S(1)}, bf16[128,2048]{1,0:T(8,128)(2,1)S(1)}, u32[]{:S(2)}, u32[]{:S(2)}) collective-permute-start(bf16[128,2048]{1,0:T(8,128)(2,1)S(1)} %slice.835), channel_id=1, source_target_pairs={{0,8},{4,12},{8,0},{12,4},{16,24},{20,28},{24,16},{28,20},{1,9},{5... | collective-permute-start | bytes 1572872 | tf_op jit(solution)/shard_map/ppermute | solution.py:426
  116.0 87.2 %collective-permute-start.22 = (bf16[128,2048]{1,0:T(8,128)(2,1)}, bf16[128,2048]{1,0:T(8,128)(2,1)}, u32[]{:S(2)}, u32[]{:S(2)}) collective-permute-start(bf16[128,2048]{1,0:T(8,128)(2,1)} %slice.909), channel_id=1, source_target_pairs={{0,16},{4,20},{8,24},{12,28},{16,0},{20,4},{24,8},{28,12},{1,17},{... | collective-permute-start | bytes 1572872 | tf_op jit(solution)/shard_map/ppermute | solution.py:426
  119.2 83.0 %collective-permute-start.21 = (bf16[128,2048]{1,0:T(8,128)(2,1)}, bf16[128,2048]{1,0:T(8,128)(2,1)}, u32[]{:S(2)}, u32[]{:S(2)}) collective-permute-start(bf16[128,2048]{1,0:T(8,128)(2,1)} %slice.908), channel_id=1, source_target_pairs={{0,8},{4,12},{8,0},{12,4},{16,24},{20,28},{24,16},{28,20},{1,9},{5... | collective-permute-start | bytes 1572872 | tf_op jit(solution)/shard_map/ppermute | solution.py:426
  120.5 25.1 %collective-permute-start.3 = (bf16[128,2048]{1,0:T(8,128)(2,1)S(1)}, bf16[128,2048]{1,0:T(8,128)(2,1)S(1)}, u32[]{:S(2)}, u32[]{:S(2)}) collective-permute-start(bf16[128,2048]{1,0:T(8,128)(2,1)S(1)} %slice.836), channel_id=1, source_target_pairs={{0,16},{4,20},{8,24},{12,28},{16,0},{20,4},{24,8},{28,12},{1,17},{... | collective-permute-start | bytes 1572872 | tf_op jit(solution)/shard_map/ppermute | solution.py:426
  197.1 234.8 %collective-permute-start.5 = (bf16[1024,768]{1,0:T(8,128)(2,1)}, bf16[1024,768]{1,0:T(8,128)(2,1)S(1)}, u32[]{:S(2)}, u32[]{:S(2)}) collective-permute-start(bf16[1024,768]{1,0:T(8,128)(2,1)} %pad_maximum_fusion.5), channel_id=1, source_target_pairs={{0,4},{4,0},{8,12},{12,8},{16,20},{20,16},{24,28},{28,24},{1,5},{5... | collective-permute-start | bytes 4718600 | tf_op jit(solution)/shard_map/ppermute | solution.py:426
  207.5 326.8 %collective-permute-start.14 = (bf16[512,2176]{1,0:T(8,128)(2,1)}, bf16[512,2176]{1,0:T(8,128)(2,1)}, u32[]{:S(2)}, u32[]{:S(2)}) collective-permute-start(bf16[512,2176]{1,0:T(8,128)(2,1)} %all-gather.21.cloned.1.call-done), channel_id=1, source_target_pairs={{0,4},{4,0},{8,12},{12,8},{16,20},{20,16},{24,28},{28,24},{1,5},{5... | collective-permute-start | bytes 6684680 | tf_op jit(solution)/shard_map/ppermute | solution.py:426
  255.7 258.8 %collective-permute-start.12 = (bf16[512,2176]{1,0:T(8,128)(2,1)}, bf16[512,2176]{1,0:T(8,128)(2,1)}, u32[]{:S(2)}, u32[]{:S(2)}) collective-permute-start(bf16[512,2176]{1,0:T(8,128)(2,1)} %all-gather.17.cloned.1.call-done), channel_id=1, source_target_pairs={{0,4},{4,0},{8,12},{12,8},{16,20},{20,16},{24,28},{28,24},{1,5},{5... | collective-permute-start | bytes 6684680 | tf_op jit(solution)/shard_map/ppermute | solution.py:426
  336.8 246.2 %collective-permute-start.13 = (bf16[2048,1024]{1,0:T(8,128)(2,1)}, bf16[2048,1024]{1,0:T(8,128)(2,1)}, u32[]{:S(2)}, u32[]{:S(2)}) collective-permute-start(bf16[2048,1024]{1,0:T(8,128)(2,1)} %all-gather.19.cloned.1.call-done), channel_id=1, source_target_pairs={{0,4},{4,0},{8,12},{12,8},{16,20},{20,16},{24,28},{28,24},{1,5},{5... | collective-permute-start | bytes 12582920 | tf_op jit(solution)/shard_map/ppermute | solution.py:426
  418.1 141.2 %collective-permute-start.10 = (bf16[2048,1024]{1,0:T(8,128)(2,1)}, bf16[2048,1024]{1,0:T(8,128)(2,1)}, u32[]{:S(2)}, u32[]{:S(2)}) collective-permute-start(bf16[2048,1024]{1,0:T(8,128)(2,1)} %all-gather.15.cloned.1.call-done), channel_id=1, source_target_pairs={{0,4},{4,0},{8,12},{12,8},{16,20},{20,16},{24,28},{28,24},{1,5},{5... | collective-permute-start | bytes 12582920 | tf_op jit(solution)/shard_map/ppermute | solution.py:426
  448.8 16.8 %all-to-all-start = ((bf16[8,256,256]{1,2,0:T(8,128)(2,1)}), bf16[8,256,256]{1,2,0:T(8,128)(2,1)S(1)}, u32[]{:S(2)}, u32[]{:S(2)}) async-start(bf16[8,256,256]{1,2,0:T(8,128)(2,1)} %copy.199), calls=%async_computation | async-start | bytes 2097152 | tf_op jit(solution)/shard_map/all_to_all | solution.py:759
  452.6 552.9 %reduce-scatter.6.cloned.1.call-start = ((), (), s32[]{:S(2)}) async-start(), calls=%async_computation.13 | async-start | bytes 1179648 | tf_op jit(solution)/shard_map/reduce_scatter | solution.py:916
  508.5 24.5 %collective-permute-start.7 = (bf16[256,2048]{1,0:T(8,128)(2,1)S(1)}, bf16[256,2048]{1,0:T(8,128)(2,1)S(1)}, u32[]{:S(2)}, u32[]{:S(2)}) collective-permute-start(bf16[256,2048]{1,0:T(8,128)(2,1)S(1)} %get-tuple-element.71), channel_id=1, source_target_pairs={{0,16},{4,20},{8,24},{12,28},{16,0},{20,4},{24,8},{28,12},{1,17},{... | collective-permute-start | bytes 3145736 | tf_op jit(solution)/shard_map/ppermute | solution.py:426
  514.5 28.0 %collective-permute-start.6 = (bf16[256,2048]{1,0:T(8,128)(2,1)S(1)}, bf16[256,2048]{1,0:T(8,128)(2,1)S(1)}, u32[]{:S(2)}, u32[]{:S(2)}) collective-permute-start(bf16[256,2048]{1,0:T(8,128)(2,1)S(1)} %get-tuple-element.71), channel_id=1, source_target_pairs={{0,8},{4,12},{8,0},{12,4},{16,24},{20,28},{24,16},{28,20},{1,9},{5... | collective-permute-start | bytes 3145736 | tf_op jit(solution)/shard_map/ppermute | solution.py:426
  533.1 17.2 %collective-permute-start.8 = (bf16[128,2048]{1,0:T(8,128)(2,1)S(1)}, bf16[128,2048]{1,0:T(8,128)(2,1)S(1)}, u32[]{:S(2)}, u32[]{:S(2)}) collective-permute-start(bf16[128,2048]{1,0:T(8,128)(2,1)S(1)} %slice.868), channel_id=1, source_target_pairs={{0,8},{4,12},{8,0},{12,4},{16,24},{20,28},{24,16},{28,20},{1,9},{5... | collective-permute-start | bytes 1572872 | tf_op jit(solution)/shard_map/ppermute | solution.py:426
  542.6 12.1 %collective-permute-start.9 = (bf16[128,2048]{1,0:T(8,128)(2,1)S(1)}, bf16[128,2048]{1,0:T(8,128)(2,1)S(1)}, u32[]{:S(2)}, u32[]{:S(2)}) collective-permute-start(bf16[128,2048]{1,0:T(8,128)(2,1)S(1)} %slice.869), channel_id=1, source_target_pairs={{0,16},{4,20},{8,24},{12,28},{16,0},{20,4},{24,8},{28,12},{1,17},{... | collective-permute-start | bytes 1572872 | tf_op jit(solution)/shard_map/ppermute | solution.py:426
  608.1 89.5 %collective-permute-start.40 = (f32[512,128]{1,0:T(8,128)}, f32[512,128]{1,0:T(8,128)}, u32[]{:S(2)}, u32[]{:S(2)}) collective-permute-start(f32[512,128]{1,0:T(8,128)} %fusion.310), channel_id=1, source_target_pairs={{0,4},{4,0},{8,12},{12,8},{16,20},{20,16},{24,28},{28,24},{1,5},{5... | collective-permute-start | bytes 786440 | tf_op jit(solution)/shard_map/ppermute | solution.py:426
  611.2 90.6 %collective-permute-start.38 = (f32[256,512]{1,0:T(8,128)}, f32[256,512]{1,0:T(8,128)}, u32[]{:S(2)}, u32[]{:S(2)}) collective-permute-start(f32[256,512]{1,0:T(8,128)} %pad_maximum_fusion.22), channel_id=1, source_target_pairs={{0,4},{4,0},{8,12},{12,8},{16,20},{20,16},{24,28},{28,24},{1,5},{5... | collective-permute-start | bytes 1572872 | tf_op jit(solution)/shard_map/ppermute | solution.py:426
  612.3 82.9 %collective-permute-start.41 = (f32[512,128]{1,0:T(8,128)}, f32[512,128]{1,0:T(8,128)}, u32[]{:S(2)}, u32[]{:S(2)}) collective-permute-start(f32[512,128]{1,0:T(8,128)} %fusion.311), channel_id=1, source_target_pairs={{0,4},{4,0},{8,12},{12,8},{16,20},{20,16},{24,28},{28,24},{1,5},{5... | collective-permute-start | bytes 786440 | tf_op jit(solution)/shard_map/ppermute | solution.py:426
  613.7 86.0 %collective-permute-start.39 = (f32[256,512]{1,0:T(8,128)}, f32[256,512]{1,0:T(8,128)}, u32[]{:S(2)}, u32[]{:S(2)}) collective-permute-start(f32[256,512]{1,0:T(8,128)} %pad_maximum_fusion.23), channel_id=1, source_target_pairs={{0,4},{4,0},{8,12},{12,8},{16,20},{20,16},{24,28},{28,24},{1,5},{5... | collective-permute-start | bytes 1572872 | tf_op jit(solution)/shard_map/ppermute | solution.py:426
  661.4 64.1 %collective-permute-start.23 = (bf16[256,2304]{1,0:T(8,128)(2,1)}, bf16[256,2304]{1,0:T(8,128)(2,1)}, u32[]{:S(2)}, u32[]{:S(2)}) collective-permute-start(bf16[256,2304]{1,0:T(8,128)(2,1)} %pad_maximum_fusion.8), channel_id=1, source_target_pairs={{0,8},{4,12},{8,0},{12,4},{16,24},{20,28},{24,16},{28,20},{1,9},{5... | collective-permute-start | bytes 3538952 | tf_op jit(solution)/shard_map/ppermute | solution.py:426
  695.3 30.2 %collective-permute-start.25 = (bf16[256,2304]{1,0:T(8,128)(2,1)S(1)}, bf16[256,2304]{1,0:T(8,128)(2,1)S(1)}, u32[]{:S(2)}, u32[]{:S(2)}) collective-permute-start(bf16[256,2304]{1,0:T(8,128)(2,1)S(1)} %pad_maximum_fusion.9), channel_id=1, source_target_pairs={{0,16},{4,20},{8,24},{12,28},{16,0},{20,4},{24,8},{28,12},{1,17},{... | collective-permute-start | bytes 3538952 | tf_op jit(solution)/shard_map/ppermute | solution.py:426
  697.5 48.6 %collective-permute-start.17 = (bf16[256,2176]{1,0:T(8,128)(2,1)S(1)}, bf16[256,2176]{1,0:T(8,128)(2,1)S(1)}, u32[]{:S(2)}, u32[]{:S(2)}) collective-permute-start(bf16[256,2176]{1,0:T(8,128)(2,1)S(1)} %pad_maximum_fusion.11), channel_id=1, source_target_pairs={{0,16},{4,20},{8,24},{12,28},{16,0},{20,4},{24,8},{28,12},{1,17},{... | collective-permute-start | bytes 3342344 | tf_op jit(solution)/shard_map/ppermute | solution.py:426
  699.7 25.0 %collective-permute-start.15 = (bf16[256,2176]{1,0:T(8,128)(2,1)S(1)}, bf16[256,2176]{1,0:T(8,128)(2,1)S(1)}, u32[]{:S(2)}, u32[]{:S(2)}) collective-permute-start(bf16[256,2176]{1,0:T(8,128)(2,1)S(1)} %pad_maximum_fusion.10), channel_id=1, source_target_pairs={{0,8},{4,12},{8,0},{12,4},{16,24},{20,28},{24,16},{28,20},{1,9},{5... | collective-permute-start | bytes 3342344 | tf_op jit(solution)/shard_map/ppermute | solution.py:426
  724.8 33.3 %collective-permute-start.16 = (bf16[128,2176]{1,0:T(8,128)(2,1)S(1)}, bf16[128,2176]{1,0:T(8,128)(2,1)S(1)}, u32[]{:S(2)}, u32[]{:S(2)}) collective-permute-start(bf16[128,2176]{1,0:T(8,128)(2,1)S(1)} %fusion.132), channel_id=1, source_target_pairs={{0,16},{4,20},{8,24},{12,28},{16,0},{20,4},{24,8},{28,12},{1,17},{... | collective-permute-start | bytes 1671176 | tf_op jit(solution)/shard_map/ppermute | solution.py:426
  726.8 32.0 %collective-permute-start.26 = (bf16[128,2304]{1,0:T(8,128)(2,1)S(1)}, bf16[128,2304]{1,0:T(8,128)(2,1)S(1)}, u32[]{:S(2)}, u32[]{:S(2)}) collective-permute-start(bf16[128,2304]{1,0:T(8,128)(2,1)S(1)} %get-tuple-element.90), channel_id=1, source_target_pairs={{0,8},{4,12},{8,0},{12,4},{16,24},{20,28},{24,16},{28,20},{1,9},{5... | collective-permute-start | bytes 1769480 | tf_op jit(solution)/shard_map/ppermute | solution.py:426
  727.8 42.9 %collective-permute-start.24 = (bf16[128,2304]{1,0:T(8,128)(2,1)S(1)}, bf16[128,2304]{1,0:T(8,128)(2,1)S(1)}, u32[]{:S(2)}, u32[]{:S(2)}) collective-permute-start(bf16[128,2304]{1,0:T(8,128)(2,1)S(1)} %get-tuple-element.91), channel_id=1, source_target_pairs={{0,16},{4,20},{8,24},{12,28},{16,0},{20,4},{24,8},{28,12},{1,17},{... | collective-permute-start | bytes 1769480 | tf_op jit(solution)/shard_map/ppermute | solution.py:426
  758.4 14.8 %collective-permute-start.18 = (bf16[128,2176]{1,0:T(8,128)(2,1)S(1)}, bf16[128,2176]{1,0:T(8,128)(2,1)S(1)}, u32[]{:S(2)}, u32[]{:S(2)}) collective-permute-start(bf16[128,2176]{1,0:T(8,128)(2,1)S(1)} %get-tuple-element.93), channel_id=1, source_target_pairs={{0,8},{4,12},{8,0},{12,4},{16,24},{20,28},{24,16},{28,20},{1,9},{5... | collective-permute-start | bytes 1671176 | tf_op jit(solution)/shard_map/ppermute | solution.py:426
  775.1 43.2 %collective-permute-start.48 = (bf16[256,128]{1,0:T(8,128)(2,1)}, bf16[256,128]{1,0:T(8,128)(2,1)}, u32[]{:S(2)}, u32[]{:S(2)}) collective-permute-start(bf16[256,128]{1,0:T(8,128)(2,1)} %get-tuple-element.65), channel_id=1, source_target_pairs={{0,16},{4,20},{8,24},{12,28},{16,0},{20,4},{24,8},{28,12},{1,17},{... | collective-permute-start | bytes 196616 | tf_op jit(solution)/shard_map/ppermute | solution.py:426
  775.5 44.9 %collective-permute-start.47 = (bf16[256,128]{1,0:T(8,128)(2,1)}, bf16[256,128]{1,0:T(8,128)(2,1)}, u32[]{:S(2)}, u32[]{:S(2)}) collective-permute-start(bf16[256,128]{1,0:T(8,128)(2,1)} %get-tuple-element.65), channel_id=1, source_target_pairs={{0,8},{4,12},{8,0},{12,4},{16,24},{20,28},{24,16},{28,20},{1,9},{5... | collective-permute-start | bytes 196616 | tf_op jit(solution)/shard_map/ppermute | solution.py:426
  783.4 52.8 %collective-permute-start.43 = (bf16[256,256]{1,0:T(8,128)(2,1)}, bf16[256,256]{1,0:T(8,128)(2,1)S(1)}, u32[]{:S(2)}, u32[]{:S(2)}) collective-permute-start(bf16[256,256]{1,0:T(8,128)(2,1)} %get-tuple-element.67), channel_id=1, source_target_pairs={{0,16},{4,20},{8,24},{12,28},{16,0},{20,4},{24,8},{28,12},{1,17},{... | collective-permute-start | bytes 393224 | tf_op jit(solution)/shard_map/ppermute | solution.py:426
  783.7 53.5 %collective-permute-start.42 = (bf16[256,256]{1,0:T(8,128)(2,1)}, bf16[256,256]{1,0:T(8,128)(2,1)S(1)}, u32[]{:S(2)}, u32[]{:S(2)}) collective-permute-start(bf16[256,256]{1,0:T(8,128)(2,1)} %get-tuple-element.67), channel_id=1, source_target_pairs={{0,8},{4,12},{8,0},{12,4},{16,24},{20,28},{24,16},{28,20},{1,9},{5... | collective-permute-start | bytes 393224 | tf_op jit(solution)/shard_map/ppermute | solution.py:426
  812.7 191.1 %collective-permute-start.52 = (f32[2,64,128]{2,1,0:T(8,128)}, f32[2,64,128]{2,1,0:T(8,128)}, u32[]{:S(2)}, u32[]{:S(2)}) collective-permute-start(f32[2,64,128]{2,1,0:T(8,128)} %get-tuple-element.216), channel_id=1, source_target_pairs={{0,4},{4,0},{8,12},{12,8},{16,20},{20,16},{24,28},{28,24},{1,5},{5... | collective-permute-start | bytes 196616 | tf_op jit(solution)/shard_map/ppermute | solution.py:426
  814.4 26.9 %all-to-all-start.1 = ((bf16[256,8,256]{2,0,1:T(8,128)(2,1)}), bf16[256,8,256]{2,0,1:T(8,128)(2,1)S(1)}, u32[]{:S(2)}, u32[]{:S(2)}) async-start(bf16[256,8,256]{2,0,1:T(8,128)(2,1)} %bitcast.378), calls=%async_computation.1 | async-start | bytes 2097152 | tf_op jit(solution)/shard_map/all_to_all | solution.py:829
  818.3 204.5 %reduce-scatter.4.cloned.1.call-start = ((), (), s32[]{:S(2)}) async-start(), calls=%async_computation.11 | async-start | bytes 983040 | tf_op jit(solution)/shard_map/reduce_scatter | solution.py:885
  819.0 13.6 %collective-permute-start.49 = (bf16[128,128]{1,0:T(8,128)(2,1)S(1)}, bf16[128,128]{1,0:T(8,128)(2,1)S(1)}, u32[]{:S(2)}, u32[]{:S(2)}) collective-permute-start(bf16[128,128]{1,0:T(8,128)(2,1)S(1)} %slice.992), channel_id=1, source_target_pairs={{0,8},{4,12},{8,0},{12,4},{16,24},{20,28},{24,16},{28,20},{1,9},{5... | collective-permute-start | bytes 98312 | tf_op jit(solution)/shard_map/ppermute | solution.py:426
  821.2 12.0 %collective-permute-start.50 = (bf16[128,128]{1,0:T(8,128)(2,1)S(1)}, bf16[128,128]{1,0:T(8,128)(2,1)S(1)}, u32[]{:S(2)}, u32[]{:S(2)}) collective-permute-start(bf16[128,128]{1,0:T(8,128)(2,1)S(1)} %slice.993), channel_id=1, source_target_pairs={{0,16},{4,20},{8,24},{12,28},{16,0},{20,4},{24,8},{28,12},{1,17},{... | collective-permute-start | bytes 98312 | tf_op jit(solution)/shard_map/ppermute | solution.py:426
  867.0 14.6 %collective-permute-start.27 = (bf16[3,1024,256]{2,1,0:T(8,128)(2,1)}, bf16[3,1024,256]{2,1,0:T(8,128)(2,1)}, u32[]{:S(2)}, u32[]{:S(2)}) collective-permute-start(bf16[3,1024,256]{2,1,0:T(8,128)(2,1)} %get-tuple-element.17), channel_id=1, source_target_pairs={{0,4},{4,0},{8,12},{12,8},{16,20},{20,16},{24,28},{28,24},{1,5},{5... | collective-permute-start | bytes 4718600 | tf_op jit(solution)/shard_map/ppermute | solution.py:426
  871.6 130.5 %collective-permute-start.51 = (f32[4,64,128]{2,1,0:T(8,128)}, f32[4,64,128]{2,1,0:T(8,128)}, u32[]{:S(2)}, u32[]{:S(2)}) collective-permute-start(f32[4,64,128]{2,1,0:T(8,128)} %constant_dynamic-slice_fusion.2), channel_id=1, source_target_pairs={{0,4},{4,0},{8,12},{12,8},{16,20},{20,16},{24,28},{28,24},{1,5},{5... | collective-permute-start | bytes 393224 | tf_op jit(solution)/shard_map/ppermute | solution.py:426
  925.4 28.9 %collective-permute-start.30 = (bf16[256,2432]{1,0:T(8,128)(2,1)S(1)}, bf16[256,2432]{1,0:T(8,128)(2,1)S(1)}, u32[]{:S(2)}, u32[]{:S(2)}) collective-permute-start(bf16[256,2432]{1,0:T(8,128)(2,1)S(1)} %pad_maximum_fusion.7), channel_id=1, source_target_pairs={{0,16},{4,20},{8,24},{12,28},{16,0},{20,4},{24,8},{28,12},{1,17},{... | collective-permute-start | bytes 3735560 | tf_op jit(solution)/shard_map/ppermute | solution.py:426
  926.5 29.7 %collective-permute-start.28 = (bf16[256,2432]{1,0:T(8,128)(2,1)S(1)}, bf16[256,2432]{1,0:T(8,128)(2,1)S(1)}, u32[]{:S(2)}, u32[]{:S(2)}) collective-permute-start(bf16[256,2432]{1,0:T(8,128)(2,1)S(1)} %pad_maximum_fusion.6), channel_id=1, source_target_pairs={{0,8},{4,12},{8,0},{12,4},{16,24},{20,28},{24,16},{28,20},{1,9},{5... | collective-permute-start | bytes 3735560 | tf_op jit(solution)/shard_map/ppermute | solution.py:426
  954.4 14.6 %collective-permute-start.31 = (bf16[128,2432]{1,0:T(8,128)(2,1)S(1)}, bf16[128,2432]{1,0:T(8,128)(2,1)S(1)}, u32[]{:S(2)}, u32[]{:S(2)}) collective-permute-start(bf16[128,2432]{1,0:T(8,128)(2,1)S(1)} %fusion.108), channel_id=1, source_target_pairs={{0,8},{4,12},{8,0},{12,4},{16,24},{20,28},{24,16},{28,20},{1,9},{5... | collective-permute-start | bytes 1867784 | tf_op jit(solution)/shard_map/ppermute | solution.py:426
  969.4 13.7 %collective-permute-start.29 = (bf16[128,2432]{1,0:T(8,128)(2,1)S(1)}, bf16[128,2432]{1,0:T(8,128)(2,1)S(1)}, u32[]{:S(2)}, u32[]{:S(2)}) collective-permute-start(bf16[128,2432]{1,0:T(8,128)(2,1)S(1)} %get-tuple-element.87), channel_id=1, source_target_pairs={{0,16},{4,20},{8,24},{12,28},{16,0},{20,4},{24,8},{28,12},{1,17},{... | collective-permute-start | bytes 1867784 | tf_op jit(solution)/shard_map/ppermute | solution.py:426
  983.4 5.8 collective-permute-start.33
  984.5 5.1 collective-permute-start.32
  985.7 14.7 %collective-permute-start.37 = (f32[4,192,128]{2,1,0:T(8,128)S(1)}, f32[4,192,128]{2,1,0:T(8,128)S(1)}, u32[]{:S(2)}, u32[]{:S(2)}) collective-permute-start(f32[4,192,128]{2,1,0:T(8,128)S(1)} %constant_dynamic-slice_fusion.12), channel_id=1, source_target_pairs={{0,4},{4,0},{8,12},{12,8},{16,20},{20,16},{24,28},{28,24},{1,5},{5... | collective-permute-start | bytes 1179656 | tf_op jit(solution)/shard_map/ppermute | solution.py:426
  989.2 4.5 collective-permute-start.34
  989.6 4.1 collective-permute-start.35
  994.6 6.5 collective-permute-start.36
  1002.1 69.2 %reduce-scatter.8.cloned.1.call-start = ((), (), s32[]{:S(2)}) async-start(), calls=%async_computation.14 | async-start | bytes 2785280 | tf_op jit(solution)/shard_map/reduce_scatter | solution.py:885
  1008.8 90.2 %all-gather.23.cloned.1.call-start = ((), (), s32[]{:S(2)}) async-start(), calls=%async_computation.12 | async-start | bytes 1769472 | tf_op jit(solution)/shard_map/all_gather | solution.py:886
  1022.8 115.8 %all-gather.25.cloned.1.call-start = ((), (), s32[]{:S(2)}) async-start(), calls=%async_computation.15 | async-start | bytes 5013504 | tf_op jit(solution)/shard_map/all_gather | solution.py:886
  (130 other events, 1893.9 us)
Sparse Core Ops, SparseCore 0:
  14.1 73.8 all-gather.10
  91.4 67.1 all-gather.26
  160.2 46.8 all-gather.20
  208.5 47.1 all-gather.16
  257.1 79.6 all-gather.18
  338.8 79.2 all-gather.14
  421.5 79.3 all-gather.12
  813.0 34.1 reduce-scatter.5
  1002.2 20.4 reduce-scatter.3
  1024.9 46.3 reduce-scatter.7
  1073.2 25.6 all-gather.22
  1100.7 37.7 all-gather.24

commit v2 on v0

--- a/solution.py
+++ b/solution.py
@@ -1,6 +1,10 @@
+import functools
+
 import jax
 import jax.numpy as jnp
 from jax import lax
+from jax.experimental import pallas as pl
+from jax.experimental.pallas import tpu as pltpu
 from jax.sharding import PartitionSpec as P
 
 HEAD_DIM = 128
@@ -410,6 +414,1053 @@
     )
 
 
+BF = jnp.bfloat16
+F32 = jnp.float32
+PLANE = 8
+CHIPS = 4
+LANES = 128
+CHUNKS = 2
+HALVES = ((1, 0), (3, 0), (2, 1), (3, 1), (2, 0), (1, 1), (0, 0), (0, 1))
+ANY = pl.BlockSpec(memory_space=pl.ANY)
+ROOMY = 56 * 2**20
+
+
+def swap(value, bits):
+    return lax.ppermute(value, "seq", [(i, i ^ bits) for i in range(PLANE)])
+
+
+def gather_halves(first, second):
+    x_first, y_second = swap(first, 2), swap(second, 4)
+    y_first, x_second = swap(first, 4), swap(second, 2)
+    far_first, far_second = swap(y_first, 2), swap(x_second, 4)
+    return [x_first, far_first, y_second, far_second, y_first, x_second, first, second]
+
+
+def blocks_of(block):
+    return [block, swap(block, 2), swap(block, 4), swap(block, 6)]
+
+
+def dot(left, right):
+    return jnp.dot(left, right, preferred_element_type=F32)
+
+
+def inner(left, right, on_left, on_right):
+    return lax.dot_general(
+        left, right, (((on_left,), (on_right,)), ((), ())), preferred_element_type=F32
+    )
+
+
+def take(value, start, count, axis):
+    return lax.dynamic_slice_in_dim(value, start, count, axis)
+
+
+def whole_spec(shape):
+    return pl.BlockSpec(shape, lambda *_: (0,) * len(shape))
+
+
+def call(body, scalars, operands, specs, shapes, out_specs, scratch=(), grid=(1,), cost=None, ties=()):
+    count = len(operands)
+
+    def run(*refs):
+        inside = refs[: 1 + count] + refs[1 + count + len(ties) :]
+        body(*inside)
+
+    return pl.pallas_call(
+        run,
+        grid_spec=pltpu.PrefetchScalarGridSpec(
+            num_scalar_prefetch=1,
+            grid=grid,
+            in_specs=list(specs) + [ANY] * len(ties),
+            out_specs=out_specs,
+            scratch_shapes=list(scratch),
+        ),
+        out_shape=shapes,
+        compiler_params=pltpu.CompilerParams(vmem_limit_bytes=ROOMY),
+        cost_estimate=None
+        if cost is None
+        else pl.CostEstimate(flops=cost[0], bytes_accessed=cost[1], transcendentals=0),
+    )(scalars, *operands, *ties)
+
+
+def hold(value, ties):
+    return pl.pallas_call(
+        lambda *refs: None,
+        in_specs=[ANY] * (1 + len(ties)),
+        out_specs=ANY,
+        out_shape=sds(value.shape, value.dtype),
+        input_output_aliases={0: 0},
+    )(value, *ties)
+
+
+def copies(pairs, sems):
+    started = [
+        pltpu.make_async_copy(source, target, sems.at[k]) for k, (source, target) in enumerate(pairs)
+    ]
+    for one in started:
+        one.start()
+    for one in started:
+        one.wait()
+
+
+def sds(shape, dtype=BF):
+    return jax.ShapeDtypeStruct(shape, dtype)
+
+
+def doc_begin(scalars, places):
+    begin = jnp.zeros_like(places)
+    for doc in range(4):
+        begin = jnp.where(scalars[3 + doc] <= places, scalars[3 + doc], begin)
+    return begin
+
+
+def adapter_mask(scalars, places):
+    which = jnp.zeros_like(places) + scalars[7]
+    for doc in range(1, 4):
+        which = jnp.where(scalars[3 + doc] <= places, scalars[7 + doc], which)
+    column = lax.broadcasted_iota(jnp.int32, (1, LANES), 1) // RANK
+    return (column == which).astype(F32)
+
+
+def rows_from(first, count):
+    return first + lax.broadcasted_iota(jnp.int32, (count, 1), 0)
+
+
+def normed(values):
+    centre = values - jnp.mean(values, axis=-1, keepdims=True)
+    factor = lax.rsqrt(jnp.mean(centre * centre, axis=-1, keepdims=True) + 1e-05)
+    return centre * factor, factor
+
+
+def cut_first_kernel(sizes, scalars, w_qkv, w_out, a_qkv, a_out, a_gu, b_out, b_down, b_qkv, out, sems):
+    share, quarter, width = sizes
+    chip, core = scalars[0], scalars[1]
+    seat = chip * 2 + core
+    pairs = []
+    for part in range(3):
+        for i in range(2):
+            column = pl.multiple_of(part * width + (2 * core + i) * quarter + chip * LANES, LANES)
+            k = part * 2 + i
+            pairs.append(
+                (w_qkv.at[:, pl.ds(column, LANES)], out.at[:quarter, k * LANES : (k + 1) * LANES])
+            )
+    rows = pl.ds(pl.multiple_of(seat * share, share), share)
+    small = slice(quarter, quarter + share)
+    pairs.append((a_qkv.at[rows], out.at[small, :384]))
+    pairs.append((a_gu.at[rows], out.at[small, 384:640]))
+    pairs.append((a_out.at[rows], out.at[small, 640:768]))
+    low = pl.ds(pl.multiple_of(seat * 16, 16), 16)
+    at = quarter + share
+    pairs.append((b_out.at[low], out.at[at : at + 16, :512]))
+    pairs.append((b_down.at[low], out.at[at + 16 : at + 32, :512]))
+    column = pl.ds(pl.multiple_of(chip * LANES, LANES), LANES)
+    for k in range(12):
+        here = pl.ds(pl.multiple_of(core * 192 + k * 16, 16), 16)
+        row, lane = up_slot(k)
+        row += at
+        pairs.append((b_qkv.at[here, column], out.at[row : row + 16, lane : lane + LANES]))
+    at += 64
+    for k in range(16):
+        row, lane = at + (k // 6) * share, (k % 6) * LANES
+        pairs.append(
+            (w_out.at[rows, k * LANES : (k + 1) * LANES], out.at[row : row + share, lane : lane + LANES])
+        )
+    copies(pairs, sems)
+
+
+def up_slot(k):
+    if k < 4:
+        return (k // 2) * 16, 512 + (k % 2) * LANES
+    return 32 + ((k - 4) // 4) * 16, ((k - 4) % 4) * LANES
+
+
+def cut_rest_kernel(sizes, scalars, w_gu, w_down, a_down, b_gu, down, gu_0, gu_1, sems):
+    ff, ff_z, ff_dev, width = sizes
+    seat = scalars[0] * 2 + scalars[1]
+    rows = pl.ds(pl.multiple_of(seat * ff_dev, ff_dev), ff_dev)
+    wide = width + LANES
+    pairs = [
+        (w_down.at[rows], down.at[:, :width]),
+        (a_down.at[rows], down.at[:, width:wide]),
+        (b_gu.at[:, rows], down.at[:, wide : wide + ff_dev]),
+    ]
+    for chunk, gu in enumerate((gu_0, gu_1)):
+        for half in range(2):
+            for i in range(2):
+                column = pl.multiple_of(half * ff + (2 * chunk + i) * ff_z + seat * ff_dev, ff_dev)
+                k = half * 2 + i
+                pairs.append(
+                    (w_gu.at[:, pl.ds(column, ff_dev)], gu.at[:, k * ff_dev : (k + 1) * ff_dev])
+                )
+    copies(pairs, sems)
+
+
+def unpack_small_kernel(share, quarter, scalars, *refs):
+    pieces = refs[:16]
+    a_qkv, a_gu, a_out, b_out, b_down = refs[16:]
+    chip, core = scalars[0], scalars[1]
+    for k in range(2):
+        for at, (rel, half) in enumerate(HALVES):
+            piece = pieces[8 * k + at]
+            tall = piece.shape[0] // 2
+            seat = (chip ^ rel) * 2 + (core if k == 0 else 1 - core)
+            for i in range(2):
+                z = half * 2 + i
+                rows = slice(i * tall, i * tall + share)
+                there = pl.ds(pl.multiple_of(z * quarter + seat * share, share), share)
+                a_qkv[there, :] = piece[rows, :384]
+                a_gu[there, :] = piece[rows, 384:640]
+                a_out[there, :] = piece[rows, 640:768]
+                there = pl.ds(pl.multiple_of(seat * 16, 16), 16)
+                columns = slice(z * quarter, (z + 1) * quarter)
+                row = i * tall + share
+                b_out[there, columns] = piece[row : row + 16, :512]
+                b_down[there, columns] = piece[row + 16 : row + 32, :512]
+
+
+def unpack_out_kernel(share, quarter, scalars, *refs):
+    pieces, out, sems = refs[:16], refs[16], refs[17]
+    chip, core = scalars[0], scalars[1]
+    pairs = []
+    for k in range(2):
+        for at, (rel, half) in enumerate(HALVES):
+            seat = (chip ^ rel) * 2 + (core if k == 0 else 1 - core)
+            for i in range(2):
+                there = pl.ds(pl.multiple_of((half * 2 + i) * quarter + seat * share, share), share)
+                for block in range(3):
+                    row = (i * 3 + block) * share
+                    lanes = min(768, out.shape[1] - block * 768)
+                    pairs.append(
+                        (
+                            pieces[8 * k + at].at[row : row + share, :lanes],
+                            out.at[there, block * 768 : block * 768 + lanes],
+                        )
+                    )
+    copies(pairs, sems)
+
+
+def norm_kernel(scalars, tokens, first, second):
+    value, _ = normed(tokens[...].astype(F32))
+    half = first.shape[0]
+    first[...] = value[:half].astype(BF)
+    second[...] = value[half:].astype(BF)
+
+
+def qkv_kernel(scalars, *refs):
+    pieces, gathered = refs[:16], refs[16]
+    down, up, cosine, sine, out, latents, weight, rows_all, sems = refs[17:]
+    chip, core = scalars[0], scalars[1]
+    half = pieces[0].shape[0]
+    quarter = weight.shape[0] // 4
+    tall = gathered.shape[0] // 4
+    pairs = [
+        (gathered.at[pl.ds(z * tall, quarter)], weight.at[pl.ds(z * quarter, quarter)]) for z in range(4)
+    ]
+    for k in range(2):
+        for at, (rel, part) in enumerate(HALVES):
+            seat = (chip ^ rel) * 2 + (core if k == 0 else 1 - core)
+            there = pl.ds(pl.multiple_of((seat * 2 + part) * half, half), half)
+            pairs.append((pieces[8 * k + at], rows_all.at[there]))
+    copies(pairs, sems)
+    step = 512
+    span = up.shape[1]
+    for start in range(0, rows_all.shape[0], step):
+        here = slice(start, start + step)
+        value = rows_all[here, :]
+        mask = adapter_mask(scalars, rows_from(start, step))
+        latent = dot(value, down[...]).astype(BF) * jnp.concatenate([mask] * 3, axis=1).astype(BF)
+        latents[here, :] = latent
+        pre = dot(value, weight[...])
+        for part in range(3):
+            block = pre[:, part * span : (part + 1) * span] + dot(
+                latent[:, part * LANES : (part + 1) * LANES], up[part * LANES : (part + 1) * LANES, :]
+            )
+            if part < 2:
+                heads = []
+                for k in range(span // HEAD_DIM):
+                    head = block[:, k * HEAD_DIM : (k + 1) * HEAD_DIM]
+                    heads.append(
+                        head * cosine[here, :] + pltpu.roll(head, HEAD_DIM // 2, 1) * sine[here, :]
+                    )
+                block = jnp.concatenate(heads, axis=1)
+            out[here, part * span : (part + 1) * span] = block.astype(BF)
+
+
+def allowed_pairs(scalars, first_row, rows, width):
+    row = rows_from(first_row, rows)
+    column = lax.broadcasted_iota(jnp.int32, (1, width), 1)
+    return (column <= row) & (column >= doc_begin(scalars, row))
+
+
+def attend_kernel(rows, scalars, query, key, value, out, lse):
+    scale = HEAD_DIM**-0.5
+    for start in range(0, query.shape[0], rows):
+        here = slice(start, start + rows)
+        width = start + rows
+        scores = inner(query[here, :], key[:width, :], 1, 1) * scale
+        scores = jnp.where(allowed_pairs(scalars, start, rows, width), scores, -1e30)
+        top = jnp.max(scores, axis=1, keepdims=True)
+        expd = jnp.exp(scores - top)
+        total = jnp.sum(expd, axis=1, keepdims=True)
+        probs = (expd * (1.0 / total)).astype(BF)
+        out[here, :] = dot(probs, value[:width, :]).astype(BF)
+        lse[here, :] = jnp.broadcast_to(top + jnp.log(total), (rows, LANES))
+
+
+def attend_back_kernel(
+    rows, scalars, query, key, value, grad, lse, latents, cosine, sine, own, other, ups,
+    dq_all, dk_sum, dv_sum,
+):
+    dk_sum[...] = jnp.zeros_like(dk_sum)
+    dv_sum[...] = jnp.zeros_like(dv_sum)
+    scale = HEAD_DIM**-0.5
+    length = query.shape[0]
+    for start in range(0, length, rows):
+        here = slice(start, start + rows)
+        width = start + rows
+        this_query = query[here, :]
+        upstream = grad[here, :]
+        scores = inner(this_query, key[:width, :], 1, 1) * scale
+        probs = jnp.where(
+            allowed_pairs(scalars, start, rows, width), jnp.exp(scores - lse[here, :1]), 0.0
+        )
+        prob_grad = inner(upstream, value[:width, :], 1, 1)
+        delta = jnp.sum(prob_grad * probs, axis=1, keepdims=True)
+        score_grad = (probs * (prob_grad - delta)).astype(BF)
+        dq_all[here, :] = dot(score_grad, key[:width, :]) * scale
+        dk_sum[:width, :] += inner(score_grad, this_query, 0, 0)
+        dv_sum[:width, :] += inner(probs.astype(BF), upstream, 0, 0)
+
+    chip, core = scalars[0], scalars[1]
+    half = own.shape[1] // 8
+    for part, total in enumerate((dq_all, dk_sum, dv_sum)):
+        for start in range(0, length, 512):
+            here = slice(start, start + 512)
+            if part == 0:
+                raw = total[here, :].astype(BF).astype(F32)
+            elif part == 1:
+                raw = (total[here, :] * scale).astype(BF).astype(F32)
+            else:
+                raw = total[here, :]
+            if part < 2:
+                raw = raw * cosine[here, :] - pltpu.roll(raw, HEAD_DIM // 2, 1) * sine[here, :]
+            total[here, :] = raw.astype(BF).astype(F32)
+        low = total[...].astype(BF)
+        ups[part] = inner(latents[:, part * LANES : (part + 1) * LANES], low, 0, 0)
+        for k, target in enumerate((own, other)):
+            for at, (rel, h) in enumerate(HALVES):
+                seat = (chip ^ rel) * 2 + (core if k == 0 else 1 - core)
+                there = pl.ds(pl.multiple_of((seat * 2 + h) * half, half), half)
+                target[part, at * half : (at + 1) * half, :] = total[there, :].astype(BF)
+
+
+def head_order(k):
+    return (k % CHIPS) * CHIPS + k // CHIPS
+
+
+def out_kernel(scalars, mixed, weight, down, up, tokens, second, first_half, second_half, latents, natural):
+    for k in range(16):
+        at = head_order(k)
+        natural[:, k * LANES : (k + 1) * LANES] = mixed[:, at * LANES : (at + 1) * LANES]
+    rows = tokens.shape[0]
+    seat = scalars[0] * 2 + scalars[1]
+    mask = adapter_mask(scalars, rows_from(seat * rows, rows)).astype(BF)
+    value = natural[...]
+    latent = dot(value, down[...]).astype(BF) * mask
+    latents[...] = latent
+    total = tokens[...].astype(F32) + (dot(value, weight[...]) + dot(latent, up[...]))
+    second[...] = total
+    norm, _ = normed(total)
+    first_half[...] = norm[: rows // 2].astype(BF)
+    second_half[...] = norm[rows // 2 :].astype(BF)
+
+
+def ff_kernel(begin, chunk, scalars, *refs):
+    select, a_gu, b_down, down_own, down_oth, gu_own, gu_oth = refs[:7]
+    norm, cot = refs[7:11], refs[11:15]
+    count = 15 if begin else 16
+    outs = refs[count : count + (1 if begin else 2)]
+    count += len(outs)
+    hidden_out, ups, downs = refs[count : count + 3]
+    rows_in, cot_in, gu_a, gu_b, down_a, down_b, sums, sems = refs[count + 3 :]
+    rows, width = rows_in.shape
+    wide = width + LANES
+    part = pl.ds(chunk * down_a.shape[0], down_a.shape[0])
+    low = rows // 4
+    pairs = [(norm[k], rows_in.at[pl.ds(k * low, low)]) for k in range(4)]
+    pairs += [(gu_own, gu_a)]
+    pairs += [(cot[k], cot_in.at[pl.ds(k * low, low)]) for k in range(4)]
+    pairs += [(down_own.at[part], down_a), (gu_oth, gu_b), (down_oth.at[part], down_b)]
+    if not begin:
+        pairs.append((refs[15], sums))
+    loads = [pltpu.make_async_copy(x, y, sems.at[k]) for k, (x, y) in enumerate(pairs)]
+    for load in loads:
+        load.start()
+    mask = select[...]
+    for load in loads[:4]:
+        load.wait()
+    z_gu = dot(rows_in[...], a_gu[...]).astype(BF) * jnp.concatenate([mask, mask], axis=1)
+    z_gate, z_up = z_gu[:, :LANES], z_gu[:, LANES:]
+    norm_grad = 0.0
+    latent_grad = 0.0
+    for side, (gu, down) in enumerate(((gu_a, down_a), (gu_b, down_b))):
+        size = gu.shape[1] // 2
+        own_ff = size // 2
+        loads[4 if side == 0 else 10].wait()
+        both = dot(rows_in[...], gu[...])
+        if side == 0:
+            for load in loads[5:9]:
+                load.wait()
+            dz_down = (inner(cot_in[...], b_down[...], 1, 1) * mask.astype(F32)).astype(BF)
+        loads[9 if side == 0 else 11].wait()
+        up_gate = jnp.concatenate(
+            [down[i * own_ff : i * own_ff + LANES, wide:] for i in range(2)], axis=1
+        )
+        up_up = jnp.concatenate(
+            [down[i * own_ff + LANES : i * own_ff + 2 * LANES, wide:] for i in range(2)], axis=1
+        )
+        gate = both[:, :size] + dot(z_gate, up_gate)
+        upper = both[:, size:] + dot(z_up, up_up)
+        sigma = 1.0 / (1.0 + jnp.exp(-gate))
+        active = gate * sigma
+        hidden = (active * upper).astype(BF)
+        hidden_out[:, side * size : (side + 1) * size] = hidden
+        hidden_grad = inner(cot_in[...], down[:, :width], 1, 1) + inner(
+            dz_down, down[:, width:wide], 1, 1
+        )
+        gate_grad = (hidden_grad * upper * sigma * (1.0 + gate * (1.0 - sigma))).astype(BF)
+        upper_grad = (hidden_grad * active).astype(BF)
+        norm_grad += inner(jnp.concatenate([gate_grad, upper_grad], axis=1), gu[...], 1, 1)
+        latent_grad += jnp.concatenate(
+            [inner(gate_grad, up_gate, 1, 1), inner(upper_grad, up_up, 1, 1)], axis=1
+        )
+        ups[side] = jnp.concatenate(
+            [inner(z_gate, gate_grad, 0, 0), inner(z_up, upper_grad, 0, 0)], axis=0
+        )
+        downs[side] = inner(hidden, dz_down, 0, 0)
+    if begin:
+        outs[0][:, :width] = norm_grad
+        outs[0][:, width:] = latent_grad
+        return
+    loads[12].wait()
+    low = rows // 2
+    for k in range(2):
+        at = slice(k * low, (k + 1) * low)
+        kind = outs[k].dtype
+        outs[k][:, :width] = (norm_grad[at] + sums[at, :width]).astype(kind)
+        outs[k][:, width:] = (latent_grad[at] + sums[at, width:]).astype(kind)
+
+
+def down_kernel(scalars, hidden_0, hidden_1, down_own, down_oth, out_0, out_1):
+    wide = out_0.shape[1]
+    size = hidden_0.shape[1] // 2
+    total = 0.0
+    for chunk, hidden in enumerate((hidden_0, hidden_1)):
+        part = slice(chunk * size, (chunk + 1) * size)
+        total += dot(hidden[:, :size], down_own[part, :wide]) + dot(hidden[:, size:], down_oth[part, :wide])
+    for k, out in enumerate((out_0, out_1)):
+
+        @pl.when(pl.program_id(0) == k)
+        def _():
+            out[...] = total.astype(out.dtype)
+
+
+def spread_kernel(places, scalars, *refs):
+    pieces, outs = refs[:8], refs[8:]
+    for k, piece in enumerate(pieces):
+        chip = scalars[0] ^ (k % 4)
+        core = scalars[1] if k < 4 else 1 - scalars[1]
+        seat = chip * 2 + core
+        at = 0
+        for out, (kind, rows, blocks) in zip(outs, places):
+            for block in range(blocks):
+                value = piece[at : at + rows, :].astype(F32)
+                at += rows
+                columns = pl.ds(block * LANES, LANES)
+                if kind == "rows":
+                    out[pl.ds(pl.multiple_of(seat * rows, rows), rows), columns] = value
+                elif kind == "core rows":
+                    row = pl.multiple_of(core * (CHIPS * rows) + chip * rows, rows)
+                    out[pl.ds(row, rows), columns] = value
+                elif kind == "columns":
+                    column = pl.multiple_of((seat * blocks + block) * LANES, LANES)
+                    out[:, pl.ds(column, LANES)] = value
+                else:
+                    row = pl.multiple_of(core * rows, rows)
+                    out[pl.ds(row, rows), pl.ds(pl.multiple_of(chip * LANES, LANES), LANES)] = value
+
+
+def ff_grads_kernel(scalars, *refs):
+    ups, downs, keep, send = refs[:4], refs[4:8], refs[8], refs[9]
+    for side, out in enumerate((keep, send)):
+        for chunk in range(CHUNKS):
+            up = ups[2 * chunk][side] + ups[2 * chunk + 1][side]
+            down = downs[2 * chunk][side] + downs[2 * chunk + 1][side]
+            rows = up.shape[0]
+            size = up.shape[1] // 2
+            for i in range(2):
+                z = 2 * chunk + i
+                count = size // LANES
+                for k in range(count):
+                    at = i * size + k * LANES
+                    out[z, k * rows : (k + 1) * rows, :] = up[:, at : at + LANES].astype(out.dtype)
+                at = count * rows
+                out[z, at : at + size, :] = down[i * size : (i + 1) * size].astype(out.dtype)
+
+
+def other_grads_kernel(quarter, scalars, *refs):
+    norm1, norm2, cot, mixed = refs[:8], refs[8:16], refs[16:24], refs[24]
+    dz_gu, dz_qkv, z_down, dz_out, up_out = (refs[25 + 4 * k : 29 + 4 * k] for k in range(5))
+    up_qkv, keep, send, columns, all_gu, all_qkv, all_down, sems = refs[45:]
+    half = norm1[0].shape[0]
+    chip, core = scalars[0], scalars[1]
+    pairs = []
+    for k, source in enumerate((norm1, norm2, cot)):
+        for z in range(4):
+            column = pl.ds(pl.multiple_of(z * quarter + chip * LANES, LANES), LANES)
+            for h in range(8):
+                target = columns.at[k, h * half : (h + 1) * half, z * LANES : (z + 1) * LANES]
+                pairs.append((source[h].at[:, column], target))
+    loads = [pltpu.make_async_copy(x, y, sems.at[k]) for k, (x, y) in enumerate(pairs)]
+    for load in loads:
+        load.start()
+    for pieces, whole in ((dz_gu, all_gu), (dz_qkv, all_qkv), (z_down, all_down)):
+        for k, (rel, h) in enumerate(HALVES):
+            whole[k * half : (k + 1) * half, :] = pieces[rel][h * half : (h + 1) * half, :]
+
+    def halves(z, at, value):
+        rows = value.shape[0] // 2
+        for k in range(2):
+            piece = value[k * rows : (k + 1) * rows]
+
+            @pl.when(core == k)
+            def _():
+                keep[z, at : at + rows, :] = piece
+
+            @pl.when(core != k)
+            def _():
+                send[z, at : at + rows, :] = piece.astype(BF)
+
+    def two_of_four(at, values):
+        rows = values[0].shape[0] // 2
+        for k in range(2):
+
+            @pl.when(core == k)
+            def _():
+                for i in range(2):
+                    here, there = 2 * k + i, 2 * (1 - k) + i
+                    keep[here, at : at + rows, :] = values[i][k * rows : (k + 1) * rows]
+                    send[here, at : at + rows, :] = values[i][(1 - k) * rows : (2 - k) * rows].astype(BF)
+                    keep[there, at : at + rows, :] = jnp.zeros((rows, LANES), F32)
+                    send[there, at : at + rows, :] = jnp.zeros((rows, LANES), BF)
+
+    low = LANES // 2
+    at = 3 * low
+    total = 0.0
+    rows = dz_out[0].shape[1]
+    for rel in range(4):
+        for k in range(2):
+            seat = (chip ^ rel) * 2 + (core if k == 0 else 1 - core)
+            here = pl.ds(pl.multiple_of(seat * rows, rows), rows)
+            total += inner(mixed[here, :], dz_out[rel][k], 0, 0)
+    two_of_four(at, [total[:LANES], total[LANES:]])
+    at += low
+    value = up_out[0][...]
+    for piece in up_out[1:]:
+        value = value + piece[...].astype(F32)
+    share = value.shape[0] // 2
+    for z in range(4):
+        for k in range(4):
+            block = value[:, (z * 4 + k) * LANES : (z * 4 + k + 1) * LANES]
+            halves(z, at + k * share, block)
+    at += low
+    at_b = at + 3 * low
+    heads = [jnp.concatenate([up_qkv[part, :, i * LANES : (i + 1) * LANES] for part in range(3)], axis=0) for i in range(2)]
+    two_of_four(at_b, heads)
+    for load in loads:
+        load.wait()
+    value = inner(columns[1], all_gu[...], 0, 0)
+    for z in range(4):
+        for k in range(2):
+            block = value[z * LANES : (z + 1) * LANES, k * LANES : (k + 1) * LANES]
+            halves(z, k * low, block)
+    value = inner(all_down[...], columns[2], 0, 0)
+    for z in range(4):
+        halves(z, 2 * low, value[:, z * LANES : (z + 1) * LANES])
+    value = inner(columns[0], all_qkv[...], 0, 0)
+    for z in range(4):
+        for k in range(3):
+            block = value[z * LANES : (z + 1) * LANES, k * LANES : (k + 1) * LANES]
+            halves(z, at + k * low, block)
+
+
+def along_line_kernel(scalars, keep, brought, mine, *outs):
+    z = scalars[2]
+    mine[...] = keep[z] + brought[z].astype(F32)
+    for k, out in enumerate(outs):
+        hop = k // 2 + 1
+        to = jnp.minimum(z + hop, 3) if k % 2 == 0 else jnp.maximum(z - hop, 0)
+        out[...] = (keep[to] + brought[to].astype(F32)).astype(BF)
+
+
+def keep_kernel(scalars, *refs):
+    count = len(refs) // 2
+    for source, target in zip(refs[:count], refs[count:]):
+        target[...] = source[...]
+
+
+def back_middle_kernel(
+    scalars, own, by_x, by_y, got_y, got_x, second, cot, a_gu, w_out, a_out, b_out, z_out,
+    grad, dz_gu_out, dz_out_out, mixed_grad, up_own, up_x, up_y, up_far,
+):
+    rows, width = second.shape
+    half = rows // 2
+    upper = own[:half] + by_x[...].astype(F32) + got_y[...].astype(F32)
+    lower = own[half:] + by_y[...].astype(F32) + got_x[...].astype(F32)
+    wide = jnp.concatenate([upper, lower], axis=0)
+    seat = scalars[0] * 2 + scalars[1]
+    mask = adapter_mask(scalars, rows_from(seat * rows, rows))
+    dz_gu = (wide[:, width:] * jnp.concatenate([mask, mask], axis=1)).astype(BF)
+    dz_gu_out[...] = dz_gu
+    upstream = wide[:, :width] + inner(dz_gu, a_gu[...], 1, 1)
+    norm, factor = normed(second[...])
+    total = cot[...].astype(F32) + norm_back(norm, factor, upstream)
+    grad[...] = total
+    low = total.astype(BF)
+    dz_out = (inner(low, b_out[...], 1, 1) * mask).astype(BF)
+    dz_out_out[...] = dz_out
+    back = (inner(low, w_out[...], 1, 1) + inner(dz_out, a_out[...], 1, 1)).astype(BF)
+    for k in range(16):
+        at = head_order(k)
+        mixed_grad[:, at * LANES : (at + 1) * LANES] = back[:, k * LANES : (k + 1) * LANES]
+    value = inner(z_out[...], low, 0, 0)
+    share = value.shape[0] // PLANE
+    for block in range(CHIPS):
+        for core in range(2):
+            at = (core * CHIPS + block) * share
+            piece = value[at : at + share]
+            for rel, out in enumerate((up_own, up_x, up_y, up_far)):
+
+                @pl.when((scalars[0] ^ rel) == block)
+                def _():
+                    out[core * share : (core + 1) * share, :] = piece.astype(out.dtype)
+
+
+def back_latent_kernel(scalars, own, other, up_own, up_oth, to_x, to_y, to_far, kept):
+    half = kept.shape[0] // 2
+    targets = {0: kept, 1: to_x, 2: to_y, 3: to_far}
+    for part in range(3):
+        at = slice(part * LANES, (part + 1) * LANES)
+        value = inner(own[part], up_own[at, :], 1, 1) + inner(other[part], up_oth[at, :], 1, 1)
+        for k, (rel, h) in enumerate(HALVES):
+            target = targets[rel]
+            target[h * half : (h + 1) * half, at] = value[k * half : (k + 1) * half].astype(target.dtype)
+
+
+def back_qkv_kernel(scalars, own, other, w_own, w_oth, out_0, out_1):
+    rows = out_0.shape[0]
+    mine = jnp.concatenate([own[part] for part in range(3)], axis=1)
+    theirs = jnp.concatenate([other[part] for part in range(3)], axis=1)
+    value = inner(mine, w_own[...], 1, 1) + inner(theirs, w_oth[...], 1, 1)
+    out_0[...] = value[:rows].astype(out_0.dtype)
+    out_1[...] = value[rows:].astype(out_1.dtype)
+
+
+def back_first_kernel(
+    scalars, own, by_x, by_y, got_y, got_x, tokens, second_grad, dz_qkv, a_qkv, input_grad
+):
+    half = tokens.shape[0] // 2
+    upper = own[:half] + by_x[...].astype(F32) + got_y[...].astype(F32)
+    lower = own[half:] + by_y[...].astype(F32) + got_x[...].astype(F32)
+    upstream = jnp.concatenate([upper, lower], axis=0) + inner(dz_qkv[...], a_qkv[...], 1, 1)
+    norm, factor = normed(tokens[...].astype(F32))
+    input_grad[...] = second_grad[...] + norm_back(norm, factor, upstream)
+
+
+def scatter_rest(send_x, send_y, onward):
+    half = onward.shape[0] // 2
+    by_x, by_y = swap(send_x, 2), swap(send_y, 4)
+    pass_y = (onward[:half] + by_x[half:].astype(F32)).astype(BF)
+    pass_x = (onward[half:] + by_y[half:].astype(F32)).astype(BF)
+    got_y, got_x = swap(pass_y, 4), swap(pass_x, 2)
+    return by_x, by_y, got_y, got_x, (pass_y, pass_x)
+
+
+def plane_shards(
+    tokens, cotangent, starts, adapter_ids,
+    w_qkv, w_out, w_gu, w_down, a_qkv, b_qkv, a_out, b_out, a_gu, b_gu, a_down, b_down,
+):
+    seat = lax.axis_index("seq")
+    z_at = lax.axis_index("fsdp")
+    z_count = lax.axis_size("fsdp")
+    core = seat % 2
+    chip = seat // 2
+    rows, width = tokens.shape[1:]
+    half = rows // 2
+    group = CHIPS * rows
+    length = rows * PLANE
+    ff = w_gu.shape[1] // 2
+    ff_z = ff // z_count
+    ff_dev = ff_z // PLANE
+    quarter = w_qkv.shape[0]
+    latent = a_out.shape[1]
+    heads_dev = width // HEAD_DIM // PLANE
+    span = heads_dev * HEAD_DIM
+    share = quarter // PLANE
+    share_b = latent // PLANE
+    wide_down = width + latent
+    wide_gu = width + 2 * latent
+    first = starts[0]
+    chosen = adapter_ids[0]
+    scalars = jnp.concatenate([jnp.stack([chip, core, z_at]).astype(jnp.int32), first, chosen])
+    stream, cot_low = tokens[0], cotangent[0]
+
+    norm_a, norm_b = call(
+        norm_kernel, scalars, [stream], [whole_spec((rows, width))],
+        [sds((half, width))] * 2, [whole_spec((half, width))] * 2,
+    )
+    tall_rows = quarter + 2 * share + 3 * share
+    first_part = call(
+        functools.partial(cut_first_kernel, (share, quarter, width)), scalars,
+        [w_qkv, w_out, a_qkv, a_out, a_gu, b_out, b_down, b_qkv], [ANY] * 8,
+        sds((tall_rows, 3 * span)), whole_spec((tall_rows, 3 * span)),
+        scratch=[pltpu.SemaphoreType.DMA((39,))],
+    )
+    first_all = lax.all_gather(first_part, "fsdp", axis=0, tiled=True)
+    down_part, gu_part_0, gu_part_1 = call(
+        functools.partial(cut_rest_kernel, (ff, ff_z, ff_dev, width)), scalars,
+        [w_gu, w_down, a_down, b_gu], [ANY] * 4,
+        [sds((ff_dev, wide_down + ff_dev))] + [sds((quarter, 4 * ff_dev))] * 2,
+        [whole_spec((ff_dev, wide_down + ff_dev))] + [whole_spec((quarter, 4 * ff_dev))] * 2,
+        scratch=[pltpu.SemaphoreType.DMA((11,))], ties=[first_part],
+    )
+    down_own = lax.all_gather(down_part, "fsdp", axis=0, tiled=True)
+    gu_own_0 = lax.all_gather(gu_part_0, "fsdp", axis=0, tiled=True)
+    gu_own_1 = lax.all_gather(gu_part_1, "fsdp", axis=0, tiled=True)
+
+    pieces1 = gather_halves(norm_a, norm_b)
+    pieces1_oth = [swap(piece, 1) for piece in pieces1]
+
+
+    cot_pieces = gather_halves(cot_low[:half], cot_low[half:])
+    first_all = hold(first_all, [pieces1_oth[1], pieces1_oth[3], cot_pieces[1], cot_pieces[3]])
+    by_z = first_all.reshape(z_count, tall_rows, 3 * span)
+
+    def rows_of(start, count, z, many):
+        return by_z[z : z + many, start : start + count].reshape(many * count, 3 * span)
+
+    pieces_small = gather_halves(rows_of(quarter, share + 32, 0, 2), rows_of(quarter, share + 32, 2, 2))
+    pieces_small += [swap(piece, 1) for piece in pieces_small]
+    ups_qkv = rows_of(quarter + share, 64, 0, 4)
+    full_a_qkv, full_a_gu, full_a_out, full_b_out, full_b_down = call(
+        functools.partial(unpack_small_kernel, share, quarter), scalars, pieces_small,
+        [whole_spec((2 * share + 64, 3 * span))] * 16,
+        [sds((width, 3 * latent)), sds((width, 2 * latent)), sds((width, latent))]
+        + [sds((latent, width))] * 2,
+        [whole_spec((width, 3 * latent)), whole_spec((width, 2 * latent)), whole_spec((width, latent))]
+        + [whole_spec((latent, width))] * 2,
+    )
+    at = quarter + 2 * share
+    out_a, out_b = rows_of(at, 3 * share, 0, 2), rows_of(at, 3 * share, 2, 2)
+    pieces_out = gather_halves(hold(out_a, [pieces_small[1]]), hold(out_b, [pieces_small[3]]))
+    pieces_out += [swap(piece, 1) for piece in pieces_out]
+    full_out = call(
+        functools.partial(unpack_out_kernel, share, quarter), scalars, pieces_out, [ANY] * 16,
+        sds((width, width)), whole_spec((width, width)), scratch=[pltpu.SemaphoreType.DMA((96,))],
+    )
+    ups_oth = swap(ups_qkv, 1)
+
+    def qkv_up(piece):
+        piece = piece.reshape(z_count, 64, 3 * span)
+        parts = []
+        for k in range(12):
+            row, lane = up_slot(k)
+            parts.append(piece[:, row : row + 16, lane : lane + LANES])
+        return jnp.concatenate(parts, axis=1).transpose(1, 0, 2).reshape(192, z_count * LANES)
+
+    mine, theirs = qkv_up(ups_qkv), qkv_up(ups_oth)
+    up_chip = jnp.where(
+        core == 0, jnp.concatenate([mine, theirs], axis=0), jnp.concatenate([theirs, mine], axis=0)
+    )
+    up_own = take(up_chip, core * span, span, 1)
+    up_oth = take(up_chip, (1 - core) * span, span, 1)
+
+    all_places = jnp.arange(length, dtype=jnp.int32)
+    all_begin, _ = doc_tables(all_places, first, chosen)
+    cosine, sine = rope_tables(all_places - all_begin, HEAD_DIM)
+    sign = jnp.where(jnp.arange(HEAD_DIM) < HEAD_DIM // 2, -1.0, 1.0)
+    turn = sine * sign[None, :]
+    rel = jnp.array([r for r, _ in HALVES], jnp.int32)
+    part = jnp.array([h for _, h in HALVES], jnp.int32)
+    group_places = ((((rel ^ chip) * 2 + core) * 2 + part) * half)[:, None] + jnp.arange(
+        half, dtype=jnp.int32
+    )
+    _, group_which = doc_tables(group_places.reshape(-1), first, chosen)
+    adapters_at = jnp.arange(latent, dtype=jnp.int32) // RANK
+    group_select = (adapters_at[None, :] == group_which[:, None]).astype(BF)
+    select = group_select[-rows:]
+
+    qkv, z_qkv, qkv_own = call(
+        qkv_kernel, scalars,
+        pieces1 + pieces1_oth + [first_all, full_a_qkv, up_own, cosine, turn],
+        [ANY] * 17
+        + [
+            whole_spec((width, 3 * latent)),
+            whole_spec((3 * latent, span)), whole_spec((length, LANES)), whole_spec((length, LANES)),
+        ],
+        [sds((length, 3 * span)), sds((length, 3 * latent)), sds((width, 3 * span))],
+        [whole_spec((length, 3 * span)), whole_spec((length, 3 * latent)), whole_spec((width, 3 * span))],
+        scratch=[pltpu.VMEM((length, width), BF), pltpu.SemaphoreType.DMA((20,))],
+        cost=(2 * length * width * (3 * span + 3 * latent), 20 * 2**20),
+    )
+    column = lambda k: pl.BlockSpec((length, LANES), lambda h, _: (0, k * heads_dev + h))
+    mixed_h, log_sums = call(
+        functools.partial(attend_kernel, rows), scalars, [qkv] * 3, [column(0), column(1), column(2)],
+        [sds((length, span)), sds((length, span), F32)], [column(0), column(0)], grid=(heads_dev,),
+        cost=(4 * heads_dev * length * length * HEAD_DIM, 8 * 2**20),
+    )
+    mixed = lax.all_to_all(mixed_h, "seq", split_axis=0, concat_axis=1, tiled=True)
+    square = whole_spec((width, width))
+    tall = whole_spec((rows, width))
+    second, norm_a, norm_b, z_out = call(
+        out_kernel, scalars, [mixed, full_out, full_a_out, full_b_out, stream],
+        [tall, square, whole_spec((width, latent)), whole_spec((latent, width)), tall],
+        [sds((rows, width), F32), sds((half, width)), sds((half, width)), sds((rows, latent))],
+        [tall, whole_spec((half, width)), whole_spec((half, width)), whole_spec((rows, latent))],
+        scratch=[pltpu.VMEM((rows, width), BF)],
+        cost=(2 * rows * width * width, 12 * 2**20),
+    )
+
+    pieces2 = gather_halves(norm_a, norm_b)
+    down_own = hold(down_own, [second])
+    down_oth = swap(down_own, 1)
+    gu_own_0 = hold(gu_own_0, [pieces2[1], pieces2[3]])
+    gu_oth_0 = swap(gu_own_0, 1)
+    step = group // 2
+
+    def feed(chunk, gu_pair, at, onward, kind):
+        operands = [group_select, full_a_gu, full_b_down, down_own, down_oth, *gu_pair]
+        operands += pieces2[4 * at : 4 * at + 4] + cot_pieces[4 * at : 4 * at + 4]
+        specs = [
+            pl.BlockSpec((step, latent), lambda *_: (at, 0)), whole_spec((width, 2 * latent)),
+            whole_spec((latent, width)),
+        ] + [ANY] * 12
+        if onward is None:
+            shapes, outs = [sds((step, wide_gu), F32)], [whole_spec((step, wide_gu))]
+        else:
+            operands.append(onward)
+            specs.append(ANY)
+            shapes, outs = [sds((rows, wide_gu), kind)] * 2, [whole_spec((rows, wide_gu))] * 2
+        shapes += [
+            sds((step, 4 * ff_dev)), sds((2, 2 * latent, 2 * ff_dev), F32), sds((2, 2 * ff_dev, latent), F32)
+        ]
+        outs += [
+            whole_spec((step, 4 * ff_dev)), whole_spec((2, 2 * latent, 2 * ff_dev)),
+            whole_spec((2, 2 * ff_dev, latent)),
+        ]
+        return call(
+            functools.partial(ff_kernel, onward is None, chunk), scalars, operands, specs,
+            shapes, outs,
+            scratch=[pltpu.VMEM((step, width), BF)] * 2 + [pltpu.VMEM((width, 4 * ff_dev), BF)] * 2
+            + [pltpu.VMEM((2 * ff_dev, wide_down + ff_dev), BF)] * 2
+            + [pltpu.VMEM((step, wide_gu) if onward is not None else (8, LANES), F32)]
+            + [pltpu.SemaphoreType.DMA((13,))],
+            cost=(step * 10 * width * ff_dev * 4, 26 * 2**20),
+        )
+
+    gu_pair = (gu_own_0, gu_oth_0)
+    sums_0, hidden_00, up_grads_00, down_grads_00 = feed(0, gu_pair, 0, None, F32)
+    sums_1, hidden_01, up_grads_01, down_grads_01 = feed(0, gu_pair, 1, None, F32)
+    gu_own_1 = hold(gu_own_1, [sums_0, sums_1])
+    gu_pair = (gu_own_1, swap(gu_own_1, 1))
+    send_x, send_y, hidden_10, up_grads_10, down_grads_10 = feed(1, gu_pair, 0, sums_0, BF)
+    pass_on, kept, hidden_11, up_grads_11, down_grads_11 = feed(1, gu_pair, 1, sums_1, F32)
+
+    def after(values, ties):
+        specs = [whole_spec(value.shape) for value in values]
+        return call(
+            keep_kernel, scalars, values, specs, [sds(v.shape, v.dtype) for v in values], specs, ties=ties
+        )
+
+    once = pl.Buffered(1)
+
+    def down_half(at, hidden_0, hidden_1, kind, ties):
+        row = pl.BlockSpec((rows, 4 * ff_dev), lambda i, _: (i, 0))
+        weight = pl.BlockSpec(
+            (z_count * ff_dev, wide_down + ff_dev), lambda i, _: (0, 0), pipeline_mode=once
+        )
+        return call(
+            down_kernel, scalars, [hidden_0, hidden_1, down_own, down_oth], [row, row, weight, weight],
+            [sds((rows, wide_down), kind)] * 2, [whole_spec((rows, wide_down))] * 2, grid=(2,),
+            cost=(2 * step * 8 * ff_dev * width, 16 * 2**20), ties=ties,
+        )
+
+    ff_rows = 2 * latent * (ff_dev // LANES) + ff_dev
+    ups = [up_grads_00, up_grads_01, up_grads_10, up_grads_11]
+    downs = [down_grads_00, down_grads_01, down_grads_10, down_grads_11]
+    ff_keep, ff_send = call(
+        ff_grads_kernel, scalars, ups + downs,
+        [whole_spec(ups[0].shape)] * 4 + [whole_spec(downs[0].shape)] * 4,
+        [sds((z_count, ff_rows, LANES), F32), sds((z_count, ff_rows, LANES))],
+        [whole_spec((z_count, ff_rows, LANES))] * 2, cost=(2**20, 12 * 2**20),
+    )
+    by_x, by_y, got_y, got_x, _ = scatter_rest(send_x, send_y, pass_on)
+    down_x, down_y = down_half(0, hidden_00, hidden_10, BF, [by_x, by_y])
+    halfspec = lambda n: pl.BlockSpec((half, n), lambda *_: (0, 0))
+    second_grad, dz_gu, dz_out, mixed_grad, *up_out = call(
+        back_middle_kernel, scalars,
+        [kept, by_x, by_y, got_y, got_x, second, cot_low, full_a_gu, full_out, full_a_out, full_b_out, z_out],
+        [whole_spec((rows, wide_gu))] + [halfspec(wide_gu)] * 4
+        + [
+            tall, tall, whole_spec((width, 2 * latent)), square, whole_spec((width, latent)),
+            whole_spec((latent, width)), whole_spec((rows, latent)),
+        ],
+        [
+            sds((rows, width), F32), sds((rows, 2 * latent)), sds((rows, latent)), sds((rows, width)),
+            sds((2 * share_b, width), F32),
+        ]
+        + [sds((2 * share_b, width))] * 3,
+        [tall, whole_spec((rows, 2 * latent)), whole_spec((rows, latent)), tall]
+        + [whole_spec((2 * share_b, width))] * 4,
+        cost=(2 * rows * width * width, 16 * 2**20), ties=[down_x, ff_send],
+    )
+    mixed_grad_h = lax.all_to_all(mixed_grad, "seq", split_axis=1, concat_axis=0, tiled=True)
+    down_on, down_kept = down_half(1, hidden_01, hidden_11, F32, [mixed_grad])
+
+    def along_line(keep, send, ties):
+        shape = keep.shape[1:]
+        brought = swap(send, 1)
+        mine, *sends = call(
+            along_line_kernel, scalars, [keep, brought], [whole_spec(keep.shape)] * 2,
+            [sds(shape, F32)] + [sds(shape)] * 6, [whole_spec(shape)] * 7, ties=ties,
+            cost=(2**20, 8 * 2**20),
+        )
+        return mine, sends
+
+    def line_sum(mine, sends, ties):
+        total = hold(mine, ties) if ties else mine
+        for k, value in enumerate(sends):
+            hop = k // 2 + 1
+            if k % 2 == 0:
+                perm = [(i, i + hop) for i in range(z_count - hop)]
+            else:
+                perm = [(i + hop, i) for i in range(z_count - hop)]
+            total = total + lax.ppermute(value, "fsdp", perm).astype(F32)
+        return total.astype(BF)
+
+    def spread(mine, places, shapes, ties):
+        plane = blocks_of(mine)
+        plane += [swap(piece, 1) for piece in plane]
+        return call(
+            functools.partial(spread_kernel, places), scalars, plane, [whole_spec(mine.shape)] * 8,
+            [sds(shape, F32) for shape in shapes], [whole_spec(shape) for shape in shapes], ties=ties,
+        )
+
+    *down_by, down_passed = scatter_rest(down_x, down_y, down_on)
+    dz_gu, dz_out, *up_out = after([dz_gu, dz_out] + up_out, [mixed_grad_h])
+    all_dz_gu = blocks_of(dz_gu)
+    all_dz_out = blocks_of(jnp.stack([dz_out, swap(dz_out, 1)]))
+    all_up_out = [up_out[0], swap(up_out[1], 2), swap(up_out[2], 4), swap(up_out[3], 6)]
+
+    result = pl.BlockSpec((3, group, HEAD_DIM), lambda h, _: (0, 0, h))
+    grads_a, grads_b, up_qkv = call(
+        functools.partial(attend_back_kernel, rows), scalars,
+        [qkv, qkv, qkv, mixed_grad_h, log_sums, z_qkv, cosine, turn],
+        [column(0), column(1), column(2), column(0), column(0), whole_spec((length, 3 * latent))]
+        + [whole_spec((length, LANES))] * 2,
+        [sds((3, group, span))] * 2 + [sds((3, latent, span), F32)],
+        [result, result, pl.BlockSpec((3, latent, HEAD_DIM), lambda h, _: (0, 0, h))],
+        scratch=[pltpu.VMEM((length, HEAD_DIM), F32)] * 3, grid=(heads_dev,),
+        cost=(10 * heads_dev * length * length * HEAD_DIM, 16 * 2**20), ties=down_passed,
+    )
+    grads_b = swap(grads_b, 1)
+    qkv_oth = swap(qkv_own, 1)
+
+    down_kept = hold(down_kept, [grads_a])
+    upper = down_kept[:half] + down_by[0][:half].astype(F32) + down_by[2].astype(F32)
+    lower = down_kept[half:] + down_by[1][:half].astype(F32) + down_by[3].astype(F32)
+    wide = jnp.concatenate([upper, lower], axis=0)
+    z_down = wide[:, width:].astype(BF) * select
+    all_z_down = blocks_of(z_down)
+    to_x, to_y, to_far, latent_kept = call(
+        back_latent_kernel, scalars, [grads_a, grads_b, up_own, up_oth],
+        [whole_spec((3, group, span))] * 2 + [whole_spec((3 * latent, span))] * 2,
+        [sds((rows, 3 * latent))] * 3 + [sds((rows, 3 * latent), F32)],
+        [whole_spec((rows, 3 * latent))] * 4,
+        cost=(4 * group * span * 3 * latent, 4 * 2**20),
+    )
+
+    def back_qkv(at, kind, ties):
+        part = pl.BlockSpec((3, step, span), lambda *_: (0, at, 0))
+        return call(
+            back_qkv_kernel, scalars, [grads_a, grads_b, qkv_own, qkv_oth],
+            [part, part] + [whole_spec((width, 3 * span))] * 2,
+            [sds((rows, width), kind)] * 2, [tall] * 2,
+            cost=(2 * group * span * 3 * width, 12 * 2**20), ties=ties,
+        )
+
+    send_x, send_y = back_qkv(0, BF, [to_x])
+    pass_on, kept = back_qkv(1, F32, [send_x])
+    by_x, by_y, got_y, got_x, passed = scatter_rest(send_x, send_y, pass_on)
+    latent_kept = hold(latent_kept, passed)
+    dz_qkv = latent_kept + swap(to_x, 2).astype(F32) + swap(to_y, 4).astype(F32)
+    dz_qkv = (dz_qkv + swap(to_far, 6).astype(F32)) * jnp.tile(select, (1, 3)).astype(F32)
+    dz_qkv = dz_qkv.astype(BF)
+    ff_mine, ff_sends = along_line(ff_keep, ff_send, [kept])
+    ff_total = line_sum(ff_mine, ff_sends, passed)
+    other_rows = 11 * LANES // 2
+    block = lambda n: [whole_spec((rows, n))] * 4
+    keep, send = call(
+        functools.partial(other_grads_kernel, quarter), scalars,
+        [*pieces1, *pieces2, *cot_pieces, mixed_h, *all_dz_gu, *blocks_of(dz_qkv), *all_z_down, *all_dz_out,
+         *all_up_out, up_qkv],
+        [ANY] * 24 + [whole_spec((length, span))] + block(2 * latent) + block(3 * latent) + block(latent)
+        + [whole_spec((2, rows, latent))] * 4 + [whole_spec((2 * share_b, width))] * 4
+        + [whole_spec((3, latent, span))],
+        [sds((z_count, other_rows, LANES), F32), sds((z_count, other_rows, LANES))],
+        [whole_spec((z_count, other_rows, LANES))] * 2,
+        scratch=[
+            pltpu.VMEM((3, group, z_count * LANES), BF), pltpu.VMEM((group, 2 * latent), BF),
+            pltpu.VMEM((group, 3 * latent), BF), pltpu.VMEM((group, latent), BF),
+            pltpu.SemaphoreType.DMA((96,)),
+        ],
+        cost=(2 * group * 512 * 768, 8 * 2**20), ties=passed,
+    )
+
+    g_b_gu, g_a_down = spread(
+        ff_total, (("columns", 2 * latent, ff_dev // LANES), ("rows", ff_dev, 1)),
+        [(2 * latent, ff_z), (ff_z, latent)], passed,
+    )
+
+    input_grad = call(
+        back_first_kernel, scalars,
+        [kept, by_x, by_y, got_y, got_x, stream, second_grad, dz_qkv, full_a_qkv],
+        [tall] + [halfspec(width)] * 4
+        + [tall, tall, whole_spec((rows, 3 * latent)), whole_spec((width, 3 * latent))],
+        sds((rows, width), F32), tall,
+        cost=(2 * rows * width * 3 * latent, 12 * 2**20),
+    )
+    activations = second + (wide[:, :width] + dot(hold(z_down, passed), full_b_down))
+    mine, sends = along_line(keep, send, [input_grad])
+    low = LANES // 2
+    g_a_gu, g_b_down, g_a_out, g_b_out, g_a_qkv, g_b_qkv = spread(
+        line_sum(mine, sends, []),
+        (
+            ("rows", low, 2), ("both", low, 1), ("rows", low, 1), ("core rows", share_b, z_count),
+            ("rows", low, 3), ("both", 3 * low, 1),
+        ),
+        [
+            (quarter, 2 * latent), (latent, quarter), (quarter, latent), (latent, quarter),
+            (quarter, 3 * latent), (3 * latent, quarter),
+        ],
+        [],
+    )
+
+    return (
+        activations[None], input_grad[None],
+        g_a_qkv, g_b_qkv, g_a_out, g_b_out, g_a_gu, g_b_gu, g_a_down, g_b_down,
+    )
+
+
 def solution(mesh):
     placed = (
         P("fsdp", "seq", None),
@@ -429,8 +1480,9 @@
         P("fsdp", None),
         P(None, "fsdp"),
     )
+    on_plane = mesh.shape["seq"] == PLANE and mesh.shape["fsdp"] == 4
     return jax.shard_map(
-        shards,
+        plane_shards if on_plane else shards,
         mesh=mesh,
         in_specs=placed,
         out_specs=(

time: 3630 us -> 730 us (0.20)
  waiting for transfers between devices: 2950 us -> 189 us
  matrix products: 339 us -> 3.17 us
  Pallas kernels: 0 us -> 303 us
  starting transfers between devices: 50.5 us -> 147 us
  local copies, waits for them, and re-layouts: 125 us -> 38 us
  other arithmetic: 80.7 us -> 23.4 us
  blocking collectives: 55 us -> 0 us
    all_gather x9 -> x4, waiting for transfers between devices: 2160 us -> 75.6 us  [the longest x1 31.3 us: plane_shards(): gu_own_0 = lax.all_gather(gu_part_0, 'fsdp', axis=0, tiled=True)]
    psum x1 -> x0, waiting for transfers between devices: 761 us -> none  [shards(): lax.psum((grads[0], grads[1], grads[2], grads[3], grads[4], grads[5], gra...]
    dot_general x69 -> x1, matrix products: 339 us -> 3.17 us  [dot(): return jnp.dot(left, right, preferred_element_type=F32)]
    pallas_call x0 -> x37, Pallas kernels: none -> 303 us  [the longest x27 303 us: call(): pl.pallas_call(run, grid_spec=pltpu.PrefetchScalarGridSpec(num_scalar_pre...]
    ppermute x0 -> x119, starting transfers between devices: none -> 140 us  [the longest x107 106 us: swap(): return lax.ppermute(value, 'seq', [(i, i ^ bits) for i in range(PLANE)])]
    ppermute x0 -> x119, waiting for transfers between devices: none -> 103 us  [the longest x107 93.4 us: swap(): return lax.ppermute(value, 'seq', [(i, i ^ bits) for i in range(PLANE)])]
    all_gather x3 -> x0, blocking collectives: 55 us -> none  [the longest x1 20.6 us: shards(): lax.all_gather(b_down, 'fsdp', axis=1, tiled=True)]
    all_to_all x8 -> x2, starting transfers between devices: 50.2 us -> 7.2 us  [the longest x1 3.68 us: plane_shards(): lax.all_to_all(mixed_grad, 'seq', split_axis=1, concat_axis=0, tiled=True)]
  transfers between devices with their start and end apart: 18 -> 125, of which waited for: 13 -> 29; matrix products, arithmetic and copies ran while one was open for 9% -> 5% of each run, Pallas kernels for 0% -> 38%
where the time goes in v2:
time: 730 us; the launch traced here: 720 us
  Pallas kernels  303 us (42%)
  waiting for transfers between devices  189 us (26%)
  starting transfers between devices  147 us (20%)
  local copies, waits for them, and re-layouts  38 us (5%)
  other arithmetic  23.4 us (3%)
  between operations  15.7 us (2%)
    pallas_call x27, Pallas kernels, call(): pl.pallas_call(run, grid_spec=pltpu.PrefetchScalarGridSpec(num_scalar_pre...  303 us
    ppermute x107, starting transfers between devices, swap(): return lax.ppermute(value, 'seq', [(i, i ^ bits) for i in range(PLANE)])  106 us
    ppermute x107, waiting for transfers between devices, swap(): return lax.ppermute(value, 'seq', [(i, i ^ bits) for i in range(PLANE)])  93.4 us
    ppermute x12, starting transfers between devices, line_sum(): total = total + lax.ppermute(value, 'fsdp', perm).astype(F32)  34.1 us
    all_gather x1, waiting for transfers between devices, plane_shards(): gu_own_0 = lax.all_gather(gu_part_0, 'fsdp', axis=0, tiled=True)  31.3 us
    all_gather x1, waiting for transfers between devices, plane_shards(): first_all = lax.all_gather(first_part, 'fsdp', axis=0, tiled=True)  28.4 us
    unnamed x217, local copies, waits for them, and re-layouts  21.4 us
    all_gather x1, waiting for transfers between devices, plane_shards(): gu_own_1 = lax.all_gather(gu_part_1, 'fsdp', axis=0, tiled=True)  15.9 us
  transfers between devices with their start and end apart: 125, of which 29 were waited for; matrix products, arithmetic and copies ran while one was open for 5% of the time, Pallas kernels for 38%

profile of v2, /device:TPU:1, one launch (start us, length us, event | category | flops | bytes accessed | tf_op | source)
XLA Modules:
  0.0 719.6 jit_solution(13197552050412620299)
XLA Ops:
  8.5 3.3 shard_map.250.refs_5_
  11.9 4.4 shard_map.259
  16.4 3.6 shard_map.249
  26.1 7.8 %collective-permute-done.1.refs_5_ = bf16[128,2048]{1,0:T(8,128)(2,1)} collective-permute-done((bf16[128,2048]{1,0:T(8,128)(2,1)}, bf16[128,2048]{1,0:T(8,128)(2,1)}, u32[]{:S(2)}, u32[]{:S(2)}) %collective-permute-start.1) | collective-permute-done | bytes 524320 | tf_op jit(solution)/shard_map/ppermute | solution.py:429
  35.1 10.9 %collective-permute-done.4.refs_6_ = bf16[128,2048]{1,0:T(8,128)(2,1)} collective-permute-done((bf16[128,2048]{1,0:T(8,128)(2,1)}, bf16[128,2048]{1,0:T(8,128)(2,1)}, u32[]{:S(2)}, u32[]{:S(2)}) %collective-permute-start.4) | collective-permute-done | bytes 524320 | tf_op jit(solution)/shard_map/ppermute | solution.py:429
  46.4 3.7 multiply_sine_fusion
  51.3 6.0 collective-permute-done.16.refs_13_.refs_22_
  57.6 10.9 %collective-permute-done.2.refs_2_ = bf16[128,2048]{1,0:T(8,128)(2,1)} collective-permute-done((bf16[128,2048]{1,0:T(8,128)(2,1)}, bf16[128,2048]{1,0:T(8,128)(2,1)}, u32[]{:S(2)}, u32[]{:S(2)}) %collective-permute-start.2) | collective-permute-done | bytes 524320 | tf_op jit(solution)/shard_map/ppermute | solution.py:429
  68.5 3.3 collective-permute-start.7
  73.8 6.0 collective-permute-done.15.refs_3_.refs_13_.refs_18_
  81.8 28.4 %all-gather.5.cloned.1.call-done.refs_0_ = bf16[3328,768]{1,0:T(8,128)(2,1)} async-done(((bf16[832,768]{1,0:T(8,128)(2,1)}), bf16[3328,768]{1,0:T(8,128)(2,1)}) %all-gather.5.cloned.1.call-update) | async-done | bytes 5111824 | tf_op jit(solution)/shard_map/all_gather | solution.py:1128
  115.8 2.4 fusion.7
  122.9 10.4 %collective-permute-done.22.refs_6_ = bf16[192,768]{1,0:T(8,128)(2,1)S(1)} collective-permute-done((bf16[192,768]{1,0:T(8,128)(2,1)S(1)}, bf16[192,768]{1,0:T(8,128)(2,1)S(1)}, u32[]{:S(2)}, u32[]{:S(2)}) %collective-permute-start.22) | collective-permute-done | bytes 294944 | tf_op jit(solution)/shard_map/ppermute | solution.py:429
  136.5 4.8 collective-permute-done.20.refs_2_.refs_1_
  147.2 5.5 shard_map.252
  157.2 22.1 %shard_map.253 = (bf16[2048,768]{1,0:T(8,128)(2,1)}, bf16[2048,384]{1,0:T(8,128)(2,1)}, bf16[2048,768]{1,0:T(8,128)(2,1)}) custom-call(s32[11]{0:T(128)} %concatenate.24.refs_0_, bf16[128,2048]{1,0:T(8,128)(2,1)} %collective-permute-done.refs_1_, bf16[128,2048]{1,0:T(8,128)(2,1)} %collective-permute-done.2.refs_2_, ...), custom_call_target="tpu_custom_call" | custom-call | flops 9663676416 | bytes 20971520 | tf_op jit(solution)/shard_map/pallas_call | solution.py:468
  183.9 16.0 %shard_map.254 = (bf16[2048,256]{1,0:T(8,128)(2,1)}, f32[2048,256]{1,0:T(8,128)}) custom-call(s32[11]{0:T(128)} %concatenate.24.refs_0_, bf16[2048,768]{1,0:T(8,128)(2,1)} %get-tuple-element.105.refs_1_.refs_2_.refs_3_, bf16[2048,768]{1,0:T(8,128)(2,1)} %get-tuple-element.105.refs_1_.refs_2_.refs_3_, bf16[2048,768]{1,0:T(8,128)(2,1)} %get-tuple-element.105.refs_1_.refs_2_.refs_3_), custom_call_target="tpu_custom_call" | custom-call | flops 4294967296 | bytes 8388608 | tf_op jit(solution)/shard_map/pallas_call | solution.py:468
  200.0 3.5 all-to-all-start
  204.9 10.5 %all-to-all-done = bf16[8,256,256]{2,1,0:T(8,128)(2,1)S(1)} async-done(((bf16[8,256,256]{2,1,0:T(8,128)(2,1)}), bf16[8,256,256]{2,1,0:T(8,128)(2,1)S(1)}, u32[]{:S(2)}, u32[]{:S(2)}) %all-to-all-start) | async-done | bytes 1048608 | tf_op jit(solution)/shard_map/all_to_all | solution.py:1221
  218.4 8.3 %shard_map.257.refs_2_.refs_9_ = bf16[2048,2048]{1,0:T(8,128)(2,1)} custom-call(s32[11]{0:T(128)} %concatenate.24.refs_0_, bf16[384,768]{1,0:T(8,128)(2,1)} %copy-done.31, bf16[384,768]{1,0:T(8,128)(2,1)} %collective-permute-done.35.refs_2_, bf16[384,768]{1,0:T(8,128)(2,1)} %copy-done.32, bf16[384,768]{1,0:T(8,128)(2,1)} %collective-permute-done.38.refs_4_, ...), custom_call_target="tpu_custom_call" | custom-call | tf_op jit(solution)/shard_map/pallas_call | solution.py:468
  226.6 9.6 %shard_map.258 = (f32[256,2048]{1,0:T(8,128)}, bf16[128,2048]{1,0:T(8,128)(2,1)}, bf16[128,2048]{1,0:T(8,128)(2,1)}, bf16[256,128]{1,0:T(8,128)(2,1)}) custom-call(s32[11]{0:T(128)} %concatenate.24.refs_0_, bf16[256,2048]{1,0:T(8,128)(2,1)} %bitcast.62, bf16[2048,2048]{1,0:T(8,128)(2,1)} %shard_map.257.refs_2_.refs_9_, ...), custom_call_target="tpu_custom_call" | custom-call | flops 2147483648 | bytes 12582912 | tf_op jit(solution)/shard_map/pallas_call | solution.py:468
  240.9 5.6 collective-permute-done.48.refs_8_.refs_13_
  246.5 6.6 collective-permute-start.49
  253.2 31.3 %all-gather.9.cloned.1.call-done.refs_0_ = bf16[2048,1024]{1,0:T(8,128)(2,1)} async-done(((bf16[512,1024]{1,0:T(8,128)(2,1)}), bf16[2048,1024]{1,0:T(8,128)(2,1)}) %all-gather.9.cloned.1.call-update) | async-done | bytes 4194320 | tf_op jit(solution)/shard_map/all_gather | solution.py:1137
  291.0 2.9 collective-permute-done.52.refs_7_
  295.9 25.7 %shard_map.262 = (f32[512,2304]{1,0:T(8,128)}, bf16[512,1024]{1,0:T(8,128)(2,1)}, f32[2,256,512]{2,1,0:T(8,128)}, f32[2,512,128]{2,1,0:T(8,128)}) custom-call(s32[11]{0:T(128)} %concatenate.24.refs_0_, bf16[1024,128]{1,0:T(8,128)(2,1)} %compare_convert_fusion.refs_1_, bf16[2048,256]{1,0:T(8,128)(2,1)} %get-tuple-element.110.refs_2_.refs_8_, ...), custom_call_target="tpu_custom_call" | custom-call | flops 10737418240 | bytes 27262976 | tf_op jit(solution)/shard_map/pallas_call | solution.py:468
  323.5 25.8 %shard_map.263 = (f32[512,2304]{1,0:T(8,128)}, bf16[512,1024]{1,0:T(8,128)(2,1)}, f32[2,256,512]{2,1,0:T(8,128)}, f32[2,512,128]{2,1,0:T(8,128)}) custom-call(s32[11]{0:T(128)} %concatenate.24.refs_0_, bf16[1024,128]{1,0:T(8,128)(2,1)} %compare_convert_fusion.refs_1_, bf16[2048,256]{1,0:T(8,128)(2,1)} %get-tuple-element.110.refs_2_.refs_8_, ...), custom_call_target="tpu_custom_call" | custom-call | flops 10737418240 | bytes 27262976 | tf_op jit(solution)/shard_map/pallas_call | solution.py:468
  349.4 15.9 %all-gather.11.cloned.1.call-done.refs_0_ = bf16[2048,1024]{1,0:T(8,128)(2,1)} async-done(((bf16[512,1024]{1,0:T(8,128)(2,1)}), bf16[2048,1024]{1,0:T(8,128)(2,1)}) %all-gather.11.cloned.1.call-update) | async-done | bytes 4194320 | tf_op jit(solution)/shard_map/all_gather | solution.py:1138
  366.0 7.0 collective-permute-done.57.refs_7_
  374.9 25.5 %shard_map.266 = (bf16[256,2304]{1,0:T(8,128)(2,1)}, bf16[256,2304]{1,0:T(8,128)(2,1)}, bf16[512,1024]{1,0:T(8,128)(2,1)}, f32[2,256,512]{2,1,0:T(8,128)}, f32[2,512,128]{2,1,0:T(8,128)}) custom-call(s32[11]{0:T(128)} %concatenate.24.refs_0_, bf16[1024,128]{1,0:T(8,128)(2,1)} %compare_convert_fusion.refs_1_, ...), custom_call_target="tpu_custom_call" | custom-call | flops 10737418240 | bytes 27262976 | tf_op jit(solution)/shard_map/pallas_call | solution.py:468
  402.9 26.6 %shard_map.265 = (f32[256,2304]{1,0:T(8,128)}, f32[256,2304]{1,0:T(8,128)}, bf16[512,1024]{1,0:T(8,128)(2,1)}, f32[2,256,512]{2,1,0:T(8,128)}, f32[2,512,128]{2,1,0:T(8,128)}) custom-call(s32[11]{0:T(128)} %concatenate.24.refs_0_, bf16[1024,128]{1,0:T(8,128)(2,1)} %compare_convert_fusion.refs_1_, bf16[2048,256]{1,0:T(8,128)(2,1)} %get-tuple-element.110.refs_2_.refs_8_, ...), custom_call_target="tpu_custom_call" | custom-call | flops 10737418240 | bytes 27262976 | tf_op jit(solution)/shard_map/pallas_call | solution.py:468
  429.6 2.7 add_convert_fusion
  433.1 11.7 %shard_map.267 = (bf16[256,2176]{1,0:T(8,128)(2,1)}, bf16[256,2176]{1,0:T(8,128)(2,1)}) custom-call(s32[11]{0:T(128)} %concatenate.24.refs_0_, bf16[512,1024]{1,0:T(8,128)(2,1)} %get-tuple-element.126.refs_1_, bf16[512,1024]{1,0:T(8,128)(2,1)} %get-tuple-element.127.refs_2_, bf16[1024,2432]{1,0:T(8,128)(2,1)} %shard_map.260.refs_4_.refs_3_, ...), custom_call_target="tpu_custom_call" | custom-call | flops 4294967296 | bytes 16777216 | tf_op jit(solution)/shard_map/pallas_call | solution.py:468
  449.0 5.0 shard_map.268
  455.1 14.2 %shard_map.269 = (f32[256,2048]{1,0:T(8,128)}, bf16[256,256]{1,0:T(8,128)(2,1)}, bf16[256,128]{1,0:T(8,128)(2,1)}, bf16[256,2048]{1,0:T(8,128)(2,1)}, f32[32,204...) custom-call(s32[11]{0:T(128)} %concatenate.24.refs_0_, ...), custom_call_target="tpu_custom_call" | custom-call | flops 2147483648 | bytes 16777216 | tf_op jit(solution)/shard_map/pallas_call | solution.py:468
  471.6 3.7 all-to-all-start.1
  475.3 12.5 %shard_map.270 = (f32[256,2176]{1,0:T(8,128)}, f32[256,2176]{1,0:T(8,128)}) custom-call(s32[11]{0:T(128)} %concatenate.24.refs_0_, bf16[512,1024]{1,0:T(8,128)(2,1)} %get-tuple-element.116.refs_1_, bf16[512,1024]{1,0:T(8,128)(2,1)} %get-tuple-element.120.refs_2_, bf16[1024,2432]{1,0:T(8,128)(2,1)} %shard_map.260.refs_4_.refs_3_, ...), custom_call_target="tpu_custom_call" | custom-call | flops 4294967296 | bytes 16777216 | tf_op jit(solution)/shard_map/pallas_call | solution.py:468
  487.8 3.6 add_convert_fusion.2
  492.4 25.2 %shard_map.271 = (bf16[3,1024,256]{2,1,0:T(8,128)(2,1)}, bf16[3,1024,256]{2,1,0:T(8,128)(2,1)}, f32[3,128,256]{2,1,0:T(8,128)}) custom-call(s32[11]{0:T(128)} %concatenate.24.refs_0_, bf16[2048,768]{1,0:T(8,128)(2,1)} %get-tuple-element.105.refs_1_.refs_2_.refs_3_, bf16[2048,768]{1,0:T(8,128)(2,1)} %get-tuple-element.105.refs_1_.refs_2_.refs_3_, ...), custom_call_target="tpu_custom_call" | custom-call | flops 10737418240 | bytes 16777216 | tf_op jit(solution)/shard_map/pallas_call | solution.py:468
  520.6 2.7 shard_map.279
  526.8 4.4 shard_map.273
  531.4 9.0 %shard_map.274 = (bf16[256,2048]{1,0:T(8,128)(2,1)}, bf16[256,2048]{1,0:T(8,128)(2,1)}) custom-call(s32[11]{0:T(128)} %concatenate.24.refs_0_, bf16[3,1024,256]{2,1,0:T(8,128)(2,1)} %get-tuple-element.144.refs_1_, bf16[3,1024,256]{2,1,0:T(8,128)(2,1)} %copy-done.19, bf16[2048,768]{1,0:T(8,128)(2,1)} %get-tuple-element.146.refs_3_, ...), custom_call_target="tpu_custom_call" | custom-call | flops 3221225472 | bytes 12582912 | tf_op jit(solution)/shard_map/pallas_call | solution.py:468
  550.7 9.4 %shard_map.275 = (f32[256,2048]{1,0:T(8,128)}, f32[256,2048]{1,0:T(8,128)}) custom-call(s32[11]{0:T(128)} %concatenate.24.refs_0_, bf16[3,1024,256]{2,1,0:T(8,128)(2,1)} %get-tuple-element.144.refs_1_, bf16[3,1024,256]{2,1,0:T(8,128)(2,1)} %copy-done.19, bf16[2048,768]{1,0:T(8,128)(2,1)} %get-tuple-element.146.refs_3_, ...), custom_call_target="tpu_custom_call" | custom-call | flops 3221225472 | bytes 12582912 | tf_op jit(solution)/shard_map/pallas_call | solution.py:468
  562.7 3.0 collective-permute-done.68.refs_2_
  568.9 2.8 add_convert_fusion.4
  573.3 2.4 collective-permute-done.72
  577.0 3.9 collective-permute-done.74
  589.2 7.1 collective-permute-done.81.refs_35_
  598.4 3.6 shard_map.283
  605.6 9.9 %shard_map.280 = (f32[4,704,128]{2,1,0:T(8,128)}, bf16[4,704,128]{2,1,0:T(8,128)(2,1)}) custom-call(s32[11]{0:T(128)} %concatenate.24.refs_0_, bf16[128,2048]{1,0:T(8,128)(2,1)} %collective-permute-done.refs_1_, bf16[128,2048]{1,0:T(8,128)(2,1)} %collective-permute-done.2.refs_2_, bf16[128,2048]{1,0:T(8,128)(2,1)} %collective-permute-done.3.refs_3_, ...), custom_call_target="tpu_custom_call" | custom-call | flops 805306368 | bytes 8388608 | tf_op jit(solution)/shard_map/pallas_call | solution.py:468
  615.4 2.6 collective-permute-start.91
  618.0 5.8 collective-permute-start.108
  628.8 9.1 %collective-permute-start.110 = (bf16[768,128]{1,0:T(8,128)(2,1)}, bf16[768,128]{1,0:T(8,128)(2,1)S(1)}, u32[]{:S(2)}, u32[]{:S(2)}) collective-permute-start(bf16[768,128]{1,0:T(8,128)(2,1)} %get-tuple-element.189), channel_id=1, source_target_pairs={{0,3},{4,7},{8,11},{12,15},{16,19},{20,23},{24,27},{28,31}} | collective-permute-start | bytes 589832 | tf_op jit(solution)/shard_map/ppermute | solution.py:1347
  642.2 4.9 collective-permute-done.111
  650.3 7.4 %shard_map.278.refs_3_ = f32[256,2048]{1,0:T(8,128)} custom-call(s32[11]{0:T(128)} %concatenate.24.refs_0_, f32[256,2048]{1,0:T(8,128)} %get-tuple-element.151.refs_1_.refs_3_, bf16[256,2048]{1,0:T(8,128)(2,1)} %copy-done.11, bf16[256,2048]{1,0:T(8,128)(2,1)} %copy-done.12, bf16[128,2048]{1,0:T(8,128)(2,1)} %collective-permute-done.70.refs_4_, ...), custom_call_target="tpu_custom_call" | custom-call | flops 402653184 | bytes 12582912 | tf_op jit(solution)/shard_map/pallas_call | solution.py:468
  658.5 3.5 shard_map.281
  664.7 2.7 collective-permute-start.94
  668.7 6.1 collective-permute-start.96
  677.4 4.3 collective-permute-start.115
  688.6 5.7 collective-permute-start.118
  696.5 2.9 collective-permute-start.104
  699.4 3.2 fusion.1
  703.2 4.1 shard_map.285
  708.8 3.8 shard_map.282
  (483 shorter events, 146.7 us)
Async XLA Ops:
  7.2 103.0 %all-gather.5.cloned.1.call-start = ((), (), s32[]{:S(2)}) async-start(), calls=%async_computation.2 | async-start | bytes 6389760 | tf_op jit(solution)/shard_map/all_gather | solution.py:1128
  11.9 227.8 %all-gather.7.cloned.1.call-start = ((), (), s32[]{:S(2)}) async-start(), calls=%async_computation.3 | async-start | bytes 6225920 | tf_op jit(solution)/shard_map/all_gather | solution.py:1136
  16.3 268.2 %all-gather.9.cloned.1.call-start = ((), (), s32[]{:S(2)}) async-start(), calls=%async_computation.4 | async-start | bytes 5242880 | tf_op jit(solution)/shard_map/all_gather | solution.py:1137
  22.0 97.4 %collective-permute-start = (bf16[128,2048]{1,0:T(8,128)(2,1)}, bf16[128,2048]{1,0:T(8,128)(2,1)}, u32[]{:S(2)}, u32[]{:S(2)}) collective-permute-start(bf16[128,2048]{1,0:T(8,128)(2,1)} %get-tuple-element.102.refs_7_), channel_id=1, source_target_pairs={{0,8},{4,12},{8,0},{12,4},{16,24},{20,28},{24,16},{28,20},{1,9},{5... | collective-permute-start | bytes 1572872 | tf_op jit(solution)/shard_map/ppermute | solution.py:429
  23.2 22.8 %collective-permute-start.4 = (bf16[128,2048]{1,0:T(8,128)(2,1)}, bf16[128,2048]{1,0:T(8,128)(2,1)}, u32[]{:S(2)}, u32[]{:S(2)}) collective-permute-start(bf16[128,2048]{1,0:T(8,128)(2,1)} %get-tuple-element.103.refs_8_), channel_id=1, source_target_pairs={{0,8},{4,12},{8,0},{12,4},{16,24},{20,28},{24,16},{28,20},{1,9},{5... | collective-permute-start | bytes 1572872 | tf_op jit(solution)/shard_map/ppermute | solution.py:429
  24.5 25.5 %collective-permute-start.14 = (bf16[128,2048]{1,0:T(8,128)(2,1)}, bf16[128,2048]{1,0:T(8,128)(2,1)}, u32[]{:S(2)}, u32[]{:S(2)}) collective-permute-start(bf16[128,2048]{1,0:T(8,128)(2,1)} %get-tuple-element.219.refs_14_.refs_23_), channel_id=1, source_target_pairs={{0,16},{4,20},{8,24},{12,28},{16,0},{20,4},{24,8},{28,12},{1,17},{... | collective-permute-start | bytes 1572872 | tf_op jit(solution)/shard_map/ppermute | solution.py:429
  24.6 32.7 %collective-permute-start.16 = (bf16[128,2048]{1,0:T(8,128)(2,1)}, bf16[128,2048]{1,0:T(8,128)(2,1)}, u32[]{:S(2)}, u32[]{:S(2)}) collective-permute-start(bf16[128,2048]{1,0:T(8,128)(2,1)} %get-tuple-element.218.refs_15_.refs_24_), channel_id=1, source_target_pairs={{0,8},{4,12},{8,0},{12,4},{16,24},{20,28},{24,16},{28,20},{1,9},{5... | collective-permute-start | bytes 1572872 | tf_op jit(solution)/shard_map/ppermute | solution.py:429
  34.0 34.5 %collective-permute-start.2 = (bf16[128,2048]{1,0:T(8,128)(2,1)}, bf16[128,2048]{1,0:T(8,128)(2,1)}, u32[]{:S(2)}, u32[]{:S(2)}) collective-permute-start(bf16[128,2048]{1,0:T(8,128)(2,1)} %collective-permute-done.1.refs_5_), channel_id=1, source_target_pairs={{0,8},{4,12},{8,0},{12,4},{16,24},{20,28},{24,16},{28,20},{1,9},{5... | collective-permute-start | bytes 1572872 | tf_op jit(solution)/shard_map/ppermute | solution.py:429
  46.0 25.8 %collective-permute-start.5 = (bf16[128,2048]{1,0:T(8,128)(2,1)}, bf16[128,2048]{1,0:T(8,128)(2,1)}, u32[]{:S(2)}, u32[]{:S(2)}) collective-permute-start(bf16[128,2048]{1,0:T(8,128)(2,1)} %collective-permute-done.4.refs_6_), channel_id=1, source_target_pairs={{0,16},{4,20},{8,24},{12,28},{16,0},{20,4},{24,8},{28,12},{1,17},{... | collective-permute-start | bytes 1572872 | tf_op jit(solution)/shard_map/ppermute | solution.py:429
  50.1 29.7 %collective-permute-start.15 = (bf16[128,2048]{1,0:T(8,128)(2,1)}, bf16[128,2048]{1,0:T(8,128)(2,1)S(1)}, u32[]{:S(2)}, u32[]{:S(2)}) collective-permute-start(bf16[128,2048]{1,0:T(8,128)(2,1)} %collective-permute-done.14.refs_12_.refs_21_), channel_id=1, source_target_pairs={{0,8},{4,12},{8,0},{12,4},{16,24},{20,28},{24,16},{28,20},{1,9},{5... | collective-permute-start | bytes 1572872 | tf_op jit(solution)/shard_map/ppermute | solution.py:429
  57.3 22.8 %collective-permute-start.17 = (bf16[128,2048]{1,0:T(8,128)(2,1)}, bf16[128,2048]{1,0:T(8,128)(2,1)S(1)}, u32[]{:S(2)}, u32[]{:S(2)}) collective-permute-start(bf16[128,2048]{1,0:T(8,128)(2,1)} %collective-permute-done.16.refs_13_.refs_22_), channel_id=1, source_target_pairs={{0,16},{4,20},{8,24},{12,28},{16,0},{20,4},{24,8},{28,12},{1,17},{... | collective-permute-start | bytes 1572872 | tf_op jit(solution)/shard_map/ppermute | solution.py:429
  79.7 40.1 %collective-permute-start.3 = (bf16[128,2048]{1,0:T(8,128)(2,1)}, bf16[128,2048]{1,0:T(8,128)(2,1)}, u32[]{:S(2)}, u32[]{:S(2)}) collective-permute-start(bf16[128,2048]{1,0:T(8,128)(2,1)} %get-tuple-element.103.refs_8_), channel_id=1, source_target_pairs={{0,16},{4,20},{8,24},{12,28},{16,0},{20,4},{24,8},{28,12},{1,17},{... | collective-permute-start | bytes 1572872 | tf_op jit(solution)/shard_map/ppermute | solution.py:429
  80.1 40.0 %collective-permute-start.12 = (bf16[128,2048]{1,0:T(8,128)(2,1)}, bf16[128,2048]{1,0:T(8,128)(2,1)S(1)}, u32[]{:S(2)}, u32[]{:S(2)}) collective-permute-start(bf16[128,2048]{1,0:T(8,128)(2,1)} %get-tuple-element.102.refs_7_), channel_id=1, source_target_pairs={{0,4},{4,0},{8,12},{12,8},{16,20},{20,16},{24,28},{28,24},{1,5},{5... | collective-permute-start | bytes 1572872 | tf_op jit(solution)/shard_map/ppermute | solution.py:429
  118.2 16.2 %collective-permute-start.18 = (bf16[192,768]{1,0:T(8,128)(2,1)S(1)}, bf16[192,768]{1,0:T(8,128)(2,1)S(1)}, u32[]{:S(2)}, u32[]{:S(2)}) collective-permute-start(bf16[192,768]{1,0:T(8,128)(2,1)S(1)} %bitcast.72), channel_id=1, source_target_pairs={{0,8},{4,12},{8,0},{12,4},{16,24},{20,28},{24,16},{28,20},{1,9},{5... | collective-permute-start | bytes 884744 | tf_op jit(solution)/shard_map/ppermute | solution.py:429
  119.8 14.8 %collective-permute-start.21 = (bf16[192,768]{1,0:T(8,128)(2,1)S(1)}, bf16[192,768]{1,0:T(8,128)(2,1)S(1)}, u32[]{:S(2)}, u32[]{:S(2)}) collective-permute-start(bf16[192,768]{1,0:T(8,128)(2,1)S(1)} %bitcast.68), channel_id=1, source_target_pairs={{0,16},{4,20},{8,24},{12,28},{16,0},{20,4},{24,8},{28,12},{1,17},{... | collective-permute-start | bytes 884744 | tf_op jit(solution)/shard_map/ppermute | solution.py:429
  120.1 15.9 %collective-permute-start.30 = (bf16[192,768]{1,0:T(8,128)(2,1)S(1)}, bf16[192,768]{1,0:T(8,128)(2,1)S(1)}, u32[]{:S(2)}, u32[]{:S(2)}) collective-permute-start(bf16[192,768]{1,0:T(8,128)(2,1)S(1)} %bitcast.73), channel_id=1, source_target_pairs={{0,4},{4,0},{8,12},{12,8},{16,20},{20,16},{24,28},{28,24},{1,5},{5... | collective-permute-start | bytes 884744 | tf_op jit(solution)/shard_map/ppermute | solution.py:429
  121.5 14.5 %collective-permute-start.31 = (bf16[192,768]{1,0:T(8,128)(2,1)S(1)}, bf16[192,768]{1,0:T(8,128)(2,1)S(1)}, u32[]{:S(2)}, u32[]{:S(2)}) collective-permute-start(bf16[192,768]{1,0:T(8,128)(2,1)S(1)} %bitcast.69), channel_id=1, source_target_pairs={{0,4},{4,0},{8,12},{12,8},{16,20},{20,16},{24,28},{28,24},{1,5},{5... | collective-permute-start | bytes 884744 | tf_op jit(solution)/shard_map/ppermute | solution.py:429
  152.7 26.6 %collective-permute-start.34 = (bf16[384,768]{1,0:T(8,128)(2,1)S(1)}, bf16[384,768]{1,0:T(8,128)(2,1)S(1)}, u32[]{:S(2)}, u32[]{:S(2)}) collective-permute-start(bf16[384,768]{1,0:T(8,128)(2,1)S(1)} %copy-done.6), channel_id=1, source_target_pairs={{0,16},{4,20},{8,24},{12,28},{16,0},{20,4},{24,8},{28,12},{1,17},{... | collective-permute-start | bytes 1769480 | tf_op jit(solution)/shard_map/ppermute | solution.py:429
  153.0 27.6 %collective-permute-start.33 = (bf16[384,768]{1,0:T(8,128)(2,1)S(1)}, bf16[384,768]{1,0:T(8,128)(2,1)S(1)}, u32[]{:S(2)}, u32[]{:S(2)}) collective-permute-start(bf16[384,768]{1,0:T(8,128)(2,1)S(1)} %copy-done.6), channel_id=1, source_target_pairs={{0,8},{4,12},{8,0},{12,4},{16,24},{20,28},{24,16},{28,20},{1,9},{5... | collective-permute-start | bytes 1769480 | tf_op jit(solution)/shard_map/ppermute | solution.py:429
  153.7 26.3 %collective-permute-start.37 = (bf16[384,768]{1,0:T(8,128)(2,1)S(1)}, bf16[384,768]{1,0:T(8,128)(2,1)}, u32[]{:S(2)}, u32[]{:S(2)}) collective-permute-start(bf16[384,768]{1,0:T(8,128)(2,1)S(1)} %copy-done.5), channel_id=1, source_target_pairs={{0,8},{4,12},{8,0},{12,4},{16,24},{20,28},{24,16},{28,20},{1,9},{5... | collective-permute-start | bytes 1769480 | tf_op jit(solution)/shard_map/ppermute | solution.py:429
  154.5 27.4 %collective-permute-start.36 = (bf16[384,768]{1,0:T(8,128)(2,1)S(1)}, bf16[384,768]{1,0:T(8,128)(2,1)S(1)}, u32[]{:S(2)}, u32[]{:S(2)}) collective-permute-start(bf16[384,768]{1,0:T(8,128)(2,1)S(1)} %copy-done.5), channel_id=1, source_target_pairs={{0,16},{4,20},{8,24},{12,28},{16,0},{20,4},{24,8},{28,12},{1,17},{... | collective-permute-start | bytes 1769480 | tf_op jit(solution)/shard_map/ppermute | solution.py:429
  155.7 48.0 %collective-permute-start.45 = (bf16[384,768]{1,0:T(8,128)(2,1)S(1)}, bf16[384,768]{1,0:T(8,128)(2,1)}, u32[]{:S(2)}, u32[]{:S(2)}) collective-permute-start(bf16[384,768]{1,0:T(8,128)(2,1)S(1)} %copy-done.6), channel_id=1, source_target_pairs={{0,4},{4,0},{8,12},{12,8},{16,20},{20,16},{24,28},{28,24},{1,5},{5... | collective-permute-start | bytes 1769480 | tf_op jit(solution)/shard_map/ppermute | solution.py:429
  179.4 24.5 %collective-permute-start.46 = (bf16[384,768]{1,0:T(8,128)(2,1)S(1)}, bf16[384,768]{1,0:T(8,128)(2,1)}, u32[]{:S(2)}, u32[]{:S(2)}) collective-permute-start(bf16[384,768]{1,0:T(8,128)(2,1)S(1)} %copy-done.5), channel_id=1, source_target_pairs={{0,4},{4,0},{8,12},{12,8},{16,20},{20,16},{24,28},{28,24},{1,5},{5... | collective-permute-start | bytes 1769480 | tf_op jit(solution)/shard_map/ppermute | solution.py:429
  180.0 24.4 %collective-permute-start.35 = (bf16[384,768]{1,0:T(8,128)(2,1)S(1)}, bf16[384,768]{1,0:T(8,128)(2,1)}, u32[]{:S(2)}, u32[]{:S(2)}) collective-permute-start(bf16[384,768]{1,0:T(8,128)(2,1)S(1)} %collective-permute-done.34.refs_5_), channel_id=1, source_target_pairs={{0,8},{4,12},{8,0},{12,4},{16,24},{20,28},{24,16},{28,20},{1,9},{5... | collective-permute-start | bytes 1769480 | tf_op jit(solution)/shard_map/ppermute | solution.py:429
  180.6 23.8 %collective-permute-start.38 = (bf16[384,768]{1,0:T(8,128)(2,1)}, bf16[384,768]{1,0:T(8,128)(2,1)}, u32[]{:S(2)}, u32[]{:S(2)}) collective-permute-start(bf16[384,768]{1,0:T(8,128)(2,1)} %collective-permute-done.37.refs_6_), channel_id=1, source_target_pairs={{0,16},{4,20},{8,24},{12,28},{16,0},{20,4},{24,8},{28,12},{1,17},{... | collective-permute-start | bytes 1769480 | tf_op jit(solution)/shard_map/ppermute | solution.py:429
  181.8 23.0 %collective-permute-start.39 = (bf16[384,768]{1,0:T(8,128)(2,1)S(1)}, bf16[384,768]{1,0:T(8,128)(2,1)}, u32[]{:S(2)}, u32[]{:S(2)}) collective-permute-start(bf16[384,768]{1,0:T(8,128)(2,1)S(1)} %collective-permute-done.33.refs_1_), channel_id=1, source_target_pairs={{0,4},{4,0},{8,12},{12,8},{16,20},{20,16},{24,28},{28,24},{1,5},{5... | collective-permute-start | bytes 1769480 | tf_op jit(solution)/shard_map/ppermute | solution.py:429
  200.0 15.4 %all-to-all-start = ((bf16[8,256,256]{2,1,0:T(8,128)(2,1)}), bf16[8,256,256]{2,1,0:T(8,128)(2,1)S(1)}, u32[]{:S(2)}, u32[]{:S(2)}) async-start(bf16[8,256,256]{2,1,0:T(8,128)(2,1)} %bitcast.61), calls=%async_computation | async-start | bytes 2097152 | tf_op jit(solution)/shard_map/all_to_all | solution.py:1221
  203.5 161.8 %all-gather.11.cloned.1.call-start = ((), (), s32[]{:S(2)}) async-start(), calls=%async_computation.5 | async-start | bytes 5242880 | tf_op jit(solution)/shard_map/all_gather | solution.py:1138
  237.4 15.7 %collective-permute-start.50 = (bf16[128,2048]{1,0:T(8,128)(2,1)}, bf16[128,2048]{1,0:T(8,128)(2,1)S(1)}, u32[]{:S(2)}, u32[]{:S(2)}) collective-permute-start(bf16[128,2048]{1,0:T(8,128)(2,1)} %get-tuple-element.115.refs_11_.refs_16_), channel_id=1, source_target_pairs={{0,8},{4,12},{8,0},{12,4},{16,24},{20,28},{24,16},{28,20},{1,9},{5... | collective-permute-start | bytes 1572872 | tf_op jit(solution)/shard_map/ppermute | solution.py:429
  239.7 51.1 %collective-permute-start.47 = (bf16[1024,2432]{1,0:T(8,128)(2,1)}, bf16[1024,2432]{1,0:T(8,128)(2,1)}, u32[]{:S(2)}, u32[]{:S(2)}) collective-permute-start(bf16[1024,2432]{1,0:T(8,128)(2,1)} %shard_map.260.refs_4_.refs_3_), channel_id=1, source_target_pairs={{0,4},{4,0},{8,12},{12,8},{16,20},{20,16},{24,28},{28,24},{1,5},{5... | collective-permute-start | bytes 14942216 | tf_op jit(solution)/shard_map/ppermute | solution.py:429
  246.5 38.1 %collective-permute-start.49 = (bf16[128,2048]{1,0:T(8,128)(2,1)S(1)}, bf16[128,2048]{1,0:T(8,128)(2,1)S(1)}, u32[]{:S(2)}, u32[]{:S(2)}) collective-permute-start(bf16[128,2048]{1,0:T(8,128)(2,1)S(1)} %collective-permute-done.48.refs_8_.refs_13_), channel_id=1, source_target_pairs={{0,8},{4,12},{8,0},{12,4},{16,24},{20,28},{24,16},{28,20},{1,9},{5... | collective-permute-start | bytes 1572872 | tf_op jit(solution)/shard_map/ppermute | solution.py:429
  253.1 31.4 %collective-permute-start.51 = (bf16[128,2048]{1,0:T(8,128)(2,1)S(1)}, bf16[128,2048]{1,0:T(8,128)(2,1)S(1)}, u32[]{:S(2)}, u32[]{:S(2)}) collective-permute-start(bf16[128,2048]{1,0:T(8,128)(2,1)S(1)} %collective-permute-done.50.refs_9_.refs_14_), channel_id=1, source_target_pairs={{0,16},{4,20},{8,24},{12,28},{16,0},{20,4},{24,8},{28,12},{1,17},{... | collective-permute-start | bytes 1572872 | tf_op jit(solution)/shard_map/ppermute | solution.py:429
  286.9 34.7 %collective-permute-start.55 = (bf16[128,2048]{1,0:T(8,128)(2,1)}, bf16[128,2048]{1,0:T(8,128)(2,1)S(1)}, u32[]{:S(2)}, u32[]{:S(2)}) collective-permute-start(bf16[128,2048]{1,0:T(8,128)(2,1)} %get-tuple-element.219.refs_14_.refs_23_), channel_id=1, source_target_pairs={{0,8},{4,12},{8,0},{12,4},{16,24},{20,28},{24,16},{28,20},{1,9},{5... | collective-permute-start | bytes 1572872 | tf_op jit(solution)/shard_map/ppermute | solution.py:429
  288.1 33.5 %collective-permute-start.56 = (bf16[128,2048]{1,0:T(8,128)(2,1)}, bf16[128,2048]{1,0:T(8,128)(2,1)S(1)}, u32[]{:S(2)}, u32[]{:S(2)}) collective-permute-start(bf16[128,2048]{1,0:T(8,128)(2,1)} %get-tuple-element.218.refs_15_.refs_24_), channel_id=1, source_target_pairs={{0,16},{4,20},{8,24},{12,28},{16,0},{20,4},{24,8},{28,12},{1,17},{... | collective-permute-start | bytes 1572872 | tf_op jit(solution)/shard_map/ppermute | solution.py:429
  290.5 31.1 %collective-permute-start.53 = (bf16[128,2048]{1,0:T(8,128)(2,1)S(1)}, bf16[128,2048]{1,0:T(8,128)(2,1)S(1)}, u32[]{:S(2)}, u32[]{:S(2)}) collective-permute-start(bf16[128,2048]{1,0:T(8,128)(2,1)S(1)} %copy-done.42), channel_id=1, source_target_pairs={{0,8},{4,12},{8,0},{12,4},{16,24},{20,28},{24,16},{28,20},{1,9},{5... | collective-permute-start | bytes 1572872 | tf_op jit(solution)/shard_map/ppermute | solution.py:429
  290.8 30.8 %collective-permute-start.54 = (bf16[128,2048]{1,0:T(8,128)(2,1)S(1)}, bf16[128,2048]{1,0:T(8,128)(2,1)S(1)}, u32[]{:S(2)}, u32[]{:S(2)}) collective-permute-start(bf16[128,2048]{1,0:T(8,128)(2,1)S(1)} %copy-done.43), channel_id=1, source_target_pairs={{0,16},{4,20},{8,24},{12,28},{16,0},{20,4},{24,8},{28,12},{1,17},{... | collective-permute-start | bytes 1572872 | tf_op jit(solution)/shard_map/ppermute | solution.py:429
  400.5 29.1 %collective-permute-start.58 = (bf16[256,2304]{1,0:T(8,128)(2,1)}, bf16[256,2304]{1,0:T(8,128)(2,1)S(1)}, u32[]{:S(2)}, u32[]{:S(2)}) collective-permute-start(bf16[256,2304]{1,0:T(8,128)(2,1)} %get-tuple-element.122), channel_id=1, source_target_pairs={{0,8},{4,12},{8,0},{12,4},{16,24},{20,28},{24,16},{28,20},{1,9},{5... | collective-permute-start | bytes 3538952 | tf_op jit(solution)/shard_map/ppermute | solution.py:429
  401.8 27.8 %collective-permute-start.59 = (bf16[256,2304]{1,0:T(8,128)(2,1)}, bf16[256,2304]{1,0:T(8,128)(2,1)S(1)}, u32[]{:S(2)}, u32[]{:S(2)}) collective-permute-start(bf16[256,2304]{1,0:T(8,128)(2,1)} %get-tuple-element.123), channel_id=1, source_target_pairs={{0,16},{4,20},{8,24},{12,28},{16,0},{20,4},{24,8},{28,12},{1,17},{... | collective-permute-start | bytes 3538952 | tf_op jit(solution)/shard_map/ppermute | solution.py:429
  432.3 21.8 %collective-permute-start.60 = (bf16[128,2304]{1,0:T(8,128)(2,1)S(1)}, bf16[128,2304]{1,0:T(8,128)(2,1)S(1)}, u32[]{:S(2)}, u32[]{:S(2)}) collective-permute-start(bf16[128,2304]{1,0:T(8,128)(2,1)S(1)} %get-tuple-element.211), channel_id=1, source_target_pairs={{0,16},{4,20},{8,24},{12,28},{16,0},{20,4},{24,8},{28,12},{1,17},{... | collective-permute-start | bytes 1769480 | tf_op jit(solution)/shard_map/ppermute | solution.py:429
  432.6 21.4 %collective-permute-start.61 = (bf16[128,2304]{1,0:T(8,128)(2,1)S(1)}, bf16[128,2304]{1,0:T(8,128)(2,1)S(1)}, u32[]{:S(2)}, u32[]{:S(2)}) collective-permute-start(bf16[128,2304]{1,0:T(8,128)(2,1)S(1)} %get-tuple-element.210), channel_id=1, source_target_pairs={{0,8},{4,12},{8,0},{12,4},{16,24},{20,28},{24,16},{28,20},{1,9},{5... | collective-permute-start | bytes 1769480 | tf_op jit(solution)/shard_map/ppermute | solution.py:429
  444.8 43.0 %collective-permute-start.62 = (bf16[256,2176]{1,0:T(8,128)(2,1)}, bf16[256,2176]{1,0:T(8,128)(2,1)S(1)}, u32[]{:S(2)}, u32[]{:S(2)}) collective-permute-start(bf16[256,2176]{1,0:T(8,128)(2,1)} %get-tuple-element.128.refs_13_), channel_id=1, source_target_pairs={{0,8},{4,12},{8,0},{12,4},{16,24},{20,28},{24,16},{28,20},{1,9},{5... | collective-permute-start | bytes 3342344 | tf_op jit(solution)/shard_map/ppermute | solution.py:429
  445.8 42.0 %collective-permute-start.63 = (bf16[256,2176]{1,0:T(8,128)(2,1)}, bf16[256,2176]{1,0:T(8,128)(2,1)S(1)}, u32[]{:S(2)}, u32[]{:S(2)}) collective-permute-start(bf16[256,2176]{1,0:T(8,128)(2,1)} %get-tuple-element.143), channel_id=1, source_target_pairs={{0,16},{4,20},{8,24},{12,28},{16,0},{20,4},{24,8},{28,12},{1,17},{... | collective-permute-start | bytes 3342344 | tf_op jit(solution)/shard_map/ppermute | solution.py:429
  447.0 84.2 %collective-permute-start.67 = (bf16[2048,768]{1,0:T(8,128)(2,1)}, bf16[2048,768]{1,0:T(8,128)(2,1)}, u32[]{:S(2)}, u32[]{:S(2)}) collective-permute-start(bf16[2048,768]{1,0:T(8,128)(2,1)} %get-tuple-element.146.refs_3_), channel_id=1, source_target_pairs={{0,4},{4,0},{8,12},{12,8},{16,20},{20,16},{24,28},{28,24},{1,5},{5... | collective-permute-start | bytes 9437192 | tf_op jit(solution)/shard_map/ppermute | solution.py:429
  471.6 19.8 %all-to-all-start.1 = ((bf16[256,8,256]{2,0,1:T(8,128)(2,1)}), bf16[256,8,256]{2,0,1:T(8,128)(2,1)S(1)}, u32[]{:S(2)}, u32[]{:S(2)}) async-start(bf16[256,8,256]{2,0,1:T(8,128)(2,1)} %bitcast.48), calls=%async_computation.1 | async-start | bytes 2097152 | tf_op jit(solution)/shard_map/all_to_all | solution.py:1326
  517.7 22.7 %collective-permute-start.64 = (bf16[128,2176]{1,0:T(8,128)(2,1)S(1)}, bf16[128,2176]{1,0:T(8,128)(2,1)S(1)}, u32[]{:S(2)}, u32[]{:S(2)}) collective-permute-start(bf16[128,2176]{1,0:T(8,128)(2,1)S(1)} %copy-done.39), channel_id=1, source_target_pairs={{0,16},{4,20},{8,24},{12,28},{16,0},{20,4},{24,8},{28,12},{1,17},{... | collective-permute-start | bytes 1671176 | tf_op jit(solution)/shard_map/ppermute | solution.py:429
  519.4 22.2 %collective-permute-start.65 = (bf16[128,2176]{1,0:T(8,128)(2,1)S(1)}, bf16[128,2176]{1,0:T(8,128)(2,1)}, u32[]{:S(2)}, u32[]{:S(2)}) collective-permute-start(bf16[128,2176]{1,0:T(8,128)(2,1)S(1)} %copy-done.38), channel_id=1, source_target_pairs={{0,8},{4,12},{8,0},{12,4},{16,24},{20,28},{24,16},{28,20},{1,9},{5... | collective-permute-start | bytes 1671176 | tf_op jit(solution)/shard_map/ppermute | solution.py:429
  525.2 35.0 %collective-permute-start.105 = (bf16[4,768,128]{2,1,0:T(8,128)(2,1)}, bf16[4,768,128]{2,1,0:T(8,128)(2,1)}, u32[]{:S(2)}, u32[]{:S(2)}) collective-permute-start(bf16[4,768,128]{2,1,0:T(8,128)(2,1)} %get-tuple-element.137.refs_14_), channel_id=1, source_target_pairs={{0,4},{4,0},{8,12},{12,8},{16,20},{20,16},{24,28},{28,24},{1,5},{5... | collective-permute-start | bytes 2359304 | tf_op jit(solution)/shard_map/ppermute | solution.py:429
  525.6 35.6 %collective-permute-start.75 = (bf16[256,256]{1,0:T(8,128)(2,1)}, bf16[256,256]{1,0:T(8,128)(2,1)}, u32[]{:S(2)}, u32[]{:S(2)}) collective-permute-start(bf16[256,256]{1,0:T(8,128)(2,1)} %get-tuple-element.162.refs_26_), channel_id=1, source_target_pairs={{0,8},{4,12},{8,0},{12,4},{16,24},{20,28},{24,16},{28,20},{1,9},{5... | collective-permute-start | bytes 393224 | tf_op jit(solution)/shard_map/ppermute | solution.py:429
  531.2 30.5 %collective-permute-start.76 = (bf16[256,256]{1,0:T(8,128)(2,1)}, bf16[256,256]{1,0:T(8,128)(2,1)}, u32[]{:S(2)}, u32[]{:S(2)}) collective-permute-start(bf16[256,256]{1,0:T(8,128)(2,1)} %get-tuple-element.162.refs_26_), channel_id=1, source_target_pairs={{0,16},{4,20},{8,24},{12,28},{16,0},{20,4},{24,8},{28,12},{1,17},{... | collective-permute-start | bytes 393224 | tf_op jit(solution)/shard_map/ppermute | solution.py:429
  541.2 24.5 %collective-permute-start.68 = (bf16[256,2048]{1,0:T(8,128)(2,1)}, bf16[256,2048]{1,0:T(8,128)(2,1)S(1)}, u32[]{:S(2)}, u32[]{:S(2)}) collective-permute-start(bf16[256,2048]{1,0:T(8,128)(2,1)} %get-tuple-element.148.refs_5_), channel_id=1, source_target_pairs={{0,8},{4,12},{8,0},{12,4},{16,24},{20,28},{24,16},{28,20},{1,9},{5... | collective-permute-start | bytes 3145736 | tf_op jit(solution)/shard_map/ppermute | solution.py:429
  541.6 25.3 %collective-permute-start.69 = (bf16[256,2048]{1,0:T(8,128)(2,1)}, bf16[256,2048]{1,0:T(8,128)(2,1)S(1)}, u32[]{:S(2)}, u32[]{:S(2)}) collective-permute-start(bf16[256,2048]{1,0:T(8,128)(2,1)} %get-tuple-element.150), channel_id=1, source_target_pairs={{0,16},{4,20},{8,24},{12,28},{16,0},{20,4},{24,8},{28,12},{1,17},{... | collective-permute-start | bytes 3145736 | tf_op jit(solution)/shard_map/ppermute | solution.py:429
  561.6 14.1 %collective-permute-start.72 = (bf16[256,384]{1,0:T(8,128)(2,1)}, bf16[256,384]{1,0:T(8,128)(2,1)}, u32[]{:S(2)}, u32[]{:S(2)}) collective-permute-start(bf16[256,384]{1,0:T(8,128)(2,1)} %get-tuple-element.147.refs_5_), channel_id=1, source_target_pairs={{0,8},{4,12},{8,0},{12,4},{16,24},{20,28},{24,16},{28,20},{1,9},{5... | collective-permute-start | bytes 589832 | tf_op jit(solution)/shard_map/ppermute | solution.py:429
  582.3 22.5 %collective-permute-start.78 = (bf16[256,384]{1,0:T(8,128)(2,1)S(1)}, bf16[256,384]{1,0:T(8,128)(2,1)S(1)}, u32[]{:S(2)}, u32[]{:S(2)}) collective-permute-start(bf16[256,384]{1,0:T(8,128)(2,1)S(1)} %multiply_convert_fusion.refs_8_.refs_30_), channel_id=1, source_target_pairs={{0,8},{4,12},{8,0},{12,4},{16,24},{20,28},{24,16},{28,20},{1,9},{5... | collective-permute-start | bytes 589832 | tf_op jit(solution)/shard_map/ppermute | solution.py:429
  583.8 21.0 %collective-permute-start.79 = (bf16[256,384]{1,0:T(8,128)(2,1)S(1)}, bf16[256,384]{1,0:T(8,128)(2,1)S(1)}, u32[]{:S(2)}, u32[]{:S(2)}) collective-permute-start(bf16[256,384]{1,0:T(8,128)(2,1)S(1)} %multiply_convert_fusion.refs_8_.refs_30_), channel_id=1, source_target_pairs={{0,16},{4,20},{8,24},{12,28},{16,0},{20,4},{24,8},{28,12},{1,17},{... | collective-permute-start | bytes 589832 | tf_op jit(solution)/shard_map/ppermute | solution.py:429
  585.2 19.6 %collective-permute-start.80 = (bf16[256,384]{1,0:T(8,128)(2,1)S(1)}, bf16[256,384]{1,0:T(8,128)(2,1)S(1)}, u32[]{:S(2)}, u32[]{:S(2)}) collective-permute-start(bf16[256,384]{1,0:T(8,128)(2,1)S(1)} %multiply_convert_fusion.refs_8_.refs_30_), channel_id=1, source_target_pairs={{0,24},{4,28},{8,16},{12,20},{16,8},{20,12},{24,0},{28,4},{1,25},{... | collective-permute-start | bytes 589832 | tf_op jit(solution)/shard_map/ppermute | solution.py:429
  602.1 23.0 %collective-permute-start.106 = (bf16[768,128]{1,0:T(8,128)(2,1)}, bf16[768,128]{1,0:T(8,128)(2,1)S(1)}, u32[]{:S(2)}, u32[]{:S(2)}) collective-permute-start(bf16[768,128]{1,0:T(8,128)(2,1)} %get-tuple-element.185), channel_id=1, source_target_pairs={{0,1},{1,2},{2,3},{4,5},{5,6},{6,7},{8,9},{9,10},{10,11},{12,13},{... | collective-permute-start | bytes 589832 | tf_op jit(solution)/shard_map/ppermute | solution.py:1347
  603.4 22.1 %collective-permute-start.107 = (bf16[768,128]{1,0:T(8,128)(2,1)}, bf16[768,128]{1,0:T(8,128)(2,1)S(1)}, u32[]{:S(2)}, u32[]{:S(2)}) collective-permute-start(bf16[768,128]{1,0:T(8,128)(2,1)} %get-tuple-element.186), channel_id=1, source_target_pairs={{1,0},{2,1},{3,2},{5,4},{6,5},{7,6},{9,8},{10,9},{11,10},{13,12},{... | collective-permute-start | bytes 589832 | tf_op jit(solution)/shard_map/ppermute | solution.py:1347
  615.4 42.2 %collective-permute-start.91 = (bf16[4,704,128]{2,1,0:T(8,128)(2,1)}, bf16[4,704,128]{2,1,0:T(8,128)(2,1)S(1)}, u32[]{:S(2)}, u32[]{:S(2)}) collective-permute-start(bf16[4,704,128]{2,1,0:T(8,128)(2,1)} %get-tuple-element.170), channel_id=1, source_target_pairs={{0,4},{4,0},{8,12},{12,8},{16,20},{20,16},{24,28},{28,24},{1,5},{5... | collective-permute-start | bytes 2162696 | tf_op jit(solution)/shard_map/ppermute | solution.py:429
  623.8 14.1 %collective-permute-start.109 = (bf16[768,128]{1,0:T(8,128)(2,1)S(1)}, bf16[768,128]{1,0:T(8,128)(2,1)}, u32[]{:S(2)}, u32[]{:S(2)}) collective-permute-start(bf16[768,128]{1,0:T(8,128)(2,1)S(1)} %copy-done.93), channel_id=1, source_target_pairs={{2,0},{3,1},{6,4},{7,5},{10,8},{11,9},{14,12},{15,13},{18,16},{19,... | collective-permute-start | bytes 589832 | tf_op jit(solution)/shard_map/ppermute | solution.py:1347
  625.1 25.1 %collective-permute-start.70 = (bf16[128,2048]{1,0:T(8,128)(2,1)S(1)}, bf16[128,2048]{1,0:T(8,128)(2,1)}, u32[]{:S(2)}, u32[]{:S(2)}) collective-permute-start(bf16[128,2048]{1,0:T(8,128)(2,1)S(1)} %copy-done.2), channel_id=1, source_target_pairs={{0,16},{4,20},{8,24},{12,28},{16,0},{20,4},{24,8},{28,12},{1,17},{... | collective-permute-start | bytes 1572872 | tf_op jit(solution)/shard_map/ppermute | solution.py:429
  625.5 24.8 %collective-permute-start.71 = (bf16[128,2048]{1,0:T(8,128)(2,1)S(1)}, bf16[128,2048]{1,0:T(8,128)(2,1)}, u32[]{:S(2)}, u32[]{:S(2)}) collective-permute-start(bf16[128,2048]{1,0:T(8,128)(2,1)S(1)} %copy-done.1), channel_id=1, source_target_pairs={{0,8},{4,12},{8,0},{12,4},{16,24},{20,28},{24,16},{28,20},{1,9},{5... | collective-permute-start | bytes 1572872 | tf_op jit(solution)/shard_map/ppermute | solution.py:429
  648.8 18.6 %collective-permute-start.112 = (bf16[768,128]{1,0:T(8,128)(2,1)S(1)}, bf16[768,128]{1,0:T(8,128)(2,1)}, u32[]{:S(2)}, u32[]{:S(2)}) collective-permute-start(bf16[768,128]{1,0:T(8,128)(2,1)S(1)} %add_convert_fusion.6.refs_1_), channel_id=1, source_target_pairs={{0,8},{4,12},{8,0},{12,4},{16,24},{20,28},{24,16},{28,20},{1,9},{5... | collective-permute-start | bytes 589832 | tf_op jit(solution)/shard_map/ppermute | solution.py:429
  650.0 18.7 %collective-permute-start.113 = (bf16[768,128]{1,0:T(8,128)(2,1)S(1)}, bf16[768,128]{1,0:T(8,128)(2,1)}, u32[]{:S(2)}, u32[]{:S(2)}) collective-permute-start(bf16[768,128]{1,0:T(8,128)(2,1)S(1)} %add_convert_fusion.6.refs_1_), channel_id=1, source_target_pairs={{0,16},{4,20},{8,24},{12,28},{16,0},{20,4},{24,8},{28,12},{1,17},{... | collective-permute-start | bytes 589832 | tf_op jit(solution)/shard_map/ppermute | solution.py:429
  667.4 14.3 %collective-permute-start.95 = (bf16[704,128]{1,0:T(8,128)(2,1)}, bf16[704,128]{1,0:T(8,128)(2,1)S(1)}, u32[]{:S(2)}, u32[]{:S(2)}) collective-permute-start(bf16[704,128]{1,0:T(8,128)(2,1)} %get-tuple-element.175), channel_id=1, source_target_pairs={{2,0},{3,1},{6,4},{7,5},{10,8},{11,9},{14,12},{15,13},{18,16},{19,... | collective-permute-start | bytes 540680 | tf_op jit(solution)/shard_map/ppermute | solution.py:1347
  (158 other events, 1683.1 us)
Sparse Core Ops, SparseCore 0:
  12.0 98.1 all-gather.4
  111.7 92.1 all-gather.6
  205.4 79.0 all-gather.8
  286.0 79.2 all-gather.10

commit v3 on v2

--- a/solution.py
+++ b/solution.py
@@ -419,10 +419,10 @@
 PLANE = 8
 CHIPS = 4
 LANES = 128
-CHUNKS = 2
+CHUNKS = ((0, 1), (2, 3))
 HALVES = ((1, 0), (3, 0), (2, 1), (3, 1), (2, 0), (1, 1), (0, 0), (0, 1))
 ANY = pl.BlockSpec(memory_space=pl.ANY)
-ROOMY = 56 * 2**20
+ROOMY = 60 * 2**20
 
 
 def swap(value, bits):
@@ -573,8 +573,9 @@
     return 32 + ((k - 4) // 4) * 16, ((k - 4) % 4) * LANES
 
 
-def cut_rest_kernel(sizes, scalars, w_gu, w_down, a_down, b_gu, down, gu_0, gu_1, sems):
+def cut_rest_kernel(sizes, scalars, w_gu, w_down, a_down, b_gu, down, *refs):
     ff, ff_z, ff_dev, width = sizes
+    parts, sems = refs[:-1], refs[-1]
     seat = scalars[0] * 2 + scalars[1]
     rows = pl.ds(pl.multiple_of(seat * ff_dev, ff_dev), ff_dev)
     wide = width + LANES
@@ -583,11 +584,11 @@
         (a_down.at[rows], down.at[:, width:wide]),
         (b_gu.at[:, rows], down.at[:, wide : wide + ff_dev]),
     ]
-    for chunk, gu in enumerate((gu_0, gu_1)):
+    for zs, gu in zip(CHUNKS, parts):
         for half in range(2):
-            for i in range(2):
-                column = pl.multiple_of(half * ff + (2 * chunk + i) * ff_z + seat * ff_dev, ff_dev)
-                k = half * 2 + i
+            for i, z in enumerate(zs):
+                column = pl.multiple_of(half * ff + z * ff_z + seat * ff_dev, ff_dev)
+                k = half * len(zs) + i
                 pairs.append(
                     (w_gu.at[:, pl.ds(column, ff_dev)], gu.at[:, k * ff_dev : (k + 1) * ff_dev])
                 )
@@ -774,74 +775,98 @@
     second_half[...] = norm[rows // 2 :].astype(BF)
 
 
-def ff_kernel(begin, chunk, scalars, *refs):
-    select, a_gu, b_down, down_own, down_oth, gu_own, gu_oth = refs[:7]
-    norm, cot = refs[7:11], refs[11:15]
-    count = 15 if begin else 16
-    outs = refs[count : count + (1 if begin else 2)]
+def ff_kernel(begin, last, sides, first_z, scalars, *refs):
+    if begin:
+        select, a_gu, b_down = refs[:3]
+        count = 3
+    else:
+        z_gu_in, dz_down_in = refs[:2]
+        count = 2
+    weights = [refs[count + 2 * k : count + 2 * k + 2] for k in range(sides)]
+    count += 2 * sides
+    norm, cot = refs[count : count + 4], refs[count + 4 : count + 8]
+    count += 8
+    if not begin:
+        sums_in = refs[count]
+        count += 1
+    outs = refs[count : count + (2 if last else 1)]
     count += len(outs)
-    hidden_out, ups, downs = refs[count : count + 3]
-    rows_in, cot_in, gu_a, gu_b, down_a, down_b, sums, sems = refs[count + 3 :]
+    results = [refs[count + 2 * k : count + 2 * k + 2] for k in range(sides)]
+    count += 2 * sides
+    if begin:
+        z_gu_out, dz_down_out = refs[count : count + 2]
+        count += 2
+    rows_in, cot_in, sums, sems = refs[count : count + 4]
+    held = [refs[count + 4 + 2 * k : count + 6 + 2 * k] for k in range(sides)]
     rows, width = rows_in.shape
     wide = width + LANES
-    part = pl.ds(chunk * down_a.shape[0], down_a.shape[0])
+    own_ff = weights[0][1].shape[0] // 4
+    many = held[0][1].shape[0] // own_ff
+    part = pl.ds(first_z * own_ff, many * own_ff)
     low = rows // 4
     pairs = [(norm[k], rows_in.at[pl.ds(k * low, low)]) for k in range(4)]
-    pairs += [(gu_own, gu_a)]
+    pairs.append((weights[0][0], held[0][0]))
     pairs += [(cot[k], cot_in.at[pl.ds(k * low, low)]) for k in range(4)]
-    pairs += [(down_own.at[part], down_a), (gu_oth, gu_b), (down_oth.at[part], down_b)]
+    pairs.append((weights[0][1].at[part], held[0][1]))
+    if sides == 2:
+        pairs += [(weights[1][0], held[1][0]), (weights[1][1].at[part], held[1][1])]
     if not begin:
-        pairs.append((refs[15], sums))
+        pairs.append((sums_in, sums))
     loads = [pltpu.make_async_copy(x, y, sems.at[k]) for k, (x, y) in enumerate(pairs)]
     for load in loads:
         load.start()
-    mask = select[...]
     for load in loads[:4]:
         load.wait()
-    z_gu = dot(rows_in[...], a_gu[...]).astype(BF) * jnp.concatenate([mask, mask], axis=1)
+    if begin:
+        mask = select[...]
+        z_gu = dot(rows_in[...], a_gu[...]).astype(BF) * jnp.concatenate([mask, mask], axis=1)
+        z_gu_out[...] = z_gu
+    else:
+        z_gu, dz_down = z_gu_in[...], dz_down_in[...]
     z_gate, z_up = z_gu[:, :LANES], z_gu[:, LANES:]
     norm_grad = 0.0
     latent_grad = 0.0
-    for side, (gu, down) in enumerate(((gu_a, down_a), (gu_b, down_b))):
+    for side, (gu, down) in enumerate(held):
         size = gu.shape[1] // 2
-        own_ff = size // 2
         loads[4 if side == 0 else 10].wait()
         both = dot(rows_in[...], gu[...])
         if side == 0:
             for load in loads[5:9]:
                 load.wait()
-            dz_down = (inner(cot_in[...], b_down[...], 1, 1) * mask.astype(F32)).astype(BF)
+            if begin:
+                dz_down = (inner(cot_in[...], b_down[...], 1, 1) * mask.astype(F32)).astype(BF)
+                dz_down_out[...] = dz_down
         loads[9 if side == 0 else 11].wait()
         up_gate = jnp.concatenate(
-            [down[i * own_ff : i * own_ff + LANES, wide:] for i in range(2)], axis=1
+            [down[i * own_ff : i * own_ff + LANES, wide:] for i in range(many)], axis=1
         )
         up_up = jnp.concatenate(
-            [down[i * own_ff + LANES : i * own_ff + 2 * LANES, wide:] for i in range(2)], axis=1
+            [down[i * own_ff + LANES : i * own_ff + 2 * LANES, wide:] for i in range(many)], axis=1
         )
         gate = both[:, :size] + dot(z_gate, up_gate)
         upper = both[:, size:] + dot(z_up, up_up)
         sigma = 1.0 / (1.0 + jnp.exp(-gate))
         active = gate * sigma
-        hidden = (active * upper).astype(BF)
-        hidden_out[:, side * size : (side + 1) * size] = hidden
+        results[side][0][...] = (active * upper).astype(BF)
         hidden_grad = inner(cot_in[...], down[:, :width], 1, 1) + inner(
             dz_down, down[:, width:wide], 1, 1
         )
-        gate_grad = (hidden_grad * upper * sigma * (1.0 + gate * (1.0 - sigma))).astype(BF)
-        upper_grad = (hidden_grad * active).astype(BF)
-        norm_grad += inner(jnp.concatenate([gate_grad, upper_grad], axis=1), gu[...], 1, 1)
+        grads = results[side][1]
+        grads[:, :size] = (hidden_grad * upper * sigma * (1.0 + gate * (1.0 - sigma))).astype(BF)
+        grads[:, size:] = (hidden_grad * active).astype(BF)
+        norm_grad += inner(grads[...], gu[...], 1, 1)
         latent_grad += jnp.concatenate(
-            [inner(gate_grad, up_gate, 1, 1), inner(upper_grad, up_up, 1, 1)], axis=1
-        )
-        ups[side] = jnp.concatenate(
-            [inner(z_gate, gate_grad, 0, 0), inner(z_up, upper_grad, 0, 0)], axis=0
-        )
-        downs[side] = inner(hidden, dz_down, 0, 0)
+            [inner(grads[:, :size], up_gate, 1, 1), inner(grads[:, size:], up_up, 1, 1)], axis=1
+        )
     if begin:
         outs[0][:, :width] = norm_grad
         outs[0][:, width:] = latent_grad
         return
-    loads[12].wait()
+    loads[-1].wait()
+    if not last:
+        outs[0][:, :width] = norm_grad + sums[:, :width]
+        outs[0][:, width:] = latent_grad + sums[:, width:]
+        return
     low = rows // 2
     for k in range(2):
         at = slice(k * low, (k + 1) * low)
@@ -850,22 +875,19 @@
         outs[k][:, width:] = (latent_grad[at] + sums[at, width:]).astype(kind)
 
 
-def down_kernel(scalars, hidden_0, hidden_1, down_own, down_oth, out_0, out_1):
-    wide = out_0.shape[1]
-    size = hidden_0.shape[1] // 2
-    total = 0.0
-    for chunk, hidden in enumerate((hidden_0, hidden_1)):
-        part = slice(chunk * size, (chunk + 1) * size)
-        total += dot(hidden[:, :size], down_own[part, :wide]) + dot(hidden[:, size:], down_oth[part, :wide])
-    for k, out in enumerate((out_0, out_1)):
-
-        @pl.when(pl.program_id(0) == k)
-        def _():
-            out[...] = total.astype(out.dtype)
+def down_kernel(begin, scalars, hidden_own, hidden_oth, down_own, down_oth, *refs):
+    outs = refs if begin else refs[1:]
+    wide = outs[0].shape[1]
+    total = dot(hidden_own[...], down_own[:, :wide]) + dot(hidden_oth[...], down_oth[:, :wide])
+    if not begin:
+        total += refs[0][...]
+    rows = outs[0].shape[0]
+    for k, out in enumerate(outs):
+        out[...] = total[k * rows : (k + 1) * rows].astype(out.dtype)
 
 
 def spread_kernel(places, scalars, *refs):
-    pieces, outs = refs[:8], refs[8:]
+    pieces, outs = [*refs[:4], *(refs[4].at[k] for k in range(4))], refs[5:]
     for k, piece in enumerate(pieces):
         chip = scalars[0] ^ (k % 4)
         core = scalars[1] if k < 4 else 1 - scalars[1]
@@ -890,27 +912,34 @@
 
 
 def ff_grads_kernel(scalars, *refs):
-    ups, downs, keep, send = refs[:4], refs[4:8], refs[8], refs[9]
-    for side, out in enumerate((keep, send)):
-        for chunk in range(CHUNKS):
-            up = ups[2 * chunk][side] + ups[2 * chunk + 1][side]
-            down = downs[2 * chunk][side] + downs[2 * chunk + 1][side]
-            rows = up.shape[0]
-            size = up.shape[1] // 2
-            for i in range(2):
-                z = 2 * chunk + i
-                count = size // LANES
-                for k in range(count):
-                    at = i * size + k * LANES
-                    out[z, k * rows : (k + 1) * rows, :] = up[:, at : at + LANES].astype(out.dtype)
-                at = count * rows
-                out[z, at : at + size, :] = down[i * size : (i + 1) * size].astype(out.dtype)
+    z_gu, dz_down, results, keep, send = refs[:2], refs[2:4], refs[4:-2], refs[-2], refs[-1]
+    at = 0
+    for zs in CHUNKS:
+        for out in (keep, send):
+            gate, upper, down = 0.0, 0.0, 0.0
+            for half in range(2):
+                hidden, grads = results[at], results[at + 1]
+                at += 2
+                size = hidden.shape[1]
+                gate += inner(z_gu[half][:, :LANES], grads[:, :size], 0, 0)
+                upper += inner(z_gu[half][:, LANES:], grads[:, size:], 0, 0)
+                down += inner(hidden[...], dz_down[half][...], 0, 0)
+            own_ff = size // len(zs)
+            rows = 2 * LANES
+            blocks = own_ff // LANES
+            for i, z in enumerate(zs):
+                for k in range(blocks):
+                    columns = slice(i * own_ff + k * LANES, i * own_ff + (k + 1) * LANES)
+                    out[z, k * rows : k * rows + LANES, :] = gate[:, columns].astype(out.dtype)
+                    out[z, k * rows + LANES : (k + 1) * rows, :] = upper[:, columns].astype(out.dtype)
+                there = slice(blocks * rows, blocks * rows + own_ff)
+                out[z, there, :] = down[i * own_ff : (i + 1) * own_ff].astype(out.dtype)
 
 
 def other_grads_kernel(quarter, scalars, *refs):
-    norm1, norm2, cot, mixed = refs[:8], refs[8:16], refs[16:24], refs[24]
-    dz_gu, dz_qkv, z_down, dz_out, up_out = (refs[25 + 4 * k : 29 + 4 * k] for k in range(5))
-    up_qkv, keep, send, columns, all_gu, all_qkv, all_down, sems = refs[45:]
+    norm1, norm2, cot, mixed = refs[:8], refs[8:16], refs[16:24], refs[24:26]
+    middle, last = refs[26:30], refs[30:34]
+    up_qkv, keep, send, columns, all_gu, all_qkv, all_down, sems = refs[34:]
     half = norm1[0].shape[0]
     chip, core = scalars[0], scalars[1]
     pairs = []
@@ -923,9 +952,12 @@
     loads = [pltpu.make_async_copy(x, y, sems.at[k]) for k, (x, y) in enumerate(pairs)]
     for load in loads:
         load.start()
-    for pieces, whole in ((dz_gu, all_gu), (dz_qkv, all_qkv), (z_down, all_down)):
-        for k, (rel, h) in enumerate(HALVES):
-            whole[k * half : (k + 1) * half, :] = pieces[rel][h * half : (h + 1) * half, :]
+    gu_wide, qkv_wide = all_gu.shape[1], all_qkv.shape[1]
+    for k, (rel, h) in enumerate(HALVES):
+        here, there = slice(h * half, (h + 1) * half), slice(k * half, (k + 1) * half)
+        all_gu[there, :] = middle[rel][here, :gu_wide]
+        all_qkv[there, :] = last[rel][here, :qkv_wide]
+        all_down[there, :] = last[rel][here, qkv_wide:]
 
     def halves(z, at, value):
         rows = value.shape[0] // 2
@@ -955,23 +987,26 @@
 
     low = LANES // 2
     at = 3 * low
-    total = 0.0
-    rows = dz_out[0].shape[1]
-    for rel in range(4):
-        for k in range(2):
-            seat = (chip ^ rel) * 2 + (core if k == 0 else 1 - core)
-            here = pl.ds(pl.multiple_of(seat * rows, rows), rows)
-            total += inner(mixed[here, :], dz_out[rel][k], 0, 0)
-    two_of_four(at, [total[:LANES], total[LANES:]])
+    rows = 2 * half
+    for k, source in enumerate(mixed):
+        total = 0.0
+        for rel in range(4):
+            here = pl.ds(pl.multiple_of(((chip ^ rel) * 2 + core) * rows, rows), rows)
+            total += inner(source[here, :], middle[rel][:, gu_wide : gu_wide + LANES], 0, 0)
+        first = 2 * (core if k == 0 else 1 - core)
+        for i in range(2):
+            halves(first + i, at, total[i * LANES : (i + 1) * LANES])
     at += low
-    value = up_out[0][...]
-    for piece in up_out[1:]:
-        value = value + piece[...].astype(F32)
-    share = value.shape[0] // 2
+    share = LANES // PLANE
     for z in range(4):
         for k in range(4):
-            block = value[:, (z * 4 + k) * LANES : (z * 4 + k + 1) * LANES]
-            halves(z, at + k * share, block)
+            block = (z * 4 + k) // 2
+            column = gu_wide + LANES + ((z * 4 + k) % 2) * LANES
+            value = 0.0
+            for rel in range(4):
+                piece = middle[rel][block * 2 * share : (block + 1) * 2 * share, column : column + LANES]
+                value = value + piece.astype(F32)
+            halves(z, at + k * share, value)
     at += low
     at_b = at + 3 * low
     heads = [jnp.concatenate([up_qkv[part, :, i * LANES : (i + 1) * LANES] for part in range(3)], axis=0) for i in range(2)]
@@ -993,13 +1028,12 @@
             halves(z, at + k * low, block)
 
 
-def along_line_kernel(scalars, keep, brought, mine, *outs):
+def along_line_kernel(scalars, keep, brought, mine, onward, sent):
     z = scalars[2]
     mine[...] = keep[z] + brought[z].astype(F32)
-    for k, out in enumerate(outs):
-        hop = k // 2 + 1
-        to = jnp.minimum(z + hop, 3) if k % 2 == 0 else jnp.maximum(z - hop, 0)
-        out[...] = (keep[to] + brought[to].astype(F32)).astype(BF)
+    onward[...] = keep[z ^ 2] + brought[z ^ 2].astype(F32)
+    for k, other in enumerate((1, 3)):
+        sent[k] = (keep[z ^ other] + brought[z ^ other].astype(F32)).astype(BF)
 
 
 def keep_kernel(scalars, *refs):
@@ -1010,8 +1044,11 @@
 
 def back_middle_kernel(
     scalars, own, by_x, by_y, got_y, got_x, second, cot, a_gu, w_out, a_out, b_out, z_out,
-    grad, dz_gu_out, dz_out_out, mixed_grad, up_own, up_x, up_y, up_far,
+    grad, mixed_grad, pack_0, pack_1, pack_2, pack_3, w_held, sem,
 ):
+    packs = (pack_0, pack_1, pack_2, pack_3)
+    load = pltpu.make_async_copy(w_out, w_held, sem)
+    load.start()
     rows, width = second.shape
     half = rows // 2
     upper = own[:half] + by_x[...].astype(F32) + got_y[...].astype(F32)
@@ -1020,29 +1057,33 @@
     seat = scalars[0] * 2 + scalars[1]
     mask = adapter_mask(scalars, rows_from(seat * rows, rows))
     dz_gu = (wide[:, width:] * jnp.concatenate([mask, mask], axis=1)).astype(BF)
-    dz_gu_out[...] = dz_gu
     upstream = wide[:, :width] + inner(dz_gu, a_gu[...], 1, 1)
     norm, factor = normed(second[...])
     total = cot[...].astype(F32) + norm_back(norm, factor, upstream)
     grad[...] = total
     low = total.astype(BF)
     dz_out = (inner(low, b_out[...], 1, 1) * mask).astype(BF)
-    dz_out_out[...] = dz_out
-    back = (inner(low, w_out[...], 1, 1) + inner(dz_out, a_out[...], 1, 1)).astype(BF)
+    value = inner(z_out[...], low, 0, 0).astype(BF)
+    load.wait()
+    back = (inner(low, w_held[...], 1, 1) + inner(dz_out, a_out[...], 1, 1)).astype(BF)
     for k in range(16):
         at = head_order(k)
         mixed_grad[:, at * LANES : (at + 1) * LANES] = back[:, k * LANES : (k + 1) * LANES]
-    value = inner(z_out[...], low, 0, 0)
     share = value.shape[0] // PLANE
+    at = dz_gu.shape[1] + LANES
+    for pack in packs:
+        pack[:, : dz_gu.shape[1]] = dz_gu
+        pack[:, dz_gu.shape[1] : at] = dz_out
     for block in range(CHIPS):
         for core in range(2):
-            at = (core * CHIPS + block) * share
-            piece = value[at : at + share]
-            for rel, out in enumerate((up_own, up_x, up_y, up_far)):
+            row = (core * CHIPS + block) * share
+            for rel, pack in enumerate(packs):
 
                 @pl.when((scalars[0] ^ rel) == block)
                 def _():
-                    out[core * share : (core + 1) * share, :] = piece.astype(out.dtype)
+                    for k in range(PLANE):
+                        there = slice(k * 2 * share + core * share, k * 2 * share + (core + 1) * share)
+                        pack[there, at:] = value[row : row + share, k * 2 * LANES : (k + 1) * 2 * LANES]
 
 
 def back_latent_kernel(scalars, own, other, up_own, up_oth, to_x, to_y, to_far, kept):
@@ -1126,16 +1167,16 @@
         scratch=[pltpu.SemaphoreType.DMA((39,))],
     )
     first_all = lax.all_gather(first_part, "fsdp", axis=0, tiled=True)
-    down_part, gu_part_0, gu_part_1 = call(
+    gates = [len(zs) * 2 * ff_dev for zs in CHUNKS]
+    down_part, *gu_parts = call(
         functools.partial(cut_rest_kernel, (ff, ff_z, ff_dev, width)), scalars,
         [w_gu, w_down, a_down, b_gu], [ANY] * 4,
-        [sds((ff_dev, wide_down + ff_dev))] + [sds((quarter, 4 * ff_dev))] * 2,
-        [whole_spec((ff_dev, wide_down + ff_dev))] + [whole_spec((quarter, 4 * ff_dev))] * 2,
-        scratch=[pltpu.SemaphoreType.DMA((11,))], ties=[first_part],
+        [sds((ff_dev, wide_down + ff_dev))] + [sds((quarter, n)) for n in gates],
+        [whole_spec((ff_dev, wide_down + ff_dev))] + [whole_spec((quarter, n)) for n in gates],
+        scratch=[pltpu.SemaphoreType.DMA((3 + 2 * z_count,))], ties=[first_part],
     )
     down_own = lax.all_gather(down_part, "fsdp", axis=0, tiled=True)
-    gu_own_0 = lax.all_gather(gu_part_0, "fsdp", axis=0, tiled=True)
-    gu_own_1 = lax.all_gather(gu_part_1, "fsdp", axis=0, tiled=True)
+    gu_owns = [lax.all_gather(part, "fsdp", axis=0, tiled=True) for part in gu_parts]
 
     pieces1 = gather_halves(norm_a, norm_b)
     pieces1_oth = [swap(piece, 1) for piece in pieces1]
@@ -1219,6 +1260,7 @@
         cost=(4 * heads_dev * length * length * HEAD_DIM, 8 * 2**20),
     )
     mixed = lax.all_to_all(mixed_h, "seq", split_axis=0, concat_axis=1, tiled=True)
+    mixed_oth = swap(mixed_h, 1)
     square = whole_spec((width, width))
     tall = whole_spec((rows, width))
     second, norm_a, norm_b, z_out = call(
@@ -1227,139 +1269,137 @@
         [sds((rows, width), F32), sds((half, width)), sds((half, width)), sds((rows, latent))],
         [tall, whole_spec((half, width)), whole_spec((half, width)), whole_spec((rows, latent))],
         scratch=[pltpu.VMEM((rows, width), BF)],
-        cost=(2 * rows * width * width, 12 * 2**20),
+        cost=(2 * rows * width * width, 12 * 2**20), ties=[mixed_oth],
     )
 
     pieces2 = gather_halves(norm_a, norm_b)
     down_own = hold(down_own, [second])
     down_oth = swap(down_own, 1)
-    gu_own_0 = hold(gu_own_0, [pieces2[1], pieces2[3]])
-    gu_oth_0 = swap(gu_own_0, 1)
     step = group // 2
 
-    def feed(chunk, gu_pair, at, onward, kind):
-        operands = [group_select, full_a_gu, full_b_down, down_own, down_oth, *gu_pair]
+    HBM = pl.BlockSpec(memory_space=pltpu.HBM)
+    size = len(CHUNKS[0]) * ff_dev
+    latents = [None, None]
+
+    def feed(place, weights, at, onward, last):
+        begin = onward is None
+        if begin:
+            operands = [group_select, full_a_gu, full_b_down]
+            specs = [
+                pl.BlockSpec((step, latent), lambda *_: (at, 0)), whole_spec((width, 2 * latent)),
+                whole_spec((latent, width)),
+            ]
+        else:
+            operands = list(latents[at])
+            specs = [whole_spec((step, 2 * latent)), whole_spec((step, latent))]
+        for pair in weights:
+            operands += pair
+            specs += [HBM, HBM]
         operands += pieces2[4 * at : 4 * at + 4] + cot_pieces[4 * at : 4 * at + 4]
-        specs = [
-            pl.BlockSpec((step, latent), lambda *_: (at, 0)), whole_spec((width, 2 * latent)),
-            whole_spec((latent, width)),
-        ] + [ANY] * 12
-        if onward is None:
+        specs += [ANY] * 8
+        if not begin:
+            operands.append(onward)
+            specs.append(HBM)
+        if last:
+            shapes, outs = [sds((rows, wide_gu), (BF, F32)[at])] * 2, [whole_spec((rows, wide_gu))] * 2
+        else:
             shapes, outs = [sds((step, wide_gu), F32)], [whole_spec((step, wide_gu))]
-        else:
-            operands.append(onward)
-            specs.append(ANY)
-            shapes, outs = [sds((rows, wide_gu), kind)] * 2, [whole_spec((rows, wide_gu))] * 2
-        shapes += [
-            sds((step, 4 * ff_dev)), sds((2, 2 * latent, 2 * ff_dev), F32), sds((2, 2 * ff_dev, latent), F32)
-        ]
-        outs += [
-            whole_spec((step, 4 * ff_dev)), whole_spec((2, 2 * latent, 2 * ff_dev)),
-            whole_spec((2, 2 * ff_dev, latent)),
-        ]
+        more = [(step, size), (step, 2 * size)] * len(weights)
+        if begin:
+            more += [(step, 2 * latent), (step, latent)]
+        shapes += [sds(shape) for shape in more]
+        outs += [whole_spec(shape) for shape in more]
         return call(
-            functools.partial(ff_kernel, onward is None, chunk), scalars, operands, specs,
-            shapes, outs,
-            scratch=[pltpu.VMEM((step, width), BF)] * 2 + [pltpu.VMEM((width, 4 * ff_dev), BF)] * 2
-            + [pltpu.VMEM((2 * ff_dev, wide_down + ff_dev), BF)] * 2
-            + [pltpu.VMEM((step, wide_gu) if onward is not None else (8, LANES), F32)]
-            + [pltpu.SemaphoreType.DMA((13,))],
-            cost=(step * 10 * width * ff_dev * 4, 26 * 2**20),
-        )
-
-    gu_pair = (gu_own_0, gu_oth_0)
-    sums_0, hidden_00, up_grads_00, down_grads_00 = feed(0, gu_pair, 0, None, F32)
-    sums_1, hidden_01, up_grads_01, down_grads_01 = feed(0, gu_pair, 1, None, F32)
-    gu_own_1 = hold(gu_own_1, [sums_0, sums_1])
-    gu_pair = (gu_own_1, swap(gu_own_1, 1))
-    send_x, send_y, hidden_10, up_grads_10, down_grads_10 = feed(1, gu_pair, 0, sums_0, BF)
-    pass_on, kept, hidden_11, up_grads_11, down_grads_11 = feed(1, gu_pair, 1, sums_1, F32)
-
-    def after(values, ties):
-        specs = [whole_spec(value.shape) for value in values]
+            functools.partial(ff_kernel, begin, last, len(weights), CHUNKS[place][0]), scalars, operands,
+            specs, shapes, outs,
+            scratch=[pltpu.VMEM((step, width), BF)] * 2
+            + [pltpu.VMEM((8, LANES) if begin else (step, wide_gu), F32), pltpu.SemaphoreType.DMA((13,))]
+            + [pltpu.VMEM((width, 2 * size), BF), pltpu.VMEM((size, wide_down + ff_dev), BF)]
+            * len(weights),
+            cost=(step * 10 * width * size * len(weights), 26 * 2**20),
+        )
+
+    def down_half(place, at, kind, total, ties):
+        weight = pl.BlockSpec((size, wide_down + ff_dev), lambda *_: (place, 0))
+        begin = total is None
+        operands = [results[place][0][at][0], results[place][1][at][0], down_own, down_oth]
+        specs = [whole_spec((step, size))] * 2 + [weight] * 2
+        if not begin:
+            operands.append(total)
+            specs.append(whole_spec((step, wide_down)))
+        shape = (step, wide_down) if begin else (rows, wide_down)
+        count = 1 if begin else 2
         return call(
-            keep_kernel, scalars, values, specs, [sds(v.shape, v.dtype) for v in values], specs, ties=ties
-        )
-
-    once = pl.Buffered(1)
-
-    def down_half(at, hidden_0, hidden_1, kind, ties):
-        row = pl.BlockSpec((rows, 4 * ff_dev), lambda i, _: (i, 0))
-        weight = pl.BlockSpec(
-            (z_count * ff_dev, wide_down + ff_dev), lambda i, _: (0, 0), pipeline_mode=once
-        )
-        return call(
-            down_kernel, scalars, [hidden_0, hidden_1, down_own, down_oth], [row, row, weight, weight],
-            [sds((rows, wide_down), kind)] * 2, [whole_spec((rows, wide_down))] * 2, grid=(2,),
-            cost=(2 * step * 8 * ff_dev * width, 16 * 2**20), ties=ties,
-        )
-
-    ff_rows = 2 * latent * (ff_dev // LANES) + ff_dev
-    ups = [up_grads_00, up_grads_01, up_grads_10, up_grads_11]
-    downs = [down_grads_00, down_grads_01, down_grads_10, down_grads_11]
-    ff_keep, ff_send = call(
-        ff_grads_kernel, scalars, ups + downs,
-        [whole_spec(ups[0].shape)] * 4 + [whole_spec(downs[0].shape)] * 4,
-        [sds((z_count, ff_rows, LANES), F32), sds((z_count, ff_rows, LANES))],
-        [whole_spec((z_count, ff_rows, LANES))] * 2, cost=(2**20, 12 * 2**20),
-    )
-    by_x, by_y, got_y, got_x, _ = scatter_rest(send_x, send_y, pass_on)
-    down_x, down_y = down_half(0, hidden_00, hidden_10, BF, [by_x, by_y])
+            functools.partial(down_kernel, begin), scalars, operands, specs,
+            [sds(shape, kind)] * count, [whole_spec(shape)] * count,
+            cost=(2 * step * 4 * ff_dev * width, 12 * 2**20), ties=ties,
+        )
+
+    results = [[[None, None], [None, None]] for _ in CHUNKS]
+    gu_own = hold(gu_owns[0], [pieces2[1], pieces2[3]])
+    weights = [(gu_own, down_own), (swap(gu_own, 1), down_oth)]
+    sums = []
+    for at in range(2):
+        total, *more = feed(0, weights, at, None, False)
+        sums.append(total)
+        results[0][0][at], results[0][1][at], latents[at] = more[:2], more[2:4], more[4:]
+    down_first = [down_half(0, at, F32, None, [sums[1]])[0] for at in range(2)]
+    gu_own = hold(gu_owns[1], sums + down_first)
+    weights = [(gu_own, down_own), (swap(gu_own, 1), down_oth)]
+    total, *results[1][0][0] = feed(1, weights[:1], 0, sums[0], False)
+    send_x, send_y, *results[1][1][0] = feed(1, weights[1:], 0, total, True)
+    pass_on, kept, *more = feed(1, weights, 1, sums[1], True)
+    results[1][0][1], results[1][1][1] = more[:2], more[2:]
+    by_x, by_y, got_y, got_x, passed = scatter_rest(send_x, send_y, pass_on)
+    down_x, down_y = down_half(1, 0, BF, down_first[0], passed)
     halfspec = lambda n: pl.BlockSpec((half, n), lambda *_: (0, 0))
-    second_grad, dz_gu, dz_out, mixed_grad, *up_out = call(
+    second_grad, mixed_grad, *packs = call(
         back_middle_kernel, scalars,
         [kept, by_x, by_y, got_y, got_x, second, cot_low, full_a_gu, full_out, full_a_out, full_b_out, z_out],
         [whole_spec((rows, wide_gu))] + [halfspec(wide_gu)] * 4
         + [
-            tall, tall, whole_spec((width, 2 * latent)), square, whole_spec((width, latent)),
+            tall, tall, whole_spec((width, 2 * latent)), ANY, whole_spec((width, latent)),
             whole_spec((latent, width)), whole_spec((rows, latent)),
         ],
         [
-            sds((rows, width), F32), sds((rows, 2 * latent)), sds((rows, latent)), sds((rows, width)),
-            sds((2 * share_b, width), F32),
+            sds((rows, width), F32), sds((rows, width)),
         ]
-        + [sds((2 * share_b, width))] * 3,
-        [tall, whole_spec((rows, 2 * latent)), whole_spec((rows, latent)), tall]
-        + [whole_spec((2 * share_b, width))] * 4,
-        cost=(2 * rows * width * width, 16 * 2**20), ties=[down_x, ff_send],
+        + [sds((rows, 5 * latent))] * 4,
+        [tall, tall] + [whole_spec((rows, 5 * latent))] * 4,
+        scratch=[pltpu.VMEM((width, width), BF), pltpu.SemaphoreType.DMA],
+        cost=(2 * rows * width * width, 16 * 2**20), ties=[down_x],
     )
     mixed_grad_h = lax.all_to_all(mixed_grad, "seq", split_axis=1, concat_axis=0, tiled=True)
-    down_on, down_kept = down_half(1, hidden_01, hidden_11, F32, [mixed_grad])
+    down_on, down_kept = down_half(1, 1, F32, down_first[1], [mixed_grad])
 
     def along_line(keep, send, ties):
         shape = keep.shape[1:]
-        brought = swap(send, 1)
-        mine, *sends = call(
-            along_line_kernel, scalars, [keep, brought], [whole_spec(keep.shape)] * 2,
-            [sds(shape, F32)] + [sds(shape)] * 6, [whole_spec(shape)] * 7, ties=ties,
-            cost=(2**20, 8 * 2**20),
-        )
-        return mine, sends
-
-    def line_sum(mine, sends, ties):
-        total = hold(mine, ties) if ties else mine
-        for k, value in enumerate(sends):
-            hop = k // 2 + 1
-            if k % 2 == 0:
-                perm = [(i, i + hop) for i in range(z_count - hop)]
-            else:
-                perm = [(i + hop, i) for i in range(z_count - hop)]
-            total = total + lax.ppermute(value, "fsdp", perm).astype(F32)
-        return total.astype(BF)
+        return call(
+            along_line_kernel, scalars, [keep, swap(send, 1)], [whole_spec(keep.shape)] * 2,
+            [sds(shape, F32)] * 2 + [sds((2, *shape))], [whole_spec(shape)] * 2 + [whole_spec((2, *shape))],
+            ties=ties, cost=(2**20, 8 * 2**20),
+        )
+
+    def line_sum(mine, onward, sent, ties):
+        brought = lax.ppermute(sent, "fsdp", [(i, i ^ 1) for i in range(z_count)])
+        onward = (onward + brought[1].astype(F32)).astype(BF)
+        far = lax.ppermute(onward, "fsdp", [(i, i ^ 2) for i in range(z_count)])
+        mine = hold(mine, ties) if ties else mine
+        return (mine + brought[0].astype(F32) + far.astype(F32)).astype(BF)
 
     def spread(mine, places, shapes, ties):
         plane = blocks_of(mine)
-        plane += [swap(piece, 1) for piece in plane]
+        plane.append(swap(jnp.stack(plane), 1))
         return call(
-            functools.partial(spread_kernel, places), scalars, plane, [whole_spec(mine.shape)] * 8,
+            functools.partial(spread_kernel, places), scalars, plane,
+            [whole_spec(piece.shape) for piece in plane],
             [sds(shape, F32) for shape in shapes], [whole_spec(shape) for shape in shapes], ties=ties,
         )
 
-    *down_by, down_passed = scatter_rest(down_x, down_y, down_on)
-    dz_gu, dz_out, *up_out = after([dz_gu, dz_out] + up_out, [mixed_grad_h])
-    all_dz_gu = blocks_of(dz_gu)
-    all_dz_out = blocks_of(jnp.stack([dz_out, swap(dz_out, 1)]))
-    all_up_out = [up_out[0], swap(up_out[1], 2), swap(up_out[2], 4), swap(up_out[3], 6)]
+    *down_by, _ = scatter_rest(
+        hold(down_x, [mixed_grad_h]), hold(down_y, [mixed_grad_h]), down_on
+    )
+    middle = [packs[0]] + [swap(hold(packs[k], [mixed_grad_h]), 2 * k) for k in (1, 2, 3)]
 
     result = pl.BlockSpec((3, group, HEAD_DIM), lambda h, _: (0, 0, h))
     grads_a, grads_b, up_qkv = call(
@@ -1370,7 +1410,7 @@
         [sds((3, group, span))] * 2 + [sds((3, latent, span), F32)],
         [result, result, pl.BlockSpec((3, latent, HEAD_DIM), lambda h, _: (0, 0, h))],
         scratch=[pltpu.VMEM((length, HEAD_DIM), F32)] * 3, grid=(heads_dev,),
-        cost=(10 * heads_dev * length * length * HEAD_DIM, 16 * 2**20), ties=down_passed,
+        cost=(10 * heads_dev * length * length * HEAD_DIM, 16 * 2**20), ties=[down_on],
     )
     grads_b = swap(grads_b, 1)
     qkv_oth = swap(qkv_own, 1)
@@ -1380,7 +1420,6 @@
     lower = down_kept[half:] + down_by[1][:half].astype(F32) + down_by[3].astype(F32)
     wide = jnp.concatenate([upper, lower], axis=0)
     z_down = wide[:, width:].astype(BF) * select
-    all_z_down = blocks_of(z_down)
     to_x, to_y, to_far, latent_kept = call(
         back_latent_kernel, scalars, [grads_a, grads_b, up_own, up_oth],
         [whole_spec((3, group, span))] * 2 + [whole_spec((3 * latent, span))] * 2,
@@ -1398,24 +1437,26 @@
             cost=(2 * group * span * 3 * width, 12 * 2**20), ties=ties,
         )
 
-    send_x, send_y = back_qkv(0, BF, [to_x])
-    pass_on, kept = back_qkv(1, F32, [send_x])
-    by_x, by_y, got_y, got_x, passed = scatter_rest(send_x, send_y, pass_on)
-    latent_kept = hold(latent_kept, passed)
+    pass_on, kept = back_qkv(1, F32, [to_x, *middle[1:]])
     dz_qkv = latent_kept + swap(to_x, 2).astype(F32) + swap(to_y, 4).astype(F32)
     dz_qkv = (dz_qkv + swap(to_far, 6).astype(F32)) * jnp.tile(select, (1, 3)).astype(F32)
-    dz_qkv = dz_qkv.astype(BF)
-    ff_mine, ff_sends = along_line(ff_keep, ff_send, [kept])
-    ff_total = line_sum(ff_mine, ff_sends, passed)
+    both = jnp.concatenate([dz_qkv.astype(BF), z_down], axis=1)
+    last = blocks_of(both)
+    ff_rows = 2 * latent * (ff_dev // LANES) + ff_dev
+    values = [one[k] for one in latents for k in range(1)] + [one[1] for one in latents]
+    values += [value for chunk in results for side in chunk for one in side for value in one]
+    ff_keep, ff_send = call(
+        ff_grads_kernel, scalars, values, [whole_spec(value.shape) for value in values],
+        [sds((z_count, ff_rows, LANES), F32), sds((z_count, ff_rows, LANES))],
+        [whole_spec((z_count, ff_rows, LANES))] * 2, cost=(2**32, 12 * 2**20), ties=[kept, both],
+    )
+    send_x, send_y = back_qkv(0, BF, [*last[1:], ff_send])
     other_rows = 11 * LANES // 2
-    block = lambda n: [whole_spec((rows, n))] * 4
     keep, send = call(
         functools.partial(other_grads_kernel, quarter), scalars,
-        [*pieces1, *pieces2, *cot_pieces, mixed_h, *all_dz_gu, *blocks_of(dz_qkv), *all_z_down, *all_dz_out,
-         *all_up_out, up_qkv],
-        [ANY] * 24 + [whole_spec((length, span))] + block(2 * latent) + block(3 * latent) + block(latent)
-        + [whole_spec((2, rows, latent))] * 4 + [whole_spec((2 * share_b, width))] * 4
-        + [whole_spec((3, latent, span))],
+        [*pieces1, *pieces2, *cot_pieces, mixed_h, mixed_oth, *middle, *last, up_qkv],
+        [ANY] * 24 + [whole_spec((length, span))] * 2 + [whole_spec((rows, 5 * latent))] * 4
+        + [whole_spec((rows, 4 * latent))] * 4 + [whole_spec((3, latent, span))],
         [sds((z_count, other_rows, LANES), F32), sds((z_count, other_rows, LANES))],
         [whole_spec((z_count, other_rows, LANES))] * 2,
         scratch=[
@@ -1423,27 +1464,28 @@
             pltpu.VMEM((group, 3 * latent), BF), pltpu.VMEM((group, latent), BF),
             pltpu.SemaphoreType.DMA((96,)),
         ],
-        cost=(2 * group * 512 * 768, 8 * 2**20), ties=passed,
-    )
-
+        cost=(2 * group * 512 * 768, 8 * 2**20), ties=[send_x],
+    )
+    ff_mine, *ff_rest = along_line(ff_keep, ff_send, [keep])
+    by_x, by_y, got_y, got_x, passed = scatter_rest(send_x, send_y, hold(pass_on, [keep]))
+    input_grad = call(
+        back_first_kernel, scalars,
+        [kept, by_x, by_y, got_y, got_x, stream, second_grad, both, full_a_qkv],
+        [tall] + [halfspec(width)] * 4
+        + [tall, tall, pl.BlockSpec((rows, 3 * latent), lambda *_: (0, 0)), whole_spec((width, 3 * latent))],
+        sds((rows, width), F32), tall,
+        cost=(2 * rows * width * 3 * latent, 12 * 2**20),
+    )
+    ff_total = line_sum(ff_mine, *ff_rest, [])
+    total = line_sum(*along_line(keep, send, []), [got_y, got_x])
+    activations = second + (wide[:, :width] + dot(hold(z_down, passed), full_b_down))
     g_b_gu, g_a_down = spread(
         ff_total, (("columns", 2 * latent, ff_dev // LANES), ("rows", ff_dev, 1)),
-        [(2 * latent, ff_z), (ff_z, latent)], passed,
-    )
-
-    input_grad = call(
-        back_first_kernel, scalars,
-        [kept, by_x, by_y, got_y, got_x, stream, second_grad, dz_qkv, full_a_qkv],
-        [tall] + [halfspec(width)] * 4
-        + [tall, tall, whole_spec((rows, 3 * latent)), whole_spec((width, 3 * latent))],
-        sds((rows, width), F32), tall,
-        cost=(2 * rows * width * 3 * latent, 12 * 2**20),
-    )
-    activations = second + (wide[:, :width] + dot(hold(z_down, passed), full_b_down))
-    mine, sends = along_line(keep, send, [input_grad])
+        [(2 * latent, ff_z), (ff_z, latent)], [input_grad],
+    )
     low = LANES // 2
     g_a_gu, g_b_down, g_a_out, g_b_out, g_a_qkv, g_b_qkv = spread(
-        line_sum(mine, sends, []),
+        total,
         (
             ("rows", low, 2), ("both", low, 1), ("rows", low, 1), ("core rows", share_b, z_count),
             ("rows", low, 3), ("both", 3 * low, 1),
@@ -1452,7 +1494,7 @@
             (quarter, 2 * latent), (latent, quarter), (quarter, latent), (latent, quarter),
             (quarter, 3 * latent), (3 * latent, quarter),
         ],
-        [],
+        [input_grad],
     )
 
     return (

time: 730 us -> 668 us (0.915)
  starting transfers between devices: 147 us -> 97.7 us
  local copies, waits for them, and re-layouts: 38 us -> 26.6 us
    ppermute x12 -> x4, starting transfers between devices: 34.1 us -> 2.3 us  [the longest x2 1.53 us: line_sum(): brought = lax.ppermute(sent, 'fsdp', [(i, i ^ 1) for i in range(z_count)])]
    ppermute x107 -> x92, starting transfers between devices: 106 us -> 85.3 us  [swap(): return lax.ppermute(value, 'seq', [(i, i ^ bits) for i in range(PLANE)])]
    ppermute x12 -> x4, waiting for transfers between devices: 9.63 us -> 19.9 us  [the longest x2 13.3 us: line_sum(): brought = lax.ppermute(sent, 'fsdp', [(i, i ^ 1) for i in range(z_count)])]
    all_gather x2, waiting for transfers between devices: 47.3 us -> 37.8 us  [plane_shards(): lax.all_gather(part, 'fsdp', axis=0, tiled=True)]
    unnamed x217 -> x175, local copies, waits for them, and re-layouts: 21.4 us -> 13.4 us
    ppermute x107 -> x92, waiting for transfers between devices: 93.4 us -> 92.5 us  [swap(): return lax.ppermute(value, 'seq', [(i, i ^ bits) for i in range(PLANE)])]
    pallas_call x27 -> x29, Pallas kernels: 303 us -> 302 us  [call(): pl.pallas_call(run, grid_spec=pltpu.PrefetchScalarGridSpec(num_scalar_pre...]
  transfers between devices with their start and end apart: 125 -> 102, of which waited for: 29 -> 30; matrix products, arithmetic and copies ran while one was open for 5% -> 5% of each run, Pallas kernels for 38% -> 39%
where the time goes in v3:
time: 668 us; the launch traced here: 658 us
  Pallas kernels  302 us (45%)
  waiting for transfers between devices  192 us (29%)
  starting transfers between devices  97.7 us (15%)
  local copies, waits for them, and re-layouts  26.6 us (4%)
  other arithmetic  21.4 us (3%)
  between operations  15.1 us (2%)
    pallas_call x29, Pallas kernels, call(): pl.pallas_call(run, grid_spec=pltpu.PrefetchScalarGridSpec(num_scalar_pre...  302 us
    ppermute x92, waiting for transfers between devices, swap(): return lax.ppermute(value, 'seq', [(i, i ^ bits) for i in range(PLANE)])  92.5 us
    ppermute x92, starting transfers between devices, swap(): return lax.ppermute(value, 'seq', [(i, i ^ bits) for i in range(PLANE)])  85.3 us
    all_gather x2, waiting for transfers between devices, plane_shards(): lax.all_gather(part, 'fsdp', axis=0, tiled=True)  37.8 us
    all_gather x1, waiting for transfers between devices, plane_shards(): first_all = lax.all_gather(first_part, 'fsdp', axis=0, tiled=True)  28.3 us
    unnamed x175, local copies, waits for them, and re-layouts  13.4 us
  transfers between devices with their start and end apart: 102, of which 30 were waited for; matrix products, arithmetic and copies ran while one was open for 5% of the time, Pallas kernels for 39%

profile of v3, /device:TPU:1, one launch (start us, length us, event | category | flops | bytes accessed | tf_op | source)
XLA Modules:
  0.0 657.6 jit_solution(960641373129655155)
XLA Ops:
  8.5 3.3 shard_map.250.refs_5_
  12.0 4.3 shard_map.259
  16.4 3.5 shard_map.249
  26.1 7.8 %collective-permute-done.1.refs_5_ = bf16[128,2048]{1,0:T(8,128)(2,1)} collective-permute-done((bf16[128,2048]{1,0:T(8,128)(2,1)}, bf16[128,2048]{1,0:T(8,128)(2,1)}, u32[]{:S(2)}, u32[]{:S(2)}) %collective-permute-start.1) | collective-permute-done | bytes 524320 | tf_op jit(solution)/shard_map/ppermute | solution.py:429
  35.1 10.9 %collective-permute-done.4.refs_6_ = bf16[128,2048]{1,0:T(8,128)(2,1)} collective-permute-done((bf16[128,2048]{1,0:T(8,128)(2,1)}, bf16[128,2048]{1,0:T(8,128)(2,1)}, u32[]{:S(2)}, u32[]{:S(2)}) %collective-permute-start.4) | collective-permute-done | bytes 524320 | tf_op jit(solution)/shard_map/ppermute | solution.py:429
  46.4 3.7 multiply_sine_fusion
  51.2 6.0 collective-permute-done.16.refs_13_.refs_12_.refs_22_
  57.6 10.9 %collective-permute-done.2.refs_2_ = bf16[128,2048]{1,0:T(8,128)(2,1)} collective-permute-done((bf16[128,2048]{1,0:T(8,128)(2,1)}, bf16[128,2048]{1,0:T(8,128)(2,1)}, u32[]{:S(2)}, u32[]{:S(2)}) %collective-permute-start.2) | collective-permute-done | bytes 524320 | tf_op jit(solution)/shard_map/ppermute | solution.py:429
  68.5 3.3 collective-permute-start.7
  73.8 6.0 collective-permute-done.15.refs_3_.refs_13_.refs_10_.refs_18_
  81.9 28.3 %all-gather.5.cloned.1.call-done.refs_0_ = bf16[3328,768]{1,0:T(8,128)(2,1)} async-done(((bf16[832,768]{1,0:T(8,128)(2,1)}), bf16[3328,768]{1,0:T(8,128)(2,1)}) %all-gather.5.cloned.1.call-update) | async-done | bytes 5111824 | tf_op jit(solution)/shard_map/all_gather | solution.py:1169
  114.1 2.5 fusion.15
  121.0 4.4 collective-permute-done.19.refs_5_
  126.5 6.2 collective-permute-done.22.refs_6_
  136.4 3.9 collective-permute-done.20.refs_2_.refs_1_
  147.8 5.5 shard_map.252
  157.3 3.6 collective-permute-done.34.refs_5_
  162.3 22.2 %shard_map.253 = (bf16[2048,768]{1,0:T(8,128)(2,1)}, bf16[2048,384]{1,0:T(8,128)(2,1)}, bf16[2048,768]{1,0:T(8,128)(2,1)}) custom-call(s32[11]{0:T(128)} %concatenate.27.refs_0_, bf16[128,2048]{1,0:T(8,128)(2,1)} %collective-permute-done.refs_1_, bf16[128,2048]{1,0:T(8,128)(2,1)} %collective-permute-done.2.refs_2_, bf16[128,2048]{1,0:T(8,128)(2,1)} %copy-done.46, ...), custom_call_target="tpu_custom_call" | custom-call | flops 9663676416 | bytes 20971520 | tf_op jit(solution)/shard_map/pallas_call | solution.py:468
  185.9 16.1 %shard_map.254 = (bf16[2048,256]{1,0:T(8,128)(2,1)}, f32[2048,256]{1,0:T(8,128)}) custom-call(s32[11]{0:T(128)} %concatenate.27.refs_0_, bf16[2048,768]{1,0:T(8,128)(2,1)} %get-tuple-element.98.refs_1_.refs_2_.refs_3_, bf16[2048,768]{1,0:T(8,128)(2,1)} %get-tuple-element.98.refs_1_.refs_2_.refs_3_, bf16[2048,768]{1,0:T(8,128)(2,1)} %get-tuple-element.98.refs_1_.refs_2_.refs_3_), custom_call_target="tpu_custom_call" | custom-call | flops 4294967296 | bytes 8388608 | tf_op jit(solution)/shard_map/pallas_call | solution.py:468
  203.3 3.7 all-to-all-start
  208.3 10.7 %all-to-all-done = bf16[8,256,256]{2,1,0:T(8,128)(2,1)S(1)} async-done(((bf16[8,256,256]{2,1,0:T(8,128)(2,1)}), bf16[8,256,256]{2,1,0:T(8,128)(2,1)S(1)}, u32[]{:S(2)}, u32[]{:S(2)}) %all-to-all-start) | async-done | bytes 1048608 | tf_op jit(solution)/shard_map/all_to_all | solution.py:1262
  220.9 8.4 %shard_map.257.refs_2_.refs_9_ = bf16[2048,2048]{1,0:T(8,128)(2,1)} custom-call(s32[11]{0:T(128)} %concatenate.27.refs_0_, bf16[384,768]{1,0:T(8,128)(2,1)} %copy-done.39, bf16[384,768]{1,0:T(8,128)(2,1)} %collective-permute-done.35.refs_2_, bf16[384,768]{1,0:T(8,128)(2,1)} %collective-permute-done.36.refs_3_, ...), custom_call_target="tpu_custom_call" | custom-call | tf_op jit(solution)/shard_map/pallas_call | solution.py:468
  230.2 9.6 %shard_map.258 = (f32[256,2048]{1,0:T(8,128)}, bf16[128,2048]{1,0:T(8,128)(2,1)}, bf16[128,2048]{1,0:T(8,128)(2,1)}, bf16[256,128]{1,0:T(8,128)(2,1)}) custom-call(s32[11]{0:T(128)} %concatenate.27.refs_0_, bf16[256,2048]{1,0:T(8,128)(2,1)} %bitcast.93, bf16[2048,2048]{1,0:T(8,128)(2,1)} %shard_map.257.refs_2_.refs_9_, ...), custom_call_target="tpu_custom_call" | custom-call | flops 2147483648 | bytes 12582912 | tf_op jit(solution)/shard_map/pallas_call | solution.py:468
  240.9 2.4 collective-permute-start.50
  244.6 5.5 collective-permute-done.48.refs_8_.refs_7_.refs_13_
  250.0 6.6 %collective-permute-start.49 = (bf16[128,2048]{1,0:T(8,128)(2,1)S(1)}, bf16[128,2048]{1,0:T(8,128)(2,1)S(1)}, u32[]{:S(2)}, u32[]{:S(2)}) collective-permute-start(bf16[128,2048]{1,0:T(8,128)(2,1)S(1)} %collective-permute-done.48.refs_8_.refs_7_.refs_13_), channel_id=1, source_target_pairs={{0,8},{4,12},{8,0},{12,4},{16,24},{20,28},{24,16},{28,20},{1,9},{5... | collective-permute-start | bytes 1572872 | tf_op jit(solution)/shard_map/ppermute | solution.py:429
  256.7 27.9 %all-gather.7.cloned.1.call-done.refs_0_ = bf16[2048,1024]{1,0:T(8,128)(2,1)} async-done(((bf16[512,1024]{1,0:T(8,128)(2,1)}), bf16[2048,1024]{1,0:T(8,128)(2,1)}) %all-gather.7.cloned.1.call-update) | async-done | bytes 4194320 | tf_op jit(solution)/shard_map/all_gather | solution.py:1179
  291.1 2.9 collective-permute-done.52.refs_6_
  294.0 22.1 %shard_map.262 = (f32[512,2304]{1,0:T(8,128)}, bf16[512,512]{1,0:T(8,128)(2,1)}, bf16[512,1024]{1,0:T(8,128)(2,1)}, bf16[512,512]{1,0:T(8,128)(2,1)}, bf16[512,1...) custom-call(s32[11]{0:T(128)} %concatenate.27.refs_0_, ...), custom_call_target="tpu_custom_call" | custom-call | flops 10737418240 | bytes 27262976 | tf_op jit(solution)/shard_map/pallas_call | solution.py:468
  316.1 8.2 %shard_map.265.refs_4_.refs_5_ = f32[512,2176]{1,0:T(8,128)} custom-call(s32[11]{0:T(128)} %concatenate.27.refs_0_, bf16[512,512]{1,0:T(8,128)(2,1)} %get-tuple-element.116.refs_1_.refs_7_, bf16[512,512]{1,0:T(8,128)(2,1)} %get-tuple-element.117.refs_2_.refs_11_, bf16[1024,2432]{1,0:T(8,128)(2,1)} %shard_map.261.refs_5_.refs_3_.refs_4_, ...), custom_call_target="tpu_custom_call" | custom-call | flops 2147483648 | bytes 12582912 | tf_op jit(solution)/shard_map/pallas_call | solution.py:468
  325.5 22.2 %shard_map.263 = (f32[512,2304]{1,0:T(8,128)}, bf16[512,512]{1,0:T(8,128)(2,1)}, bf16[512,1024]{1,0:T(8,128)(2,1)}, bf16[512,512]{1,0:T(8,128)(2,1)}, bf16[512,1...) custom-call(s32[11]{0:T(128)} %concatenate.27.refs_0_, ...), custom_call_target="tpu_custom_call" | custom-call | flops 10737418240 | bytes 27262976 | tf_op jit(solution)/shard_map/pallas_call | solution.py:468
  347.7 8.2 %shard_map.264.refs_3_.refs_5_ = f32[512,2176]{1,0:T(8,128)} custom-call(s32[11]{0:T(128)} %concatenate.27.refs_0_, bf16[512,512]{1,0:T(8,128)(2,1)} %get-tuple-element.114.refs_1_.refs_5_, bf16[512,512]{1,0:T(8,128)(2,1)} %get-tuple-element.115.refs_2_.refs_9_, bf16[1024,2432]{1,0:T(8,128)(2,1)} %shard_map.261.refs_5_.refs_3_.refs_4_, ...), custom_call_target="tpu_custom_call" | custom-call | flops 2147483648 | bytes 12582912 | tf_op jit(solution)/shard_map/pallas_call | solution.py:468
  355.9 9.9 %all-gather.11.cloned.1.call-done.refs_0_ = bf16[2048,1024]{1,0:T(8,128)(2,1)} async-done(((bf16[512,1024]{1,0:T(8,128)(2,1)}), bf16[2048,1024]{1,0:T(8,128)(2,1)}) %all-gather.11.cloned.1.call-update) | async-done | bytes 4194320 | tf_op jit(solution)/shard_map/all_gather | solution.py:1179
  366.5 13.7 %shard_map.268 = (f32[512,2304]{1,0:T(8,128)}, bf16[512,512]{1,0:T(8,128)(2,1)}, bf16[512,1024]{1,0:T(8,128)(2,1)}) custom-call(s32[11]{0:T(128)} %concatenate.27.refs_0_, bf16[512,256]{1,0:T(8,128)(2,1)} %get-tuple-element.121.refs_1_, bf16[512,128]{1,0:T(8,128)(2,1)} %get-tuple-element.122.refs_2_.refs_3_, bf16[2048,1024]{1,0:T(8,128)(2,1)} %shard_map.266.refs_3_, ...), custom_call_target="tpu_custom_call" | custom-call | flops 5368709120 | bytes 27262976 | tf_op jit(solution)/shard_map/pallas_call | solution.py:468
  380.2 13.5 %shard_map.269 = (bf16[256,2304]{1,0:T(8,128)(2,1)}, bf16[256,2304]{1,0:T(8,128)(2,1)}, bf16[512,512]{1,0:T(8,128)(2,1)}, bf16[512,1024]{1,0:T(8,128)(2,1)}) custom-call(s32[11]{0:T(128)} %concatenate.27.refs_0_, bf16[512,256]{1,0:T(8,128)(2,1)} %get-tuple-element.121.refs_1_, bf16[512,128]{1,0:T(8,128)(2,1)} %get-tuple-element.122.refs_2_.refs_3_, ...), custom_call_target="tpu_custom_call" | custom-call | flops 5368709120 | bytes 27262976 | tf_op jit(solution)/shard_map/pallas_call | solution.py:468
  396.2 21.5 %shard_map.267 = (f32[256,2304]{1,0:T(8,128)}, f32[256,2304]{1,0:T(8,128)}, bf16[512,512]{1,0:T(8,128)(2,1)}, bf16[512,1024]{1,0:T(8,128)(2,1)}, bf16[512,512]{1,0:T(8,128)(2,1)}, /*index=5*/bf16[512,1024]{1,0:T(8,128)(2,1)}) custom-call(s32[11]{0:T(128)} %concatenate.27.refs_0_, bf16[512,256]{1,0:T(8,128)(2,1)} %get-tuple-element.109.refs_1_.refs_2_, ...), custom_call_target="tpu_custom_call" | custom-call | flops 10737418240 | bytes 27262976 | tf_op jit(solution)/shard_map/pallas_call | solution.py:468
  417.7 3.8 collective-permute-done.59.refs_2_
  422.5 2.3 add_convert_fusion
  426.8 8.7 %shard_map.270 = (bf16[256,2176]{1,0:T(8,128)(2,1)}, bf16[256,2176]{1,0:T(8,128)(2,1)}) custom-call(s32[11]{0:T(128)} %concatenate.27.refs_0_, bf16[512,512]{1,0:T(8,128)(2,1)} %get-tuple-element.128.refs_1_.refs_13_, bf16[512,512]{1,0:T(8,128)(2,1)} %get-tuple-element.129.refs_2_.refs_17_, bf16[1024,2432]{1,0:T(8,128)(2,1)} %shard_map.261.refs_5_.refs_3_.refs_4_, ...), custom_call_target="tpu_custom_call" | custom-call | flops 2147483648 | bytes 12582912 | tf_op jit(solution)/shard_map/pallas_call | solution.py:468
  435.5 3.1 collective-permute-done.61.refs_4_
  440.3 13.3 %shard_map.271 = (f32[256,2048]{1,0:T(8,128)}, bf16[256,2048]{1,0:T(8,128)(2,1)}, bf16[256,640]{1,0:T(8,128)(2,1)}, bf16[256,640]{1,0:T(8,128)(2,1)}, bf16[256,6...) custom-call(s32[11]{0:T(128)} %concatenate.27.refs_0_, f32[256,2304]{1,0:T(8,128)} %get-tuple-element.120.refs_1_, ...), custom_call_target="tpu_custom_call" | custom-call | flops 2147483648 | bytes 16777216 | tf_op jit(solution)/shard_map/pallas_call | solution.py:468
  453.7 2.3 copy.139
  455.9 6.2 all-to-all-start.1
  462.3 9.4 %shard_map.272 = (f32[256,2176]{1,0:T(8,128)}, f32[256,2176]{1,0:T(8,128)}) custom-call(s32[11]{0:T(128)} %concatenate.27.refs_0_, bf16[512,512]{1,0:T(8,128)(2,1)} %get-tuple-element.118.refs_1_.refs_15_, bf16[512,512]{1,0:T(8,128)(2,1)} %get-tuple-element.119.refs_2_.refs_19_, bf16[1024,2432]{1,0:T(8,128)(2,1)} %shard_map.261.refs_5_.refs_3_.refs_4_, ...), custom_call_target="tpu_custom_call" | custom-call | flops 2147483648 | bytes 12582912 | tf_op jit(solution)/shard_map/pallas_call | solution.py:468
  471.7 2.3 all-to-all-done.1
  476.2 3.3 collective-permute-start.63
  479.5 25.0 %shard_map.273 = (bf16[3,1024,256]{2,1,0:T(8,128)(2,1)}, bf16[3,1024,256]{2,1,0:T(8,128)(2,1)}, f32[3,128,256]{2,1,0:T(8,128)}) custom-call(s32[11]{0:T(128)} %concatenate.27.refs_0_, bf16[2048,768]{1,0:T(8,128)(2,1)} %get-tuple-element.98.refs_1_.refs_2_.refs_3_, bf16[2048,768]{1,0:T(8,128)(2,1)} %get-tuple-element.98.refs_1_.refs_2_.refs_3_, ...), custom_call_target="tpu_custom_call" | custom-call | flops 10737418240 | bytes 16777216 | tf_op jit(solution)/shard_map/pallas_call | solution.py:468
  512.0 4.4 shard_map.277
  517.1 6.1 collective-permute-done.70.refs_7_.refs_29_
  524.8 9.4 %shard_map.281 = (f32[256,2048]{1,0:T(8,128)}, f32[256,2048]{1,0:T(8,128)}) custom-call(s32[11]{0:T(128)} %concatenate.27.refs_0_, bf16[3,1024,256]{2,1,0:T(8,128)(2,1)} %get-tuple-element.136.refs_1_, bf16[3,1024,256]{2,1,0:T(8,128)(2,1)} %collective-permute-done.67.refs_2_, bf16[2048,768]{1,0:T(8,128)(2,1)} %get-tuple-element.139.refs_3_, ...), custom_call_target="tpu_custom_call" | custom-call | flops 3221225472 | bytes 12582912 | tf_op jit(solution)/shard_map/pallas_call | solution.py:468
  540.1 3.1 collective-permute-done.74
  547.2 8.8 %shard_map.282 = (f32[4,768,128]{2,1,0:T(8,128)}, bf16[4,768,128]{2,1,0:T(8,128)(2,1)}) custom-call(s32[11]{0:T(128)} %concatenate.27.refs_0_, bf16[512,256]{1,0:T(8,128)(2,1)} %get-tuple-element.121.refs_1_, bf16[512,256]{1,0:T(8,128)(2,1)} %get-tuple-element.109.refs_1_.refs_2_, bf16[512,128]{1,0:T(8,128)(2,1)} %get-tuple-element.122.refs_2_.refs_3_, ...), custom_call_target="tpu_custom_call" | custom-call | flops 4294967296 | bytes 12582912 | tf_op jit(solution)/shard_map/pallas_call | solution.py:468
  558.1 8.8 %shard_map.283 = (bf16[256,2048]{1,0:T(8,128)(2,1)}, bf16[256,2048]{1,0:T(8,128)(2,1)}) custom-call(s32[11]{0:T(128)} %concatenate.27.refs_0_, bf16[3,1024,256]{2,1,0:T(8,128)(2,1)} %get-tuple-element.136.refs_1_, bf16[3,1024,256]{2,1,0:T(8,128)(2,1)} %collective-permute-done.67.refs_2_, bf16[2048,768]{1,0:T(8,128)(2,1)} %get-tuple-element.139.refs_3_, ...), custom_call_target="tpu_custom_call" | custom-call | flops 3221225472 | bytes 12582912 | tf_op jit(solution)/shard_map/pallas_call | solution.py:468
  569.1 2.3 collective-permute-start.89
  571.4 9.6 %shard_map.284 = (f32[4,704,128]{2,1,0:T(8,128)}, bf16[4,704,128]{2,1,0:T(8,128)(2,1)}) custom-call(s32[11]{0:T(128)} %concatenate.27.refs_0_, bf16[128,2048]{1,0:T(8,128)(2,1)} %collective-permute-done.refs_1_, bf16[128,2048]{1,0:T(8,128)(2,1)} %collective-permute-done.2.refs_2_, bf16[128,2048]{1,0:T(8,128)(2,1)} %copy-done.46, ...), custom_call_target="tpu_custom_call" | custom-call | flops 805306368 | bytes 8388608 | tf_op jit(solution)/shard_map/pallas_call | solution.py:468
  582.0 3.6 shard_map.291
  585.6 3.3 shard_map.288
  596.7 11.2 %collective-permute-done.83 = bf16[2,704,128]{2,1,0:T(8,128)(2,1)S(1)} collective-permute-done((bf16[2,704,128]{2,1,0:T(8,128)(2,1)}, bf16[2,704,128]{2,1,0:T(8,128)(2,1)S(1)}, u32[]{:S(2)}, u32[]{:S(2)}) %collective-permute-start.83) | collective-permute-done | bytes 360480 | tf_op jit(solution)/shard_map/ppermute | solution.py:1384
  611.7 6.6 %collective-permute-done.84 = bf16[704,128]{1,0:T(8,128)(2,1)S(1)} collective-permute-done((bf16[704,128]{1,0:T(8,128)(2,1)S(1)}, bf16[704,128]{1,0:T(8,128)(2,1)S(1)}, u32[]{:S(2)}, u32[]{:S(2)}) %collective-permute-start.84) | collective-permute-done | bytes 180256 | tf_op jit(solution)/shard_map/ppermute | solution.py:1386
  626.5 2.7 collective-permute-done.87.refs_4_
  632.3 3.2 fusion.1
  635.4 7.4 %shard_map.287.refs_6_ = f32[256,2048]{1,0:T(8,128)} custom-call(s32[11]{0:T(128)} %concatenate.27.refs_0_, f32[256,2048]{1,0:T(8,128)} %get-tuple-element.158.refs_21_.refs_1_, bf16[256,2048]{1,0:T(8,128)(2,1)} %collective-permute-done.78.refs_2_, bf16[256,2048]{1,0:T(8,128)(2,1)} %collective-permute-done.79.refs_3_, bf16[128,2048]{1,0:T(8,128)(2,1)} %copy-done.20, ...), custom_call_target="tpu_custom_call" | custom-call | flops 402653184 | bytes 12582912 | tf_op jit(solution)/shard_map/pallas_call | solution.py:468
  642.8 4.1 shard_map.292
  647.0 3.9 shard_map.290
  (406 shorter events, 114.6 us)
Async XLA Ops:
  7.2 103.0 %all-gather.5.cloned.1.call-start = ((), (), s32[]{:S(2)}) async-start(), calls=%async_computation.2 | async-start | bytes 6389760 | tf_op jit(solution)/shard_map/all_gather | solution.py:1169
  11.9 231.4 %all-gather.9.cloned.1.call-start = ((), (), s32[]{:S(2)}) async-start(), calls=%async_computation.4 | async-start | bytes 6225920 | tf_op jit(solution)/shard_map/all_gather | solution.py:1178
  16.3 268.2 %all-gather.7.cloned.1.call-start = ((), (), s32[]{:S(2)}) async-start(), calls=%async_computation.3 | async-start | bytes 5242880 | tf_op jit(solution)/shard_map/all_gather | solution.py:1179
  19.9 14.0 %collective-permute-start.1 = (bf16[128,2048]{1,0:T(8,128)(2,1)}, bf16[128,2048]{1,0:T(8,128)(2,1)}, u32[]{:S(2)}, u32[]{:S(2)}) collective-permute-start(bf16[128,2048]{1,0:T(8,128)(2,1)} %get-tuple-element.95.refs_7_), channel_id=1, source_target_pairs={{0,16},{4,20},{8,24},{12,28},{16,0},{20,4},{24,8},{28,12},{1,17},{... | collective-permute-start | bytes 1572872 | tf_op jit(solution)/shard_map/ppermute | solution.py:429
  22.0 95.9 %collective-permute-start = (bf16[128,2048]{1,0:T(8,128)(2,1)}, bf16[128,2048]{1,0:T(8,128)(2,1)}, u32[]{:S(2)}, u32[]{:S(2)}) collective-permute-start(bf16[128,2048]{1,0:T(8,128)(2,1)} %get-tuple-element.95.refs_7_), channel_id=1, source_target_pairs={{0,8},{4,12},{8,0},{12,4},{16,24},{20,28},{24,16},{28,20},{1,9},{5... | collective-permute-start | bytes 1572872 | tf_op jit(solution)/shard_map/ppermute | solution.py:429
  23.2 22.8 %collective-permute-start.4 = (bf16[128,2048]{1,0:T(8,128)(2,1)}, bf16[128,2048]{1,0:T(8,128)(2,1)}, u32[]{:S(2)}, u32[]{:S(2)}) collective-permute-start(bf16[128,2048]{1,0:T(8,128)(2,1)} %get-tuple-element.96.refs_8_), channel_id=1, source_target_pairs={{0,8},{4,12},{8,0},{12,4},{16,24},{20,28},{24,16},{28,20},{1,9},{5... | collective-permute-start | bytes 1572872 | tf_op jit(solution)/shard_map/ppermute | solution.py:429
  24.5 25.5 %collective-permute-start.14 = (bf16[128,2048]{1,0:T(8,128)(2,1)}, bf16[128,2048]{1,0:T(8,128)(2,1)}, u32[]{:S(2)}, u32[]{:S(2)}) collective-permute-start(bf16[128,2048]{1,0:T(8,128)(2,1)} %get-tuple-element.205.refs_14_.refs_13_.refs_23_), channel_id=1, source_target_pairs={{0,16},{4,20},{8,24},{12,28},{16,0},{20,4},{24,8},{28,12},{1,17},{... | collective-permute-start | bytes 1572872 | tf_op jit(solution)/shard_map/ppermute | solution.py:429
  24.5 32.7 %collective-permute-start.16 = (bf16[128,2048]{1,0:T(8,128)(2,1)}, bf16[128,2048]{1,0:T(8,128)(2,1)}, u32[]{:S(2)}, u32[]{:S(2)}) collective-permute-start(bf16[128,2048]{1,0:T(8,128)(2,1)} %get-tuple-element.204.refs_15_.refs_14_.refs_24_), channel_id=1, source_target_pairs={{0,8},{4,12},{8,0},{12,4},{16,24},{20,28},{24,16},{28,20},{1,9},{5... | collective-permute-start | bytes 1572872 | tf_op jit(solution)/shard_map/ppermute | solution.py:429
  34.0 34.5 %collective-permute-start.2 = (bf16[128,2048]{1,0:T(8,128)(2,1)}, bf16[128,2048]{1,0:T(8,128)(2,1)}, u32[]{:S(2)}, u32[]{:S(2)}) collective-permute-start(bf16[128,2048]{1,0:T(8,128)(2,1)} %collective-permute-done.1.refs_5_), channel_id=1, source_target_pairs={{0,8},{4,12},{8,0},{12,4},{16,24},{20,28},{24,16},{28,20},{1,9},{5... | collective-permute-start | bytes 1572872 | tf_op jit(solution)/shard_map/ppermute | solution.py:429
  46.0 25.8 %collective-permute-start.5 = (bf16[128,2048]{1,0:T(8,128)(2,1)}, bf16[128,2048]{1,0:T(8,128)(2,1)}, u32[]{:S(2)}, u32[]{:S(2)}) collective-permute-start(bf16[128,2048]{1,0:T(8,128)(2,1)} %collective-permute-done.4.refs_6_), channel_id=1, source_target_pairs={{0,16},{4,20},{8,24},{12,28},{16,0},{20,4},{24,8},{28,12},{1,17},{... | collective-permute-start | bytes 1572872 | tf_op jit(solution)/shard_map/ppermute | solution.py:429
  50.1 29.7 %collective-permute-start.15 = (bf16[128,2048]{1,0:T(8,128)(2,1)}, bf16[128,2048]{1,0:T(8,128)(2,1)S(1)}, u32[]{:S(2)}, u32[]{:S(2)}) collective-permute-start(bf16[128,2048]{1,0:T(8,128)(2,1)} %collective-permute-done.14.refs_12_.refs_11_.refs_21_), channel_id=1, source_target_pairs={{0,8},{4,12},{8,0},{12,4},{16,24},{20,28},{24,16},{28,20},{1,9},{5... | collective-permute-start | bytes 1572872 | tf_op jit(solution)/shard_map/ppermute | solution.py:429
  57.3 22.8 %collective-permute-start.17 = (bf16[128,2048]{1,0:T(8,128)(2,1)}, bf16[128,2048]{1,0:T(8,128)(2,1)S(1)}, u32[]{:S(2)}, u32[]{:S(2)}) collective-permute-start(bf16[128,2048]{1,0:T(8,128)(2,1)} %collective-permute-done.16.refs_13_.refs_12_.refs_22_), channel_id=1, source_target_pairs={{0,16},{4,20},{8,24},{12,28},{16,0},{20,4},{24,8},{28,12},{1,17},{... | collective-permute-start | bytes 1572872 | tf_op jit(solution)/shard_map/ppermute | solution.py:429
  68.5 13.3 %collective-permute-start.7 = (bf16[128,2048]{1,0:T(8,128)(2,1)}, bf16[128,2048]{1,0:T(8,128)(2,1)}, u32[]{:S(2)}, u32[]{:S(2)}) collective-permute-start(bf16[128,2048]{1,0:T(8,128)(2,1)} %collective-permute-done.2.refs_2_), channel_id=1, source_target_pairs={{0,4},{4,0},{8,12},{12,8},{16,20},{20,16},{24,28},{28,24},{1,5},{5... | collective-permute-start | bytes 1572872 | tf_op jit(solution)/shard_map/ppermute | solution.py:429
  79.7 39.5 %collective-permute-start.3 = (bf16[128,2048]{1,0:T(8,128)(2,1)}, bf16[128,2048]{1,0:T(8,128)(2,1)S(1)}, u32[]{:S(2)}, u32[]{:S(2)}) collective-permute-start(bf16[128,2048]{1,0:T(8,128)(2,1)} %get-tuple-element.96.refs_8_), channel_id=1, source_target_pairs={{0,16},{4,20},{8,24},{12,28},{16,0},{20,4},{24,8},{28,12},{1,17},{... | collective-permute-start | bytes 1572872 | tf_op jit(solution)/shard_map/ppermute | solution.py:429
  80.1 39.4 %collective-permute-start.12 = (bf16[128,2048]{1,0:T(8,128)(2,1)}, bf16[128,2048]{1,0:T(8,128)(2,1)}, u32[]{:S(2)}, u32[]{:S(2)}) collective-permute-start(bf16[128,2048]{1,0:T(8,128)(2,1)} %get-tuple-element.95.refs_7_), channel_id=1, source_target_pairs={{0,4},{4,0},{8,12},{12,8},{16,20},{20,16},{24,28},{28,24},{1,5},{5... | collective-permute-start | bytes 1572872 | tf_op jit(solution)/shard_map/ppermute | solution.py:429
  81.8 38.0 %collective-permute-start.13 = (bf16[128,2048]{1,0:T(8,128)(2,1)}, bf16[128,2048]{1,0:T(8,128)(2,1)}, u32[]{:S(2)}, u32[]{:S(2)}) collective-permute-start(bf16[128,2048]{1,0:T(8,128)(2,1)} %get-tuple-element.96.refs_8_), channel_id=1, source_target_pairs={{0,4},{4,0},{8,12},{12,8},{16,20},{20,16},{24,28},{28,24},{1,5},{5... | collective-permute-start | bytes 1572872 | tf_op jit(solution)/shard_map/ppermute | solution.py:429
  117.9 16.0 %collective-permute-start.18 = (bf16[192,768]{1,0:T(8,128)(2,1)S(1)}, bf16[192,768]{1,0:T(8,128)(2,1)S(1)}, u32[]{:S(2)}, u32[]{:S(2)}) collective-permute-start(bf16[192,768]{1,0:T(8,128)(2,1)S(1)} %bitcast.105), channel_id=1, source_target_pairs={{0,8},{4,12},{8,0},{12,4},{16,24},{20,28},{24,16},{28,20},{1,9},{5... | collective-permute-start | bytes 884744 | tf_op jit(solution)/shard_map/ppermute | solution.py:429
  119.2 13.5 %collective-permute-start.22 = (bf16[192,768]{1,0:T(8,128)(2,1)S(1)}, bf16[192,768]{1,0:T(8,128)(2,1)S(1)}, u32[]{:S(2)}, u32[]{:S(2)}) collective-permute-start(bf16[192,768]{1,0:T(8,128)(2,1)S(1)} %bitcast.100), channel_id=1, source_target_pairs={{0,8},{4,12},{8,0},{12,4},{16,24},{20,28},{24,16},{28,20},{1,9},{5... | collective-permute-start | bytes 884744 | tf_op jit(solution)/shard_map/ppermute | solution.py:429
  119.5 14.7 %collective-permute-start.21 = (bf16[192,768]{1,0:T(8,128)(2,1)S(1)}, bf16[192,768]{1,0:T(8,128)(2,1)S(1)}, u32[]{:S(2)}, u32[]{:S(2)}) collective-permute-start(bf16[192,768]{1,0:T(8,128)(2,1)S(1)} %bitcast.101), channel_id=1, source_target_pairs={{0,16},{4,20},{8,24},{12,28},{16,0},{20,4},{24,8},{28,12},{1,17},{... | collective-permute-start | bytes 884744 | tf_op jit(solution)/shard_map/ppermute | solution.py:429
  119.8 16.0 %collective-permute-start.30 = (bf16[192,768]{1,0:T(8,128)(2,1)S(1)}, bf16[192,768]{1,0:T(8,128)(2,1)S(1)}, u32[]{:S(2)}, u32[]{:S(2)}) collective-permute-start(bf16[192,768]{1,0:T(8,128)(2,1)S(1)} %bitcast.106), channel_id=1, source_target_pairs={{0,4},{4,0},{8,12},{12,8},{16,20},{20,16},{24,28},{28,24},{1,5},{5... | collective-permute-start | bytes 884744 | tf_op jit(solution)/shard_map/ppermute | solution.py:429
  145.8 15.1 %collective-permute-start.34 = (bf16[384,768]{1,0:T(8,128)(2,1)}, bf16[384,768]{1,0:T(8,128)(2,1)S(1)}, u32[]{:S(2)}, u32[]{:S(2)}) collective-permute-start(bf16[384,768]{1,0:T(8,128)(2,1)} %shard_map.255.refs_7_), channel_id=1, source_target_pairs={{0,16},{4,20},{8,24},{12,28},{16,0},{20,4},{24,8},{28,12},{1,17},{... | collective-permute-start | bytes 1769480 | tf_op jit(solution)/shard_map/ppermute | solution.py:429
  153.3 31.7 %collective-permute-start.33 = (bf16[384,768]{1,0:T(8,128)(2,1)S(1)}, bf16[384,768]{1,0:T(8,128)(2,1)S(1)}, u32[]{:S(2)}, u32[]{:S(2)}) collective-permute-start(bf16[384,768]{1,0:T(8,128)(2,1)S(1)} %copy-done.6), channel_id=1, source_target_pairs={{0,8},{4,12},{8,0},{12,4},{16,24},{20,28},{24,16},{28,20},{1,9},{5... | collective-permute-start | bytes 1769480 | tf_op jit(solution)/shard_map/ppermute | solution.py:429
  153.6 30.9 %collective-permute-start.37 = (bf16[384,768]{1,0:T(8,128)(2,1)S(1)}, bf16[384,768]{1,0:T(8,128)(2,1)}, u32[]{:S(2)}, u32[]{:S(2)}) collective-permute-start(bf16[384,768]{1,0:T(8,128)(2,1)S(1)} %copy-done.5), channel_id=1, source_target_pairs={{0,8},{4,12},{8,0},{12,4},{16,24},{20,28},{24,16},{28,20},{1,9},{5... | collective-permute-start | bytes 1769480 | tf_op jit(solution)/shard_map/ppermute | solution.py:429
  154.8 30.5 %collective-permute-start.36 = (bf16[384,768]{1,0:T(8,128)(2,1)S(1)}, bf16[384,768]{1,0:T(8,128)(2,1)}, u32[]{:S(2)}, u32[]{:S(2)}) collective-permute-start(bf16[384,768]{1,0:T(8,128)(2,1)S(1)} %copy-done.5), channel_id=1, source_target_pairs={{0,16},{4,20},{8,24},{12,28},{16,0},{20,4},{24,8},{28,12},{1,17},{... | collective-permute-start | bytes 1769480 | tf_op jit(solution)/shard_map/ppermute | solution.py:429
  156.0 29.8 %collective-permute-start.45 = (bf16[384,768]{1,0:T(8,128)(2,1)S(1)}, bf16[384,768]{1,0:T(8,128)(2,1)S(1)}, u32[]{:S(2)}, u32[]{:S(2)}) collective-permute-start(bf16[384,768]{1,0:T(8,128)(2,1)S(1)} %copy-done.6), channel_id=1, source_target_pairs={{0,4},{4,0},{8,12},{12,8},{16,20},{20,16},{24,28},{28,24},{1,5},{5... | collective-permute-start | bytes 1769480 | tf_op jit(solution)/shard_map/ppermute | solution.py:429
  160.9 41.1 %collective-permute-start.46 = (bf16[384,768]{1,0:T(8,128)(2,1)S(1)}, bf16[384,768]{1,0:T(8,128)(2,1)S(1)}, u32[]{:S(2)}, u32[]{:S(2)}) collective-permute-start(bf16[384,768]{1,0:T(8,128)(2,1)S(1)} %copy-done.5), channel_id=1, source_target_pairs={{0,4},{4,0},{8,12},{12,8},{16,20},{20,16},{24,28},{28,24},{1,5},{5... | collective-permute-start | bytes 1769480 | tf_op jit(solution)/shard_map/ppermute | solution.py:429
  184.5 22.6 %collective-permute-start.35 = (bf16[384,768]{1,0:T(8,128)(2,1)S(1)}, bf16[384,768]{1,0:T(8,128)(2,1)}, u32[]{:S(2)}, u32[]{:S(2)}) collective-permute-start(bf16[384,768]{1,0:T(8,128)(2,1)S(1)} %collective-permute-done.34.refs_5_), channel_id=1, source_target_pairs={{0,8},{4,12},{8,0},{12,4},{16,24},{20,28},{24,16},{28,20},{1,9},{5... | collective-permute-start | bytes 1769480 | tf_op jit(solution)/shard_map/ppermute | solution.py:429
  185.0 22.3 %collective-permute-start.38 = (bf16[384,768]{1,0:T(8,128)(2,1)}, bf16[384,768]{1,0:T(8,128)(2,1)}, u32[]{:S(2)}, u32[]{:S(2)}) collective-permute-start(bf16[384,768]{1,0:T(8,128)(2,1)} %collective-permute-done.37.refs_6_), channel_id=1, source_target_pairs={{0,16},{4,20},{8,24},{12,28},{16,0},{20,4},{24,8},{28,12},{1,17},{... | collective-permute-start | bytes 1769480 | tf_op jit(solution)/shard_map/ppermute | solution.py:429
  185.3 22.5 %collective-permute-start.39 = (bf16[384,768]{1,0:T(8,128)(2,1)S(1)}, bf16[384,768]{1,0:T(8,128)(2,1)}, u32[]{:S(2)}, u32[]{:S(2)}) collective-permute-start(bf16[384,768]{1,0:T(8,128)(2,1)S(1)} %collective-permute-done.33.refs_1_), channel_id=1, source_target_pairs={{0,4},{4,0},{8,12},{12,8},{16,20},{20,16},{24,28},{28,24},{1,5},{5... | collective-permute-start | bytes 1769480 | tf_op jit(solution)/shard_map/ppermute | solution.py:429
  185.8 22.0 %collective-permute-start.41 = (bf16[384,768]{1,0:T(8,128)(2,1)}, bf16[384,768]{1,0:T(8,128)(2,1)}, u32[]{:S(2)}, u32[]{:S(2)}) collective-permute-start(bf16[384,768]{1,0:T(8,128)(2,1)} %collective-permute-done.36.refs_3_), channel_id=1, source_target_pairs={{0,4},{4,0},{8,12},{12,8},{16,20},{20,16},{24,28},{28,24},{1,5},{5... | collective-permute-start | bytes 1769480 | tf_op jit(solution)/shard_map/ppermute | solution.py:429
  202.9 26.4 %collective-permute-start.47 = (bf16[2048,256]{1,0:T(8,128)(2,1)}, bf16[2048,256]{1,0:T(8,128)(2,1)S(1)}, u32[]{:S(2)}, u32[]{:S(2)}) collective-permute-start(bf16[2048,256]{1,0:T(8,128)(2,1)} %get-tuple-element.99.refs_25_), channel_id=1, source_target_pairs={{0,4},{4,0},{8,12},{12,8},{16,20},{20,16},{24,28},{28,24},{1,5},{5... | collective-permute-start | bytes 3145736 | tf_op jit(solution)/shard_map/ppermute | solution.py:429
  203.3 15.7 %all-to-all-start = ((bf16[8,256,256]{2,1,0:T(8,128)(2,1)}), bf16[8,256,256]{2,1,0:T(8,128)(2,1)S(1)}, u32[]{:S(2)}, u32[]{:S(2)}) async-start(bf16[8,256,256]{2,1,0:T(8,128)(2,1)} %bitcast.96), calls=%async_computation | async-start | bytes 2097152 | tf_op jit(solution)/shard_map/all_to_all | solution.py:1262
  207.0 158.9 %all-gather.11.cloned.1.call-start = ((), (), s32[]{:S(2)}) async-start(), calls=%async_computation.5 | async-start | bytes 5242880 | tf_op jit(solution)/shard_map/all_gather | solution.py:1179
  240.9 15.8 %collective-permute-start.50 = (bf16[128,2048]{1,0:T(8,128)(2,1)}, bf16[128,2048]{1,0:T(8,128)(2,1)S(1)}, u32[]{:S(2)}, u32[]{:S(2)}) collective-permute-start(bf16[128,2048]{1,0:T(8,128)(2,1)} %get-tuple-element.107.refs_11_.refs_10_.refs_16_), channel_id=1, source_target_pairs={{0,8},{4,12},{8,0},{12,4},{16,24},{20,28},{24,16},{28,20},{1,9},{5... | collective-permute-start | bytes 1572872 | tf_op jit(solution)/shard_map/ppermute | solution.py:429
  243.3 47.5 %collective-permute-start.53 = (bf16[1024,2432]{1,0:T(8,128)(2,1)}, bf16[1024,2432]{1,0:T(8,128)(2,1)}, u32[]{:S(2)}, u32[]{:S(2)}) collective-permute-start(bf16[1024,2432]{1,0:T(8,128)(2,1)} %shard_map.261.refs_5_.refs_3_.refs_4_), channel_id=1, source_target_pairs={{0,4},{4,0},{8,12},{12,8},{16,20},{20,16},{24,28},{28,24},{1,5},{5... | collective-permute-start | bytes 14942216 | tf_op jit(solution)/shard_map/ppermute | solution.py:429
  250.0 34.5 %collective-permute-start.49 = (bf16[128,2048]{1,0:T(8,128)(2,1)S(1)}, bf16[128,2048]{1,0:T(8,128)(2,1)S(1)}, u32[]{:S(2)}, u32[]{:S(2)}) collective-permute-start(bf16[128,2048]{1,0:T(8,128)(2,1)S(1)} %collective-permute-done.48.refs_8_.refs_7_.refs_13_), channel_id=1, source_target_pairs={{0,8},{4,12},{8,0},{12,4},{16,24},{20,28},{24,16},{28,20},{1,9},{5... | collective-permute-start | bytes 1572872 | tf_op jit(solution)/shard_map/ppermute | solution.py:429
  256.7 27.9 %collective-permute-start.51 = (bf16[128,2048]{1,0:T(8,128)(2,1)S(1)}, bf16[128,2048]{1,0:T(8,128)(2,1)S(1)}, u32[]{:S(2)}, u32[]{:S(2)}) collective-permute-start(bf16[128,2048]{1,0:T(8,128)(2,1)S(1)} %collective-permute-done.50.refs_9_.refs_8_.refs_14_), channel_id=1, source_target_pairs={{0,16},{4,20},{8,24},{12,28},{16,0},{20,4},{24,8},{28,12},{1,17},{... | collective-permute-start | bytes 1572872 | tf_op jit(solution)/shard_map/ppermute | solution.py:429
  286.9 37.4 %collective-permute-start.56 = (bf16[128,2048]{1,0:T(8,128)(2,1)}, bf16[128,2048]{1,0:T(8,128)(2,1)S(1)}, u32[]{:S(2)}, u32[]{:S(2)}) collective-permute-start(bf16[128,2048]{1,0:T(8,128)(2,1)} %get-tuple-element.205.refs_14_.refs_13_.refs_23_), channel_id=1, source_target_pairs={{0,8},{4,12},{8,0},{12,4},{16,24},{20,28},{24,16},{28,20},{1,9},{5... | collective-permute-start | bytes 1572872 | tf_op jit(solution)/shard_map/ppermute | solution.py:429
  288.2 36.1 %collective-permute-start.57 = (bf16[128,2048]{1,0:T(8,128)(2,1)}, bf16[128,2048]{1,0:T(8,128)(2,1)S(1)}, u32[]{:S(2)}, u32[]{:S(2)}) collective-permute-start(bf16[128,2048]{1,0:T(8,128)(2,1)} %get-tuple-element.204.refs_15_.refs_14_.refs_24_), channel_id=1, source_target_pairs={{0,16},{4,20},{8,24},{12,28},{16,0},{20,4},{24,8},{28,12},{1,17},{... | collective-permute-start | bytes 1572872 | tf_op jit(solution)/shard_map/ppermute | solution.py:429
  290.6 33.7 %collective-permute-start.54 = (bf16[128,2048]{1,0:T(8,128)(2,1)S(1)}, bf16[128,2048]{1,0:T(8,128)(2,1)S(1)}, u32[]{:S(2)}, u32[]{:S(2)}) collective-permute-start(bf16[128,2048]{1,0:T(8,128)(2,1)S(1)} %copy-done.47), channel_id=1, source_target_pairs={{0,8},{4,12},{8,0},{12,4},{16,24},{20,28},{24,16},{28,20},{1,9},{5... | collective-permute-start | bytes 1572872 | tf_op jit(solution)/shard_map/ppermute | solution.py:429
  290.9 33.5 %collective-permute-start.55 = (bf16[128,2048]{1,0:T(8,128)(2,1)S(1)}, bf16[128,2048]{1,0:T(8,128)(2,1)}, u32[]{:S(2)}, u32[]{:S(2)}) collective-permute-start(bf16[128,2048]{1,0:T(8,128)(2,1)S(1)} %copy-done.48), channel_id=1, source_target_pairs={{0,16},{4,20},{8,24},{12,28},{16,0},{20,4},{24,8},{28,12},{1,17},{... | collective-permute-start | bytes 1572872 | tf_op jit(solution)/shard_map/ppermute | solution.py:429
  365.8 14.4 %collective-permute-start.58 = (bf16[2048,1024]{1,0:T(8,128)(2,1)}, bf16[2048,1024]{1,0:T(8,128)(2,1)}, u32[]{:S(2)}, u32[]{:S(2)}) collective-permute-start(bf16[2048,1024]{1,0:T(8,128)(2,1)} %shard_map.266.refs_3_), channel_id=1, source_target_pairs={{0,4},{4,0},{8,12},{12,8},{16,20},{20,16},{24,28},{28,24},{1,5},{5... | collective-permute-start | bytes 12582920 | tf_op jit(solution)/shard_map/ppermute | solution.py:429
  393.7 27.9 %collective-permute-start.59 = (bf16[256,2304]{1,0:T(8,128)(2,1)}, bf16[256,2304]{1,0:T(8,128)(2,1)S(1)}, u32[]{:S(2)}, u32[]{:S(2)}) collective-permute-start(bf16[256,2304]{1,0:T(8,128)(2,1)} %get-tuple-element.124), channel_id=1, source_target_pairs={{0,8},{4,12},{8,0},{12,4},{16,24},{20,28},{24,16},{28,20},{1,9},{5... | collective-permute-start | bytes 3538952 | tf_op jit(solution)/shard_map/ppermute | solution.py:429
  395.0 27.5 %collective-permute-start.60 = (bf16[256,2304]{1,0:T(8,128)(2,1)}, bf16[256,2304]{1,0:T(8,128)(2,1)S(1)}, u32[]{:S(2)}, u32[]{:S(2)}) collective-permute-start(bf16[256,2304]{1,0:T(8,128)(2,1)} %get-tuple-element.125), channel_id=1, source_target_pairs={{0,16},{4,20},{8,24},{12,28},{16,0},{20,4},{24,8},{28,12},{1,17},{... | collective-permute-start | bytes 3538952 | tf_op jit(solution)/shard_map/ppermute | solution.py:429
  424.8 13.8 %collective-permute-start.61 = (bf16[128,2304]{1,0:T(8,128)(2,1)S(1)}, bf16[128,2304]{1,0:T(8,128)(2,1)S(1)}, u32[]{:S(2)}, u32[]{:S(2)}) collective-permute-start(bf16[128,2304]{1,0:T(8,128)(2,1)S(1)} %get-tuple-element.197.refs_6_), channel_id=1, source_target_pairs={{0,16},{4,20},{8,24},{12,28},{16,0},{20,4},{24,8},{28,12},{1,17},{... | collective-permute-start | bytes 1769480 | tf_op jit(solution)/shard_map/ppermute | solution.py:429
  426.1 13.4 %collective-permute-start.62 = (bf16[128,2304]{1,0:T(8,128)(2,1)S(1)}, bf16[128,2304]{1,0:T(8,128)(2,1)S(1)}, u32[]{:S(2)}, u32[]{:S(2)}) collective-permute-start(bf16[128,2304]{1,0:T(8,128)(2,1)S(1)} %get-tuple-element.196.refs_7_), channel_id=1, source_target_pairs={{0,8},{4,12},{8,0},{12,4},{16,24},{20,28},{24,16},{28,20},{1,9},{5... | collective-permute-start | bytes 1769480 | tf_op jit(solution)/shard_map/ppermute | solution.py:429
  455.9 18.1 %all-to-all-start.1 = ((bf16[256,8,256]{2,0,1:T(8,128)(2,1)}), bf16[256,8,256]{2,0,1:T(8,128)(2,1)S(1)}, u32[]{:S(2)}, u32[]{:S(2)}) async-start(bf16[256,8,256]{2,0,1:T(8,128)(2,1)} %bitcast.74), calls=%async_computation.1 | async-start | bytes 2097152 | tf_op jit(solution)/shard_map/all_to_all | solution.py:1372
  462.1 48.1 %collective-permute-start.68 = (bf16[2048,768]{1,0:T(8,128)(2,1)}, bf16[2048,768]{1,0:T(8,128)(2,1)}, u32[]{:S(2)}, u32[]{:S(2)}) collective-permute-start(bf16[2048,768]{1,0:T(8,128)(2,1)} %get-tuple-element.139.refs_3_), channel_id=1, source_target_pairs={{0,4},{4,0},{8,12},{12,8},{16,20},{20,16},{24,28},{28,24},{1,5},{5... | collective-permute-start | bytes 9437192 | tf_op jit(solution)/shard_map/ppermute | solution.py:429
  475.0 31.9 %collective-permute-start.65 = (bf16[256,2176]{1,0:T(8,128)(2,1)}, bf16[256,2176]{1,0:T(8,128)(2,1)}, u32[]{:S(2)}, u32[]{:S(2)}) collective-permute-start(bf16[256,2176]{1,0:T(8,128)(2,1)} %shard_map.276), channel_id=1, source_target_pairs={{0,16},{4,20},{8,24},{12,28},{16,0},{20,4},{24,8},{28,12},{1,17},{... | collective-permute-start | bytes 3342344 | tf_op jit(solution)/shard_map/ppermute | solution.py:429
  476.2 31.6 %collective-permute-start.63 = (bf16[256,2176]{1,0:T(8,128)(2,1)S(1)}, bf16[256,2176]{1,0:T(8,128)(2,1)}, u32[]{:S(2)}, u32[]{:S(2)}) collective-permute-start(bf16[256,2176]{1,0:T(8,128)(2,1)S(1)} %copy-done.7), channel_id=1, source_target_pairs={{0,8},{4,12},{8,0},{12,4},{16,24},{20,28},{24,16},{28,20},{1,9},{5... | collective-permute-start | bytes 3342344 | tf_op jit(solution)/shard_map/ppermute | solution.py:429
  506.8 16.4 %collective-permute-start.70 = (bf16[256,640]{1,0:T(8,128)(2,1)}, bf16[256,640]{1,0:T(8,128)(2,1)}, u32[]{:S(2)}, u32[]{:S(2)}) collective-permute-start(bf16[256,640]{1,0:T(8,128)(2,1)} %shard_map.279), channel_id=1, source_target_pairs={{0,16},{4,20},{8,24},{12,28},{16,0},{20,4},{24,8},{28,12},{1,17},{... | collective-permute-start | bytes 983048 | tf_op jit(solution)/shard_map/ppermute | solution.py:429
  507.8 16.0 %collective-permute-start.69 = (bf16[256,640]{1,0:T(8,128)(2,1)}, bf16[256,640]{1,0:T(8,128)(2,1)}, u32[]{:S(2)}, u32[]{:S(2)}) collective-permute-start(bf16[256,640]{1,0:T(8,128)(2,1)} %shard_map.278), channel_id=1, source_target_pairs={{0,8},{4,12},{8,0},{12,4},{16,24},{20,28},{24,16},{28,20},{1,9},{5... | collective-permute-start | bytes 983048 | tf_op jit(solution)/shard_map/ppermute | solution.py:429
  510.2 25.0 %collective-permute-start.64 = (bf16[128,2176]{1,0:T(8,128)(2,1)}, bf16[128,2176]{1,0:T(8,128)(2,1)S(1)}, u32[]{:S(2)}, u32[]{:S(2)}) collective-permute-start(bf16[128,2176]{1,0:T(8,128)(2,1)} %get-tuple-element.200), channel_id=1, source_target_pairs={{0,16},{4,20},{8,24},{12,28},{16,0},{20,4},{24,8},{28,12},{1,17},{... | collective-permute-start | bytes 1671176 | tf_op jit(solution)/shard_map/ppermute | solution.py:429
  510.7 25.2 %collective-permute-start.66 = (bf16[128,2176]{1,0:T(8,128)(2,1)S(1)}, bf16[128,2176]{1,0:T(8,128)(2,1)}, u32[]{:S(2)}, u32[]{:S(2)}) collective-permute-start(bf16[128,2176]{1,0:T(8,128)(2,1)S(1)} %get-tuple-element.201), channel_id=1, source_target_pairs={{0,8},{4,12},{8,0},{12,4},{16,24},{20,28},{24,16},{28,20},{1,9},{5... | collective-permute-start | bytes 1671176 | tf_op jit(solution)/shard_map/ppermute | solution.py:429
  516.4 23.7 %collective-permute-start.72 = (bf16[256,384]{1,0:T(8,128)(2,1)}, bf16[256,384]{1,0:T(8,128)(2,1)}, u32[]{:S(2)}, u32[]{:S(2)}) collective-permute-start(bf16[256,384]{1,0:T(8,128)(2,1)} %get-tuple-element.140.refs_5_), channel_id=1, source_target_pairs={{0,8},{4,12},{8,0},{12,4},{16,24},{20,28},{24,16},{28,20},{1,9},{5... | collective-permute-start | bytes 589832 | tf_op jit(solution)/shard_map/ppermute | solution.py:429
  523.3 16.9 %collective-permute-start.73 = (bf16[256,384]{1,0:T(8,128)(2,1)}, bf16[256,384]{1,0:T(8,128)(2,1)}, u32[]{:S(2)}, u32[]{:S(2)}) collective-permute-start(bf16[256,384]{1,0:T(8,128)(2,1)} %get-tuple-element.147), channel_id=1, source_target_pairs={{0,16},{4,20},{8,24},{12,28},{16,0},{20,4},{24,8},{28,12},{1,17},{... | collective-permute-start | bytes 589832 | tf_op jit(solution)/shard_map/ppermute | solution.py:429
  523.8 19.5 %collective-permute-start.74 = (bf16[256,384]{1,0:T(8,128)(2,1)}, bf16[256,384]{1,0:T(8,128)(2,1)}, u32[]{:S(2)}, u32[]{:S(2)}) collective-permute-start(bf16[256,384]{1,0:T(8,128)(2,1)} %get-tuple-element.148), channel_id=1, source_target_pairs={{0,24},{4,28},{8,16},{12,20},{16,8},{20,12},{24,0},{28,4},{1,25},{... | collective-permute-start | bytes 589832 | tf_op jit(solution)/shard_map/ppermute | solution.py:429
  566.9 23.4 %collective-permute-start.78 = (bf16[256,2048]{1,0:T(8,128)(2,1)}, bf16[256,2048]{1,0:T(8,128)(2,1)}, u32[]{:S(2)}, u32[]{:S(2)}) collective-permute-start(bf16[256,2048]{1,0:T(8,128)(2,1)} %get-tuple-element.160.refs_36_), channel_id=1, source_target_pairs={{0,8},{4,12},{8,0},{12,4},{16,24},{20,28},{24,16},{28,20},{1,9},{5... | collective-permute-start | bytes 3145736 | tf_op jit(solution)/shard_map/ppermute | solution.py:429
  568.1 22.9 %collective-permute-start.79 = (bf16[256,2048]{1,0:T(8,128)(2,1)}, bf16[256,2048]{1,0:T(8,128)(2,1)}, u32[]{:S(2)}, u32[]{:S(2)}) collective-permute-start(bf16[256,2048]{1,0:T(8,128)(2,1)} %get-tuple-element.162), channel_id=1, source_target_pairs={{0,16},{4,20},{8,24},{12,28},{16,0},{20,4},{24,8},{28,12},{1,17},{... | collective-permute-start | bytes 3145736 | tf_op jit(solution)/shard_map/ppermute | solution.py:429
  588.9 19.1 %collective-permute-start.83 = (bf16[2,704,128]{2,1,0:T(8,128)(2,1)}, bf16[2,704,128]{2,1,0:T(8,128)(2,1)S(1)}, u32[]{:S(2)}, u32[]{:S(2)}) collective-permute-start(bf16[2,704,128]{2,1,0:T(8,128)(2,1)} %get-tuple-element.166), channel_id=1, source_target_pairs={{0,1},{1,0},{2,3},{3,2},{4,5},{5,4},{6,7},{7,6},{8,9},{9,8},{10,11... | collective-permute-start | bytes 1081352 | tf_op jit(solution)/shard_map/ppermute | solution.py:1384
  592.6 17.5 %collective-permute-start.80 = (bf16[128,2048]{1,0:T(8,128)(2,1)S(1)}, bf16[128,2048]{1,0:T(8,128)(2,1)S(1)}, u32[]{:S(2)}, u32[]{:S(2)}) collective-permute-start(bf16[128,2048]{1,0:T(8,128)(2,1)S(1)} %get-tuple-element.203.refs_1_), channel_id=1, source_target_pairs={{0,16},{4,20},{8,24},{12,28},{16,0},{20,4},{24,8},{28,12},{1,17},{... | collective-permute-start | bytes 1572872 | tf_op jit(solution)/shard_map/ppermute | solution.py:429
  593.6 17.3 %collective-permute-start.81 = (bf16[128,2048]{1,0:T(8,128)(2,1)S(1)}, bf16[128,2048]{1,0:T(8,128)(2,1)S(1)}, u32[]{:S(2)}, u32[]{:S(2)}) collective-permute-start(bf16[128,2048]{1,0:T(8,128)(2,1)S(1)} %get-tuple-element.202.refs_2_), channel_id=1, source_target_pairs={{0,8},{4,12},{8,0},{12,4},{16,24},{20,28},{24,16},{28,20},{1,9},{5... | collective-permute-start | bytes 1572872 | tf_op jit(solution)/shard_map/ppermute | solution.py:429
  625.2 17.6 %collective-permute-start.95 = (bf16[4,768,128]{2,1,0:T(8,128)(2,1)}, bf16[4,768,128]{2,1,0:T(8,128)(2,1)}, u32[]{:S(2)}, u32[]{:S(2)}) collective-permute-start(bf16[4,768,128]{2,1,0:T(8,128)(2,1)} %pad_maximum_fusion.1), channel_id=1, source_target_pairs={{0,4},{4,0},{8,12},{12,8},{16,20},{20,16},{24,28},{28,24},{1,5},{5... | collective-permute-start | bytes 2359304 | tf_op jit(solution)/shard_map/ppermute | solution.py:429
  630.2 16.7 %collective-permute-start.88 = (bf16[4,704,128]{2,1,0:T(8,128)(2,1)}, bf16[4,704,128]{2,1,0:T(8,128)(2,1)}, u32[]{:S(2)}, u32[]{:S(2)}) collective-permute-start(bf16[4,704,128]{2,1,0:T(8,128)(2,1)} %pad_maximum_fusion.2), channel_id=1, source_target_pairs={{0,4},{4,0},{8,12},{12,8},{16,20},{20,16},{24,28},{28,24},{1,5},{5... | collective-permute-start | bytes 2162696 | tf_op jit(solution)/shard_map/ppermute | solution.py:429
  (114 other events, 1253.4 us)
Sparse Core Ops, SparseCore 0:
  12.0 98.1 all-gather.4
  111.7 92.1 all-gather.8
  205.5 79.0 all-gather.6
  287.0 78.7 all-gather.10

commit v4 on v3

--- a/solution.py
+++ b/solution.py
@@ -558,7 +558,7 @@
         row, lane = up_slot(k)
         row += at
         pairs.append((b_qkv.at[here, column], out.at[row : row + 16, lane : lane + LANES]))
-    at += 64
+    at += 32
     for k in range(16):
         row, lane = at + (k // 6) * share, (k % 6) * LANES
         pairs.append(
@@ -568,9 +568,8 @@
 
 
 def up_slot(k):
-    if k < 4:
-        return (k // 2) * 16, 512 + (k % 2) * LANES
-    return 32 + ((k - 4) // 4) * 16, ((k - 4) % 4) * LANES
+    row = (k // 2) * 16 if k < 4 else 32 + 2 * 64 + ((k - 4) // 2) * 16
+    return row, 512 + (k % 2) * LANES
 
 
 def cut_rest_kernel(sizes, scalars, w_gu, w_down, a_down, b_gu, down, *refs):
@@ -1159,7 +1158,7 @@
         norm_kernel, scalars, [stream], [whole_spec((rows, width))],
         [sds((half, width))] * 2, [whole_spec((half, width))] * 2,
     )
-    tall_rows = quarter + 2 * share + 3 * share
+    tall_rows = quarter + share + 32 + 3 * share
     first_part = call(
         functools.partial(cut_first_kernel, (share, quarter, width)), scalars,
         [w_qkv, w_out, a_qkv, a_out, a_gu, b_out, b_down, b_qkv], [ANY] * 8,
@@ -1191,7 +1190,10 @@
 
     pieces_small = gather_halves(rows_of(quarter, share + 32, 0, 2), rows_of(quarter, share + 32, 2, 2))
     pieces_small += [swap(piece, 1) for piece in pieces_small]
-    ups_qkv = rows_of(quarter + share, 64, 0, 4)
+    ups_qkv = jnp.concatenate(
+        [by_z[:, quarter + share + row : quarter + share + row + 16, lane : lane + LANES] for row, lane in map(up_slot, range(12))],
+        axis=1,
+    )
     full_a_qkv, full_a_gu, full_a_out, full_b_out, full_b_down = call(
         functools.partial(unpack_small_kernel, share, quarter), scalars, pieces_small,
         [whole_spec((2 * share + 64, 3 * span))] * 16,
@@ -1200,7 +1202,7 @@
         [whole_spec((width, 3 * latent)), whole_spec((width, 2 * latent)), whole_spec((width, latent))]
         + [whole_spec((latent, width))] * 2,
     )
-    at = quarter + 2 * share
+    at = quarter + share + 32
     out_a, out_b = rows_of(at, 3 * share, 0, 2), rows_of(at, 3 * share, 2, 2)
     pieces_out = gather_halves(hold(out_a, [pieces_small[1]]), hold(out_b, [pieces_small[3]]))
     pieces_out += [swap(piece, 1) for piece in pieces_out]
@@ -1211,12 +1213,7 @@
     ups_oth = swap(ups_qkv, 1)
 
     def qkv_up(piece):
-        piece = piece.reshape(z_count, 64, 3 * span)
-        parts = []
-        for k in range(12):
-            row, lane = up_slot(k)
-            parts.append(piece[:, row : row + 16, lane : lane + LANES])
-        return jnp.concatenate(parts, axis=1).transpose(1, 0, 2).reshape(192, z_count * LANES)
+        return piece.transpose(1, 0, 2).reshape(192, z_count * LANES)
 
     mine, theirs = qkv_up(ups_qkv), qkv_up(ups_oth)
     up_chip = jnp.where(
@@ -1351,7 +1348,7 @@
     pass_on, kept, *more = feed(1, weights, 1, sums[1], True)
     results[1][0][1], results[1][1][1] = more[:2], more[2:]
     by_x, by_y, got_y, got_x, passed = scatter_rest(send_x, send_y, pass_on)
-    down_x, down_y = down_half(1, 0, BF, down_first[0], passed)
+    down_x, down_y = (hold(x, [got_y, got_x]) for x in down_half(1, 0, BF, down_first[0], passed))
     halfspec = lambda n: pl.BlockSpec((half, n), lambda *_: (0, 0))
     second_grad, mixed_grad, *packs = call(
         back_middle_kernel, scalars,
@@ -1396,9 +1393,7 @@
             [sds(shape, F32) for shape in shapes], [whole_spec(shape) for shape in shapes], ties=ties,
         )
 
-    *down_by, _ = scatter_rest(
-        hold(down_x, [mixed_grad_h]), hold(down_y, [mixed_grad_h]), down_on
-    )
+    *down_by, down_passed = scatter_rest(down_x, down_y, down_on)
     middle = [packs[0]] + [swap(hold(packs[k], [mixed_grad_h]), 2 * k) for k in (1, 2, 3)]
 
     result = pl.BlockSpec((3, group, HEAD_DIM), lambda h, _: (0, 0, h))
@@ -1410,7 +1405,7 @@
         [sds((3, group, span))] * 2 + [sds((3, latent, span), F32)],
         [result, result, pl.BlockSpec((3, latent, HEAD_DIM), lambda h, _: (0, 0, h))],
         scratch=[pltpu.VMEM((length, HEAD_DIM), F32)] * 3, grid=(heads_dev,),
-        cost=(10 * heads_dev * length * length * HEAD_DIM, 16 * 2**20), ties=[down_on],
+        cost=(10 * heads_dev * length * length * HEAD_DIM, 16 * 2**20), ties=down_passed,
     )
     grads_b = swap(grads_b, 1)
     qkv_oth = swap(qkv_own, 1)
@@ -1425,7 +1420,7 @@
         [whole_spec((3, group, span))] * 2 + [whole_spec((3 * latent, span))] * 2,
         [sds((rows, 3 * latent))] * 3 + [sds((rows, 3 * latent), F32)],
         [whole_spec((rows, 3 * latent))] * 4,
-        cost=(4 * group * span * 3 * latent, 4 * 2**20),
+        cost=(4 * group * span * 3 * latent, 4 * 2**20), ties=[z_down],
     )
 
     def back_qkv(at, kind, ties):
@@ -1476,12 +1471,12 @@
         sds((rows, width), F32), tall,
         cost=(2 * rows * width * 3 * latent, 12 * 2**20),
     )
-    ff_total = line_sum(ff_mine, *ff_rest, [])
-    total = line_sum(*along_line(keep, send, []), [got_y, got_x])
     activations = second + (wide[:, :width] + dot(hold(z_down, passed), full_b_down))
+    ff_total = line_sum(ff_mine, *ff_rest, [activations])
+    total = line_sum(*along_line(keep, send, []), [input_grad])
     g_b_gu, g_a_down = spread(
         ff_total, (("columns", 2 * latent, ff_dev // LANES), ("rows", ff_dev, 1)),
-        [(2 * latent, ff_z), (ff_z, latent)], [input_grad],
+        [(2 * latent, ff_z), (ff_z, latent)], [],
     )
     low = LANES // 2
     g_a_gu, g_b_down, g_a_out, g_b_out, g_a_qkv, g_b_qkv = spread(
@@ -1494,7 +1489,7 @@
             (quarter, 2 * latent), (latent, quarter), (quarter, latent), (latent, quarter),
             (quarter, 3 * latent), (3 * latent, quarter),
         ],
-        [input_grad],
+        [g_b_gu],
     )
 
     return (

time: 668 us -> 650 us (0.973)
  waiting for transfers between devices: 192 us -> 161 us
  starting transfers between devices: 97.7 us -> 108 us
    ppermute x92, waiting for transfers between devices: 92.5 us -> 66 us  [swap(): return lax.ppermute(value, 'seq', [(i, i ^ bits) for i in range(PLANE)])]
    ppermute x92, starting transfers between devices: 85.3 us -> 98.3 us  [swap(): return lax.ppermute(value, 'seq', [(i, i ^ bits) for i in range(PLANE)])]
    unnamed x175 -> x155, local copies, waits for them, and re-layouts: 13.4 us -> 15.4 us
  transfers between devices with their start and end apart: 102 -> 102, of which waited for: 30 -> 22; matrix products, arithmetic and copies ran while one was open for 5% -> 5% of each run, Pallas kernels for 39% -> 44%
where the time goes in v4:
time: 650 us; the launch traced here: 639 us
  Pallas kernels  302 us (46%)
  waiting for transfers between devices  161 us (25%)
  starting transfers between devices  108 us (17%)
  local copies, waits for them, and re-layouts  25.7 us (4%)
  other arithmetic  24.3 us (4%)
  between operations  15 us (2%)
    pallas_call x29, Pallas kernels, call(): pl.pallas_call(run, grid_spec=pltpu.PrefetchScalarGridSpec(num_scalar_pre...  302 us
    ppermute x92, starting transfers between devices, swap(): return lax.ppermute(value, 'seq', [(i, i ^ bits) for i in range(PLANE)])  98.3 us
    ppermute x92, waiting for transfers between devices, swap(): return lax.ppermute(value, 'seq', [(i, i ^ bits) for i in range(PLANE)])  66 us
    all_gather x2, waiting for transfers between devices, plane_shards(): lax.all_gather(part, 'fsdp', axis=0, tiled=True)  41.4 us
    all_gather x1, waiting for transfers between devices, plane_shards(): first_all = lax.all_gather(first_part, 'fsdp', axis=0, tiled=True)  34.9 us
    unnamed x155, local copies, waits for them, and re-layouts  15.4 us
  transfers between devices with their start and end apart: 102, of which 22 were waited for; matrix products, arithmetic and copies ran while one was open for 5% of the time, Pallas kernels for 44%

profile of v4, /device:TPU:1, one launch (start us, length us, event | category | flops | bytes accessed | tf_op | source)
XLA Modules:
  0.0 639.3 jit_solution(769400723565412374)
XLA Ops:
  8.5 3.3 shard_map.250.refs_5_
  11.9 4.4 shard_map.259
  16.4 3.5 shard_map.249
  23.7 10.3 %collective-permute-done.1.refs_5_ = bf16[128,2048]{1,0:T(8,128)(2,1)S(1)} collective-permute-done((bf16[128,2048]{1,0:T(8,128)(2,1)}, bf16[128,2048]{1,0:T(8,128)(2,1)S(1)}, u32[]{:S(2)}, u32[]{:S(2)}) %collective-permute-start.1) | collective-permute-done | bytes 524320 | tf_op jit(solution)/shard_map/ppermute | solution.py:429
  36.3 8.9 %collective-permute-done.14.refs_12_.refs_11_.refs_21_ = bf16[128,2048]{1,0:T(8,128)(2,1)} collective-permute-done((bf16[128,2048]{1,0:T(8,128)(2,1)S(1)}, bf16[128,2048]{1,0:T(8,128)(2,1)}, u32[]{:S(2)}, u32[]{:S(2)}) %collective-permute-start.14) | collective-permute-done | bytes 524320 | tf_op jit(solution)/shard_map/ppermute | solution.py:429
  47.6 9.6 %collective-permute-done.2.refs_2_ = bf16[128,2048]{1,0:T(8,128)(2,1)} collective-permute-done((bf16[128,2048]{1,0:T(8,128)(2,1)S(1)}, bf16[128,2048]{1,0:T(8,128)(2,1)}, u32[]{:S(2)}, u32[]{:S(2)}) %collective-permute-start.2) | collective-permute-done | bytes 524320 | tf_op jit(solution)/shard_map/ppermute | solution.py:429
  57.2 3.3 collective-permute-start.7
  62.0 6.5 %collective-permute-done.15.refs_3_.refs_13_.refs_10_.refs_18_ = bf16[128,2048]{1,0:T(8,128)(2,1)S(1)} collective-permute-done((bf16[128,2048]{1,0:T(8,128)(2,1)}, bf16[128,2048]{1,0:T(8,128)(2,1)S(1)}, u32[]{:S(2)}, u32[]{:S(2)}) %collective-permute-start.15) | collective-permute-done | bytes 524320 | tf_op jit(solution)/shard_map/ppermute | solution.py:429
  68.9 2.9 collective-permute-start.12
  71.9 34.9 %all-gather.5.cloned.1.call-done.refs_0_ = bf16[3200,768]{1,0:T(8,128)(2,1)} async-done(((bf16[800,768]{1,0:T(8,128)(2,1)}), bf16[3200,768]{1,0:T(8,128)(2,1)}) %all-gather.5.cloned.1.call-update) | async-done | bytes 4915216 | tf_op jit(solution)/shard_map/all_gather | solution.py:1168
  117.2 2.4 collective-permute-start.31
  119.7 5.0 collective-permute-done.22.refs_6_
  126.2 2.3 collective-permute-start.24
  128.5 3.7 multiply_sine_fusion
  136.3 2.3 fusion.14
  143.0 5.5 shard_map.252
  152.4 2.6 collective-permute-done.34.refs_5_
  156.2 22.2 %shard_map.253 = (bf16[2048,768]{1,0:T(8,128)(2,1)}, bf16[2048,384]{1,0:T(8,128)(2,1)}, bf16[2048,768]{1,0:T(8,128)(2,1)}) custom-call(s32[11]{0:T(128)} %concatenate.24.refs_0_, bf16[128,2048]{1,0:T(8,128)(2,1)} %collective-permute-done.refs_1_, bf16[128,2048]{1,0:T(8,128)(2,1)} %collective-permute-done.2.refs_2_, ...), custom_call_target="tpu_custom_call" | custom-call | flops 9663676416 | bytes 20971520 | tf_op jit(solution)/shard_map/pallas_call | solution.py:468
  179.9 16.0 %shard_map.254 = (bf16[2048,256]{1,0:T(8,128)(2,1)}, f32[2048,256]{1,0:T(8,128)}) custom-call(s32[11]{0:T(128)} %concatenate.24.refs_0_, bf16[2048,768]{1,0:T(8,128)(2,1)} %get-tuple-element.98.refs_1_.refs_2_.refs_3_, bf16[2048,768]{1,0:T(8,128)(2,1)} %get-tuple-element.98.refs_1_.refs_2_.refs_3_, bf16[2048,768]{1,0:T(8,128)(2,1)} %get-tuple-element.98.refs_1_.refs_2_.refs_3_), custom_call_target="tpu_custom_call" | custom-call | flops 4294967296 | bytes 8388608 | tf_op jit(solution)/shard_map/pallas_call | solution.py:468
  196.4 3.6 all-to-all-start
  201.3 10.7 %all-to-all-done = bf16[8,256,256]{2,1,0:T(8,128)(2,1)S(1)} async-done(((bf16[8,256,256]{2,1,0:T(8,128)(2,1)}), bf16[8,256,256]{2,1,0:T(8,128)(2,1)S(1)}, u32[]{:S(2)}, u32[]{:S(2)}) %all-to-all-start) | async-done | bytes 1048608 | tf_op jit(solution)/shard_map/all_to_all | solution.py:1259
  214.0 8.4 %shard_map.257.refs_2_.refs_9_ = bf16[2048,2048]{1,0:T(8,128)(2,1)} custom-call(s32[11]{0:T(128)} %concatenate.24.refs_0_, bf16[384,768]{1,0:T(8,128)(2,1)} %copy-done.41, bf16[384,768]{1,0:T(8,128)(2,1)} %collective-permute-done.35.refs_2_, bf16[384,768]{1,0:T(8,128)(2,1)} %collective-permute-done.36.refs_3_, ...), custom_call_target="tpu_custom_call" | custom-call | tf_op jit(solution)/shard_map/pallas_call | solution.py:468
  223.4 9.6 %shard_map.258 = (f32[256,2048]{1,0:T(8,128)}, bf16[128,2048]{1,0:T(8,128)(2,1)}, bf16[128,2048]{1,0:T(8,128)(2,1)}, bf16[256,128]{1,0:T(8,128)(2,1)}) custom-call(s32[11]{0:T(128)} %concatenate.24.refs_0_, bf16[256,2048]{1,0:T(8,128)(2,1)} %bitcast.87, bf16[2048,2048]{1,0:T(8,128)(2,1)} %shard_map.257.refs_2_.refs_9_, ...), custom_call_target="tpu_custom_call" | custom-call | flops 2147483648 | bytes 12582912 | tf_op jit(solution)/shard_map/pallas_call | solution.py:468
  234.1 2.3 collective-permute-start.50
  237.8 5.6 collective-permute-done.48.refs_8_.refs_7_.refs_13_
  243.3 6.5 %collective-permute-start.49 = (bf16[128,2048]{1,0:T(8,128)(2,1)}, bf16[128,2048]{1,0:T(8,128)(2,1)S(1)}, u32[]{:S(2)}, u32[]{:S(2)}) collective-permute-start(bf16[128,2048]{1,0:T(8,128)(2,1)} %collective-permute-done.48.refs_8_.refs_7_.refs_13_), channel_id=1, source_target_pairs={{0,8},{4,12},{8,0},{12,4},{16,24},{20,28},{24,16},{28,20},{1,9},{5... | collective-permute-start | bytes 1572872 | tf_op jit(solution)/shard_map/ppermute | solution.py:429
  249.9 31.4 %all-gather.7.cloned.1.call-done.refs_0_ = bf16[2048,1024]{1,0:T(8,128)(2,1)} async-done(((bf16[512,1024]{1,0:T(8,128)(2,1)}), bf16[2048,1024]{1,0:T(8,128)(2,1)}) %all-gather.7.cloned.1.call-update) | async-done | bytes 4194320 | tf_op jit(solution)/shard_map/all_gather | solution.py:1178
  287.8 2.9 collective-permute-done.52.refs_6_
  290.7 22.1 %shard_map.262 = (f32[512,2304]{1,0:T(8,128)}, bf16[512,512]{1,0:T(8,128)(2,1)}, bf16[512,1024]{1,0:T(8,128)(2,1)}, bf16[512,512]{1,0:T(8,128)(2,1)}, bf16[512,1...) custom-call(s32[11]{0:T(128)} %concatenate.24.refs_0_, ...), custom_call_target="tpu_custom_call" | custom-call | flops 10737418240 | bytes 27262976 | tf_op jit(solution)/shard_map/pallas_call | solution.py:468
  312.8 8.2 %shard_map.265.refs_4_.refs_5_ = f32[512,2176]{1,0:T(8,128)} custom-call(s32[11]{0:T(128)} %concatenate.24.refs_0_, bf16[512,512]{1,0:T(8,128)(2,1)} %get-tuple-element.116.refs_1_.refs_7_, bf16[512,512]{1,0:T(8,128)(2,1)} %get-tuple-element.117.refs_2_.refs_11_, bf16[1024,2432]{1,0:T(8,128)(2,1)} %shard_map.261.refs_5_.refs_3_.refs_4_, ...), custom_call_target="tpu_custom_call" | custom-call | flops 2147483648 | bytes 12582912 | tf_op jit(solution)/shard_map/pallas_call | solution.py:468
  322.2 22.2 %shard_map.263 = (f32[512,2304]{1,0:T(8,128)}, bf16[512,512]{1,0:T(8,128)(2,1)}, bf16[512,1024]{1,0:T(8,128)(2,1)}, bf16[512,512]{1,0:T(8,128)(2,1)}, bf16[512,1...) custom-call(s32[11]{0:T(128)} %concatenate.24.refs_0_, ...), custom_call_target="tpu_custom_call" | custom-call | flops 10737418240 | bytes 27262976 | tf_op jit(solution)/shard_map/pallas_call | solution.py:468
  344.4 8.2 %shard_map.264.refs_3_.refs_5_ = f32[512,2176]{1,0:T(8,128)} custom-call(s32[11]{0:T(128)} %concatenate.24.refs_0_, bf16[512,512]{1,0:T(8,128)(2,1)} %get-tuple-element.114.refs_1_.refs_5_, bf16[512,512]{1,0:T(8,128)(2,1)} %get-tuple-element.115.refs_2_.refs_9_, bf16[1024,2432]{1,0:T(8,128)(2,1)} %shard_map.261.refs_5_.refs_3_.refs_4_, ...), custom_call_target="tpu_custom_call" | custom-call | flops 2147483648 | bytes 12582912 | tf_op jit(solution)/shard_map/pallas_call | solution.py:468
  352.6 10.0 %all-gather.11.cloned.1.call-done.refs_0_ = bf16[2048,1024]{1,0:T(8,128)(2,1)} async-done(((bf16[512,1024]{1,0:T(8,128)(2,1)}), bf16[2048,1024]{1,0:T(8,128)(2,1)}) %all-gather.11.cloned.1.call-update) | async-done | bytes 4194320 | tf_op jit(solution)/shard_map/all_gather | solution.py:1178
  363.2 13.7 %shard_map.268 = (f32[512,2304]{1,0:T(8,128)}, bf16[512,512]{1,0:T(8,128)(2,1)}, bf16[512,1024]{1,0:T(8,128)(2,1)}) custom-call(s32[11]{0:T(128)} %concatenate.24.refs_0_, bf16[512,256]{1,0:T(8,128)(2,1)} %get-tuple-element.121.refs_1_, bf16[512,128]{1,0:T(8,128)(2,1)} %get-tuple-element.122.refs_2_.refs_3_, bf16[2048,1024]{1,0:T(8,128)(2,1)} %shard_map.266.refs_3_, ...), custom_call_target="tpu_custom_call" | custom-call | flops 5368709120 | bytes 27262976 | tf_op jit(solution)/shard_map/pallas_call | solution.py:468
  377.0 13.4 %shard_map.269 = (bf16[256,2304]{1,0:T(8,128)(2,1)}, bf16[256,2304]{1,0:T(8,128)(2,1)}, bf16[512,512]{1,0:T(8,128)(2,1)}, bf16[512,1024]{1,0:T(8,128)(2,1)}) custom-call(s32[11]{0:T(128)} %concatenate.24.refs_0_, bf16[512,256]{1,0:T(8,128)(2,1)} %get-tuple-element.121.refs_1_, bf16[512,128]{1,0:T(8,128)(2,1)} %get-tuple-element.122.refs_2_.refs_3_, ...), custom_call_target="tpu_custom_call" | custom-call | flops 5368709120 | bytes 27262976 | tf_op jit(solution)/shard_map/pallas_call | solution.py:468
  392.9 21.5 %shard_map.267 = (f32[256,2304]{1,0:T(8,128)}, f32[256,2304]{1,0:T(8,128)}, bf16[512,512]{1,0:T(8,128)(2,1)}, bf16[512,1024]{1,0:T(8,128)(2,1)}, bf16[512,512]{1,0:T(8,128)(2,1)}, /*index=5*/bf16[512,1024]{1,0:T(8,128)(2,1)}) custom-call(s32[11]{0:T(128)} %concatenate.24.refs_0_, bf16[512,256]{1,0:T(8,128)(2,1)} %get-tuple-element.109.refs_1_.refs_2_, ...), custom_call_target="tpu_custom_call" | custom-call | flops 10737418240 | bytes 27262976 | tf_op jit(solution)/shard_map/pallas_call | solution.py:468
  414.4 3.8 collective-permute-done.59.refs_2_
  419.2 3.3 add_convert_fusion
  424.4 8.7 %shard_map.270 = (bf16[256,2176]{1,0:T(8,128)(2,1)}, bf16[256,2176]{1,0:T(8,128)(2,1)}) custom-call(s32[11]{0:T(128)} %concatenate.24.refs_0_, bf16[512,512]{1,0:T(8,128)(2,1)} %get-tuple-element.128.refs_1_.refs_13_, bf16[512,512]{1,0:T(8,128)(2,1)} %get-tuple-element.129.refs_2_.refs_17_, bf16[1024,2432]{1,0:T(8,128)(2,1)} %shard_map.261.refs_5_.refs_3_.refs_4_, ...), custom_call_target="tpu_custom_call" | custom-call | flops 2147483648 | bytes 12582912 | tf_op jit(solution)/shard_map/pallas_call | solution.py:468
  433.1 3.3 collective-permute-done.61.refs_1_.refs_4_
  439.7 2.3 collective-permute-start.68
  442.0 13.3 %shard_map.272 = (f32[256,2048]{1,0:T(8,128)}, bf16[256,2048]{1,0:T(8,128)(2,1)}, bf16[256,640]{1,0:T(8,128)(2,1)}, bf16[256,640]{1,0:T(8,128)(2,1)}, bf16[256,6...) custom-call(s32[11]{0:T(128)} %concatenate.24.refs_0_, f32[256,2304]{1,0:T(8,128)} %get-tuple-element.120.refs_1_, ...), custom_call_target="tpu_custom_call" | custom-call | flops 2147483648 | bytes 16777216 | tf_op jit(solution)/shard_map/pallas_call | solution.py:468
  457.6 3.9 all-to-all-start.1
  461.5 9.4 %shard_map.273 = (f32[256,2176]{1,0:T(8,128)}, f32[256,2176]{1,0:T(8,128)}) custom-call(s32[11]{0:T(128)} %concatenate.24.refs_0_, bf16[512,512]{1,0:T(8,128)(2,1)} %get-tuple-element.118.refs_1_.refs_15_, bf16[512,512]{1,0:T(8,128)(2,1)} %get-tuple-element.119.refs_2_.refs_19_, bf16[1024,2432]{1,0:T(8,128)(2,1)} %shard_map.261.refs_5_.refs_3_.refs_4_, ...), custom_call_target="tpu_custom_call" | custom-call | flops 2147483648 | bytes 12582912 | tf_op jit(solution)/shard_map/pallas_call | solution.py:468
  471.0 3.6 add_convert_fusion.2
  478.1 25.0 %shard_map.275 = (bf16[3,1024,256]{2,1,0:T(8,128)(2,1)}, bf16[3,1024,256]{2,1,0:T(8,128)(2,1)}, f32[3,128,256]{2,1,0:T(8,128)}) custom-call(s32[11]{0:T(128)} %concatenate.24.refs_0_, bf16[2048,768]{1,0:T(8,128)(2,1)} %get-tuple-element.98.refs_1_.refs_2_.refs_3_, bf16[2048,768]{1,0:T(8,128)(2,1)} %get-tuple-element.98.refs_1_.refs_2_.refs_3_, ...), custom_call_target="tpu_custom_call" | custom-call | flops 10737418240 | bytes 16777216 | tf_op jit(solution)/shard_map/pallas_call | solution.py:468
  506.8 2.4 fusion.3
  513.2 4.4 shard_map.277
  521.8 9.3 %shard_map.281 = (f32[256,2048]{1,0:T(8,128)}, f32[256,2048]{1,0:T(8,128)}) custom-call(s32[11]{0:T(128)} %concatenate.24.refs_0_, bf16[3,1024,256]{2,1,0:T(8,128)(2,1)} %get-tuple-element.137.refs_1_, bf16[3,1024,256]{2,1,0:T(8,128)(2,1)} %copy-done.23, bf16[2048,768]{1,0:T(8,128)(2,1)} %get-tuple-element.139.refs_3_, ...), custom_call_target="tpu_custom_call" | custom-call | flops 3221225472 | bytes 12582912 | tf_op jit(solution)/shard_map/pallas_call | solution.py:468
  534.1 8.8 %shard_map.282 = (f32[4,768,128]{2,1,0:T(8,128)}, bf16[4,768,128]{2,1,0:T(8,128)(2,1)}) custom-call(s32[11]{0:T(128)} %concatenate.24.refs_0_, bf16[512,256]{1,0:T(8,128)(2,1)} %get-tuple-element.121.refs_1_, bf16[512,256]{1,0:T(8,128)(2,1)} %get-tuple-element.109.refs_1_.refs_2_, bf16[512,128]{1,0:T(8,128)(2,1)} %get-tuple-element.122.refs_2_.refs_3_, ...), custom_call_target="tpu_custom_call" | custom-call | flops 4294967296 | bytes 12582912 | tf_op jit(solution)/shard_map/pallas_call | solution.py:468
  546.0 8.7 %shard_map.283 = (bf16[256,2048]{1,0:T(8,128)(2,1)}, bf16[256,2048]{1,0:T(8,128)(2,1)}) custom-call(s32[11]{0:T(128)} %concatenate.24.refs_0_, bf16[3,1024,256]{2,1,0:T(8,128)(2,1)} %get-tuple-element.137.refs_1_, bf16[3,1024,256]{2,1,0:T(8,128)(2,1)} %copy-done.23, bf16[2048,768]{1,0:T(8,128)(2,1)} %get-tuple-element.139.refs_3_, ...), custom_call_target="tpu_custom_call" | custom-call | flops 3221225472 | bytes 12582912 | tf_op jit(solution)/shard_map/pallas_call | solution.py:468
  555.8 9.6 %shard_map.284 = (f32[4,704,128]{2,1,0:T(8,128)}, bf16[4,704,128]{2,1,0:T(8,128)(2,1)}) custom-call(s32[11]{0:T(128)} %concatenate.24.refs_0_, bf16[128,2048]{1,0:T(8,128)(2,1)} %collective-permute-done.refs_1_, bf16[128,2048]{1,0:T(8,128)(2,1)} %collective-permute-done.2.refs_2_, bf16[128,2048]{1,0:T(8,128)(2,1)} %collective-permute-done.3.refs_3_, ...), custom_call_target="tpu_custom_call" | custom-call | flops 805306368 | bytes 8388608 | tf_op jit(solution)/shard_map/pallas_call | solution.py:468
  565.4 2.7 collective-permute-start.82
  569.0 3.4 shard_map.290
  573.2 3.3 shard_map.288
  577.9 5.3 collective-permute-done.90
  584.8 3.1 fusion.4
  589.4 3.2 fusion.refs_1_
  592.6 2.6 collective-permute-done.83
  601.4 7.4 %shard_map.287.refs_1_ = f32[256,2048]{1,0:T(8,128)} custom-call(s32[11]{0:T(128)} %concatenate.24.refs_0_, f32[256,2048]{1,0:T(8,128)} %get-tuple-element.158.refs_21_.refs_1_, bf16[256,2048]{1,0:T(8,128)(2,1)} %collective-permute-done.78.refs_2_, bf16[256,2048]{1,0:T(8,128)(2,1)} %collective-permute-done.79.refs_3_, ...), custom_call_target="tpu_custom_call" | custom-call | flops 402653184 | bytes 12582912 | tf_op jit(solution)/shard_map/pallas_call | solution.py:468
  612.7 5.2 collective-permute-start.95
  618.1 4.7 collective-permute-start.88
  623.6 4.1 shard_map.292
  628.7 3.9 shard_map.293
  (384 shorter events, 105.5 us)
Async XLA Ops:
  7.2 99.7 %all-gather.5.cloned.1.call-start = ((), (), s32[]{:S(2)}) async-start(), calls=%async_computation.2 | async-start | bytes 6144000 | tf_op jit(solution)/shard_map/all_gather | solution.py:1168
  11.8 224.6 %all-gather.9.cloned.1.call-start = ((), (), s32[]{:S(2)}) async-start(), calls=%async_computation.4 | async-start | bytes 6225920 | tf_op jit(solution)/shard_map/all_gather | solution.py:1177
  16.3 265.0 %all-gather.7.cloned.1.call-start = ((), (), s32[]{:S(2)}) async-start(), calls=%async_computation.3 | async-start | bytes 5242880 | tf_op jit(solution)/shard_map/all_gather | solution.py:1178
  19.9 14.1 %collective-permute-start.1 = (bf16[128,2048]{1,0:T(8,128)(2,1)}, bf16[128,2048]{1,0:T(8,128)(2,1)S(1)}, u32[]{:S(2)}, u32[]{:S(2)}) collective-permute-start(bf16[128,2048]{1,0:T(8,128)(2,1)} %get-tuple-element.95.refs_7_), channel_id=1, source_target_pairs={{0,16},{4,20},{8,24},{12,28},{16,0},{20,4},{24,8},{28,12},{1,17},{... | collective-permute-start | bytes 1572872 | tf_op jit(solution)/shard_map/ppermute | solution.py:429
  22.0 13.1 %collective-permute-start.4 = (bf16[128,2048]{1,0:T(8,128)(2,1)}, bf16[128,2048]{1,0:T(8,128)(2,1)S(1)}, u32[]{:S(2)}, u32[]{:S(2)}) collective-permute-start(bf16[128,2048]{1,0:T(8,128)(2,1)} %get-tuple-element.96.refs_8_), channel_id=1, source_target_pairs={{0,8},{4,12},{8,0},{12,4},{16,24},{20,28},{24,16},{28,20},{1,9},{5... | collective-permute-start | bytes 1572872 | tf_op jit(solution)/shard_map/ppermute | solution.py:429
  23.3 21.9 %collective-permute-start.14 = (bf16[128,2048]{1,0:T(8,128)(2,1)S(1)}, bf16[128,2048]{1,0:T(8,128)(2,1)}, u32[]{:S(2)}, u32[]{:S(2)}) collective-permute-start(bf16[128,2048]{1,0:T(8,128)(2,1)S(1)} %get-tuple-element.205.refs_14_.refs_13_.refs_23_), channel_id=1, source_target_pairs={{0,16},{4,20},{8,24},{12,28},{16,0},{20,4},{24,8},{28,12},{1,17},{... | collective-permute-start | bytes 1572872 | tf_op jit(solution)/shard_map/ppermute | solution.py:429
  23.6 22.7 %collective-permute-start.16 = (bf16[128,2048]{1,0:T(8,128)(2,1)S(1)}, bf16[128,2048]{1,0:T(8,128)(2,1)}, u32[]{:S(2)}, u32[]{:S(2)}) collective-permute-start(bf16[128,2048]{1,0:T(8,128)(2,1)S(1)} %get-tuple-element.204.refs_15_.refs_14_.refs_24_), channel_id=1, source_target_pairs={{0,8},{4,12},{8,0},{12,4},{16,24},{20,28},{24,16},{28,20},{1,9},{5... | collective-permute-start | bytes 1572872 | tf_op jit(solution)/shard_map/ppermute | solution.py:429
  34.0 23.2 %collective-permute-start.2 = (bf16[128,2048]{1,0:T(8,128)(2,1)S(1)}, bf16[128,2048]{1,0:T(8,128)(2,1)}, u32[]{:S(2)}, u32[]{:S(2)}) collective-permute-start(bf16[128,2048]{1,0:T(8,128)(2,1)S(1)} %collective-permute-done.1.refs_5_), channel_id=1, source_target_pairs={{0,8},{4,12},{8,0},{12,4},{16,24},{20,28},{24,16},{28,20},{1,9},{5... | collective-permute-start | bytes 1572872 | tf_op jit(solution)/shard_map/ppermute | solution.py:429
  35.1 25.5 %collective-permute-start.5 = (bf16[128,2048]{1,0:T(8,128)(2,1)S(1)}, bf16[128,2048]{1,0:T(8,128)(2,1)}, u32[]{:S(2)}, u32[]{:S(2)}) collective-permute-start(bf16[128,2048]{1,0:T(8,128)(2,1)S(1)} %collective-permute-done.4.refs_6_), channel_id=1, source_target_pairs={{0,16},{4,20},{8,24},{12,28},{16,0},{20,4},{24,8},{28,12},{1,17},{... | collective-permute-start | bytes 1572872 | tf_op jit(solution)/shard_map/ppermute | solution.py:429
  45.2 23.2 %collective-permute-start.15 = (bf16[128,2048]{1,0:T(8,128)(2,1)}, bf16[128,2048]{1,0:T(8,128)(2,1)S(1)}, u32[]{:S(2)}, u32[]{:S(2)}) collective-permute-start(bf16[128,2048]{1,0:T(8,128)(2,1)} %collective-permute-done.14.refs_12_.refs_11_.refs_21_), channel_id=1, source_target_pairs={{0,8},{4,12},{8,0},{12,4},{16,24},{20,28},{24,16},{28,20},{1,9},{5... | collective-permute-start | bytes 1572872 | tf_op jit(solution)/shard_map/ppermute | solution.py:429
  46.3 22.6 %collective-permute-start.17 = (bf16[128,2048]{1,0:T(8,128)(2,1)}, bf16[128,2048]{1,0:T(8,128)(2,1)S(1)}, u32[]{:S(2)}, u32[]{:S(2)}) collective-permute-start(bf16[128,2048]{1,0:T(8,128)(2,1)} %collective-permute-done.16.refs_13_.refs_12_.refs_22_), channel_id=1, source_target_pairs={{0,16},{4,20},{8,24},{12,28},{16,0},{20,4},{24,8},{28,12},{1,17},{... | collective-permute-start | bytes 1572872 | tf_op jit(solution)/shard_map/ppermute | solution.py:429
  57.2 14.6 %collective-permute-start.7 = (bf16[128,2048]{1,0:T(8,128)(2,1)}, bf16[128,2048]{1,0:T(8,128)(2,1)}, u32[]{:S(2)}, u32[]{:S(2)}) collective-permute-start(bf16[128,2048]{1,0:T(8,128)(2,1)} %collective-permute-done.2.refs_2_), channel_id=1, source_target_pairs={{0,4},{4,0},{8,12},{12,8},{16,20},{20,16},{24,28},{28,24},{1,5},{5... | collective-permute-start | bytes 1572872 | tf_op jit(solution)/shard_map/ppermute | solution.py:429
  60.6 50.0 %collective-permute-start = (bf16[128,2048]{1,0:T(8,128)(2,1)S(1)}, bf16[128,2048]{1,0:T(8,128)(2,1)}, u32[]{:S(2)}, u32[]{:S(2)}) collective-permute-start(bf16[128,2048]{1,0:T(8,128)(2,1)S(1)} %copy-done.44), channel_id=1, source_target_pairs={{0,8},{4,12},{8,0},{12,4},{16,24},{20,28},{24,16},{28,20},{1,9},{5... | collective-permute-start | bytes 1572872 | tf_op jit(solution)/shard_map/ppermute | solution.py:429
  68.5 43.3 %collective-permute-start.3 = (bf16[128,2048]{1,0:T(8,128)(2,1)S(1)}, bf16[128,2048]{1,0:T(8,128)(2,1)}, u32[]{:S(2)}, u32[]{:S(2)}) collective-permute-start(bf16[128,2048]{1,0:T(8,128)(2,1)S(1)} %copy-done.45), channel_id=1, source_target_pairs={{0,16},{4,20},{8,24},{12,28},{16,0},{20,4},{24,8},{28,12},{1,17},{... | collective-permute-start | bytes 1572872 | tf_op jit(solution)/shard_map/ppermute | solution.py:429
  68.9 43.2 %collective-permute-start.12 = (bf16[128,2048]{1,0:T(8,128)(2,1)S(1)}, bf16[128,2048]{1,0:T(8,128)(2,1)}, u32[]{:S(2)}, u32[]{:S(2)}) collective-permute-start(bf16[128,2048]{1,0:T(8,128)(2,1)S(1)} %copy-done.44), channel_id=1, source_target_pairs={{0,4},{4,0},{8,12},{12,8},{16,20},{20,16},{24,28},{28,24},{1,5},{5... | collective-permute-start | bytes 1572872 | tf_op jit(solution)/shard_map/ppermute | solution.py:429
  71.8 40.6 %collective-permute-start.13 = (bf16[128,2048]{1,0:T(8,128)(2,1)S(1)}, bf16[128,2048]{1,0:T(8,128)(2,1)}, u32[]{:S(2)}, u32[]{:S(2)}) collective-permute-start(bf16[128,2048]{1,0:T(8,128)(2,1)S(1)} %copy-done.45), channel_id=1, source_target_pairs={{0,4},{4,0},{8,12},{12,8},{16,20},{20,16},{24,28},{28,24},{1,5},{5... | collective-permute-start | bytes 1572872 | tf_op jit(solution)/shard_map/ppermute | solution.py:429
  110.5 15.4 %collective-permute-start.18 = (bf16[192,768]{1,0:T(8,128)(2,1)S(1)}, bf16[192,768]{1,0:T(8,128)(2,1)S(1)}, u32[]{:S(2)}, u32[]{:S(2)}) collective-permute-start(bf16[192,768]{1,0:T(8,128)(2,1)S(1)} %bitcast.99), channel_id=1, source_target_pairs={{0,8},{4,12},{8,0},{12,4},{16,24},{20,28},{24,16},{28,20},{1,9},{5... | collective-permute-start | bytes 884744 | tf_op jit(solution)/shard_map/ppermute | solution.py:429
  112.1 14.1 %collective-permute-start.21 = (bf16[192,768]{1,0:T(8,128)(2,1)S(1)}, bf16[192,768]{1,0:T(8,128)(2,1)}, u32[]{:S(2)}, u32[]{:S(2)}) collective-permute-start(bf16[192,768]{1,0:T(8,128)(2,1)S(1)} %bitcast.95), channel_id=1, source_target_pairs={{0,16},{4,20},{8,24},{12,28},{16,0},{20,4},{24,8},{28,12},{1,17},{... | collective-permute-start | bytes 884744 | tf_op jit(solution)/shard_map/ppermute | solution.py:429
  115.2 17.0 %collective-permute-start.30 = (bf16[192,768]{1,0:T(8,128)(2,1)S(1)}, bf16[192,768]{1,0:T(8,128)(2,1)S(1)}, u32[]{:S(2)}, u32[]{:S(2)}) collective-permute-start(bf16[192,768]{1,0:T(8,128)(2,1)S(1)} %bitcast.100), channel_id=1, source_target_pairs={{0,4},{4,0},{8,12},{12,8},{16,20},{20,16},{24,28},{28,24},{1,5},{5... | collective-permute-start | bytes 884744 | tf_op jit(solution)/shard_map/ppermute | solution.py:429
  117.2 15.0 %collective-permute-start.31 = (bf16[192,768]{1,0:T(8,128)(2,1)S(1)}, bf16[192,768]{1,0:T(8,128)(2,1)S(1)}, u32[]{:S(2)}, u32[]{:S(2)}) collective-permute-start(bf16[192,768]{1,0:T(8,128)(2,1)S(1)} %bitcast.96), channel_id=1, source_target_pairs={{0,4},{4,0},{8,12},{12,8},{16,20},{20,16},{24,28},{28,24},{1,5},{5... | collective-permute-start | bytes 884744 | tf_op jit(solution)/shard_map/ppermute | solution.py:429
  139.8 15.2 %collective-permute-start.34 = (bf16[384,768]{1,0:T(8,128)(2,1)}, bf16[384,768]{1,0:T(8,128)(2,1)S(1)}, u32[]{:S(2)}, u32[]{:S(2)}) collective-permute-start(bf16[384,768]{1,0:T(8,128)(2,1)} %shard_map.255.refs_7_), channel_id=1, source_target_pairs={{0,16},{4,20},{8,24},{12,28},{16,0},{20,4},{24,8},{28,12},{1,17},{... | collective-permute-start | bytes 1769480 | tf_op jit(solution)/shard_map/ppermute | solution.py:429
  148.4 30.5 %collective-permute-start.33 = (bf16[384,768]{1,0:T(8,128)(2,1)S(1)}, bf16[384,768]{1,0:T(8,128)(2,1)S(1)}, u32[]{:S(2)}, u32[]{:S(2)}) collective-permute-start(bf16[384,768]{1,0:T(8,128)(2,1)S(1)} %copy-done.6), channel_id=1, source_target_pairs={{0,8},{4,12},{8,0},{12,4},{16,24},{20,28},{24,16},{28,20},{1,9},{5... | collective-permute-start | bytes 1769480 | tf_op jit(solution)/shard_map/ppermute | solution.py:429
  148.8 29.6 %collective-permute-start.37 = (bf16[384,768]{1,0:T(8,128)(2,1)S(1)}, bf16[384,768]{1,0:T(8,128)(2,1)}, u32[]{:S(2)}, u32[]{:S(2)}) collective-permute-start(bf16[384,768]{1,0:T(8,128)(2,1)S(1)} %copy-done.3), channel_id=1, source_target_pairs={{0,8},{4,12},{8,0},{12,4},{16,24},{20,28},{24,16},{28,20},{1,9},{5... | collective-permute-start | bytes 1769480 | tf_op jit(solution)/shard_map/ppermute | solution.py:429
  150.0 29.3 %collective-permute-start.36 = (bf16[384,768]{1,0:T(8,128)(2,1)S(1)}, bf16[384,768]{1,0:T(8,128)(2,1)}, u32[]{:S(2)}, u32[]{:S(2)}) collective-permute-start(bf16[384,768]{1,0:T(8,128)(2,1)S(1)} %copy-done.3), channel_id=1, source_target_pairs={{0,16},{4,20},{8,24},{12,28},{16,0},{20,4},{24,8},{28,12},{1,17},{... | collective-permute-start | bytes 1769480 | tf_op jit(solution)/shard_map/ppermute | solution.py:429
  151.2 28.6 %collective-permute-start.45 = (bf16[384,768]{1,0:T(8,128)(2,1)S(1)}, bf16[384,768]{1,0:T(8,128)(2,1)S(1)}, u32[]{:S(2)}, u32[]{:S(2)}) collective-permute-start(bf16[384,768]{1,0:T(8,128)(2,1)S(1)} %copy-done.6), channel_id=1, source_target_pairs={{0,4},{4,0},{8,12},{12,8},{16,20},{20,16},{24,28},{28,24},{1,5},{5... | collective-permute-start | bytes 1769480 | tf_op jit(solution)/shard_map/ppermute | solution.py:429
  155.0 41.0 %collective-permute-start.46 = (bf16[384,768]{1,0:T(8,128)(2,1)S(1)}, bf16[384,768]{1,0:T(8,128)(2,1)}, u32[]{:S(2)}, u32[]{:S(2)}) collective-permute-start(bf16[384,768]{1,0:T(8,128)(2,1)S(1)} %copy-done.3), channel_id=1, source_target_pairs={{0,4},{4,0},{8,12},{12,8},{16,20},{20,16},{24,28},{28,24},{1,5},{5... | collective-permute-start | bytes 1769480 | tf_op jit(solution)/shard_map/ppermute | solution.py:429
  178.4 21.8 %collective-permute-start.35 = (bf16[384,768]{1,0:T(8,128)(2,1)S(1)}, bf16[384,768]{1,0:T(8,128)(2,1)}, u32[]{:S(2)}, u32[]{:S(2)}) collective-permute-start(bf16[384,768]{1,0:T(8,128)(2,1)S(1)} %collective-permute-done.34.refs_5_), channel_id=1, source_target_pairs={{0,8},{4,12},{8,0},{12,4},{16,24},{20,28},{24,16},{28,20},{1,9},{5... | collective-permute-start | bytes 1769480 | tf_op jit(solution)/shard_map/ppermute | solution.py:429
  179.0 21.4 %collective-permute-start.38 = (bf16[384,768]{1,0:T(8,128)(2,1)}, bf16[384,768]{1,0:T(8,128)(2,1)}, u32[]{:S(2)}, u32[]{:S(2)}) collective-permute-start(bf16[384,768]{1,0:T(8,128)(2,1)} %collective-permute-done.37.refs_6_), channel_id=1, source_target_pairs={{0,16},{4,20},{8,24},{12,28},{16,0},{20,4},{24,8},{28,12},{1,17},{... | collective-permute-start | bytes 1769480 | tf_op jit(solution)/shard_map/ppermute | solution.py:429
  179.2 21.6 %collective-permute-start.39 = (bf16[384,768]{1,0:T(8,128)(2,1)S(1)}, bf16[384,768]{1,0:T(8,128)(2,1)}, u32[]{:S(2)}, u32[]{:S(2)}) collective-permute-start(bf16[384,768]{1,0:T(8,128)(2,1)S(1)} %collective-permute-done.33.refs_1_), channel_id=1, source_target_pairs={{0,4},{4,0},{8,12},{12,8},{16,20},{20,16},{24,28},{28,24},{1,5},{5... | collective-permute-start | bytes 1769480 | tf_op jit(solution)/shard_map/ppermute | solution.py:429
  179.8 21.1 %collective-permute-start.41 = (bf16[384,768]{1,0:T(8,128)(2,1)}, bf16[384,768]{1,0:T(8,128)(2,1)}, u32[]{:S(2)}, u32[]{:S(2)}) collective-permute-start(bf16[384,768]{1,0:T(8,128)(2,1)} %collective-permute-done.36.refs_3_), channel_id=1, source_target_pairs={{0,4},{4,0},{8,12},{12,8},{16,20},{20,16},{24,28},{28,24},{1,5},{5... | collective-permute-start | bytes 1769480 | tf_op jit(solution)/shard_map/ppermute | solution.py:429
  195.9 26.5 %collective-permute-start.47 = (bf16[2048,256]{1,0:T(8,128)(2,1)}, bf16[2048,256]{1,0:T(8,128)(2,1)S(1)}, u32[]{:S(2)}, u32[]{:S(2)}) collective-permute-start(bf16[2048,256]{1,0:T(8,128)(2,1)} %get-tuple-element.99.refs_25_), channel_id=1, source_target_pairs={{0,4},{4,0},{8,12},{12,8},{16,20},{20,16},{24,28},{28,24},{1,5},{5... | collective-permute-start | bytes 3145736 | tf_op jit(solution)/shard_map/ppermute | solution.py:429
  196.4 15.6 %all-to-all-start = ((bf16[8,256,256]{2,1,0:T(8,128)(2,1)}), bf16[8,256,256]{2,1,0:T(8,128)(2,1)S(1)}, u32[]{:S(2)}, u32[]{:S(2)}) async-start(bf16[8,256,256]{2,1,0:T(8,128)(2,1)} %bitcast.90), calls=%async_computation | async-start | bytes 2097152 | tf_op jit(solution)/shard_map/all_to_all | solution.py:1259
  200.0 162.5 %all-gather.11.cloned.1.call-start = ((), (), s32[]{:S(2)}) async-start(), calls=%async_computation.5 | async-start | bytes 5242880 | tf_op jit(solution)/shard_map/all_gather | solution.py:1178
  234.1 15.7 %collective-permute-start.50 = (bf16[128,2048]{1,0:T(8,128)(2,1)}, bf16[128,2048]{1,0:T(8,128)(2,1)}, u32[]{:S(2)}, u32[]{:S(2)}) collective-permute-start(bf16[128,2048]{1,0:T(8,128)(2,1)} %get-tuple-element.107.refs_11_.refs_10_.refs_16_), channel_id=1, source_target_pairs={{0,8},{4,12},{8,0},{12,4},{16,24},{20,28},{24,16},{28,20},{1,9},{5... | collective-permute-start | bytes 1572872 | tf_op jit(solution)/shard_map/ppermute | solution.py:429
  236.5 51.1 %collective-permute-start.53 = (bf16[1024,2432]{1,0:T(8,128)(2,1)}, bf16[1024,2432]{1,0:T(8,128)(2,1)}, u32[]{:S(2)}, u32[]{:S(2)}) collective-permute-start(bf16[1024,2432]{1,0:T(8,128)(2,1)} %shard_map.261.refs_5_.refs_3_.refs_4_), channel_id=1, source_target_pairs={{0,4},{4,0},{8,12},{12,8},{16,20},{20,16},{24,28},{28,24},{1,5},{5... | collective-permute-start | bytes 14942216 | tf_op jit(solution)/shard_map/ppermute | solution.py:429
  243.3 37.9 %collective-permute-start.49 = (bf16[128,2048]{1,0:T(8,128)(2,1)}, bf16[128,2048]{1,0:T(8,128)(2,1)S(1)}, u32[]{:S(2)}, u32[]{:S(2)}) collective-permute-start(bf16[128,2048]{1,0:T(8,128)(2,1)} %collective-permute-done.48.refs_8_.refs_7_.refs_13_), channel_id=1, source_target_pairs={{0,8},{4,12},{8,0},{12,4},{16,24},{20,28},{24,16},{28,20},{1,9},{5... | collective-permute-start | bytes 1572872 | tf_op jit(solution)/shard_map/ppermute | solution.py:429
  249.9 31.4 %collective-permute-start.51 = (bf16[128,2048]{1,0:T(8,128)(2,1)}, bf16[128,2048]{1,0:T(8,128)(2,1)S(1)}, u32[]{:S(2)}, u32[]{:S(2)}) collective-permute-start(bf16[128,2048]{1,0:T(8,128)(2,1)} %collective-permute-done.50.refs_9_.refs_8_.refs_14_), channel_id=1, source_target_pairs={{0,16},{4,20},{8,24},{12,28},{16,0},{20,4},{24,8},{28,12},{1,17},{... | collective-permute-start | bytes 1572872 | tf_op jit(solution)/shard_map/ppermute | solution.py:429
  283.6 37.4 %collective-permute-start.56 = (bf16[128,2048]{1,0:T(8,128)(2,1)S(1)}, bf16[128,2048]{1,0:T(8,128)(2,1)S(1)}, u32[]{:S(2)}, u32[]{:S(2)}) collective-permute-start(bf16[128,2048]{1,0:T(8,128)(2,1)S(1)} %copy-done.19), channel_id=1, source_target_pairs={{0,8},{4,12},{8,0},{12,4},{16,24},{20,28},{24,16},{28,20},{1,9},{5... | collective-permute-start | bytes 1572872 | tf_op jit(solution)/shard_map/ppermute | solution.py:429
  284.9 36.1 %collective-permute-start.57 = (bf16[128,2048]{1,0:T(8,128)(2,1)S(1)}, bf16[128,2048]{1,0:T(8,128)(2,1)S(1)}, u32[]{:S(2)}, u32[]{:S(2)}) collective-permute-start(bf16[128,2048]{1,0:T(8,128)(2,1)S(1)} %copy-done.17), channel_id=1, source_target_pairs={{0,16},{4,20},{8,24},{12,28},{16,0},{20,4},{24,8},{28,12},{1,17},{... | collective-permute-start | bytes 1572872 | tf_op jit(solution)/shard_map/ppermute | solution.py:429
  287.3 33.7 %collective-permute-start.54 = (bf16[128,2048]{1,0:T(8,128)(2,1)S(1)}, bf16[128,2048]{1,0:T(8,128)(2,1)S(1)}, u32[]{:S(2)}, u32[]{:S(2)}) collective-permute-start(bf16[128,2048]{1,0:T(8,128)(2,1)S(1)} %copy-done.48), channel_id=1, source_target_pairs={{0,8},{4,12},{8,0},{12,4},{16,24},{20,28},{24,16},{28,20},{1,9},{5... | collective-permute-start | bytes 1572872 | tf_op jit(solution)/shard_map/ppermute | solution.py:429
  287.6 33.4 %collective-permute-start.55 = (bf16[128,2048]{1,0:T(8,128)(2,1)S(1)}, bf16[128,2048]{1,0:T(8,128)(2,1)}, u32[]{:S(2)}, u32[]{:S(2)}) collective-permute-start(bf16[128,2048]{1,0:T(8,128)(2,1)S(1)} %copy-done.49), channel_id=1, source_target_pairs={{0,16},{4,20},{8,24},{12,28},{16,0},{20,4},{24,8},{28,12},{1,17},{... | collective-permute-start | bytes 1572872 | tf_op jit(solution)/shard_map/ppermute | solution.py:429
  362.5 14.4 %collective-permute-start.58 = (bf16[2048,1024]{1,0:T(8,128)(2,1)}, bf16[2048,1024]{1,0:T(8,128)(2,1)}, u32[]{:S(2)}, u32[]{:S(2)}) collective-permute-start(bf16[2048,1024]{1,0:T(8,128)(2,1)} %shard_map.266.refs_3_), channel_id=1, source_target_pairs={{0,4},{4,0},{8,12},{12,8},{16,20},{20,16},{24,28},{28,24},{1,5},{5... | collective-permute-start | bytes 12582920 | tf_op jit(solution)/shard_map/ppermute | solution.py:429
  390.4 27.9 %collective-permute-start.59 = (bf16[256,2304]{1,0:T(8,128)(2,1)}, bf16[256,2304]{1,0:T(8,128)(2,1)S(1)}, u32[]{:S(2)}, u32[]{:S(2)}) collective-permute-start(bf16[256,2304]{1,0:T(8,128)(2,1)} %get-tuple-element.124), channel_id=1, source_target_pairs={{0,8},{4,12},{8,0},{12,4},{16,24},{20,28},{24,16},{28,20},{1,9},{5... | collective-permute-start | bytes 3538952 | tf_op jit(solution)/shard_map/ppermute | solution.py:429
  391.7 27.5 %collective-permute-start.60 = (bf16[256,2304]{1,0:T(8,128)(2,1)}, bf16[256,2304]{1,0:T(8,128)(2,1)S(1)}, u32[]{:S(2)}, u32[]{:S(2)}) collective-permute-start(bf16[256,2304]{1,0:T(8,128)(2,1)} %get-tuple-element.125), channel_id=1, source_target_pairs={{0,16},{4,20},{8,24},{12,28},{16,0},{20,4},{24,8},{28,12},{1,17},{... | collective-permute-start | bytes 3538952 | tf_op jit(solution)/shard_map/ppermute | solution.py:429
  422.5 13.9 %collective-permute-start.61 = (bf16[128,2304]{1,0:T(8,128)(2,1)}, bf16[128,2304]{1,0:T(8,128)(2,1)S(1)}, u32[]{:S(2)}, u32[]{:S(2)}) collective-permute-start(bf16[128,2304]{1,0:T(8,128)(2,1)} %get-tuple-element.197.refs_6_), channel_id=1, source_target_pairs={{0,16},{4,20},{8,24},{12,28},{16,0},{20,4},{24,8},{28,12},{1,17},{... | collective-permute-start | bytes 1769480 | tf_op jit(solution)/shard_map/ppermute | solution.py:429
  423.7 13.7 %collective-permute-start.62 = (bf16[128,2304]{1,0:T(8,128)(2,1)}, bf16[128,2304]{1,0:T(8,128)(2,1)S(1)}, u32[]{:S(2)}, u32[]{:S(2)}) collective-permute-start(bf16[128,2304]{1,0:T(8,128)(2,1)} %get-tuple-element.196.refs_7_), channel_id=1, source_target_pairs={{0,8},{4,12},{8,0},{12,4},{16,24},{20,28},{24,16},{28,20},{1,9},{5... | collective-permute-start | bytes 1769480 | tf_op jit(solution)/shard_map/ppermute | solution.py:429
  438.1 32.8 %collective-permute-start.64 = (bf16[256,2176]{1,0:T(8,128)(2,1)}, bf16[256,2176]{1,0:T(8,128)(2,1)S(1)}, u32[]{:S(2)}, u32[]{:S(2)}) collective-permute-start(bf16[256,2176]{1,0:T(8,128)(2,1)} %shard_map.274), channel_id=1, source_target_pairs={{0,16},{4,20},{8,24},{12,28},{16,0},{20,4},{24,8},{28,12},{1,17},{... | collective-permute-start | bytes 3342344 | tf_op jit(solution)/shard_map/ppermute | solution.py:429
  438.6 32.3 %collective-permute-start.63 = (bf16[256,2176]{1,0:T(8,128)(2,1)}, bf16[256,2176]{1,0:T(8,128)(2,1)S(1)}, u32[]{:S(2)}, u32[]{:S(2)}) collective-permute-start(bf16[256,2176]{1,0:T(8,128)(2,1)} %shard_map.271.refs_13_), channel_id=1, source_target_pairs={{0,8},{4,12},{8,0},{12,4},{16,24},{20,28},{24,16},{28,20},{1,9},{5... | collective-permute-start | bytes 3342344 | tf_op jit(solution)/shard_map/ppermute | solution.py:429
  439.7 78.1 %collective-permute-start.68 = (bf16[2048,768]{1,0:T(8,128)(2,1)}, bf16[2048,768]{1,0:T(8,128)(2,1)}, u32[]{:S(2)}, u32[]{:S(2)}) collective-permute-start(bf16[2048,768]{1,0:T(8,128)(2,1)} %get-tuple-element.139.refs_3_), channel_id=1, source_target_pairs={{0,4},{4,0},{8,12},{12,8},{16,20},{20,16},{24,28},{28,24},{1,5},{5... | collective-permute-start | bytes 9437192 | tf_op jit(solution)/shard_map/ppermute | solution.py:429
  457.6 19.5 %all-to-all-start.1 = ((bf16[256,8,256]{2,0,1:T(8,128)(2,1)}), bf16[256,8,256]{2,0,1:T(8,128)(2,1)S(1)}, u32[]{:S(2)}, u32[]{:S(2)}) async-start(bf16[256,8,256]{2,0,1:T(8,128)(2,1)} %bitcast.69), calls=%async_computation.1 | async-start | bytes 2097152 | tf_op jit(solution)/shard_map/all_to_all | solution.py:1369
  474.5 30.4 %collective-permute-start.65 = (bf16[128,2176]{1,0:T(8,128)(2,1)}, bf16[128,2176]{1,0:T(8,128)(2,1)S(1)}, u32[]{:S(2)}, u32[]{:S(2)}) collective-permute-start(bf16[128,2176]{1,0:T(8,128)(2,1)} %get-tuple-element.201.refs_9_), channel_id=1, source_target_pairs={{0,16},{4,20},{8,24},{12,28},{16,0},{20,4},{24,8},{28,12},{1,17},{... | collective-permute-start | bytes 1671176 | tf_op jit(solution)/shard_map/ppermute | solution.py:429
  475.9 29.7 %collective-permute-start.66 = (bf16[128,2176]{1,0:T(8,128)(2,1)}, bf16[128,2176]{1,0:T(8,128)(2,1)}, u32[]{:S(2)}, u32[]{:S(2)}) collective-permute-start(bf16[128,2176]{1,0:T(8,128)(2,1)} %get-tuple-element.200.refs_10_), channel_id=1, source_target_pairs={{0,8},{4,12},{8,0},{12,4},{16,24},{20,28},{24,16},{28,20},{1,9},{5... | collective-permute-start | bytes 1671176 | tf_op jit(solution)/shard_map/ppermute | solution.py:429
  504.1 14.5 %collective-permute-start.71 = (bf16[256,640]{1,0:T(8,128)(2,1)}, bf16[256,640]{1,0:T(8,128)(2,1)}, u32[]{:S(2)}, u32[]{:S(2)}) collective-permute-start(bf16[256,640]{1,0:T(8,128)(2,1)} %shard_map.280), channel_id=1, source_target_pairs={{0,24},{4,28},{8,16},{12,20},{16,8},{20,12},{24,0},{28,4},{1,25},{... | collective-permute-start | bytes 983048 | tf_op jit(solution)/shard_map/ppermute | solution.py:429
  504.9 16.9 %collective-permute-start.70 = (bf16[256,640]{1,0:T(8,128)(2,1)}, bf16[256,640]{1,0:T(8,128)(2,1)}, u32[]{:S(2)}, u32[]{:S(2)}) collective-permute-start(bf16[256,640]{1,0:T(8,128)(2,1)} %shard_map.279), channel_id=1, source_target_pairs={{0,16},{4,20},{8,24},{12,28},{16,0},{20,4},{24,8},{28,12},{1,17},{... | collective-permute-start | bytes 983048 | tf_op jit(solution)/shard_map/ppermute | solution.py:429
  505.6 16.2 %collective-permute-start.69 = (bf16[256,640]{1,0:T(8,128)(2,1)}, bf16[256,640]{1,0:T(8,128)(2,1)}, u32[]{:S(2)}, u32[]{:S(2)}) collective-permute-start(bf16[256,640]{1,0:T(8,128)(2,1)} %shard_map.278), channel_id=1, source_target_pairs={{0,8},{4,12},{8,0},{12,4},{16,24},{20,28},{24,16},{28,20},{1,9},{5... | collective-permute-start | bytes 983048 | tf_op jit(solution)/shard_map/ppermute | solution.py:429
  517.6 13.6 %collective-permute-start.72 = (bf16[256,384]{1,0:T(8,128)(2,1)}, bf16[256,384]{1,0:T(8,128)(2,1)S(1)}, u32[]{:S(2)}, u32[]{:S(2)}) collective-permute-start(bf16[256,384]{1,0:T(8,128)(2,1)} %get-tuple-element.140.refs_5_), channel_id=1, source_target_pairs={{0,8},{4,12},{8,0},{12,4},{16,24},{20,28},{24,16},{28,20},{1,9},{5... | collective-permute-start | bytes 589832 | tf_op jit(solution)/shard_map/ppermute | solution.py:429
  517.9 13.3 %collective-permute-start.73 = (bf16[256,384]{1,0:T(8,128)(2,1)}, bf16[256,384]{1,0:T(8,128)(2,1)S(1)}, u32[]{:S(2)}, u32[]{:S(2)}) collective-permute-start(bf16[256,384]{1,0:T(8,128)(2,1)} %get-tuple-element.147), channel_id=1, source_target_pairs={{0,16},{4,20},{8,24},{12,28},{16,0},{20,4},{24,8},{28,12},{1,17},{... | collective-permute-start | bytes 589832 | tf_op jit(solution)/shard_map/ppermute | solution.py:429
  531.3 13.2 %collective-permute-start.75 = (bf16[256,512]{1,0:T(8,128)(2,1)S(1)}, bf16[256,512]{1,0:T(8,128)(2,1)S(1)}, u32[]{:S(2)}, u32[]{:S(2)}) collective-permute-start(bf16[256,512]{1,0:T(8,128)(2,1)S(1)} %pad_maximum_fusion.3.refs_22_.refs_31_.refs_8_), channel_id=1, source_target_pairs={{0,8},{4,12},{8,0},{12,4},{16,24},{20,28},{24,16},{28,20},{1,9},{5... | collective-permute-start | bytes 786440 | tf_op jit(solution)/shard_map/ppermute | solution.py:429
  542.9 25.2 %collective-permute-start.89 = (bf16[4,768,128]{2,1,0:T(8,128)(2,1)}, bf16[4,768,128]{2,1,0:T(8,128)(2,1)S(1)}, u32[]{:S(2)}, u32[]{:S(2)}) collective-permute-start(bf16[4,768,128]{2,1,0:T(8,128)(2,1)} %get-tuple-element.159.refs_8_), channel_id=1, source_target_pairs={{0,4},{4,0},{8,12},{12,8},{16,20},{20,16},{24,28},{28,24},{1,5},{5... | collective-permute-start | bytes 2359304 | tf_op jit(solution)/shard_map/ppermute | solution.py:429
  554.8 30.1 %collective-permute-start.78 = (bf16[256,2048]{1,0:T(8,128)(2,1)}, bf16[256,2048]{1,0:T(8,128)(2,1)}, u32[]{:S(2)}, u32[]{:S(2)}) collective-permute-start(bf16[256,2048]{1,0:T(8,128)(2,1)} %get-tuple-element.160.refs_36_), channel_id=1, source_target_pairs={{0,8},{4,12},{8,0},{12,4},{16,24},{20,28},{24,16},{28,20},{1,9},{5... | collective-permute-start | bytes 3145736 | tf_op jit(solution)/shard_map/ppermute | solution.py:429
  555.0 29.8 %collective-permute-start.79 = (bf16[256,2048]{1,0:T(8,128)(2,1)}, bf16[256,2048]{1,0:T(8,128)(2,1)}, u32[]{:S(2)}, u32[]{:S(2)}) collective-permute-start(bf16[256,2048]{1,0:T(8,128)(2,1)} %get-tuple-element.162), channel_id=1, source_target_pairs={{0,16},{4,20},{8,24},{12,28},{16,0},{20,4},{24,8},{28,12},{1,17},{... | collective-permute-start | bytes 3145736 | tf_op jit(solution)/shard_map/ppermute | solution.py:429
  576.5 18.7 %collective-permute-start.83 = (bf16[2,704,128]{2,1,0:T(8,128)(2,1)}, bf16[2,704,128]{2,1,0:T(8,128)(2,1)}, u32[]{:S(2)}, u32[]{:S(2)}) collective-permute-start(bf16[2,704,128]{2,1,0:T(8,128)(2,1)} %get-tuple-element.166), channel_id=1, source_target_pairs={{0,1},{1,0},{2,3},{3,2},{4,5},{5,4},{6,7},{7,6},{8,9},{9,8},{10,11... | collective-permute-start | bytes 1081352 | tf_op jit(solution)/shard_map/ppermute | solution.py:1381
  597.4 14.0 %collective-permute-start.92 = (bf16[768,128]{1,0:T(8,128)(2,1)S(1)}, bf16[768,128]{1,0:T(8,128)(2,1)S(1)}, u32[]{:S(2)}, u32[]{:S(2)}) collective-permute-start(bf16[768,128]{1,0:T(8,128)(2,1)S(1)} %fusion.8.refs_1_), channel_id=1, source_target_pairs={{0,8},{4,12},{8,0},{12,4},{16,24},{20,28},{24,16},{28,20},{1,9},{5... | collective-permute-start | bytes 589832 | tf_op jit(solution)/shard_map/ppermute | solution.py:429
  598.4 14.2 %collective-permute-start.93 = (bf16[768,128]{1,0:T(8,128)(2,1)S(1)}, bf16[768,128]{1,0:T(8,128)(2,1)S(1)}, u32[]{:S(2)}, u32[]{:S(2)}) collective-permute-start(bf16[768,128]{1,0:T(8,128)(2,1)S(1)} %fusion.8.refs_1_), channel_id=1, source_target_pairs={{0,16},{4,20},{8,24},{12,28},{16,0},{20,4},{24,8},{28,12},{1,17},{... | collective-permute-start | bytes 589832 | tf_op jit(solution)/shard_map/ppermute | solution.py:429
  (109 other events, 1489.0 us)
Sparse Core Ops, SparseCore 0:
  11.9 94.8 all-gather.4
  108.4 92.1 all-gather.8
  202.2 79.0 all-gather.6
  283.7 78.7 all-gather.10

commit v5 on v4

--- a/solution.py
+++ b/solution.py
@@ -423,6 +423,7 @@
 HALVES = ((1, 0), (3, 0), (2, 1), (3, 1), (2, 0), (1, 1), (0, 0), (0, 1))
 ANY = pl.BlockSpec(memory_space=pl.ANY)
 ROOMY = 60 * 2**20
+SMALL = 28 * 2**20
 
 
 def swap(value, bits):
@@ -458,7 +459,9 @@
     return pl.BlockSpec(shape, lambda *_: (0,) * len(shape))
 
 
-def call(body, scalars, operands, specs, shapes, out_specs, scratch=(), grid=(1,), cost=None, ties=()):
+def call(
+    body, scalars, operands, specs, shapes, out_specs, scratch=(), grid=(1,), cost=None, ties=(), room=ROOMY
+):
     count = len(operands)
 
     def run(*refs):
@@ -475,7 +478,7 @@
             scratch_shapes=list(scratch),
         ),
         out_shape=shapes,
-        compiler_params=pltpu.CompilerParams(vmem_limit_bytes=ROOMY),
+        compiler_params=pltpu.CompilerParams(vmem_limit_bytes=room),
         cost_estimate=None
         if cost is None
         else pl.CostEstimate(flops=cost[0], bytes_accessed=cost[1], transcendentals=0),
@@ -1374,7 +1377,7 @@
         return call(
             along_line_kernel, scalars, [keep, swap(send, 1)], [whole_spec(keep.shape)] * 2,
             [sds(shape, F32)] * 2 + [sds((2, *shape))], [whole_spec(shape)] * 2 + [whole_spec((2, *shape))],
-            ties=ties, cost=(2**20, 8 * 2**20),
+            ties=ties, cost=(2**20, 8 * 2**20), room=SMALL,
         )
 
     def line_sum(mine, onward, sent, ties):
@@ -1391,6 +1394,7 @@
             functools.partial(spread_kernel, places), scalars, plane,
             [whole_spec(piece.shape) for piece in plane],
             [sds(shape, F32) for shape in shapes], [whole_spec(shape) for shape in shapes], ties=ties,
+            room=SMALL,
         )
 
     *down_by, down_passed = scatter_rest(down_x, down_y, down_on)
@@ -1420,7 +1424,7 @@
         [whole_spec((3, group, span))] * 2 + [whole_spec((3 * latent, span))] * 2,
         [sds((rows, 3 * latent))] * 3 + [sds((rows, 3 * latent), F32)],
         [whole_spec((rows, 3 * latent))] * 4,
-        cost=(4 * group * span * 3 * latent, 4 * 2**20), ties=[z_down],
+        cost=(4 * group * span * 3 * latent, 4 * 2**20), room=SMALL, ties=[z_down],
     )
 
     def back_qkv(at, kind, ties):
@@ -1429,7 +1433,7 @@
             back_qkv_kernel, scalars, [grads_a, grads_b, qkv_own, qkv_oth],
             [part, part] + [whole_spec((width, 3 * span))] * 2,
             [sds((rows, width), kind)] * 2, [tall] * 2,
-            cost=(2 * group * span * 3 * width, 12 * 2**20), ties=ties,
+            cost=(2 * group * span * 3 * width, 12 * 2**20), room=SMALL, ties=ties,
         )
 
     pass_on, kept = back_qkv(1, F32, [to_x, *middle[1:]])
@@ -1469,7 +1473,7 @@
         [tall] + [halfspec(width)] * 4
         + [tall, tall, pl.BlockSpec((rows, 3 * latent), lambda *_: (0, 0)), whole_spec((width, 3 * latent))],
         sds((rows, width), F32), tall,
-        cost=(2 * rows * width * 3 * latent, 12 * 2**20),
+        cost=(2 * rows * width * 3 * latent, 12 * 2**20), room=SMALL,
     )
     activations = second + (wide[:, :width] + dot(hold(z_down, passed), full_b_down))
     ff_total = line_sum(ff_mine, *ff_rest, [activations])

time: 650 us -> 646 us (level)
  Pallas kernels: 302 us -> 288 us
  local copies, waits for them, and re-layouts: 25.7 us -> 38.5 us
    pallas_call x29, Pallas kernels: 302 us -> 288 us  [call(): pl.pallas_call(run, grid_spec=pltpu.PrefetchScalarGridSpec(num_scalar_pre...]
    unnamed x155 -> x171, local copies, waits for them, and re-layouts: 15.4 us -> 23.2 us
  transfers between devices with their start and end apart: 102 -> 102, of which waited for: 22 -> 20; matrix products, arithmetic and copies ran while one was open for 5% -> 7% of each run, Pallas kernels for 44% -> 42%
where the time goes in v5:
time: 646 us; the launch traced here: 636 us
  Pallas kernels  288 us (45%)
  waiting for transfers between devices  158 us (24%)
  starting transfers between devices  106 us (16%)
  local copies, waits for them, and re-layouts  38.5 us (6%)
  other arithmetic  27 us (4%)
  between operations  15 us (2%)
    pallas_call x29, Pallas kernels, call(): pl.pallas_call(run, grid_spec=pltpu.PrefetchScalarGridSpec(num_scalar_pre...  288 us
    ppermute x92, starting transfers between devices, swap(): return lax.ppermute(value, 'seq', [(i, i ^ bits) for i in range(PLANE)])  96.5 us
    ppermute x92, waiting for transfers between devices, swap(): return lax.ppermute(value, 'seq', [(i, i ^ bits) for i in range(PLANE)])  63.1 us
    all_gather x2, waiting for transfers between devices, plane_shards(): lax.all_gather(part, 'fsdp', axis=0, tiled=True)  41.5 us
    all_gather x1, waiting for transfers between devices, plane_shards(): first_all = lax.all_gather(first_part, 'fsdp', axis=0, tiled=True)  35 us
    unnamed x171, local copies, waits for them, and re-layouts  23.2 us
  transfers between devices with their start and end apart: 102, of which 20 were waited for; matrix products, arithmetic and copies ran while one was open for 7% of the time, Pallas kernels for 42%

profile of v5, /device:TPU:1, one launch (start us, length us, event | category | flops | bytes accessed | tf_op | source)
XLA Modules:
  0.0 635.7 jit_solution(4715405166077851209)
XLA Ops:
  8.6 3.3 shard_map.250.refs_5_
  12.0 4.4 shard_map.259
  16.4 3.6 shard_map.249
  20.0 2.1 collective-permute-start.1
  23.8 10.3 %collective-permute-done.1.refs_5_ = bf16[128,2048]{1,0:T(8,128)(2,1)S(1)} collective-permute-done((bf16[128,2048]{1,0:T(8,128)(2,1)}, bf16[128,2048]{1,0:T(8,128)(2,1)S(1)}, u32[]{:S(2)}, u32[]{:S(2)}) %collective-permute-start.1) | collective-permute-done | bytes 524320 | tf_op jit(solution)/shard_map/ppermute | solution.py:430
  36.4 8.9 %collective-permute-done.14.refs_12_.refs_11_.refs_21_ = bf16[128,2048]{1,0:T(8,128)(2,1)S(1)} collective-permute-done((bf16[128,2048]{1,0:T(8,128)(2,1)S(1)}, bf16[128,2048]{1,0:T(8,128)(2,1)S(1)}, u32[]{:S(2)}, u32[]{:S(2)}) %collective-permute-start.14) | collective-permute-done | bytes 524320 | tf_op jit(solution)/shard_map/ppermute | solution.py:430
  47.7 9.6 %collective-permute-done.2.refs_2_ = bf16[128,2048]{1,0:T(8,128)(2,1)} collective-permute-done((bf16[128,2048]{1,0:T(8,128)(2,1)S(1)}, bf16[128,2048]{1,0:T(8,128)(2,1)}, u32[]{:S(2)}, u32[]{:S(2)}) %collective-permute-start.2) | collective-permute-done | bytes 524320 | tf_op jit(solution)/shard_map/ppermute | solution.py:430
  57.3 3.3 collective-permute-start.7
  62.1 6.5 %collective-permute-done.15.refs_3_.refs_13_.refs_10_.refs_18_ = bf16[128,2048]{1,0:T(8,128)(2,1)S(1)} collective-permute-done((bf16[128,2048]{1,0:T(8,128)(2,1)S(1)}, bf16[128,2048]{1,0:T(8,128)(2,1)S(1)}, u32[]{:S(2)}, u32[]{:S(2)}) %collective-permute-start.15) | collective-permute-done | bytes 524320 | tf_op jit(solution)/shard_map/ppermute | solution.py:430
  69.0 2.9 collective-permute-start.12
  72.0 35.0 %all-gather.5.cloned.1.call-done.refs_0_ = bf16[3200,768]{1,0:T(8,128)(2,1)} async-done(((bf16[800,768]{1,0:T(8,128)(2,1)}), bf16[3200,768]{1,0:T(8,128)(2,1)}) %all-gather.5.cloned.1.call-update) | async-done | bytes 4915216 | tf_op jit(solution)/shard_map/all_gather | solution.py:1171
  117.3 2.4 collective-permute-start.31
  119.8 5.0 collective-permute-done.22.refs_6_
  126.3 2.3 collective-permute-start.24
  128.6 3.7 multiply_sine_fusion
  136.4 2.3 fusion.14
  143.0 5.5 shard_map.252
  152.4 2.6 collective-permute-done.34.refs_5_
  156.4 22.2 %shard_map.253 = (bf16[2048,768]{1,0:T(8,128)(2,1)}, bf16[2048,384]{1,0:T(8,128)(2,1)}, bf16[2048,768]{1,0:T(8,128)(2,1)}) custom-call(s32[11]{0:T(128)} %concatenate.24.refs_0_, bf16[128,2048]{1,0:T(8,128)(2,1)} %collective-permute-done.refs_1_, bf16[128,2048]{1,0:T(8,128)(2,1)} %collective-permute-done.2.refs_2_, ...), custom_call_target="tpu_custom_call" | custom-call | flops 9663676416 | bytes 20971520 | tf_op jit(solution)/shard_map/pallas_call | solution.py:471
  180.1 16.0 %shard_map.254 = (bf16[2048,256]{1,0:T(8,128)(2,1)}, f32[2048,256]{1,0:T(8,128)}) custom-call(s32[11]{0:T(128)} %concatenate.24.refs_0_, bf16[2048,768]{1,0:T(8,128)(2,1)} %get-tuple-element.98.refs_1_.refs_2_.refs_3_, bf16[2048,768]{1,0:T(8,128)(2,1)} %get-tuple-element.98.refs_1_.refs_2_.refs_3_, bf16[2048,768]{1,0:T(8,128)(2,1)} %get-tuple-element.98.refs_1_.refs_2_.refs_3_), custom_call_target="tpu_custom_call" | custom-call | flops 4294967296 | bytes 8388608 | tf_op jit(solution)/shard_map/pallas_call | solution.py:471
  196.6 3.6 all-to-all-start
  201.5 10.7 %all-to-all-done = bf16[8,256,256]{2,1,0:T(8,128)(2,1)S(1)} async-done(((bf16[8,256,256]{2,1,0:T(8,128)(2,1)}), bf16[8,256,256]{2,1,0:T(8,128)(2,1)S(1)}, u32[]{:S(2)}, u32[]{:S(2)}) %all-to-all-start) | async-done | bytes 1048608 | tf_op jit(solution)/shard_map/all_to_all | solution.py:1262
  214.1 8.3 %shard_map.257.refs_2_.refs_9_ = bf16[2048,2048]{1,0:T(8,128)(2,1)} custom-call(s32[11]{0:T(128)} %concatenate.24.refs_0_, bf16[384,768]{1,0:T(8,128)(2,1)} %copy-done.56, bf16[384,768]{1,0:T(8,128)(2,1)} %collective-permute-done.35.refs_2_, bf16[384,768]{1,0:T(8,128)(2,1)} %collective-permute-done.36.refs_3_, ...), custom_call_target="tpu_custom_call" | custom-call | tf_op jit(solution)/shard_map/pallas_call | solution.py:471
  223.5 9.6 %shard_map.258 = (f32[256,2048]{1,0:T(8,128)}, bf16[128,2048]{1,0:T(8,128)(2,1)}, bf16[128,2048]{1,0:T(8,128)(2,1)}, bf16[256,128]{1,0:T(8,128)(2,1)}) custom-call(s32[11]{0:T(128)} %concatenate.24.refs_0_, bf16[256,2048]{1,0:T(8,128)(2,1)} %bitcast.91, bf16[2048,2048]{1,0:T(8,128)(2,1)} %shard_map.257.refs_2_.refs_9_, ...), custom_call_target="tpu_custom_call" | custom-call | flops 2147483648 | bytes 12582912 | tf_op jit(solution)/shard_map/pallas_call | solution.py:471
  234.2 2.3 collective-permute-start.50
  237.8 5.6 collective-permute-done.48.refs_8_.refs_7_.refs_13_
  243.4 6.4 %collective-permute-start.49 = (bf16[128,2048]{1,0:T(8,128)(2,1)}, bf16[128,2048]{1,0:T(8,128)(2,1)S(1)}, u32[]{:S(2)}, u32[]{:S(2)}) collective-permute-start(bf16[128,2048]{1,0:T(8,128)(2,1)} %collective-permute-done.48.refs_8_.refs_7_.refs_13_), channel_id=1, source_target_pairs={{0,8},{4,12},{8,0},{12,4},{16,24},{20,28},{24,16},{28,20},{1,9},{5... | collective-permute-start | bytes 1572872 | tf_op jit(solution)/shard_map/ppermute | solution.py:430
  249.9 31.5 %all-gather.7.cloned.1.call-done.refs_0_ = bf16[2048,1024]{1,0:T(8,128)(2,1)} async-done(((bf16[512,1024]{1,0:T(8,128)(2,1)}), bf16[2048,1024]{1,0:T(8,128)(2,1)}) %all-gather.7.cloned.1.call-update) | async-done | bytes 4194320 | tf_op jit(solution)/shard_map/all_gather | solution.py:1181
  287.9 2.9 collective-permute-done.52.refs_6_
  290.8 22.1 %shard_map.262 = (f32[512,2304]{1,0:T(8,128)}, bf16[512,512]{1,0:T(8,128)(2,1)}, bf16[512,1024]{1,0:T(8,128)(2,1)}, bf16[512,512]{1,0:T(8,128)(2,1)}, bf16[512,1...) custom-call(s32[11]{0:T(128)} %concatenate.24.refs_0_, ...), custom_call_target="tpu_custom_call" | custom-call | flops 10737418240 | bytes 27262976 | tf_op jit(solution)/shard_map/pallas_call | solution.py:471
  312.9 8.2 %shard_map.265.refs_4_.refs_5_ = f32[512,2176]{1,0:T(8,128)} custom-call(s32[11]{0:T(128)} %concatenate.24.refs_0_, bf16[512,512]{1,0:T(8,128)(2,1)} %get-tuple-element.116.refs_1_.refs_7_, bf16[512,512]{1,0:T(8,128)(2,1)} %get-tuple-element.117.refs_2_.refs_11_, bf16[1024,2432]{1,0:T(8,128)(2,1)} %shard_map.261.refs_5_.refs_3_.refs_4_, ...), custom_call_target="tpu_custom_call" | custom-call | flops 2147483648 | bytes 12582912 | tf_op jit(solution)/shard_map/pallas_call | solution.py:471
  322.3 22.2 %shard_map.263 = (f32[512,2304]{1,0:T(8,128)}, bf16[512,512]{1,0:T(8,128)(2,1)}, bf16[512,1024]{1,0:T(8,128)(2,1)}, bf16[512,512]{1,0:T(8,128)(2,1)}, bf16[512,1...) custom-call(s32[11]{0:T(128)} %concatenate.24.refs_0_, ...), custom_call_target="tpu_custom_call" | custom-call | flops 10737418240 | bytes 27262976 | tf_op jit(solution)/shard_map/pallas_call | solution.py:471
  344.5 8.2 %shard_map.264.refs_3_.refs_5_ = f32[512,2176]{1,0:T(8,128)} custom-call(s32[11]{0:T(128)} %concatenate.24.refs_0_, bf16[512,512]{1,0:T(8,128)(2,1)} %get-tuple-element.114.refs_1_.refs_5_, bf16[512,512]{1,0:T(8,128)(2,1)} %get-tuple-element.115.refs_2_.refs_9_, bf16[1024,2432]{1,0:T(8,128)(2,1)} %shard_map.261.refs_5_.refs_3_.refs_4_, ...), custom_call_target="tpu_custom_call" | custom-call | flops 2147483648 | bytes 12582912 | tf_op jit(solution)/shard_map/pallas_call | solution.py:471
  352.7 10.0 %all-gather.11.cloned.1.call-done.refs_0_ = bf16[2048,1024]{1,0:T(8,128)(2,1)} async-done(((bf16[512,1024]{1,0:T(8,128)(2,1)}), bf16[2048,1024]{1,0:T(8,128)(2,1)}) %all-gather.11.cloned.1.call-update) | async-done | bytes 4194320 | tf_op jit(solution)/shard_map/all_gather | solution.py:1181
  363.3 13.7 %shard_map.268 = (f32[512,2304]{1,0:T(8,128)}, bf16[512,512]{1,0:T(8,128)(2,1)}, bf16[512,1024]{1,0:T(8,128)(2,1)}) custom-call(s32[11]{0:T(128)} %concatenate.24.refs_0_, bf16[512,256]{1,0:T(8,128)(2,1)} %get-tuple-element.121.refs_1_, bf16[512,128]{1,0:T(8,128)(2,1)} %get-tuple-element.122.refs_2_.refs_3_, bf16[2048,1024]{1,0:T(8,128)(2,1)} %shard_map.266.refs_3_, ...), custom_call_target="tpu_custom_call" | custom-call | flops 5368709120 | bytes 27262976 | tf_op jit(solution)/shard_map/pallas_call | solution.py:471
  377.0 13.4 %shard_map.269 = (bf16[256,2304]{1,0:T(8,128)(2,1)}, bf16[256,2304]{1,0:T(8,128)(2,1)}, bf16[512,512]{1,0:T(8,128)(2,1)}, bf16[512,1024]{1,0:T(8,128)(2,1)}) custom-call(s32[11]{0:T(128)} %concatenate.24.refs_0_, bf16[512,256]{1,0:T(8,128)(2,1)} %get-tuple-element.121.refs_1_, bf16[512,128]{1,0:T(8,128)(2,1)} %get-tuple-element.122.refs_2_.refs_3_, ...), custom_call_target="tpu_custom_call" | custom-call | flops 5368709120 | bytes 27262976 | tf_op jit(solution)/shard_map/pallas_call | solution.py:471
  393.0 21.5 %shard_map.267 = (f32[256,2304]{1,0:T(8,128)}, f32[256,2304]{1,0:T(8,128)}, bf16[512,512]{1,0:T(8,128)(2,1)}, bf16[512,1024]{1,0:T(8,128)(2,1)}, bf16[512,512]{1,0:T(8,128)(2,1)}, /*index=5*/bf16[512,1024]{1,0:T(8,128)(2,1)}) custom-call(s32[11]{0:T(128)} %concatenate.24.refs_0_, bf16[512,256]{1,0:T(8,128)(2,1)} %get-tuple-element.109.refs_1_.refs_2_, ...), custom_call_target="tpu_custom_call" | custom-call | flops 10737418240 | bytes 27262976 | tf_op jit(solution)/shard_map/pallas_call | solution.py:471
  414.5 3.9 collective-permute-done.59.refs_2_
  419.3 3.1 add_convert_fusion
  424.4 8.6 %shard_map.270 = (bf16[256,2176]{1,0:T(8,128)(2,1)}, bf16[256,2176]{1,0:T(8,128)(2,1)}) custom-call(s32[11]{0:T(128)} %concatenate.24.refs_0_, bf16[512,512]{1,0:T(8,128)(2,1)} %get-tuple-element.128.refs_1_.refs_13_, bf16[512,512]{1,0:T(8,128)(2,1)} %get-tuple-element.129.refs_2_.refs_17_, bf16[1024,2432]{1,0:T(8,128)(2,1)} %shard_map.261.refs_5_.refs_3_.refs_4_, ...), custom_call_target="tpu_custom_call" | custom-call | flops 2147483648 | bytes 12582912 | tf_op jit(solution)/shard_map/pallas_call | solution.py:471
  433.0 3.3 collective-permute-done.61.refs_1_.refs_4_
  439.7 2.2 collective-permute-start.68
  441.9 13.4 %shard_map.272 = (f32[256,2048]{1,0:T(8,128)}, bf16[256,2048]{1,0:T(8,128)(2,1)}, bf16[256,640]{1,0:T(8,128)(2,1)}, bf16[256,640]{1,0:T(8,128)(2,1)}, bf16[256,6...) custom-call(s32[11]{0:T(128)} %concatenate.24.refs_0_, f32[256,2304]{1,0:T(8,128)} %get-tuple-element.120.refs_1_, ...), custom_call_target="tpu_custom_call" | custom-call | flops 2147483648 | bytes 16777216 | tf_op jit(solution)/shard_map/pallas_call | solution.py:471
  455.3 2.3 copy.137
  457.5 3.9 all-to-all-start.1
  461.4 9.4 %shard_map.273 = (f32[256,2176]{1,0:T(8,128)}, f32[256,2176]{1,0:T(8,128)}) custom-call(s32[11]{0:T(128)} %concatenate.24.refs_0_, bf16[512,512]{1,0:T(8,128)(2,1)} %get-tuple-element.118.refs_1_.refs_15_, bf16[512,512]{1,0:T(8,128)(2,1)} %get-tuple-element.119.refs_2_.refs_19_, bf16[1024,2432]{1,0:T(8,128)(2,1)} %shard_map.261.refs_5_.refs_3_.refs_4_, ...), custom_call_target="tpu_custom_call" | custom-call | flops 2147483648 | bytes 12582912 | tf_op jit(solution)/shard_map/pallas_call | solution.py:471
  470.8 3.3 add_convert_fusion.2
  477.7 25.0 %shard_map.275 = (bf16[3,1024,256]{2,1,0:T(8,128)(2,1)}, bf16[3,1024,256]{2,1,0:T(8,128)(2,1)}, f32[3,128,256]{2,1,0:T(8,128)}) custom-call(s32[11]{0:T(128)} %concatenate.24.refs_0_, bf16[2048,768]{1,0:T(8,128)(2,1)} %get-tuple-element.98.refs_1_.refs_2_.refs_3_, bf16[2048,768]{1,0:T(8,128)(2,1)} %get-tuple-element.98.refs_1_.refs_2_.refs_3_, ...), custom_call_target="tpu_custom_call" | custom-call | flops 10737418240 | bytes 16777216 | tf_op jit(solution)/shard_map/pallas_call | solution.py:471
  506.5 2.4 fusion.3
  522.1 6.0 shard_map.281
  532.4 8.9 %shard_map.282 = (f32[4,768,128]{2,1,0:T(8,128)}, bf16[4,768,128]{2,1,0:T(8,128)(2,1)}) custom-call(s32[11]{0:T(128)} %concatenate.24.refs_0_, bf16[512,256]{1,0:T(8,128)(2,1)} %get-tuple-element.121.refs_1_, bf16[512,256]{1,0:T(8,128)(2,1)} %get-tuple-element.109.refs_1_.refs_2_, bf16[512,128]{1,0:T(8,128)(2,1)} %get-tuple-element.122.refs_2_.refs_3_, ...), custom_call_target="tpu_custom_call" | custom-call | flops 4294967296 | bytes 12582912 | tf_op jit(solution)/shard_map/pallas_call | solution.py:471
  541.3 2.8 collective-permute-start.89
  544.2 2.0 copy-done.26
  547.4 7.2 %shard_map.283 = (bf16[256,2048]{1,0:T(8,128)(2,1)}, bf16[256,2048]{1,0:T(8,128)(2,1)}) custom-call(s32[11]{0:T(128)S(1)} %copy-done.23, bf16[3,1024,256]{2,1,0:T(8,128)(2,1)S(1)} %copy-done.5, bf16[3,1024,256]{2,1,0:T(8,128)(2,1)S(1)} %collective-permute-done.67.refs_2_, bf16[2048,768]{1,0:T(8,128)(2,1)S(1)} %copy-done.26, ...), custom_call_target="tpu_custom_call" | custom-call | flops 3221225472 | bytes 12582912 | tf_op jit(solution)/shard_map/pallas_call | solution.py:471
  556.1 9.7 %shard_map.284 = (f32[4,704,128]{2,1,0:T(8,128)}, bf16[4,704,128]{2,1,0:T(8,128)(2,1)}) custom-call(s32[11]{0:T(128)} %concatenate.24.refs_0_, bf16[128,2048]{1,0:T(8,128)(2,1)} %collective-permute-done.refs_1_, bf16[128,2048]{1,0:T(8,128)(2,1)} %collective-permute-done.2.refs_2_, bf16[128,2048]{1,0:T(8,128)(2,1)} %collective-permute-done.3.refs_3_, ...), custom_call_target="tpu_custom_call" | custom-call | flops 805306368 | bytes 8388608 | tf_op jit(solution)/shard_map/pallas_call | solution.py:471
  568.5 2.5 shard_map.290
  573.9 2.5 shard_map.288
  577.1 5.7 collective-permute-done.90
  588.1 3.8 fusion.refs_1_
  603.2 4.9 shard_map.287.refs_1_
  613.4 4.1 collective-permute-start.95
  617.7 3.6 collective-permute-start.88
  621.3 3.7 shard_map.292
  626.6 2.3 shard_map.293
  (400 shorter events, 118.0 us)
Async XLA Ops:
  7.2 99.7 %all-gather.5.cloned.1.call-start = ((), (), s32[]{:S(2)}) async-start(), calls=%async_computation.2 | async-start | bytes 6144000 | tf_op jit(solution)/shard_map/all_gather | solution.py:1171
  11.9 224.6 %all-gather.9.cloned.1.call-start = ((), (), s32[]{:S(2)}) async-start(), calls=%async_computation.4 | async-start | bytes 6225920 | tf_op jit(solution)/shard_map/all_gather | solution.py:1180
  16.4 265.0 %all-gather.7.cloned.1.call-start = ((), (), s32[]{:S(2)}) async-start(), calls=%async_computation.3 | async-start | bytes 5242880 | tf_op jit(solution)/shard_map/all_gather | solution.py:1181
  20.0 14.1 %collective-permute-start.1 = (bf16[128,2048]{1,0:T(8,128)(2,1)}, bf16[128,2048]{1,0:T(8,128)(2,1)S(1)}, u32[]{:S(2)}, u32[]{:S(2)}) collective-permute-start(bf16[128,2048]{1,0:T(8,128)(2,1)} %get-tuple-element.95.refs_7_), channel_id=1, source_target_pairs={{0,16},{4,20},{8,24},{12,28},{16,0},{20,4},{24,8},{28,12},{1,17},{... | collective-permute-start | bytes 1572872 | tf_op jit(solution)/shard_map/ppermute | solution.py:430
  23.4 21.9 %collective-permute-start.14 = (bf16[128,2048]{1,0:T(8,128)(2,1)S(1)}, bf16[128,2048]{1,0:T(8,128)(2,1)S(1)}, u32[]{:S(2)}, u32[]{:S(2)}) collective-permute-start(bf16[128,2048]{1,0:T(8,128)(2,1)S(1)} %get-tuple-element.205.refs_14_.refs_13_.refs_23_), channel_id=1, source_target_pairs={{0,16},{4,20},{8,24},{12,28},{16,0},{20,4},{24,8},{28,12},{1,17},{... | collective-permute-start | bytes 1572872 | tf_op jit(solution)/shard_map/ppermute | solution.py:430
  23.7 22.7 %collective-permute-start.16 = (bf16[128,2048]{1,0:T(8,128)(2,1)S(1)}, bf16[128,2048]{1,0:T(8,128)(2,1)}, u32[]{:S(2)}, u32[]{:S(2)}) collective-permute-start(bf16[128,2048]{1,0:T(8,128)(2,1)S(1)} %get-tuple-element.204.refs_15_.refs_14_.refs_24_), channel_id=1, source_target_pairs={{0,8},{4,12},{8,0},{12,4},{16,24},{20,28},{24,16},{28,20},{1,9},{5... | collective-permute-start | bytes 1572872 | tf_op jit(solution)/shard_map/ppermute | solution.py:430
  34.1 23.2 %collective-permute-start.2 = (bf16[128,2048]{1,0:T(8,128)(2,1)S(1)}, bf16[128,2048]{1,0:T(8,128)(2,1)}, u32[]{:S(2)}, u32[]{:S(2)}) collective-permute-start(bf16[128,2048]{1,0:T(8,128)(2,1)S(1)} %collective-permute-done.1.refs_5_), channel_id=1, source_target_pairs={{0,8},{4,12},{8,0},{12,4},{16,24},{20,28},{24,16},{28,20},{1,9},{5... | collective-permute-start | bytes 1572872 | tf_op jit(solution)/shard_map/ppermute | solution.py:430
  35.1 25.5 %collective-permute-start.5 = (bf16[128,2048]{1,0:T(8,128)(2,1)S(1)}, bf16[128,2048]{1,0:T(8,128)(2,1)}, u32[]{:S(2)}, u32[]{:S(2)}) collective-permute-start(bf16[128,2048]{1,0:T(8,128)(2,1)S(1)} %collective-permute-done.4.refs_6_), channel_id=1, source_target_pairs={{0,16},{4,20},{8,24},{12,28},{16,0},{20,4},{24,8},{28,12},{1,17},{... | collective-permute-start | bytes 1572872 | tf_op jit(solution)/shard_map/ppermute | solution.py:430
  45.3 23.2 %collective-permute-start.15 = (bf16[128,2048]{1,0:T(8,128)(2,1)S(1)}, bf16[128,2048]{1,0:T(8,128)(2,1)S(1)}, u32[]{:S(2)}, u32[]{:S(2)}) collective-permute-start(bf16[128,2048]{1,0:T(8,128)(2,1)S(1)} %collective-permute-done.14.refs_12_.refs_11_.refs_21_), channel_id=1, source_target_pairs={{0,8},{4,12},{8,0},{12,4},{16,24},{20,28},{24,16},{28,20},{1,9},{5... | collective-permute-start | bytes 1572872 | tf_op jit(solution)/shard_map/ppermute | solution.py:430
  46.4 22.6 %collective-permute-start.17 = (bf16[128,2048]{1,0:T(8,128)(2,1)}, bf16[128,2048]{1,0:T(8,128)(2,1)S(1)}, u32[]{:S(2)}, u32[]{:S(2)}) collective-permute-start(bf16[128,2048]{1,0:T(8,128)(2,1)} %collective-permute-done.16.refs_13_.refs_12_.refs_22_), channel_id=1, source_target_pairs={{0,16},{4,20},{8,24},{12,28},{16,0},{20,4},{24,8},{28,12},{1,17},{... | collective-permute-start | bytes 1572872 | tf_op jit(solution)/shard_map/ppermute | solution.py:430
  57.3 14.6 %collective-permute-start.7 = (bf16[128,2048]{1,0:T(8,128)(2,1)}, bf16[128,2048]{1,0:T(8,128)(2,1)}, u32[]{:S(2)}, u32[]{:S(2)}) collective-permute-start(bf16[128,2048]{1,0:T(8,128)(2,1)} %collective-permute-done.2.refs_2_), channel_id=1, source_target_pairs={{0,4},{4,0},{8,12},{12,8},{16,20},{20,16},{24,28},{28,24},{1,5},{5... | collective-permute-start | bytes 1572872 | tf_op jit(solution)/shard_map/ppermute | solution.py:430
  60.7 49.9 %collective-permute-start = (bf16[128,2048]{1,0:T(8,128)(2,1)S(1)}, bf16[128,2048]{1,0:T(8,128)(2,1)}, u32[]{:S(2)}, u32[]{:S(2)}) collective-permute-start(bf16[128,2048]{1,0:T(8,128)(2,1)S(1)} %copy-done.59), channel_id=1, source_target_pairs={{0,8},{4,12},{8,0},{12,4},{16,24},{20,28},{24,16},{28,20},{1,9},{5... | collective-permute-start | bytes 1572872 | tf_op jit(solution)/shard_map/ppermute | solution.py:430
  68.6 43.3 %collective-permute-start.3 = (bf16[128,2048]{1,0:T(8,128)(2,1)S(1)}, bf16[128,2048]{1,0:T(8,128)(2,1)}, u32[]{:S(2)}, u32[]{:S(2)}) collective-permute-start(bf16[128,2048]{1,0:T(8,128)(2,1)S(1)} %copy-done.60), channel_id=1, source_target_pairs={{0,16},{4,20},{8,24},{12,28},{16,0},{20,4},{24,8},{28,12},{1,17},{... | collective-permute-start | bytes 1572872 | tf_op jit(solution)/shard_map/ppermute | solution.py:430
  69.0 43.2 %collective-permute-start.12 = (bf16[128,2048]{1,0:T(8,128)(2,1)S(1)}, bf16[128,2048]{1,0:T(8,128)(2,1)}, u32[]{:S(2)}, u32[]{:S(2)}) collective-permute-start(bf16[128,2048]{1,0:T(8,128)(2,1)S(1)} %copy-done.59), channel_id=1, source_target_pairs={{0,4},{4,0},{8,12},{12,8},{16,20},{20,16},{24,28},{28,24},{1,5},{5... | collective-permute-start | bytes 1572872 | tf_op jit(solution)/shard_map/ppermute | solution.py:430
  71.9 40.6 %collective-permute-start.13 = (bf16[128,2048]{1,0:T(8,128)(2,1)S(1)}, bf16[128,2048]{1,0:T(8,128)(2,1)}, u32[]{:S(2)}, u32[]{:S(2)}) collective-permute-start(bf16[128,2048]{1,0:T(8,128)(2,1)S(1)} %copy-done.60), channel_id=1, source_target_pairs={{0,4},{4,0},{8,12},{12,8},{16,20},{20,16},{24,28},{28,24},{1,5},{5... | collective-permute-start | bytes 1572872 | tf_op jit(solution)/shard_map/ppermute | solution.py:430
  110.6 15.4 %collective-permute-start.18 = (bf16[192,768]{1,0:T(8,128)(2,1)S(1)}, bf16[192,768]{1,0:T(8,128)(2,1)S(1)}, u32[]{:S(2)}, u32[]{:S(2)}) collective-permute-start(bf16[192,768]{1,0:T(8,128)(2,1)S(1)} %bitcast.101), channel_id=1, source_target_pairs={{0,8},{4,12},{8,0},{12,4},{16,24},{20,28},{24,16},{28,20},{1,9},{5... | collective-permute-start | bytes 884744 | tf_op jit(solution)/shard_map/ppermute | solution.py:430
  112.2 14.1 %collective-permute-start.21 = (bf16[192,768]{1,0:T(8,128)(2,1)S(1)}, bf16[192,768]{1,0:T(8,128)(2,1)}, u32[]{:S(2)}, u32[]{:S(2)}) collective-permute-start(bf16[192,768]{1,0:T(8,128)(2,1)S(1)} %bitcast.97), channel_id=1, source_target_pairs={{0,16},{4,20},{8,24},{12,28},{16,0},{20,4},{24,8},{28,12},{1,17},{... | collective-permute-start | bytes 884744 | tf_op jit(solution)/shard_map/ppermute | solution.py:430
  115.3 17.0 %collective-permute-start.30 = (bf16[192,768]{1,0:T(8,128)(2,1)S(1)}, bf16[192,768]{1,0:T(8,128)(2,1)S(1)}, u32[]{:S(2)}, u32[]{:S(2)}) collective-permute-start(bf16[192,768]{1,0:T(8,128)(2,1)S(1)} %bitcast.102), channel_id=1, source_target_pairs={{0,4},{4,0},{8,12},{12,8},{16,20},{20,16},{24,28},{28,24},{1,5},{5... | collective-permute-start | bytes 884744 | tf_op jit(solution)/shard_map/ppermute | solution.py:430
  117.3 15.0 %collective-permute-start.31 = (bf16[192,768]{1,0:T(8,128)(2,1)S(1)}, bf16[192,768]{1,0:T(8,128)(2,1)S(1)}, u32[]{:S(2)}, u32[]{:S(2)}) collective-permute-start(bf16[192,768]{1,0:T(8,128)(2,1)S(1)} %bitcast.98), channel_id=1, source_target_pairs={{0,4},{4,0},{8,12},{12,8},{16,20},{20,16},{24,28},{28,24},{1,5},{5... | collective-permute-start | bytes 884744 | tf_op jit(solution)/shard_map/ppermute | solution.py:430
  139.8 15.2 %collective-permute-start.34 = (bf16[384,768]{1,0:T(8,128)(2,1)}, bf16[384,768]{1,0:T(8,128)(2,1)}, u32[]{:S(2)}, u32[]{:S(2)}) collective-permute-start(bf16[384,768]{1,0:T(8,128)(2,1)} %shard_map.255.refs_7_), channel_id=1, source_target_pairs={{0,16},{4,20},{8,24},{12,28},{16,0},{20,4},{24,8},{28,12},{1,17},{... | collective-permute-start | bytes 1769480 | tf_op jit(solution)/shard_map/ppermute | solution.py:430
  148.5 30.7 %collective-permute-start.33 = (bf16[384,768]{1,0:T(8,128)(2,1)S(1)}, bf16[384,768]{1,0:T(8,128)(2,1)S(1)}, u32[]{:S(2)}, u32[]{:S(2)}) collective-permute-start(bf16[384,768]{1,0:T(8,128)(2,1)S(1)} %copy-done.35), channel_id=1, source_target_pairs={{0,8},{4,12},{8,0},{12,4},{16,24},{20,28},{24,16},{28,20},{1,9},{5... | collective-permute-start | bytes 1769480 | tf_op jit(solution)/shard_map/ppermute | solution.py:430
  148.8 29.8 %collective-permute-start.37 = (bf16[384,768]{1,0:T(8,128)(2,1)S(1)}, bf16[384,768]{1,0:T(8,128)(2,1)}, u32[]{:S(2)}, u32[]{:S(2)}) collective-permute-start(bf16[384,768]{1,0:T(8,128)(2,1)S(1)} %copy-done.32), channel_id=1, source_target_pairs={{0,8},{4,12},{8,0},{12,4},{16,24},{20,28},{24,16},{28,20},{1,9},{5... | collective-permute-start | bytes 1769480 | tf_op jit(solution)/shard_map/ppermute | solution.py:430
  150.0 29.4 %collective-permute-start.36 = (bf16[384,768]{1,0:T(8,128)(2,1)S(1)}, bf16[384,768]{1,0:T(8,128)(2,1)}, u32[]{:S(2)}, u32[]{:S(2)}) collective-permute-start(bf16[384,768]{1,0:T(8,128)(2,1)S(1)} %copy-done.32), channel_id=1, source_target_pairs={{0,16},{4,20},{8,24},{12,28},{16,0},{20,4},{24,8},{28,12},{1,17},{... | collective-permute-start | bytes 1769480 | tf_op jit(solution)/shard_map/ppermute | solution.py:430
  151.2 28.8 %collective-permute-start.45 = (bf16[384,768]{1,0:T(8,128)(2,1)S(1)}, bf16[384,768]{1,0:T(8,128)(2,1)S(1)}, u32[]{:S(2)}, u32[]{:S(2)}) collective-permute-start(bf16[384,768]{1,0:T(8,128)(2,1)S(1)} %copy-done.35), channel_id=1, source_target_pairs={{0,4},{4,0},{8,12},{12,8},{16,20},{20,16},{24,28},{28,24},{1,5},{5... | collective-permute-start | bytes 1769480 | tf_op jit(solution)/shard_map/ppermute | solution.py:430
  155.0 41.1 %collective-permute-start.46 = (bf16[384,768]{1,0:T(8,128)(2,1)S(1)}, bf16[384,768]{1,0:T(8,128)(2,1)}, u32[]{:S(2)}, u32[]{:S(2)}) collective-permute-start(bf16[384,768]{1,0:T(8,128)(2,1)S(1)} %copy-done.32), channel_id=1, source_target_pairs={{0,4},{4,0},{8,12},{12,8},{16,20},{20,16},{24,28},{28,24},{1,5},{5... | collective-permute-start | bytes 1769480 | tf_op jit(solution)/shard_map/ppermute | solution.py:430
  178.6 21.8 %collective-permute-start.35 = (bf16[384,768]{1,0:T(8,128)(2,1)}, bf16[384,768]{1,0:T(8,128)(2,1)}, u32[]{:S(2)}, u32[]{:S(2)}) collective-permute-start(bf16[384,768]{1,0:T(8,128)(2,1)} %collective-permute-done.34.refs_5_), channel_id=1, source_target_pairs={{0,8},{4,12},{8,0},{12,4},{16,24},{20,28},{24,16},{28,20},{1,9},{5... | collective-permute-start | bytes 1769480 | tf_op jit(solution)/shard_map/ppermute | solution.py:430
  179.1 21.4 %collective-permute-start.38 = (bf16[384,768]{1,0:T(8,128)(2,1)}, bf16[384,768]{1,0:T(8,128)(2,1)}, u32[]{:S(2)}, u32[]{:S(2)}) collective-permute-start(bf16[384,768]{1,0:T(8,128)(2,1)} %collective-permute-done.37.refs_6_), channel_id=1, source_target_pairs={{0,16},{4,20},{8,24},{12,28},{16,0},{20,4},{24,8},{28,12},{1,17},{... | collective-permute-start | bytes 1769480 | tf_op jit(solution)/shard_map/ppermute | solution.py:430
  179.4 21.6 %collective-permute-start.39 = (bf16[384,768]{1,0:T(8,128)(2,1)S(1)}, bf16[384,768]{1,0:T(8,128)(2,1)}, u32[]{:S(2)}, u32[]{:S(2)}) collective-permute-start(bf16[384,768]{1,0:T(8,128)(2,1)S(1)} %collective-permute-done.33.refs_1_), channel_id=1, source_target_pairs={{0,4},{4,0},{8,12},{12,8},{16,20},{20,16},{24,28},{28,24},{1,5},{5... | collective-permute-start | bytes 1769480 | tf_op jit(solution)/shard_map/ppermute | solution.py:430
  180.0 21.1 %collective-permute-start.41 = (bf16[384,768]{1,0:T(8,128)(2,1)}, bf16[384,768]{1,0:T(8,128)(2,1)}, u32[]{:S(2)}, u32[]{:S(2)}) collective-permute-start(bf16[384,768]{1,0:T(8,128)(2,1)} %collective-permute-done.36.refs_3_), channel_id=1, source_target_pairs={{0,4},{4,0},{8,12},{12,8},{16,20},{20,16},{24,28},{28,24},{1,5},{5... | collective-permute-start | bytes 1769480 | tf_op jit(solution)/shard_map/ppermute | solution.py:430
  196.1 26.4 %collective-permute-start.47 = (bf16[2048,256]{1,0:T(8,128)(2,1)}, bf16[2048,256]{1,0:T(8,128)(2,1)S(1)}, u32[]{:S(2)}, u32[]{:S(2)}) collective-permute-start(bf16[2048,256]{1,0:T(8,128)(2,1)} %get-tuple-element.99.refs_25_), channel_id=1, source_target_pairs={{0,4},{4,0},{8,12},{12,8},{16,20},{20,16},{24,28},{28,24},{1,5},{5... | collective-permute-start | bytes 3145736 | tf_op jit(solution)/shard_map/ppermute | solution.py:430
  196.6 15.5 %all-to-all-start = ((bf16[8,256,256]{2,1,0:T(8,128)(2,1)}), bf16[8,256,256]{2,1,0:T(8,128)(2,1)S(1)}, u32[]{:S(2)}, u32[]{:S(2)}) async-start(bf16[8,256,256]{2,1,0:T(8,128)(2,1)} %bitcast.94), calls=%async_computation | async-start | bytes 2097152 | tf_op jit(solution)/shard_map/all_to_all | solution.py:1262
  200.2 162.4 %all-gather.11.cloned.1.call-start = ((), (), s32[]{:S(2)}) async-start(), calls=%async_computation.5 | async-start | bytes 5242880 | tf_op jit(solution)/shard_map/all_gather | solution.py:1181
  234.2 15.7 %collective-permute-start.50 = (bf16[128,2048]{1,0:T(8,128)(2,1)}, bf16[128,2048]{1,0:T(8,128)(2,1)}, u32[]{:S(2)}, u32[]{:S(2)}) collective-permute-start(bf16[128,2048]{1,0:T(8,128)(2,1)} %get-tuple-element.107.refs_11_.refs_10_.refs_16_), channel_id=1, source_target_pairs={{0,8},{4,12},{8,0},{12,4},{16,24},{20,28},{24,16},{28,20},{1,9},{5... | collective-permute-start | bytes 1572872 | tf_op jit(solution)/shard_map/ppermute | solution.py:430
  236.5 51.1 %collective-permute-start.53 = (bf16[1024,2432]{1,0:T(8,128)(2,1)}, bf16[1024,2432]{1,0:T(8,128)(2,1)}, u32[]{:S(2)}, u32[]{:S(2)}) collective-permute-start(bf16[1024,2432]{1,0:T(8,128)(2,1)} %shard_map.261.refs_5_.refs_3_.refs_4_), channel_id=1, source_target_pairs={{0,4},{4,0},{8,12},{12,8},{16,20},{20,16},{24,28},{28,24},{1,5},{5... | collective-permute-start | bytes 14942216 | tf_op jit(solution)/shard_map/ppermute | solution.py:430
  243.4 38.0 %collective-permute-start.49 = (bf16[128,2048]{1,0:T(8,128)(2,1)}, bf16[128,2048]{1,0:T(8,128)(2,1)S(1)}, u32[]{:S(2)}, u32[]{:S(2)}) collective-permute-start(bf16[128,2048]{1,0:T(8,128)(2,1)} %collective-permute-done.48.refs_8_.refs_7_.refs_13_), channel_id=1, source_target_pairs={{0,8},{4,12},{8,0},{12,4},{16,24},{20,28},{24,16},{28,20},{1,9},{5... | collective-permute-start | bytes 1572872 | tf_op jit(solution)/shard_map/ppermute | solution.py:430
  249.8 31.5 %collective-permute-start.51 = (bf16[128,2048]{1,0:T(8,128)(2,1)}, bf16[128,2048]{1,0:T(8,128)(2,1)S(1)}, u32[]{:S(2)}, u32[]{:S(2)}) collective-permute-start(bf16[128,2048]{1,0:T(8,128)(2,1)} %collective-permute-done.50.refs_9_.refs_8_.refs_14_), channel_id=1, source_target_pairs={{0,16},{4,20},{8,24},{12,28},{16,0},{20,4},{24,8},{28,12},{1,17},{... | collective-permute-start | bytes 1572872 | tf_op jit(solution)/shard_map/ppermute | solution.py:430
  283.7 37.4 %collective-permute-start.56 = (bf16[128,2048]{1,0:T(8,128)(2,1)S(1)}, bf16[128,2048]{1,0:T(8,128)(2,1)S(1)}, u32[]{:S(2)}, u32[]{:S(2)}) collective-permute-start(bf16[128,2048]{1,0:T(8,128)(2,1)S(1)} %copy-done.48), channel_id=1, source_target_pairs={{0,8},{4,12},{8,0},{12,4},{16,24},{20,28},{24,16},{28,20},{1,9},{5... | collective-permute-start | bytes 1572872 | tf_op jit(solution)/shard_map/ppermute | solution.py:430
  285.0 36.1 %collective-permute-start.57 = (bf16[128,2048]{1,0:T(8,128)(2,1)S(1)}, bf16[128,2048]{1,0:T(8,128)(2,1)S(1)}, u32[]{:S(2)}, u32[]{:S(2)}) collective-permute-start(bf16[128,2048]{1,0:T(8,128)(2,1)S(1)} %copy-done.46), channel_id=1, source_target_pairs={{0,16},{4,20},{8,24},{12,28},{16,0},{20,4},{24,8},{28,12},{1,17},{... | collective-permute-start | bytes 1572872 | tf_op jit(solution)/shard_map/ppermute | solution.py:430
  287.4 33.8 %collective-permute-start.54 = (bf16[128,2048]{1,0:T(8,128)(2,1)S(1)}, bf16[128,2048]{1,0:T(8,128)(2,1)S(1)}, u32[]{:S(2)}, u32[]{:S(2)}) collective-permute-start(bf16[128,2048]{1,0:T(8,128)(2,1)S(1)} %copy-done.64), channel_id=1, source_target_pairs={{0,8},{4,12},{8,0},{12,4},{16,24},{20,28},{24,16},{28,20},{1,9},{5... | collective-permute-start | bytes 1572872 | tf_op jit(solution)/shard_map/ppermute | solution.py:430
  287.7 33.5 %collective-permute-start.55 = (bf16[128,2048]{1,0:T(8,128)(2,1)S(1)}, bf16[128,2048]{1,0:T(8,128)(2,1)}, u32[]{:S(2)}, u32[]{:S(2)}) collective-permute-start(bf16[128,2048]{1,0:T(8,128)(2,1)S(1)} %copy-done.65), channel_id=1, source_target_pairs={{0,16},{4,20},{8,24},{12,28},{16,0},{20,4},{24,8},{28,12},{1,17},{... | collective-permute-start | bytes 1572872 | tf_op jit(solution)/shard_map/ppermute | solution.py:430
  362.6 14.4 %collective-permute-start.58 = (bf16[2048,1024]{1,0:T(8,128)(2,1)}, bf16[2048,1024]{1,0:T(8,128)(2,1)}, u32[]{:S(2)}, u32[]{:S(2)}) collective-permute-start(bf16[2048,1024]{1,0:T(8,128)(2,1)} %shard_map.266.refs_3_), channel_id=1, source_target_pairs={{0,4},{4,0},{8,12},{12,8},{16,20},{20,16},{24,28},{28,24},{1,5},{5... | collective-permute-start | bytes 12582920 | tf_op jit(solution)/shard_map/ppermute | solution.py:430
  390.5 27.9 %collective-permute-start.59 = (bf16[256,2304]{1,0:T(8,128)(2,1)}, bf16[256,2304]{1,0:T(8,128)(2,1)S(1)}, u32[]{:S(2)}, u32[]{:S(2)}) collective-permute-start(bf16[256,2304]{1,0:T(8,128)(2,1)} %get-tuple-element.124), channel_id=1, source_target_pairs={{0,8},{4,12},{8,0},{12,4},{16,24},{20,28},{24,16},{28,20},{1,9},{5... | collective-permute-start | bytes 3538952 | tf_op jit(solution)/shard_map/ppermute | solution.py:430
  391.8 27.5 %collective-permute-start.60 = (bf16[256,2304]{1,0:T(8,128)(2,1)}, bf16[256,2304]{1,0:T(8,128)(2,1)S(1)}, u32[]{:S(2)}, u32[]{:S(2)}) collective-permute-start(bf16[256,2304]{1,0:T(8,128)(2,1)} %get-tuple-element.125), channel_id=1, source_target_pairs={{0,16},{4,20},{8,24},{12,28},{16,0},{20,4},{24,8},{28,12},{1,17},{... | collective-permute-start | bytes 3538952 | tf_op jit(solution)/shard_map/ppermute | solution.py:430
  422.3 14.0 %collective-permute-start.61 = (bf16[128,2304]{1,0:T(8,128)(2,1)}, bf16[128,2304]{1,0:T(8,128)(2,1)S(1)}, u32[]{:S(2)}, u32[]{:S(2)}) collective-permute-start(bf16[128,2304]{1,0:T(8,128)(2,1)} %get-tuple-element.197.refs_6_), channel_id=1, source_target_pairs={{0,16},{4,20},{8,24},{12,28},{16,0},{20,4},{24,8},{28,12},{1,17},{... | collective-permute-start | bytes 1769480 | tf_op jit(solution)/shard_map/ppermute | solution.py:430
  423.6 13.4 %collective-permute-start.62 = (bf16[128,2304]{1,0:T(8,128)(2,1)S(1)}, bf16[128,2304]{1,0:T(8,128)(2,1)S(1)}, u32[]{:S(2)}, u32[]{:S(2)}) collective-permute-start(bf16[128,2304]{1,0:T(8,128)(2,1)S(1)} %get-tuple-element.196.refs_7_), channel_id=1, source_target_pairs={{0,8},{4,12},{8,0},{12,4},{16,24},{20,28},{24,16},{28,20},{1,9},{5... | collective-permute-start | bytes 1769480 | tf_op jit(solution)/shard_map/ppermute | solution.py:430
  437.9 32.9 %collective-permute-start.64 = (bf16[256,2176]{1,0:T(8,128)(2,1)}, bf16[256,2176]{1,0:T(8,128)(2,1)S(1)}, u32[]{:S(2)}, u32[]{:S(2)}) collective-permute-start(bf16[256,2176]{1,0:T(8,128)(2,1)} %shard_map.274), channel_id=1, source_target_pairs={{0,16},{4,20},{8,24},{12,28},{16,0},{20,4},{24,8},{28,12},{1,17},{... | collective-permute-start | bytes 3342344 | tf_op jit(solution)/shard_map/ppermute | solution.py:430
  438.6 32.3 %collective-permute-start.63 = (bf16[256,2176]{1,0:T(8,128)(2,1)}, bf16[256,2176]{1,0:T(8,128)(2,1)}, u32[]{:S(2)}, u32[]{:S(2)}) collective-permute-start(bf16[256,2176]{1,0:T(8,128)(2,1)} %shard_map.271.refs_13_), channel_id=1, source_target_pairs={{0,8},{4,12},{8,0},{12,4},{16,24},{20,28},{24,16},{28,20},{1,9},{5... | collective-permute-start | bytes 3342344 | tf_op jit(solution)/shard_map/ppermute | solution.py:430
  439.7 80.3 %collective-permute-start.68 = (bf16[2048,768]{1,0:T(8,128)(2,1)}, bf16[2048,768]{1,0:T(8,128)(2,1)}, u32[]{:S(2)}, u32[]{:S(2)}) collective-permute-start(bf16[2048,768]{1,0:T(8,128)(2,1)} %get-tuple-element.139.refs_3_), channel_id=1, source_target_pairs={{0,4},{4,0},{8,12},{12,8},{16,20},{20,16},{24,28},{28,24},{1,5},{5... | collective-permute-start | bytes 9437192 | tf_op jit(solution)/shard_map/ppermute | solution.py:430
  457.5 19.2 %all-to-all-start.1 = ((bf16[256,8,256]{2,0,1:T(8,128)(2,1)}), bf16[256,8,256]{2,0,1:T(8,128)(2,1)S(1)}, u32[]{:S(2)}, u32[]{:S(2)}) async-start(bf16[256,8,256]{2,0,1:T(8,128)(2,1)} %bitcast.69), calls=%async_computation.1 | async-start | bytes 2097152 | tf_op jit(solution)/shard_map/all_to_all | solution.py:1372
  474.1 30.5 %collective-permute-start.65 = (bf16[128,2176]{1,0:T(8,128)(2,1)}, bf16[128,2176]{1,0:T(8,128)(2,1)}, u32[]{:S(2)}, u32[]{:S(2)}) collective-permute-start(bf16[128,2176]{1,0:T(8,128)(2,1)} %get-tuple-element.201.refs_9_), channel_id=1, source_target_pairs={{0,16},{4,20},{8,24},{12,28},{16,0},{20,4},{24,8},{28,12},{1,17},{... | collective-permute-start | bytes 1671176 | tf_op jit(solution)/shard_map/ppermute | solution.py:430
  475.5 30.0 %collective-permute-start.66 = (bf16[128,2176]{1,0:T(8,128)(2,1)}, bf16[128,2176]{1,0:T(8,128)(2,1)}, u32[]{:S(2)}, u32[]{:S(2)}) collective-permute-start(bf16[128,2176]{1,0:T(8,128)(2,1)} %get-tuple-element.200.refs_10_), channel_id=1, source_target_pairs={{0,8},{4,12},{8,0},{12,4},{16,24},{20,28},{24,16},{28,20},{1,9},{5... | collective-permute-start | bytes 1671176 | tf_op jit(solution)/shard_map/ppermute | solution.py:430
  502.7 14.2 %collective-permute-start.67 = (bf16[3,1024,256]{2,1,0:T(8,128)(2,1)}, bf16[3,1024,256]{2,1,0:T(8,128)(2,1)S(1)}, u32[]{:S(2)}, u32[]{:S(2)}) collective-permute-start(bf16[3,1024,256]{2,1,0:T(8,128)(2,1)} %get-tuple-element.138), channel_id=1, source_target_pairs={{0,4},{4,0},{8,12},{12,8},{16,20},{20,16},{24,28},{28,24},{1,5},{5... | collective-permute-start | bytes 4718600 | tf_op jit(solution)/shard_map/ppermute | solution.py:430
  503.7 16.9 %collective-permute-start.71 = (bf16[256,640]{1,0:T(8,128)(2,1)}, bf16[256,640]{1,0:T(8,128)(2,1)}, u32[]{:S(2)}, u32[]{:S(2)}) collective-permute-start(bf16[256,640]{1,0:T(8,128)(2,1)} %shard_map.280), channel_id=1, source_target_pairs={{0,24},{4,28},{8,16},{12,20},{16,8},{20,12},{24,0},{28,4},{1,25},{... | collective-permute-start | bytes 983048 | tf_op jit(solution)/shard_map/ppermute | solution.py:430
  504.7 17.4 %collective-permute-start.70 = (bf16[256,640]{1,0:T(8,128)(2,1)}, bf16[256,640]{1,0:T(8,128)(2,1)}, u32[]{:S(2)}, u32[]{:S(2)}) collective-permute-start(bf16[256,640]{1,0:T(8,128)(2,1)} %shard_map.279), channel_id=1, source_target_pairs={{0,16},{4,20},{8,24},{12,28},{16,0},{20,4},{24,8},{28,12},{1,17},{... | collective-permute-start | bytes 983048 | tf_op jit(solution)/shard_map/ppermute | solution.py:430
  505.5 16.6 %collective-permute-start.69 = (bf16[256,640]{1,0:T(8,128)(2,1)}, bf16[256,640]{1,0:T(8,128)(2,1)}, u32[]{:S(2)}, u32[]{:S(2)}) collective-permute-start(bf16[256,640]{1,0:T(8,128)(2,1)} %shard_map.278), channel_id=1, source_target_pairs={{0,8},{4,12},{8,0},{12,4},{16,24},{20,28},{24,16},{28,20},{1,9},{5... | collective-permute-start | bytes 983048 | tf_op jit(solution)/shard_map/ppermute | solution.py:430
  529.6 14.5 %collective-permute-start.75 = (bf16[256,512]{1,0:T(8,128)(2,1)S(1)}, bf16[256,512]{1,0:T(8,128)(2,1)S(1)}, u32[]{:S(2)}, u32[]{:S(2)}) collective-permute-start(bf16[256,512]{1,0:T(8,128)(2,1)S(1)} %pad_maximum_fusion.3.refs_22_.refs_31_.refs_8_), channel_id=1, source_target_pairs={{0,8},{4,12},{8,0},{12,4},{16,24},{20,28},{24,16},{28,20},{1,9},{5... | collective-permute-start | bytes 786440 | tf_op jit(solution)/shard_map/ppermute | solution.py:430
  530.7 13.4 %collective-permute-start.76 = (bf16[256,512]{1,0:T(8,128)(2,1)S(1)}, bf16[256,512]{1,0:T(8,128)(2,1)S(1)}, u32[]{:S(2)}, u32[]{:S(2)}) collective-permute-start(bf16[256,512]{1,0:T(8,128)(2,1)S(1)} %pad_maximum_fusion.3.refs_22_.refs_31_.refs_8_), channel_id=1, source_target_pairs={{0,16},{4,20},{8,24},{12,28},{16,0},{20,4},{24,8},{28,12},{1,17},{... | collective-permute-start | bytes 786440 | tf_op jit(solution)/shard_map/ppermute | solution.py:430
  541.3 25.7 %collective-permute-start.89 = (bf16[4,768,128]{2,1,0:T(8,128)(2,1)}, bf16[4,768,128]{2,1,0:T(8,128)(2,1)}, u32[]{:S(2)}, u32[]{:S(2)}) collective-permute-start(bf16[4,768,128]{2,1,0:T(8,128)(2,1)} %get-tuple-element.159.refs_8_), channel_id=1, source_target_pairs={{0,4},{4,0},{8,12},{12,8},{16,20},{20,16},{24,28},{28,24},{1,5},{5... | collective-permute-start | bytes 2359304 | tf_op jit(solution)/shard_map/ppermute | solution.py:430
  554.6 30.6 %collective-permute-start.78 = (bf16[256,2048]{1,0:T(8,128)(2,1)}, bf16[256,2048]{1,0:T(8,128)(2,1)S(1)}, u32[]{:S(2)}, u32[]{:S(2)}) collective-permute-start(bf16[256,2048]{1,0:T(8,128)(2,1)} %get-tuple-element.160.refs_36_), channel_id=1, source_target_pairs={{0,8},{4,12},{8,0},{12,4},{16,24},{20,28},{24,16},{28,20},{1,9},{5... | collective-permute-start | bytes 3145736 | tf_op jit(solution)/shard_map/ppermute | solution.py:430
  555.6 29.6 %collective-permute-start.79 = (bf16[256,2048]{1,0:T(8,128)(2,1)}, bf16[256,2048]{1,0:T(8,128)(2,1)S(1)}, u32[]{:S(2)}, u32[]{:S(2)}) collective-permute-start(bf16[256,2048]{1,0:T(8,128)(2,1)} %get-tuple-element.162), channel_id=1, source_target_pairs={{0,16},{4,20},{8,24},{12,28},{16,0},{20,4},{24,8},{28,12},{1,17},{... | collective-permute-start | bytes 3145736 | tf_op jit(solution)/shard_map/ppermute | solution.py:430
  576.3 17.0 %collective-permute-start.83 = (bf16[2,704,128]{2,1,0:T(8,128)(2,1)}, bf16[2,704,128]{2,1,0:T(8,128)(2,1)}, u32[]{:S(2)}, u32[]{:S(2)}) collective-permute-start(bf16[2,704,128]{2,1,0:T(8,128)(2,1)} %get-tuple-element.166), channel_id=1, source_target_pairs={{0,1},{1,0},{2,3},{3,2},{4,5},{5,4},{6,7},{7,6},{8,9},{9,8},{10,11... | collective-permute-start | bytes 1081352 | tf_op jit(solution)/shard_map/ppermute | solution.py:1384
  597.4 13.4 %collective-permute-start.92 = (bf16[768,128]{1,0:T(8,128)(2,1)}, bf16[768,128]{1,0:T(8,128)(2,1)}, u32[]{:S(2)}, u32[]{:S(2)}) collective-permute-start(bf16[768,128]{1,0:T(8,128)(2,1)} %fusion.8.refs_1_), channel_id=1, source_target_pairs={{0,8},{4,12},{8,0},{12,4},{16,24},{20,28},{24,16},{28,20},{1,9},{5... | collective-permute-start | bytes 589832 | tf_op jit(solution)/shard_map/ppermute | solution.py:430
  597.9 14.2 %collective-permute-start.93 = (bf16[768,128]{1,0:T(8,128)(2,1)}, bf16[768,128]{1,0:T(8,128)(2,1)}, u32[]{:S(2)}, u32[]{:S(2)}) collective-permute-start(bf16[768,128]{1,0:T(8,128)(2,1)} %fusion.8.refs_1_), channel_id=1, source_target_pairs={{0,16},{4,20},{8,24},{12,28},{16,0},{20,4},{24,8},{28,12},{1,17},{... | collective-permute-start | bytes 589832 | tf_op jit(solution)/shard_map/ppermute | solution.py:430
  598.7 13.4 %collective-permute-start.94 = (bf16[768,128]{1,0:T(8,128)(2,1)}, bf16[768,128]{1,0:T(8,128)(2,1)}, u32[]{:S(2)}, u32[]{:S(2)}) collective-permute-start(bf16[768,128]{1,0:T(8,128)(2,1)} %fusion.8.refs_1_), channel_id=1, source_target_pairs={{0,24},{4,28},{8,16},{12,20},{16,8},{20,12},{24,0},{28,4},{1,25},{... | collective-permute-start | bytes 589832 | tf_op jit(solution)/shard_map/ppermute | solution.py:430
  (117 other events, 1481.3 us)
Sparse Core Ops, SparseCore 0:
  12.0 94.8 all-gather.4
  108.5 92.1 all-gather.8
  202.3 79.0 all-gather.6
  283.8 78.7 all-gather.10

commit v6 on v5

--- a/solution.py
+++ b/solution.py
@@ -1438,7 +1438,7 @@
 
     pass_on, kept = back_qkv(1, F32, [to_x, *middle[1:]])
     dz_qkv = latent_kept + swap(to_x, 2).astype(F32) + swap(to_y, 4).astype(F32)
-    dz_qkv = (dz_qkv + swap(to_far, 6).astype(F32)) * jnp.tile(select, (1, 3)).astype(F32)
+    dz_qkv = (dz_qkv + swap(to_far, 6).astype(F32)) * jnp.concatenate([select] * 3, axis=1).astype(F32)
     both = jnp.concatenate([dz_qkv.astype(BF), z_down], axis=1)
     last = blocks_of(both)
     ff_rows = 2 * latent * (ff_dev // LANES) + ff_dev

time: 646 us -> 647 us (level)
    ppermute x92, waiting for transfers between devices: 63.1 us -> 69.9 us  [swap(): return lax.ppermute(value, 'seq', [(i, i ^ bits) for i in range(PLANE)])]
    unnamed x171 -> x169, local copies, waits for them, and re-layouts: 23.2 us -> 24 us
  transfers between devices with their start and end apart: 102 -> 102, of which waited for: 20 -> 23; matrix products, arithmetic and copies ran while one was open for 7% -> 6% of each run, Pallas kernels for 42% -> 42%
where the time goes in v6:
time: 647 us; the launch traced here: 636 us
  Pallas kernels  288 us (45%)
  waiting for transfers between devices  164 us (25%)
  starting transfers between devices  105 us (16%)
  local copies, waits for them, and re-layouts  34 us (5%)
  other arithmetic  26.3 us (4%)
  between operations  15 us (2%)
    pallas_call x29, Pallas kernels, call(): pl.pallas_call(run, grid_spec=pltpu.PrefetchScalarGridSpec(num_scalar_pre...  288 us
    ppermute x92, starting transfers between devices, swap(): return lax.ppermute(value, 'seq', [(i, i ^ bits) for i in range(PLANE)])  96 us
    ppermute x92, waiting for transfers between devices, swap(): return lax.ppermute(value, 'seq', [(i, i ^ bits) for i in range(PLANE)])  69.9 us
    all_gather x2, waiting for transfers between devices, plane_shards(): lax.all_gather(part, 'fsdp', axis=0, tiled=True)  40.7 us
    all_gather x1, waiting for transfers between devices, plane_shards(): first_all = lax.all_gather(first_part, 'fsdp', axis=0, tiled=True)  35 us
    unnamed x169, local copies, waits for them, and re-layouts  24 us
  transfers between devices with their start and end apart: 102, of which 23 were waited for; matrix products, arithmetic and copies ran while one was open for 6% of the time, Pallas kernels for 42%

profile of v6, /device:TPU:1, one launch (start us, length us, event | category | flops | bytes accessed | tf_op | source)
XLA Modules:
  0.0 636.0 jit_solution(12137701536665342154)
XLA Ops:
  8.5 3.3 shard_map.250.refs_5_
  11.9 4.3 shard_map.259
  16.4 3.5 shard_map.249
  19.9 2.1 collective-permute-start.1
  23.7 10.3 %collective-permute-done.1.refs_5_ = bf16[128,2048]{1,0:T(8,128)(2,1)S(1)} collective-permute-done((bf16[128,2048]{1,0:T(8,128)(2,1)}, bf16[128,2048]{1,0:T(8,128)(2,1)S(1)}, u32[]{:S(2)}, u32[]{:S(2)}) %collective-permute-start.1) | collective-permute-done | bytes 524320 | tf_op jit(solution)/shard_map/ppermute | solution.py:430
  36.3 8.9 %collective-permute-done.14.refs_12_.refs_11_.refs_21_ = bf16[128,2048]{1,0:T(8,128)(2,1)S(1)} collective-permute-done((bf16[128,2048]{1,0:T(8,128)(2,1)S(1)}, bf16[128,2048]{1,0:T(8,128)(2,1)S(1)}, u32[]{:S(2)}, u32[]{:S(2)}) %collective-permute-start.14) | collective-permute-done | bytes 524320 | tf_op jit(solution)/shard_map/ppermute | solution.py:430
  47.6 9.6 %collective-permute-done.2.refs_2_ = bf16[128,2048]{1,0:T(8,128)(2,1)} collective-permute-done((bf16[128,2048]{1,0:T(8,128)(2,1)S(1)}, bf16[128,2048]{1,0:T(8,128)(2,1)}, u32[]{:S(2)}, u32[]{:S(2)}) %collective-permute-start.2) | collective-permute-done | bytes 524320 | tf_op jit(solution)/shard_map/ppermute | solution.py:430
  57.2 3.3 collective-permute-start.7
  62.0 6.4 %collective-permute-done.15.refs_3_.refs_13_.refs_10_.refs_18_ = bf16[128,2048]{1,0:T(8,128)(2,1)S(1)} collective-permute-done((bf16[128,2048]{1,0:T(8,128)(2,1)S(1)}, bf16[128,2048]{1,0:T(8,128)(2,1)S(1)}, u32[]{:S(2)}, u32[]{:S(2)}) %collective-permute-start.15) | collective-permute-done | bytes 524320 | tf_op jit(solution)/shard_map/ppermute | solution.py:430
  68.8 3.0 collective-permute-start.12
  71.9 35.0 %all-gather.5.cloned.1.call-done.refs_0_ = bf16[3200,768]{1,0:T(8,128)(2,1)} async-done(((bf16[800,768]{1,0:T(8,128)(2,1)}), bf16[3200,768]{1,0:T(8,128)(2,1)}) %all-gather.5.cloned.1.call-update) | async-done | bytes 4915216 | tf_op jit(solution)/shard_map/all_gather | solution.py:1171
  117.3 2.4 collective-permute-start.31
  119.7 5.0 collective-permute-done.22.refs_6_
  126.2 2.3 collective-permute-start.24
  128.5 3.7 multiply_sine_fusion
  136.3 2.3 fusion.14
  142.9 5.5 shard_map.252
  152.4 2.6 collective-permute-done.34.refs_5_
  156.3 22.2 %shard_map.253 = (bf16[2048,768]{1,0:T(8,128)(2,1)}, bf16[2048,384]{1,0:T(8,128)(2,1)}, bf16[2048,768]{1,0:T(8,128)(2,1)}) custom-call(s32[11]{0:T(128)} %concatenate.27.refs_0_, bf16[128,2048]{1,0:T(8,128)(2,1)} %collective-permute-done.refs_1_, bf16[128,2048]{1,0:T(8,128)(2,1)} %collective-permute-done.2.refs_2_, ...), custom_call_target="tpu_custom_call" | custom-call | flops 9663676416 | bytes 20971520 | tf_op jit(solution)/shard_map/pallas_call | solution.py:471
  180.0 16.0 %shard_map.254 = (bf16[2048,256]{1,0:T(8,128)(2,1)}, f32[2048,256]{1,0:T(8,128)}) custom-call(s32[11]{0:T(128)} %concatenate.27.refs_0_, bf16[2048,768]{1,0:T(8,128)(2,1)} %get-tuple-element.98.refs_1_.refs_2_.refs_3_, bf16[2048,768]{1,0:T(8,128)(2,1)} %get-tuple-element.98.refs_1_.refs_2_.refs_3_, bf16[2048,768]{1,0:T(8,128)(2,1)} %get-tuple-element.98.refs_1_.refs_2_.refs_3_), custom_call_target="tpu_custom_call" | custom-call | flops 4294967296 | bytes 8388608 | tf_op jit(solution)/shard_map/pallas_call | solution.py:471
  197.4 3.6 all-to-all-start
  202.3 10.7 %all-to-all-done = bf16[8,256,256]{2,1,0:T(8,128)(2,1)S(1)} async-done(((bf16[8,256,256]{2,1,0:T(8,128)(2,1)}), bf16[8,256,256]{2,1,0:T(8,128)(2,1)S(1)}, u32[]{:S(2)}, u32[]{:S(2)}) %all-to-all-start) | async-done | bytes 1048608 | tf_op jit(solution)/shard_map/all_to_all | solution.py:1262
  214.8 8.3 %shard_map.257.refs_2_.refs_9_ = bf16[2048,2048]{1,0:T(8,128)(2,1)} custom-call(s32[11]{0:T(128)} %concatenate.27.refs_0_, bf16[384,768]{1,0:T(8,128)(2,1)} %collective-permute-done.33.refs_1_, bf16[384,768]{1,0:T(8,128)(2,1)} %collective-permute-done.35.refs_2_, bf16[384,768]{1,0:T(8,128)(2,1)} %collective-permute-done.36.refs_3_, ...), custom_call_target="tpu_custom_call" | custom-call | tf_op jit(solution)/shard_map/pallas_call | solution.py:471
  224.2 9.6 %shard_map.258 = (f32[256,2048]{1,0:T(8,128)}, bf16[128,2048]{1,0:T(8,128)(2,1)}, bf16[128,2048]{1,0:T(8,128)(2,1)}, bf16[256,128]{1,0:T(8,128)(2,1)}) custom-call(s32[11]{0:T(128)} %concatenate.27.refs_0_, bf16[256,2048]{1,0:T(8,128)(2,1)} %bitcast.90, bf16[2048,2048]{1,0:T(8,128)(2,1)} %shard_map.257.refs_2_.refs_9_, ...), custom_call_target="tpu_custom_call" | custom-call | flops 2147483648 | bytes 12582912 | tf_op jit(solution)/shard_map/pallas_call | solution.py:471
  234.9 2.3 collective-permute-start.50
  238.5 5.6 collective-permute-done.48.refs_8_.refs_7_.refs_13_
  244.1 6.5 %collective-permute-start.49 = (bf16[128,2048]{1,0:T(8,128)(2,1)}, bf16[128,2048]{1,0:T(8,128)(2,1)S(1)}, u32[]{:S(2)}, u32[]{:S(2)}) collective-permute-start(bf16[128,2048]{1,0:T(8,128)(2,1)} %collective-permute-done.48.refs_8_.refs_7_.refs_13_), channel_id=1, source_target_pairs={{0,8},{4,12},{8,0},{12,4},{16,24},{20,28},{24,16},{28,20},{1,9},{5... | collective-permute-start | bytes 1572872 | tf_op jit(solution)/shard_map/ppermute | solution.py:430
  250.6 30.7 %all-gather.7.cloned.1.call-done.refs_0_ = bf16[2048,1024]{1,0:T(8,128)(2,1)} async-done(((bf16[512,1024]{1,0:T(8,128)(2,1)}), bf16[2048,1024]{1,0:T(8,128)(2,1)}) %all-gather.7.cloned.1.call-update) | async-done | bytes 4194320 | tf_op jit(solution)/shard_map/all_gather | solution.py:1181
  287.9 2.9 collective-permute-done.52.refs_6_
  290.8 22.1 %shard_map.262 = (f32[512,2304]{1,0:T(8,128)}, bf16[512,512]{1,0:T(8,128)(2,1)}, bf16[512,1024]{1,0:T(8,128)(2,1)}, bf16[512,512]{1,0:T(8,128)(2,1)}, bf16[512,1...) custom-call(s32[11]{0:T(128)} %concatenate.27.refs_0_, ...), custom_call_target="tpu_custom_call" | custom-call | flops 10737418240 | bytes 27262976 | tf_op jit(solution)/shard_map/pallas_call | solution.py:471
  312.9 8.2 %shard_map.265.refs_4_.refs_5_ = f32[512,2176]{1,0:T(8,128)} custom-call(s32[11]{0:T(128)} %concatenate.27.refs_0_, bf16[512,512]{1,0:T(8,128)(2,1)} %get-tuple-element.116.refs_1_.refs_7_, bf16[512,512]{1,0:T(8,128)(2,1)} %get-tuple-element.117.refs_2_.refs_11_, bf16[1024,2432]{1,0:T(8,128)(2,1)} %shard_map.261.refs_5_.refs_3_.refs_4_, ...), custom_call_target="tpu_custom_call" | custom-call | flops 2147483648 | bytes 12582912 | tf_op jit(solution)/shard_map/pallas_call | solution.py:471
  322.3 22.2 %shard_map.263 = (f32[512,2304]{1,0:T(8,128)}, bf16[512,512]{1,0:T(8,128)(2,1)}, bf16[512,1024]{1,0:T(8,128)(2,1)}, bf16[512,512]{1,0:T(8,128)(2,1)}, bf16[512,1...) custom-call(s32[11]{0:T(128)} %concatenate.27.refs_0_, ...), custom_call_target="tpu_custom_call" | custom-call | flops 10737418240 | bytes 27262976 | tf_op jit(solution)/shard_map/pallas_call | solution.py:471
  344.5 8.1 %shard_map.264.refs_3_.refs_5_ = f32[512,2176]{1,0:T(8,128)} custom-call(s32[11]{0:T(128)} %concatenate.27.refs_0_, bf16[512,512]{1,0:T(8,128)(2,1)} %get-tuple-element.114.refs_1_.refs_5_, bf16[512,512]{1,0:T(8,128)(2,1)} %get-tuple-element.115.refs_2_.refs_9_, bf16[1024,2432]{1,0:T(8,128)(2,1)} %shard_map.261.refs_5_.refs_3_.refs_4_, ...), custom_call_target="tpu_custom_call" | custom-call | flops 2147483648 | bytes 12582912 | tf_op jit(solution)/shard_map/pallas_call | solution.py:471
  352.6 9.9 %all-gather.11.cloned.1.call-done.refs_0_ = bf16[2048,1024]{1,0:T(8,128)(2,1)} async-done(((bf16[512,1024]{1,0:T(8,128)(2,1)}), bf16[2048,1024]{1,0:T(8,128)(2,1)}) %all-gather.11.cloned.1.call-update) | async-done | bytes 4194320 | tf_op jit(solution)/shard_map/all_gather | solution.py:1181
  363.3 13.7 %shard_map.268 = (f32[512,2304]{1,0:T(8,128)}, bf16[512,512]{1,0:T(8,128)(2,1)}, bf16[512,1024]{1,0:T(8,128)(2,1)}) custom-call(s32[11]{0:T(128)} %concatenate.27.refs_0_, bf16[512,256]{1,0:T(8,128)(2,1)} %get-tuple-element.121.refs_1_, bf16[512,128]{1,0:T(8,128)(2,1)} %get-tuple-element.122.refs_2_.refs_3_, bf16[2048,1024]{1,0:T(8,128)(2,1)} %shard_map.266.refs_3_, ...), custom_call_target="tpu_custom_call" | custom-call | flops 5368709120 | bytes 27262976 | tf_op jit(solution)/shard_map/pallas_call | solution.py:471
  377.0 13.5 %shard_map.269 = (bf16[256,2304]{1,0:T(8,128)(2,1)}, bf16[256,2304]{1,0:T(8,128)(2,1)}, bf16[512,512]{1,0:T(8,128)(2,1)}, bf16[512,1024]{1,0:T(8,128)(2,1)}) custom-call(s32[11]{0:T(128)} %concatenate.27.refs_0_, bf16[512,256]{1,0:T(8,128)(2,1)} %get-tuple-element.121.refs_1_, bf16[512,128]{1,0:T(8,128)(2,1)} %get-tuple-element.122.refs_2_.refs_3_, ...), custom_call_target="tpu_custom_call" | custom-call | flops 5368709120 | bytes 27262976 | tf_op jit(solution)/shard_map/pallas_call | solution.py:471
  392.9 21.5 %shard_map.267 = (f32[256,2304]{1,0:T(8,128)}, f32[256,2304]{1,0:T(8,128)}, bf16[512,512]{1,0:T(8,128)(2,1)}, bf16[512,1024]{1,0:T(8,128)(2,1)}, bf16[512,512]{1,0:T(8,128)(2,1)}, /*index=5*/bf16[512,1024]{1,0:T(8,128)(2,1)}) custom-call(s32[11]{0:T(128)} %concatenate.27.refs_0_, bf16[512,256]{1,0:T(8,128)(2,1)} %get-tuple-element.109.refs_1_.refs_2_, ...), custom_call_target="tpu_custom_call" | custom-call | flops 10737418240 | bytes 27262976 | tf_op jit(solution)/shard_map/pallas_call | solution.py:471
  414.5 3.9 collective-permute-done.59.refs_2_
  419.2 3.1 add_convert_fusion
  424.3 8.7 %shard_map.270 = (bf16[256,2176]{1,0:T(8,128)(2,1)}, bf16[256,2176]{1,0:T(8,128)(2,1)}) custom-call(s32[11]{0:T(128)} %concatenate.27.refs_0_, bf16[512,512]{1,0:T(8,128)(2,1)} %get-tuple-element.128.refs_1_.refs_13_, bf16[512,512]{1,0:T(8,128)(2,1)} %get-tuple-element.129.refs_2_.refs_17_, bf16[1024,2432]{1,0:T(8,128)(2,1)} %shard_map.261.refs_5_.refs_3_.refs_4_, ...), custom_call_target="tpu_custom_call" | custom-call | flops 2147483648 | bytes 12582912 | tf_op jit(solution)/shard_map/pallas_call | solution.py:471
  433.0 3.3 collective-permute-done.61.refs_1_.refs_4_
  439.6 2.2 collective-permute-start.68
  441.8 13.3 %shard_map.272 = (f32[256,2048]{1,0:T(8,128)}, bf16[256,2048]{1,0:T(8,128)(2,1)}, bf16[256,640]{1,0:T(8,128)(2,1)}, bf16[256,640]{1,0:T(8,128)(2,1)}, bf16[256,6...) custom-call(s32[11]{0:T(128)} %concatenate.27.refs_0_, f32[256,2304]{1,0:T(8,128)} %get-tuple-element.120.refs_1_, ...), custom_call_target="tpu_custom_call" | custom-call | flops 2147483648 | bytes 16777216 | tf_op jit(solution)/shard_map/pallas_call | solution.py:471
  455.2 2.3 copy.117
  457.4 3.9 all-to-all-start.1
  461.4 9.4 %shard_map.273 = (f32[256,2176]{1,0:T(8,128)}, f32[256,2176]{1,0:T(8,128)}) custom-call(s32[11]{0:T(128)} %concatenate.27.refs_0_, bf16[512,512]{1,0:T(8,128)(2,1)} %get-tuple-element.118.refs_1_.refs_15_, bf16[512,512]{1,0:T(8,128)(2,1)} %get-tuple-element.119.refs_2_.refs_19_, bf16[1024,2432]{1,0:T(8,128)(2,1)} %shard_map.261.refs_5_.refs_3_.refs_4_, ...), custom_call_target="tpu_custom_call" | custom-call | flops 2147483648 | bytes 12582912 | tf_op jit(solution)/shard_map/pallas_call | solution.py:471
  470.7 3.3 add_convert_fusion.2
  477.6 25.0 %shard_map.275 = (bf16[3,1024,256]{2,1,0:T(8,128)(2,1)}, bf16[3,1024,256]{2,1,0:T(8,128)(2,1)}, f32[3,128,256]{2,1,0:T(8,128)}) custom-call(s32[11]{0:T(128)} %concatenate.27.refs_0_, bf16[2048,768]{1,0:T(8,128)(2,1)} %get-tuple-element.98.refs_1_.refs_2_.refs_3_, bf16[2048,768]{1,0:T(8,128)(2,1)} %get-tuple-element.98.refs_1_.refs_2_.refs_3_, ...), custom_call_target="tpu_custom_call" | custom-call | flops 10737418240 | bytes 16777216 | tf_op jit(solution)/shard_map/pallas_call | solution.py:471
  506.3 2.4 fusion.3
  515.2 6.2 collective-permute-done.70.refs_7_.refs_29_
  521.5 6.0 shard_map.281
  533.0 8.9 %shard_map.282 = (f32[4,768,128]{2,1,0:T(8,128)}, bf16[4,768,128]{2,1,0:T(8,128)(2,1)}) custom-call(s32[11]{0:T(128)} %concatenate.27.refs_0_, bf16[512,256]{1,0:T(8,128)(2,1)} %get-tuple-element.121.refs_1_, bf16[512,256]{1,0:T(8,128)(2,1)} %get-tuple-element.109.refs_1_.refs_2_, bf16[512,128]{1,0:T(8,128)(2,1)} %get-tuple-element.122.refs_2_.refs_3_, ...), custom_call_target="tpu_custom_call" | custom-call | flops 4294967296 | bytes 12582912 | tf_op jit(solution)/shard_map/pallas_call | solution.py:471
  546.5 7.2 %shard_map.283 = (bf16[256,2048]{1,0:T(8,128)(2,1)}, bf16[256,2048]{1,0:T(8,128)(2,1)}) custom-call(s32[11]{0:T(128)S(1)} %copy-done.25, bf16[3,1024,256]{2,1,0:T(8,128)(2,1)S(1)} %copy-done.5, bf16[3,1024,256]{2,1,0:T(8,128)(2,1)S(1)} %collective-permute-done.67.refs_2_, bf16[2048,768]{1,0:T(8,128)(2,1)S(1)} %copy-done.28, ...), custom_call_target="tpu_custom_call" | custom-call | flops 3221225472 | bytes 12582912 | tf_op jit(solution)/shard_map/pallas_call | solution.py:471
  555.4 9.7 %shard_map.284 = (f32[4,704,128]{2,1,0:T(8,128)}, bf16[4,704,128]{2,1,0:T(8,128)(2,1)}) custom-call(s32[11]{0:T(128)} %concatenate.27.refs_0_, bf16[128,2048]{1,0:T(8,128)(2,1)} %collective-permute-done.refs_1_, bf16[128,2048]{1,0:T(8,128)(2,1)} %collective-permute-done.2.refs_2_, bf16[128,2048]{1,0:T(8,128)(2,1)} %collective-permute-done.3.refs_3_, ...), custom_call_target="tpu_custom_call" | custom-call | flops 805306368 | bytes 8388608 | tf_op jit(solution)/shard_map/pallas_call | solution.py:471
  565.1 2.3 collective-permute-start.82
  568.7 2.5 shard_map.290
  574.1 2.5 shard_map.288
  577.3 5.7 collective-permute-done.90
  588.2 3.8 fusion.refs_1_
  603.4 4.9 shard_map.287.refs_1_
  613.6 4.4 collective-permute-start.95
  618.1 3.5 collective-permute-start.88
  621.6 3.7 shard_map.292
  626.9 2.3 shard_map.293
  (395 shorter events, 115.2 us)
Async XLA Ops:
  7.2 99.7 %all-gather.5.cloned.1.call-start = ((), (), s32[]{:S(2)}) async-start(), calls=%async_computation.2 | async-start | bytes 6144000 | tf_op jit(solution)/shard_map/all_gather | solution.py:1171
  11.9 225.3 %all-gather.9.cloned.1.call-start = ((), (), s32[]{:S(2)}) async-start(), calls=%async_computation.4 | async-start | bytes 6225920 | tf_op jit(solution)/shard_map/all_gather | solution.py:1180
  16.3 265.0 %all-gather.7.cloned.1.call-start = ((), (), s32[]{:S(2)}) async-start(), calls=%async_computation.3 | async-start | bytes 5242880 | tf_op jit(solution)/shard_map/all_gather | solution.py:1181
  19.9 14.1 %collective-permute-start.1 = (bf16[128,2048]{1,0:T(8,128)(2,1)}, bf16[128,2048]{1,0:T(8,128)(2,1)S(1)}, u32[]{:S(2)}, u32[]{:S(2)}) collective-permute-start(bf16[128,2048]{1,0:T(8,128)(2,1)} %get-tuple-element.95.refs_7_), channel_id=1, source_target_pairs={{0,16},{4,20},{8,24},{12,28},{16,0},{20,4},{24,8},{28,12},{1,17},{... | collective-permute-start | bytes 1572872 | tf_op jit(solution)/shard_map/ppermute | solution.py:430
  22.0 13.1 %collective-permute-start.4 = (bf16[128,2048]{1,0:T(8,128)(2,1)}, bf16[128,2048]{1,0:T(8,128)(2,1)S(1)}, u32[]{:S(2)}, u32[]{:S(2)}) collective-permute-start(bf16[128,2048]{1,0:T(8,128)(2,1)} %get-tuple-element.96.refs_8_), channel_id=1, source_target_pairs={{0,8},{4,12},{8,0},{12,4},{16,24},{20,28},{24,16},{28,20},{1,9},{5... | collective-permute-start | bytes 1572872 | tf_op jit(solution)/shard_map/ppermute | solution.py:430
  23.3 21.9 %collective-permute-start.14 = (bf16[128,2048]{1,0:T(8,128)(2,1)S(1)}, bf16[128,2048]{1,0:T(8,128)(2,1)S(1)}, u32[]{:S(2)}, u32[]{:S(2)}) collective-permute-start(bf16[128,2048]{1,0:T(8,128)(2,1)S(1)} %get-tuple-element.205.refs_14_.refs_13_.refs_23_), channel_id=1, source_target_pairs={{0,16},{4,20},{8,24},{12,28},{16,0},{20,4},{24,8},{28,12},{1,17},{... | collective-permute-start | bytes 1572872 | tf_op jit(solution)/shard_map/ppermute | solution.py:430
  23.6 22.7 %collective-permute-start.16 = (bf16[128,2048]{1,0:T(8,128)(2,1)S(1)}, bf16[128,2048]{1,0:T(8,128)(2,1)S(1)}, u32[]{:S(2)}, u32[]{:S(2)}) collective-permute-start(bf16[128,2048]{1,0:T(8,128)(2,1)S(1)} %get-tuple-element.204.refs_15_.refs_14_.refs_24_), channel_id=1, source_target_pairs={{0,8},{4,12},{8,0},{12,4},{16,24},{20,28},{24,16},{28,20},{1,9},{5... | collective-permute-start | bytes 1572872 | tf_op jit(solution)/shard_map/ppermute | solution.py:430
  34.0 23.2 %collective-permute-start.2 = (bf16[128,2048]{1,0:T(8,128)(2,1)S(1)}, bf16[128,2048]{1,0:T(8,128)(2,1)}, u32[]{:S(2)}, u32[]{:S(2)}) collective-permute-start(bf16[128,2048]{1,0:T(8,128)(2,1)S(1)} %collective-permute-done.1.refs_5_), channel_id=1, source_target_pairs={{0,8},{4,12},{8,0},{12,4},{16,24},{20,28},{24,16},{28,20},{1,9},{5... | collective-permute-start | bytes 1572872 | tf_op jit(solution)/shard_map/ppermute | solution.py:430
  35.1 25.5 %collective-permute-start.5 = (bf16[128,2048]{1,0:T(8,128)(2,1)S(1)}, bf16[128,2048]{1,0:T(8,128)(2,1)}, u32[]{:S(2)}, u32[]{:S(2)}) collective-permute-start(bf16[128,2048]{1,0:T(8,128)(2,1)S(1)} %collective-permute-done.4.refs_6_), channel_id=1, source_target_pairs={{0,16},{4,20},{8,24},{12,28},{16,0},{20,4},{24,8},{28,12},{1,17},{... | collective-permute-start | bytes 1572872 | tf_op jit(solution)/shard_map/ppermute | solution.py:430
  45.2 23.2 %collective-permute-start.15 = (bf16[128,2048]{1,0:T(8,128)(2,1)S(1)}, bf16[128,2048]{1,0:T(8,128)(2,1)S(1)}, u32[]{:S(2)}, u32[]{:S(2)}) collective-permute-start(bf16[128,2048]{1,0:T(8,128)(2,1)S(1)} %collective-permute-done.14.refs_12_.refs_11_.refs_21_), channel_id=1, source_target_pairs={{0,8},{4,12},{8,0},{12,4},{16,24},{20,28},{24,16},{28,20},{1,9},{5... | collective-permute-start | bytes 1572872 | tf_op jit(solution)/shard_map/ppermute | solution.py:430
  46.3 22.5 %collective-permute-start.17 = (bf16[128,2048]{1,0:T(8,128)(2,1)S(1)}, bf16[128,2048]{1,0:T(8,128)(2,1)S(1)}, u32[]{:S(2)}, u32[]{:S(2)}) collective-permute-start(bf16[128,2048]{1,0:T(8,128)(2,1)S(1)} %collective-permute-done.16.refs_13_.refs_12_.refs_22_), channel_id=1, source_target_pairs={{0,16},{4,20},{8,24},{12,28},{16,0},{20,4},{24,8},{28,12},{1,17},{... | collective-permute-start | bytes 1572872 | tf_op jit(solution)/shard_map/ppermute | solution.py:430
  57.2 14.5 %collective-permute-start.7 = (bf16[128,2048]{1,0:T(8,128)(2,1)}, bf16[128,2048]{1,0:T(8,128)(2,1)}, u32[]{:S(2)}, u32[]{:S(2)}) collective-permute-start(bf16[128,2048]{1,0:T(8,128)(2,1)} %collective-permute-done.2.refs_2_), channel_id=1, source_target_pairs={{0,4},{4,0},{8,12},{12,8},{16,20},{20,16},{24,28},{28,24},{1,5},{5... | collective-permute-start | bytes 1572872 | tf_op jit(solution)/shard_map/ppermute | solution.py:430
  60.6 49.9 %collective-permute-start = (bf16[128,2048]{1,0:T(8,128)(2,1)S(1)}, bf16[128,2048]{1,0:T(8,128)(2,1)}, u32[]{:S(2)}, u32[]{:S(2)}) collective-permute-start(bf16[128,2048]{1,0:T(8,128)(2,1)S(1)} %copy-done.59), channel_id=1, source_target_pairs={{0,8},{4,12},{8,0},{12,4},{16,24},{20,28},{24,16},{28,20},{1,9},{5... | collective-permute-start | bytes 1572872 | tf_op jit(solution)/shard_map/ppermute | solution.py:430
  68.5 43.4 %collective-permute-start.3 = (bf16[128,2048]{1,0:T(8,128)(2,1)}, bf16[128,2048]{1,0:T(8,128)(2,1)}, u32[]{:S(2)}, u32[]{:S(2)}) collective-permute-start(bf16[128,2048]{1,0:T(8,128)(2,1)} %get-tuple-element.96.refs_8_), channel_id=1, source_target_pairs={{0,16},{4,20},{8,24},{12,28},{16,0},{20,4},{24,8},{28,12},{1,17},{... | collective-permute-start | bytes 1572872 | tf_op jit(solution)/shard_map/ppermute | solution.py:430
  68.8 43.3 %collective-permute-start.12 = (bf16[128,2048]{1,0:T(8,128)(2,1)S(1)}, bf16[128,2048]{1,0:T(8,128)(2,1)}, u32[]{:S(2)}, u32[]{:S(2)}) collective-permute-start(bf16[128,2048]{1,0:T(8,128)(2,1)S(1)} %copy-done.59), channel_id=1, source_target_pairs={{0,4},{4,0},{8,12},{12,8},{16,20},{20,16},{24,28},{28,24},{1,5},{5... | collective-permute-start | bytes 1572872 | tf_op jit(solution)/shard_map/ppermute | solution.py:430
  71.8 40.6 %collective-permute-start.13 = (bf16[128,2048]{1,0:T(8,128)(2,1)}, bf16[128,2048]{1,0:T(8,128)(2,1)}, u32[]{:S(2)}, u32[]{:S(2)}) collective-permute-start(bf16[128,2048]{1,0:T(8,128)(2,1)} %get-tuple-element.96.refs_8_), channel_id=1, source_target_pairs={{0,4},{4,0},{8,12},{12,8},{16,20},{20,16},{24,28},{28,24},{1,5},{5... | collective-permute-start | bytes 1572872 | tf_op jit(solution)/shard_map/ppermute | solution.py:430
  110.6 15.4 %collective-permute-start.18 = (bf16[192,768]{1,0:T(8,128)(2,1)S(1)}, bf16[192,768]{1,0:T(8,128)(2,1)S(1)}, u32[]{:S(2)}, u32[]{:S(2)}) collective-permute-start(bf16[192,768]{1,0:T(8,128)(2,1)S(1)} %bitcast.99), channel_id=1, source_target_pairs={{0,8},{4,12},{8,0},{12,4},{16,24},{20,28},{24,16},{28,20},{1,9},{5... | collective-permute-start | bytes 884744 | tf_op jit(solution)/shard_map/ppermute | solution.py:430
  112.1 14.1 %collective-permute-start.21 = (bf16[192,768]{1,0:T(8,128)(2,1)S(1)}, bf16[192,768]{1,0:T(8,128)(2,1)}, u32[]{:S(2)}, u32[]{:S(2)}) collective-permute-start(bf16[192,768]{1,0:T(8,128)(2,1)S(1)} %bitcast.95), channel_id=1, source_target_pairs={{0,16},{4,20},{8,24},{12,28},{16,0},{20,4},{24,8},{28,12},{1,17},{... | collective-permute-start | bytes 884744 | tf_op jit(solution)/shard_map/ppermute | solution.py:430
  115.2 17.0 %collective-permute-start.30 = (bf16[192,768]{1,0:T(8,128)(2,1)S(1)}, bf16[192,768]{1,0:T(8,128)(2,1)S(1)}, u32[]{:S(2)}, u32[]{:S(2)}) collective-permute-start(bf16[192,768]{1,0:T(8,128)(2,1)S(1)} %bitcast.100), channel_id=1, source_target_pairs={{0,4},{4,0},{8,12},{12,8},{16,20},{20,16},{24,28},{28,24},{1,5},{5... | collective-permute-start | bytes 884744 | tf_op jit(solution)/shard_map/ppermute | solution.py:430
  117.3 15.0 %collective-permute-start.31 = (bf16[192,768]{1,0:T(8,128)(2,1)S(1)}, bf16[192,768]{1,0:T(8,128)(2,1)S(1)}, u32[]{:S(2)}, u32[]{:S(2)}) collective-permute-start(bf16[192,768]{1,0:T(8,128)(2,1)S(1)} %bitcast.96), channel_id=1, source_target_pairs={{0,4},{4,0},{8,12},{12,8},{16,20},{20,16},{24,28},{28,24},{1,5},{5... | collective-permute-start | bytes 884744 | tf_op jit(solution)/shard_map/ppermute | solution.py:430
  139.8 15.2 %collective-permute-start.34 = (bf16[384,768]{1,0:T(8,128)(2,1)}, bf16[384,768]{1,0:T(8,128)(2,1)}, u32[]{:S(2)}, u32[]{:S(2)}) collective-permute-start(bf16[384,768]{1,0:T(8,128)(2,1)} %shard_map.255.refs_7_), channel_id=1, source_target_pairs={{0,16},{4,20},{8,24},{12,28},{16,0},{20,4},{24,8},{28,12},{1,17},{... | collective-permute-start | bytes 1769480 | tf_op jit(solution)/shard_map/ppermute | solution.py:430
  148.4 30.7 %collective-permute-start.33 = (bf16[384,768]{1,0:T(8,128)(2,1)S(1)}, bf16[384,768]{1,0:T(8,128)(2,1)}, u32[]{:S(2)}, u32[]{:S(2)}) collective-permute-start(bf16[384,768]{1,0:T(8,128)(2,1)S(1)} %copy-done.37), channel_id=1, source_target_pairs={{0,8},{4,12},{8,0},{12,4},{16,24},{20,28},{24,16},{28,20},{1,9},{5... | collective-permute-start | bytes 1769480 | tf_op jit(solution)/shard_map/ppermute | solution.py:430
  148.8 29.8 %collective-permute-start.37 = (bf16[384,768]{1,0:T(8,128)(2,1)S(1)}, bf16[384,768]{1,0:T(8,128)(2,1)}, u32[]{:S(2)}, u32[]{:S(2)}) collective-permute-start(bf16[384,768]{1,0:T(8,128)(2,1)S(1)} %copy-done.34), channel_id=1, source_target_pairs={{0,8},{4,12},{8,0},{12,4},{16,24},{20,28},{24,16},{28,20},{1,9},{5... | collective-permute-start | bytes 1769480 | tf_op jit(solution)/shard_map/ppermute | solution.py:430
  150.0 29.4 %collective-permute-start.36 = (bf16[384,768]{1,0:T(8,128)(2,1)S(1)}, bf16[384,768]{1,0:T(8,128)(2,1)}, u32[]{:S(2)}, u32[]{:S(2)}) collective-permute-start(bf16[384,768]{1,0:T(8,128)(2,1)S(1)} %copy-done.34), channel_id=1, source_target_pairs={{0,16},{4,20},{8,24},{12,28},{16,0},{20,4},{24,8},{28,12},{1,17},{... | collective-permute-start | bytes 1769480 | tf_op jit(solution)/shard_map/ppermute | solution.py:430
  151.2 28.8 %collective-permute-start.45 = (bf16[384,768]{1,0:T(8,128)(2,1)S(1)}, bf16[384,768]{1,0:T(8,128)(2,1)S(1)}, u32[]{:S(2)}, u32[]{:S(2)}) collective-permute-start(bf16[384,768]{1,0:T(8,128)(2,1)S(1)} %copy-done.37), channel_id=1, source_target_pairs={{0,4},{4,0},{8,12},{12,8},{16,20},{20,16},{24,28},{28,24},{1,5},{5... | collective-permute-start | bytes 1769480 | tf_op jit(solution)/shard_map/ppermute | solution.py:430
  155.0 41.1 %collective-permute-start.46 = (bf16[384,768]{1,0:T(8,128)(2,1)S(1)}, bf16[384,768]{1,0:T(8,128)(2,1)S(1)}, u32[]{:S(2)}, u32[]{:S(2)}) collective-permute-start(bf16[384,768]{1,0:T(8,128)(2,1)S(1)} %copy-done.34), channel_id=1, source_target_pairs={{0,4},{4,0},{8,12},{12,8},{16,20},{20,16},{24,28},{28,24},{1,5},{5... | collective-permute-start | bytes 1769480 | tf_op jit(solution)/shard_map/ppermute | solution.py:430
  178.6 22.6 %collective-permute-start.35 = (bf16[384,768]{1,0:T(8,128)(2,1)}, bf16[384,768]{1,0:T(8,128)(2,1)}, u32[]{:S(2)}, u32[]{:S(2)}) collective-permute-start(bf16[384,768]{1,0:T(8,128)(2,1)} %collective-permute-done.34.refs_5_), channel_id=1, source_target_pairs={{0,8},{4,12},{8,0},{12,4},{16,24},{20,28},{24,16},{28,20},{1,9},{5... | collective-permute-start | bytes 1769480 | tf_op jit(solution)/shard_map/ppermute | solution.py:430
  179.1 22.2 %collective-permute-start.38 = (bf16[384,768]{1,0:T(8,128)(2,1)}, bf16[384,768]{1,0:T(8,128)(2,1)}, u32[]{:S(2)}, u32[]{:S(2)}) collective-permute-start(bf16[384,768]{1,0:T(8,128)(2,1)} %collective-permute-done.37.refs_6_), channel_id=1, source_target_pairs={{0,16},{4,20},{8,24},{12,28},{16,0},{20,4},{24,8},{28,12},{1,17},{... | collective-permute-start | bytes 1769480 | tf_op jit(solution)/shard_map/ppermute | solution.py:430
  179.4 22.4 %collective-permute-start.39 = (bf16[384,768]{1,0:T(8,128)(2,1)}, bf16[384,768]{1,0:T(8,128)(2,1)}, u32[]{:S(2)}, u32[]{:S(2)}) collective-permute-start(bf16[384,768]{1,0:T(8,128)(2,1)} %collective-permute-done.33.refs_1_), channel_id=1, source_target_pairs={{0,4},{4,0},{8,12},{12,8},{16,20},{20,16},{24,28},{28,24},{1,5},{5... | collective-permute-start | bytes 1769480 | tf_op jit(solution)/shard_map/ppermute | solution.py:430
  180.0 21.9 %collective-permute-start.41 = (bf16[384,768]{1,0:T(8,128)(2,1)}, bf16[384,768]{1,0:T(8,128)(2,1)}, u32[]{:S(2)}, u32[]{:S(2)}) collective-permute-start(bf16[384,768]{1,0:T(8,128)(2,1)} %collective-permute-done.36.refs_3_), channel_id=1, source_target_pairs={{0,4},{4,0},{8,12},{12,8},{16,20},{20,16},{24,28},{28,24},{1,5},{5... | collective-permute-start | bytes 1769480 | tf_op jit(solution)/shard_map/ppermute | solution.py:430
  196.9 26.2 %collective-permute-start.47 = (bf16[2048,256]{1,0:T(8,128)(2,1)}, bf16[2048,256]{1,0:T(8,128)(2,1)S(1)}, u32[]{:S(2)}, u32[]{:S(2)}) collective-permute-start(bf16[2048,256]{1,0:T(8,128)(2,1)} %get-tuple-element.99.refs_25_), channel_id=1, source_target_pairs={{0,4},{4,0},{8,12},{12,8},{16,20},{20,16},{24,28},{28,24},{1,5},{5... | collective-permute-start | bytes 3145736 | tf_op jit(solution)/shard_map/ppermute | solution.py:430
  197.4 15.5 %all-to-all-start = ((bf16[8,256,256]{2,1,0:T(8,128)(2,1)}), bf16[8,256,256]{2,1,0:T(8,128)(2,1)S(1)}, u32[]{:S(2)}, u32[]{:S(2)}) async-start(bf16[8,256,256]{2,1,0:T(8,128)(2,1)} %bitcast.93), calls=%async_computation | async-start | bytes 2097152 | tf_op jit(solution)/shard_map/all_to_all | solution.py:1262
  201.0 161.6 %all-gather.11.cloned.1.call-start = ((), (), s32[]{:S(2)}) async-start(), calls=%async_computation.5 | async-start | bytes 5242880 | tf_op jit(solution)/shard_map/all_gather | solution.py:1181
  234.9 15.7 %collective-permute-start.50 = (bf16[128,2048]{1,0:T(8,128)(2,1)}, bf16[128,2048]{1,0:T(8,128)(2,1)}, u32[]{:S(2)}, u32[]{:S(2)}) collective-permute-start(bf16[128,2048]{1,0:T(8,128)(2,1)} %get-tuple-element.107.refs_11_.refs_10_.refs_16_), channel_id=1, source_target_pairs={{0,8},{4,12},{8,0},{12,4},{16,24},{20,28},{24,16},{28,20},{1,9},{5... | collective-permute-start | bytes 1572872 | tf_op jit(solution)/shard_map/ppermute | solution.py:430
  237.2 50.4 %collective-permute-start.53 = (bf16[1024,2432]{1,0:T(8,128)(2,1)}, bf16[1024,2432]{1,0:T(8,128)(2,1)}, u32[]{:S(2)}, u32[]{:S(2)}) collective-permute-start(bf16[1024,2432]{1,0:T(8,128)(2,1)} %shard_map.261.refs_5_.refs_3_.refs_4_), channel_id=1, source_target_pairs={{0,4},{4,0},{8,12},{12,8},{16,20},{20,16},{24,28},{28,24},{1,5},{5... | collective-permute-start | bytes 14942216 | tf_op jit(solution)/shard_map/ppermute | solution.py:430
  244.1 37.2 %collective-permute-start.49 = (bf16[128,2048]{1,0:T(8,128)(2,1)}, bf16[128,2048]{1,0:T(8,128)(2,1)S(1)}, u32[]{:S(2)}, u32[]{:S(2)}) collective-permute-start(bf16[128,2048]{1,0:T(8,128)(2,1)} %collective-permute-done.48.refs_8_.refs_7_.refs_13_), channel_id=1, source_target_pairs={{0,8},{4,12},{8,0},{12,4},{16,24},{20,28},{24,16},{28,20},{1,9},{5... | collective-permute-start | bytes 1572872 | tf_op jit(solution)/shard_map/ppermute | solution.py:430
  250.6 30.7 %collective-permute-start.51 = (bf16[128,2048]{1,0:T(8,128)(2,1)}, bf16[128,2048]{1,0:T(8,128)(2,1)S(1)}, u32[]{:S(2)}, u32[]{:S(2)}) collective-permute-start(bf16[128,2048]{1,0:T(8,128)(2,1)} %collective-permute-done.50.refs_9_.refs_8_.refs_14_), channel_id=1, source_target_pairs={{0,16},{4,20},{8,24},{12,28},{16,0},{20,4},{24,8},{28,12},{1,17},{... | collective-permute-start | bytes 1572872 | tf_op jit(solution)/shard_map/ppermute | solution.py:430
  283.7 37.4 %collective-permute-start.56 = (bf16[128,2048]{1,0:T(8,128)(2,1)S(1)}, bf16[128,2048]{1,0:T(8,128)(2,1)S(1)}, u32[]{:S(2)}, u32[]{:S(2)}) collective-permute-start(bf16[128,2048]{1,0:T(8,128)(2,1)S(1)} %copy-done.50), channel_id=1, source_target_pairs={{0,8},{4,12},{8,0},{12,4},{16,24},{20,28},{24,16},{28,20},{1,9},{5... | collective-permute-start | bytes 1572872 | tf_op jit(solution)/shard_map/ppermute | solution.py:430
  285.0 36.1 %collective-permute-start.57 = (bf16[128,2048]{1,0:T(8,128)(2,1)S(1)}, bf16[128,2048]{1,0:T(8,128)(2,1)S(1)}, u32[]{:S(2)}, u32[]{:S(2)}) collective-permute-start(bf16[128,2048]{1,0:T(8,128)(2,1)S(1)} %copy-done.48), channel_id=1, source_target_pairs={{0,16},{4,20},{8,24},{12,28},{16,0},{20,4},{24,8},{28,12},{1,17},{... | collective-permute-start | bytes 1572872 | tf_op jit(solution)/shard_map/ppermute | solution.py:430
  287.3 33.8 %collective-permute-start.54 = (bf16[128,2048]{1,0:T(8,128)(2,1)S(1)}, bf16[128,2048]{1,0:T(8,128)(2,1)S(1)}, u32[]{:S(2)}, u32[]{:S(2)}) collective-permute-start(bf16[128,2048]{1,0:T(8,128)(2,1)S(1)} %copy-done.64), channel_id=1, source_target_pairs={{0,8},{4,12},{8,0},{12,4},{16,24},{20,28},{24,16},{28,20},{1,9},{5... | collective-permute-start | bytes 1572872 | tf_op jit(solution)/shard_map/ppermute | solution.py:430
  287.6 33.5 %collective-permute-start.55 = (bf16[128,2048]{1,0:T(8,128)(2,1)}, bf16[128,2048]{1,0:T(8,128)(2,1)}, u32[]{:S(2)}, u32[]{:S(2)}) collective-permute-start(bf16[128,2048]{1,0:T(8,128)(2,1)} %get-tuple-element.107.refs_11_.refs_10_.refs_16_), channel_id=1, source_target_pairs={{0,16},{4,20},{8,24},{12,28},{16,0},{20,4},{24,8},{28,12},{1,17},{... | collective-permute-start | bytes 1572872 | tf_op jit(solution)/shard_map/ppermute | solution.py:430
  362.6 14.4 %collective-permute-start.58 = (bf16[2048,1024]{1,0:T(8,128)(2,1)}, bf16[2048,1024]{1,0:T(8,128)(2,1)}, u32[]{:S(2)}, u32[]{:S(2)}) collective-permute-start(bf16[2048,1024]{1,0:T(8,128)(2,1)} %shard_map.266.refs_3_), channel_id=1, source_target_pairs={{0,4},{4,0},{8,12},{12,8},{16,20},{20,16},{24,28},{28,24},{1,5},{5... | collective-permute-start | bytes 12582920 | tf_op jit(solution)/shard_map/ppermute | solution.py:430
  390.4 27.9 %collective-permute-start.59 = (bf16[256,2304]{1,0:T(8,128)(2,1)}, bf16[256,2304]{1,0:T(8,128)(2,1)S(1)}, u32[]{:S(2)}, u32[]{:S(2)}) collective-permute-start(bf16[256,2304]{1,0:T(8,128)(2,1)} %get-tuple-element.124), channel_id=1, source_target_pairs={{0,8},{4,12},{8,0},{12,4},{16,24},{20,28},{24,16},{28,20},{1,9},{5... | collective-permute-start | bytes 3538952 | tf_op jit(solution)/shard_map/ppermute | solution.py:430
  391.7 27.5 %collective-permute-start.60 = (bf16[256,2304]{1,0:T(8,128)(2,1)}, bf16[256,2304]{1,0:T(8,128)(2,1)S(1)}, u32[]{:S(2)}, u32[]{:S(2)}) collective-permute-start(bf16[256,2304]{1,0:T(8,128)(2,1)} %get-tuple-element.125), channel_id=1, source_target_pairs={{0,16},{4,20},{8,24},{12,28},{16,0},{20,4},{24,8},{28,12},{1,17},{... | collective-permute-start | bytes 3538952 | tf_op jit(solution)/shard_map/ppermute | solution.py:430
  422.3 14.0 %collective-permute-start.61 = (bf16[128,2304]{1,0:T(8,128)(2,1)}, bf16[128,2304]{1,0:T(8,128)(2,1)S(1)}, u32[]{:S(2)}, u32[]{:S(2)}) collective-permute-start(bf16[128,2304]{1,0:T(8,128)(2,1)} %get-tuple-element.197.refs_6_), channel_id=1, source_target_pairs={{0,16},{4,20},{8,24},{12,28},{16,0},{20,4},{24,8},{28,12},{1,17},{... | collective-permute-start | bytes 1769480 | tf_op jit(solution)/shard_map/ppermute | solution.py:430
  423.6 13.4 %collective-permute-start.62 = (bf16[128,2304]{1,0:T(8,128)(2,1)S(1)}, bf16[128,2304]{1,0:T(8,128)(2,1)S(1)}, u32[]{:S(2)}, u32[]{:S(2)}) collective-permute-start(bf16[128,2304]{1,0:T(8,128)(2,1)S(1)} %get-tuple-element.196.refs_7_), channel_id=1, source_target_pairs={{0,8},{4,12},{8,0},{12,4},{16,24},{20,28},{24,16},{28,20},{1,9},{5... | collective-permute-start | bytes 1769480 | tf_op jit(solution)/shard_map/ppermute | solution.py:430
  437.8 32.9 %collective-permute-start.64 = (bf16[256,2176]{1,0:T(8,128)(2,1)}, bf16[256,2176]{1,0:T(8,128)(2,1)S(1)}, u32[]{:S(2)}, u32[]{:S(2)}) collective-permute-start(bf16[256,2176]{1,0:T(8,128)(2,1)} %shard_map.274), channel_id=1, source_target_pairs={{0,16},{4,20},{8,24},{12,28},{16,0},{20,4},{24,8},{28,12},{1,17},{... | collective-permute-start | bytes 3342344 | tf_op jit(solution)/shard_map/ppermute | solution.py:430
  438.5 32.2 %collective-permute-start.63 = (bf16[256,2176]{1,0:T(8,128)(2,1)}, bf16[256,2176]{1,0:T(8,128)(2,1)}, u32[]{:S(2)}, u32[]{:S(2)}) collective-permute-start(bf16[256,2176]{1,0:T(8,128)(2,1)} %shard_map.271.refs_13_), channel_id=1, source_target_pairs={{0,8},{4,12},{8,0},{12,4},{16,24},{20,28},{24,16},{28,20},{1,9},{5... | collective-permute-start | bytes 3342344 | tf_op jit(solution)/shard_map/ppermute | solution.py:430
  439.6 73.5 %collective-permute-start.68 = (bf16[2048,768]{1,0:T(8,128)(2,1)}, bf16[2048,768]{1,0:T(8,128)(2,1)}, u32[]{:S(2)}, u32[]{:S(2)}) collective-permute-start(bf16[2048,768]{1,0:T(8,128)(2,1)} %get-tuple-element.139.refs_3_), channel_id=1, source_target_pairs={{0,4},{4,0},{8,12},{12,8},{16,20},{20,16},{24,28},{28,24},{1,5},{5... | collective-permute-start | bytes 9437192 | tf_op jit(solution)/shard_map/ppermute | solution.py:430
  457.4 19.2 %all-to-all-start.1 = ((bf16[256,8,256]{2,0,1:T(8,128)(2,1)}), bf16[256,8,256]{2,0,1:T(8,128)(2,1)S(1)}, u32[]{:S(2)}, u32[]{:S(2)}) async-start(bf16[256,8,256]{2,0,1:T(8,128)(2,1)} %bitcast.68), calls=%async_computation.1 | async-start | bytes 2097152 | tf_op jit(solution)/shard_map/all_to_all | solution.py:1372
  474.0 30.6 %collective-permute-start.65 = (bf16[128,2176]{1,0:T(8,128)(2,1)}, bf16[128,2176]{1,0:T(8,128)(2,1)S(1)}, u32[]{:S(2)}, u32[]{:S(2)}) collective-permute-start(bf16[128,2176]{1,0:T(8,128)(2,1)} %get-tuple-element.201.refs_9_), channel_id=1, source_target_pairs={{0,16},{4,20},{8,24},{12,28},{16,0},{20,4},{24,8},{28,12},{1,17},{... | collective-permute-start | bytes 1671176 | tf_op jit(solution)/shard_map/ppermute | solution.py:430
  475.4 29.9 %collective-permute-start.66 = (bf16[128,2176]{1,0:T(8,128)(2,1)}, bf16[128,2176]{1,0:T(8,128)(2,1)}, u32[]{:S(2)}, u32[]{:S(2)}) collective-permute-start(bf16[128,2176]{1,0:T(8,128)(2,1)} %get-tuple-element.200.refs_10_), channel_id=1, source_target_pairs={{0,8},{4,12},{8,0},{12,4},{16,24},{20,28},{24,16},{28,20},{1,9},{5... | collective-permute-start | bytes 1671176 | tf_op jit(solution)/shard_map/ppermute | solution.py:430
  504.6 16.8 %collective-permute-start.70 = (bf16[256,640]{1,0:T(8,128)(2,1)}, bf16[256,640]{1,0:T(8,128)(2,1)S(1)}, u32[]{:S(2)}, u32[]{:S(2)}) collective-permute-start(bf16[256,640]{1,0:T(8,128)(2,1)} %shard_map.279), channel_id=1, source_target_pairs={{0,16},{4,20},{8,24},{12,28},{16,0},{20,4},{24,8},{28,12},{1,17},{... | collective-permute-start | bytes 983048 | tf_op jit(solution)/shard_map/ppermute | solution.py:430
  505.4 16.1 %collective-permute-start.69 = (bf16[256,640]{1,0:T(8,128)(2,1)}, bf16[256,640]{1,0:T(8,128)(2,1)S(1)}, u32[]{:S(2)}, u32[]{:S(2)}) collective-permute-start(bf16[256,640]{1,0:T(8,128)(2,1)} %shard_map.278), channel_id=1, source_target_pairs={{0,8},{4,12},{8,0},{12,4},{16,24},{20,28},{24,16},{28,20},{1,9},{5... | collective-permute-start | bytes 983048 | tf_op jit(solution)/shard_map/ppermute | solution.py:430
  512.5 17.6 %collective-permute-start.72 = (bf16[256,384]{1,0:T(8,128)(2,1)S(1)}, bf16[256,384]{1,0:T(8,128)(2,1)S(1)}, u32[]{:S(2)}, u32[]{:S(2)}) collective-permute-start(bf16[256,384]{1,0:T(8,128)(2,1)S(1)} %get-tuple-element.140.refs_5_), channel_id=1, source_target_pairs={{0,8},{4,12},{8,0},{12,4},{16,24},{20,28},{24,16},{28,20},{1,9},{5... | collective-permute-start | bytes 589832 | tf_op jit(solution)/shard_map/ppermute | solution.py:430
  513.1 17.0 %collective-permute-start.73 = (bf16[256,384]{1,0:T(8,128)(2,1)S(1)}, bf16[256,384]{1,0:T(8,128)(2,1)S(1)}, u32[]{:S(2)}, u32[]{:S(2)}) collective-permute-start(bf16[256,384]{1,0:T(8,128)(2,1)S(1)} %get-tuple-element.147), channel_id=1, source_target_pairs={{0,16},{4,20},{8,24},{12,28},{16,0},{20,4},{24,8},{28,12},{1,17},{... | collective-permute-start | bytes 589832 | tf_op jit(solution)/shard_map/ppermute | solution.py:430
  514.2 15.9 %collective-permute-start.74 = (bf16[256,384]{1,0:T(8,128)(2,1)S(1)}, bf16[256,384]{1,0:T(8,128)(2,1)S(1)}, u32[]{:S(2)}, u32[]{:S(2)}) collective-permute-start(bf16[256,384]{1,0:T(8,128)(2,1)S(1)} %get-tuple-element.148), channel_id=1, source_target_pairs={{0,24},{4,28},{8,16},{12,20},{16,8},{20,12},{24,0},{28,4},{1,25},{... | collective-permute-start | bytes 589832 | tf_op jit(solution)/shard_map/ppermute | solution.py:430
  541.9 25.5 %collective-permute-start.89 = (bf16[4,768,128]{2,1,0:T(8,128)(2,1)}, bf16[4,768,128]{2,1,0:T(8,128)(2,1)}, u32[]{:S(2)}, u32[]{:S(2)}) collective-permute-start(bf16[4,768,128]{2,1,0:T(8,128)(2,1)} %get-tuple-element.159.refs_8_), channel_id=1, source_target_pairs={{0,4},{4,0},{8,12},{12,8},{16,20},{20,16},{24,28},{28,24},{1,5},{5... | collective-permute-start | bytes 2359304 | tf_op jit(solution)/shard_map/ppermute | solution.py:430
  553.8 31.7 %collective-permute-start.78 = (bf16[256,2048]{1,0:T(8,128)(2,1)}, bf16[256,2048]{1,0:T(8,128)(2,1)S(1)}, u32[]{:S(2)}, u32[]{:S(2)}) collective-permute-start(bf16[256,2048]{1,0:T(8,128)(2,1)} %get-tuple-element.160.refs_36_), channel_id=1, source_target_pairs={{0,8},{4,12},{8,0},{12,4},{16,24},{20,28},{24,16},{28,20},{1,9},{5... | collective-permute-start | bytes 3145736 | tf_op jit(solution)/shard_map/ppermute | solution.py:430
  554.6 30.9 %collective-permute-start.79 = (bf16[256,2048]{1,0:T(8,128)(2,1)}, bf16[256,2048]{1,0:T(8,128)(2,1)S(1)}, u32[]{:S(2)}, u32[]{:S(2)}) collective-permute-start(bf16[256,2048]{1,0:T(8,128)(2,1)} %get-tuple-element.162), channel_id=1, source_target_pairs={{0,16},{4,20},{8,24},{12,28},{16,0},{20,4},{24,8},{28,12},{1,17},{... | collective-permute-start | bytes 3145736 | tf_op jit(solution)/shard_map/ppermute | solution.py:430
  576.6 17.1 %collective-permute-start.83 = (bf16[2,704,128]{2,1,0:T(8,128)(2,1)}, bf16[2,704,128]{2,1,0:T(8,128)(2,1)}, u32[]{:S(2)}, u32[]{:S(2)}) collective-permute-start(bf16[2,704,128]{2,1,0:T(8,128)(2,1)} %get-tuple-element.166), channel_id=1, source_target_pairs={{0,1},{1,0},{2,3},{3,2},{4,5},{5,4},{6,7},{7,6},{8,9},{9,8},{10,11... | collective-permute-start | bytes 1081352 | tf_op jit(solution)/shard_map/ppermute | solution.py:1384
  597.5 13.5 %collective-permute-start.92 = (bf16[768,128]{1,0:T(8,128)(2,1)}, bf16[768,128]{1,0:T(8,128)(2,1)}, u32[]{:S(2)}, u32[]{:S(2)}) collective-permute-start(bf16[768,128]{1,0:T(8,128)(2,1)} %fusion.8.refs_1_), channel_id=1, source_target_pairs={{0,8},{4,12},{8,0},{12,4},{16,24},{20,28},{24,16},{28,20},{1,9},{5... | collective-permute-start | bytes 589832 | tf_op jit(solution)/shard_map/ppermute | solution.py:430
  598.5 13.8 %collective-permute-start.93 = (bf16[768,128]{1,0:T(8,128)(2,1)}, bf16[768,128]{1,0:T(8,128)(2,1)}, u32[]{:S(2)}, u32[]{:S(2)}) collective-permute-start(bf16[768,128]{1,0:T(8,128)(2,1)} %fusion.8.refs_1_), channel_id=1, source_target_pairs={{0,16},{4,20},{8,24},{12,28},{16,0},{20,4},{24,8},{28,12},{1,17},{... | collective-permute-start | bytes 589832 | tf_op jit(solution)/shard_map/ppermute | solution.py:430
  599.0 13.2 %collective-permute-start.94 = (bf16[768,128]{1,0:T(8,128)(2,1)}, bf16[768,128]{1,0:T(8,128)(2,1)}, u32[]{:S(2)}, u32[]{:S(2)}) collective-permute-start(bf16[768,128]{1,0:T(8,128)(2,1)} %fusion.8.refs_1_), channel_id=1, source_target_pairs={{0,24},{4,28},{8,16},{12,20},{16,8},{20,12},{24,0},{28,4},{1,25},{... | collective-permute-start | bytes 589832 | tf_op jit(solution)/shard_map/ppermute | solution.py:430
  (116 other events, 1442.7 us)
Sparse Core Ops, SparseCore 0:
  12.0 94.8 all-gather.4
  108.4 92.1 all-gather.8
  202.2 79.0 all-gather.6
  283.8 78.7 all-gather.10
